TPU v7x, 32 devices: a whole 2x2x4 slice. The times are simulated.
32 devices in a mesh: groups: 2 (over x), segment: 2 (over core), block: 8 (over z, y).
Axes of the slice: x: 2, y: 2, z: 4, core: 2. Of those that a mesh axis runs over, the one named last changes fastest.
Arguments:
- tokens: float32 [1024, 16384], P(('groups', 'segment'), 'block'), parts along dimension 0, may hold values from -32 to 32
- gains: float32 [2, 2, 16384], P('segment', None, 'block'), may hold values from 0.1 to 1.9
- right_factors: float32 [2, 2, 128, 128, 128], P('segment', None, 'block'), may hold values from -0.5 to 0.5
- left_factors: float32 [2, 2, 128, 128, 128], P('segment', None, 'block'), may hold values from -0.5 to 0.5
Outputs:
- output: float32 [1024, 16384], P(('groups', 'segment'), 'block'), parts along dimension 0
There are 2 independent parts, one for each index of `groups`. A program takes and returns all parts, laid end to end along the dimension named above; an argument that names none is the same for every part. Nothing has to cross between parts.
All inputs are finite; a program needn't handle non-finite values.
Results may differ from a plain program's by a relative error of at most 0.0003.
Values sent between devices are 32-bit elements; how exact they have to be, the bound alone decides.
No kernel may reach another device: no remote copies, remote signals or barrier semaphores. Data moves between devices by JAX's collectives and lax.ppermute only.
A program may use at most 64 MiB of HBM per device.

v0:
```python
import jax
import jax.numpy as jnp
from jax import lax
from jax.sharding import PartitionSpec as P

D = 16384


epsilon = 1e-06
exact = lax.Precision.HIGHEST


def shifted(block, axis, distance):
    devices = range(lax.axis_size(axis))
    route = [((i - distance) % len(devices), i) for i in devices]
    return lax.ppermute(block, axis, route)


def apply_layer(current, gain_row, right_part, left_part):
    blocks_here = right_part.shape[0]
    block_size = right_part.shape[1]
    width_here, token_count = current.shape
    partial_squares = jnp.sum(current * current, axis=0)
    sum_squares = lax.psum(partial_squares, "block")
    normed = current * lax.rsqrt(sum_squares / D + epsilon)[None, :] * gain_row[:, None]
    inner = jnp.einsum(
        "bit,bij->bjt",
        normed.reshape(blocks_here, block_size, token_count),
        right_part,
        precision=exact,
    )
    combined = jnp.einsum(
        "bjt,jbc->cjt",
        lax.all_to_all(inner, "block", split_axis=1, concat_axis=0, tiled=True),
        left_part,
        precision=exact,
    )
    mixed = lax.all_to_all(combined, "block", split_axis=0, concat_axis=1, tiled=True)
    return current + mixed.reshape(width_here, token_count) * jax.nn.silu(normed)


def body(tokens, gains, right_factors, left_factors):
    current = tokens.T
    rounds = right_factors.shape[1]
    layer_count = 2 * rounds
    segment_index = lax.axis_index("segment")
    for moment in range(layer_count + 1):
        holding = jnp.remainder(moment - segment_index, 2)
        layer_index = moment - holding
        active = (layer_index >= 0) & (layer_index < layer_count)
        round_index = jnp.clip(layer_index // 2, 0, rounds - 1)
        gain_row = lax.dynamic_index_in_dim(gains[0], round_index, 0, keepdims=False)
        right_part = lax.dynamic_index_in_dim(right_factors[0], round_index, 0, keepdims=False)
        left_part = lax.dynamic_index_in_dim(left_factors[0], round_index, 0, keepdims=False)
        updated = apply_layer(current, gain_row, right_part, left_part)
        current = jnp.where(active, updated, current)
        if moment < layer_count:
            current = shifted(current, "segment", 1)
    return current.T


def solution(mesh):
    placed = (
        P(("groups", "segment"), "block"),
        P("segment", None, "block"),
        P("segment", None, "block", None, None),
        P("segment", None, "block", None, None),
    )
    return jax.shard_map(
        body,
        mesh=mesh,
        in_specs=placed,
        out_specs=P(("groups", "segment"), "block"),
        check_vma=False,
    )
```

profile of v0, /device:TPU:0, one launch (start us, length us, event | category | flops | bytes accessed | tf_op | source)
XLA Modules:
  0.0 698.1 jit_solution(2861334446131708136)
XLA Ops:
  0.0 3.0 copy.79
  3.0 1.9 fusion.1
  4.9 23.1 %psum.35 = f32[256]{0:T(256)S(1)} all-reduce(f32[256]{0:T(256)S(1)} %fusion.1), channel_id=1, replica_groups=mesh['groups'=2,'segment'=2,'block'=8] {'block'}, use_global_device_ids=true, to_apply=%region_1.2 | all-reduce | flops 256 | bytes 2048 | tf_op jit(solution)/shard_map/psum | solution.py:24
  28.1 1.9 fusion.2
  30.1 2.0 fusion.16
  32.0 1.2 copy.82
  33.3 47.2 %all_to_all.165 = f32[16,128,256]{2,0,1:T(8,128)S(1)} all-to-all(f32[16,128,256]{2,0,1:T(8,128)S(1)} %copy.82), channel_id=1, replica_groups=mesh['groups'=2,'segment'=2,'block'=8] {'block'}, dimensions={1} | all-to-all | bytes 4194304 | tf_op jit(solution)/shard_map/all_to_all | solution.py:34
  80.7 1.3 copy-done.10
  82.1 2.1 convolution_bitcast_fusion.4
  84.1 2.5 copy.84
  86.6 4.3 all-to-all-start.1
  91.0 46.6 %all-to-all-done.1 = f32[128,16,256]{2,1,0:T(8,128)} async-done(((f32[128,16,256]{2,1,0:T(8,128)}), f32[128,16,256]{2,1,0:T(8,128)}, u32[]{:S(2)}, u32[]{:S(2)}) %all-to-all-start.1) | async-done | bytes 2097184 | tf_op jit(solution)/shard_map/all_to_all | solution.py:38
  137.6 1.9 copy.85
  140.8 4.1 collective-permute-done
  144.9 1.3 copy-done.4
  146.5 19.5 %psum.36 = f32[256]{0:T(256)S(1)} all-reduce(f32[256]{0:T(256)S(1)} %multiply_reduce_fusion.3), channel_id=1, replica_groups=mesh['groups'=2,'segment'=2,'block'=8] {'block'}, use_global_device_ids=true, to_apply=%region_3.4 | all-reduce | flops 256 | bytes 2048 | tf_op jit(solution)/shard_map/psum | solution.py:24
  166.0 1.9 multiply_multiply_fusion.3
  167.9 2.0 fusion.13
  169.9 1.2 copy.88
  171.1 47.5 %all_to_all.166 = f32[16,128,256]{2,0,1:T(8,128)S(1)} all-to-all(f32[16,128,256]{2,0,1:T(8,128)S(1)} %copy.88), channel_id=1, replica_groups=mesh['groups'=2,'segment'=2,'block'=8] {'block'}, dimensions={1} | all-to-all | bytes 4194304 | tf_op jit(solution)/shard_map/all_to_all | solution.py:34
  218.9 1.3 copy-done.11
  220.3 2.1 convolution_bitcast_fusion.3
  222.3 2.5 copy.90
  224.8 4.3 all-to-all-start.3
  229.2 46.6 %all-to-all-done.3 = f32[128,16,256]{2,1,0:T(8,128)} async-done(((f32[128,16,256]{2,1,0:T(8,128)}), f32[128,16,256]{2,1,0:T(8,128)}, u32[]{:S(2)}, u32[]{:S(2)}) %all-to-all-start.3) | async-done | bytes 2097184 | tf_op jit(solution)/shard_map/all_to_all | solution.py:38
  275.8 1.9 copy.91
  279.0 4.1 collective-permute-done.1
  283.1 1.3 copy-done.6
  284.7 19.7 %psum.37 = f32[256]{0:T(256)S(1)} all-reduce(f32[256]{0:T(256)S(1)} %multiply_reduce_fusion.2), channel_id=1, replica_groups=mesh['groups'=2,'segment'=2,'block'=8] {'block'}, use_global_device_ids=true, to_apply=%region_5.6 | all-reduce | flops 256 | bytes 2048 | tf_op jit(solution)/shard_map/psum | solution.py:24
  304.4 1.9 multiply_multiply_fusion.2
  306.3 2.0 fusion.10
  309.5 47.5 %all_to_all.167 = f32[16,128,256]{2,0,1:T(8,128)S(1)} all-to-all(f32[16,128,256]{2,0,1:T(8,128)S(1)} %copy.94), channel_id=1, replica_groups=mesh['groups'=2,'segment'=2,'block'=8] {'block'}, dimensions={1} | all-to-all | bytes 4194304 | tf_op jit(solution)/shard_map/all_to_all | solution.py:34
  357.3 1.3 copy-done.12
  358.6 2.1 convolution_bitcast_fusion.2
  360.7 2.5 copy.96
  363.2 4.3 all-to-all-start.5
  367.6 46.6 %all-to-all-done.5 = f32[128,16,256]{2,1,0:T(8,128)} async-done(((f32[128,16,256]{2,1,0:T(8,128)}), f32[128,16,256]{2,1,0:T(8,128)}, u32[]{:S(2)}, u32[]{:S(2)}) %all-to-all-start.5) | async-done | bytes 2097184 | tf_op jit(solution)/shard_map/all_to_all | solution.py:38
  414.2 1.9 copy.97
  417.3 4.1 collective-permute-done.2
  421.5 1.3 copy-done.8
  423.1 19.4 %psum.38 = f32[256]{0:T(256)S(1)} all-reduce(f32[256]{0:T(256)S(1)} %multiply_reduce_fusion.1), channel_id=1, replica_groups=mesh['groups'=2,'segment'=2,'block'=8] {'block'}, use_global_device_ids=true, to_apply=%region_7.8 | all-reduce | flops 256 | bytes 2048 | tf_op jit(solution)/shard_map/psum | solution.py:24
  442.5 1.9 multiply_multiply_fusion.1
  444.5 2.0 fusion.7
  447.7 47.5 %all_to_all.168 = f32[16,128,256]{2,0,1:T(8,128)S(1)} all-to-all(f32[16,128,256]{2,0,1:T(8,128)S(1)} %copy.100), channel_id=1, replica_groups=mesh['groups'=2,'segment'=2,'block'=8] {'block'}, dimensions={1} | all-to-all | bytes 4194304 | tf_op jit(solution)/shard_map/all_to_all | solution.py:34
  495.4 1.3 copy-done.13
  496.8 2.1 convolution_bitcast_fusion.1
  498.9 2.5 copy.102
  501.4 4.3 all-to-all-start.7
  505.7 46.6 %all-to-all-done.7 = f32[128,16,256]{2,1,0:T(8,128)} async-done(((f32[128,16,256]{2,1,0:T(8,128)}), f32[128,16,256]{2,1,0:T(8,128)}, u32[]{:S(2)}, u32[]{:S(2)}) %all-to-all-start.7) | async-done | bytes 2097184 | tf_op jit(solution)/shard_map/all_to_all | solution.py:38
  552.3 1.9 copy.103
  555.5 4.1 collective-permute-done.3
  559.6 1.3 copy-done.2
  561.3 19.5 %psum.39 = f32[256]{0:T(256)S(1)} all-reduce(f32[256]{0:T(256)S(1)} %multiply_reduce_fusion), channel_id=1, replica_groups=mesh['groups'=2,'segment'=2,'block'=8] {'block'}, use_global_device_ids=true, to_apply=%region_9.10 | all-reduce | flops 256 | bytes 2048 | tf_op jit(solution)/shard_map/psum | solution.py:24
  580.7 1.9 multiply_multiply_fusion
  582.7 2.0 fusion.4
  585.9 47.5 %all_to_all.169 = f32[16,128,256]{2,0,1:T(8,128)S(1)} all-to-all(f32[16,128,256]{2,0,1:T(8,128)S(1)} %copy.106), channel_id=1, replica_groups=mesh['groups'=2,'segment'=2,'block'=8] {'block'}, dimensions={1} | all-to-all | bytes 4194304 | tf_op jit(solution)/shard_map/all_to_all | solution.py:34
  633.6 1.3 copy-done.14
  635.0 2.1 convolution_bitcast_fusion
  637.0 2.5 copy.108
  639.6 4.3 all-to-all-start.9
  643.9 46.6 %all-to-all-done.9 = f32[128,16,256]{2,1,0:T(8,128)} async-done(((f32[128,16,256]{2,1,0:T(8,128)}), f32[128,16,256]{2,1,0:T(8,128)}, u32[]{:S(2)}, u32[]{:S(2)}) %all-to-all-start.9) | async-done | bytes 2097184 | tf_op jit(solution)/shard_map/all_to_all | solution.py:38
  690.5 1.9 copy.109
  692.7 2.2 fusion
  694.9 2.9 copy.110
  (49 shorter events, 11.3 us)
Async XLA Ops:
  0.0 30.0 %copy-start = (f32[1,2,16,128,128]{4,3,2,1,0:T(8,128)S(1)}, f32[1,2,16,128,128]{4,3,2,1,0:T(8,128)}, u32[]{:S(2)}) copy-start(f32[1,2,16,128,128]{4,3,2,1,0:T(8,128)} %param.6) | copy-start | bytes 6291460
  3.0 25.0 %copy-start.15 = (f32[1,2,2048]{2,1,0:T(2,128)S(1)}, f32[1,2,2048]{2,1,0:T(2,128)}, u32[]{:S(2)}) copy-start(f32[1,2,2048]{2,1,0:T(2,128)} %param.5) | copy-start | bytes 49156
  80.5 1.6 copy-start.10
  86.6 51.0 %all-to-all-start.1 = ((f32[128,16,256]{2,1,0:T(8,128)}), f32[128,16,256]{2,1,0:T(8,128)}, u32[]{:S(2)}, u32[]{:S(2)}) async-start(f32[128,16,256]{2,1,0:T(8,128)} %copy.84), calls=%async_computation.1 | async-start | bytes 4194304 | tf_op jit(solution)/shard_map/all_to_all | solution.py:38
  137.6 2.2 copy-start.1
  140.7 4.2 collective-permute-start
  144.9 1.3 copy-start.4
  218.7 1.6 copy-start.11
  224.8 51.0 %all-to-all-start.3 = ((f32[128,16,256]{2,1,0:T(8,128)}), f32[128,16,256]{2,1,0:T(8,128)}, u32[]{:S(2)}, u32[]{:S(2)}) async-start(f32[128,16,256]{2,1,0:T(8,128)} %copy.90), calls=%async_computation.3 | async-start | bytes 4194304 | tf_op jit(solution)/shard_map/all_to_all | solution.py:38
  275.8 2.2 copy-start.5
  278.9 4.2 collective-permute-start.1
  283.1 1.3 copy-start.6
  357.0 1.6 copy-start.12
  363.2 51.0 %all-to-all-start.5 = ((f32[128,16,256]{2,1,0:T(8,128)}), f32[128,16,256]{2,1,0:T(8,128)}, u32[]{:S(2)}, u32[]{:S(2)}) async-start(f32[128,16,256]{2,1,0:T(8,128)} %copy.96), calls=%async_computation.5 | async-start | bytes 4194304 | tf_op jit(solution)/shard_map/all_to_all | solution.py:38
  414.2 2.2 copy-start.7
  417.3 4.2 collective-permute-start.2
  421.5 1.3 copy-start.8
  495.2 1.6 copy-start.13
  501.4 51.0 %all-to-all-start.7 = ((f32[128,16,256]{2,1,0:T(8,128)}), f32[128,16,256]{2,1,0:T(8,128)}, u32[]{:S(2)}, u32[]{:S(2)}) async-start(f32[128,16,256]{2,1,0:T(8,128)} %copy.102), calls=%async_computation.7 | async-start | bytes 4194304 | tf_op jit(solution)/shard_map/all_to_all | solution.py:38
  552.3 2.2 copy-start.9
  555.4 4.2 collective-permute-start.3
  559.6 1.3 copy-start.2
  633.4 1.6 copy-start.14
  639.6 51.0 %all-to-all-start.9 = ((f32[128,16,256]{2,1,0:T(8,128)}), f32[128,16,256]{2,1,0:T(8,128)}, u32[]{:S(2)}, u32[]{:S(2)}) async-start(f32[128,16,256]{2,1,0:T(8,128)} %copy.108), calls=%async_computation.9 | async-start | bytes 4194304 | tf_op jit(solution)/shard_map/all_to_all | solution.py:38
  690.5 2.2 copy-start.3
where the time goes:
time: 706 us; the launch traced here: 698 us
  blocking collectives  338 us (48%)
  waiting for transfers between devices  250 us (35%)
  local copies, waits for them, and re-layouts  48.9 us (7%)
  starting transfers between devices  22 us (3%)
  matrix products  20.2 us (3%)
  other arithmetic  18.4 us (3%)
    all_to_all x5, blocking collectives, apply_layer(): lax.all_to_all(inner, 'block', split_axis=1, concat_axis=0, tiled=True)  237 us
    all_to_all x5, waiting for transfers between devices, apply_layer(): lax.all_to_all(combined, 'block', split_axis=0, concat_axis=1, tiled=True)  233 us
    psum x5, blocking collectives, apply_layer(): sum_squares = lax.psum(partial_squares, 'block')  101 us
    all_to_all x5, starting transfers between devices, apply_layer(): lax.all_to_all(combined, 'block', split_axis=0, concat_axis=1, tiled=True)  21.7 us
    ppermute x4, waiting for transfers between devices, shifted(): return lax.ppermute(block, axis, route)  16.6 us
    unnamed x33, local copies, waits for them, and re-layouts  16.5 us
  transfers between devices with their start and end apart: 9, of which 9 were waited for; matrix products, arithmetic and copies ran while one was open for 0% of the time, Pallas kernels for 0%

commit v1 on v0

v1 whole, which is shorter than its diff:
```python
import functools

import jax
import jax.numpy as jnp
from jax import lax
from jax.experimental import pallas as pl
from jax.experimental.pallas import tpu as pltpu
from jax.sharding import PartitionSpec as P

epsilon = 1e-06
exact = lax.Precision.HIGHEST
LANES = 128
ROWS = 8
PLANES = 4
QUARTERS = 4
CHUNKS = 2


def row_offset(step, mate, plane, quarter):
    start = ((plane + step) % PLANES) * (QUARTERS * ROWS) + (quarter ^ mate) * ROWS
    return pl.ds(pl.multiple_of(start, ROWS), ROWS)


def product(weight, value):
    return lax.dot_general(
        weight, value, (((0,), (0,)), ((), ())), precision=exact, preferred_element_type=jnp.float32
    )


def pick(parts, index, group):
    if len(parts) == 1:
        return parts[0][index]
    half = index // 4
    inside = index - half * 4
    return jnp.where(half == group, parts[0][inside], parts[1][inside])


def layer_edge_kernel(width, has_mix, has_next, place, *refs):
    refs = list(refs)

    def take(count):
        head = refs[:count]
        del refs[:count]
        return head

    plane, quarter, group = place[0], place[1], place[2]
    current = take(PLANES)
    if has_mix:
        old_gain = take(PLANES)
        squares_in = take(QUARTERS)
        mixed = [take(QUARTERS) for _ in range(CHUNKS)]
    if has_next:
        gain = take(PLANES)
        weights = [take(1 if step == 0 else 2) for step in range(PLANES)]
    fresh = take(PLANES) if has_mix else current
    if has_next:
        send = [take(QUARTERS) for _ in range(CHUNKS)]
        square_ref, tile = take(2)
        square_ref[...] = jnp.zeros_like(square_ref)
    per_chunk = PLANES // CHUNKS

    if has_mix:
        total = sum(ref[pl.ds(512, ROWS), :] for ref in squares_in)
        scale = lax.rsqrt(jnp.sum(total, axis=0, keepdims=True) / width + epsilon)
        for step in range(PLANES):

            @pl.loop(0, ROWS)
            def _(index, step=step):
                for other in range(PLANES):
                    for mate in range(QUARTERS):
                        where = row_offset(other, mate, plane, quarter)
                        value = current[step][index, where, :]
                        block = (other % per_chunk) * 32 + step * ROWS + index
                        start = pl.multiple_of(block * ROWS, ROWS)
                        mix = mixed[other // per_chunk][mate][pl.ds(start, ROWS), :]
                        normed = value * scale * old_gain[step][index, where, :]
                        value = value + (mix * scale) * (normed / (1.0 + jnp.exp(-normed)))
                        fresh[step][index, where, :] = value

    if has_next:
        for step in range(PLANES):

            @pl.loop(0, ROWS)
            def _(index, step=step):
                value = fresh[step][index]
                square_ref[...] += jnp.sum((value * value).reshape(16, ROWS, LANES), axis=0)
                weight = pick(weights[step], index, group)
                tile[index] = product(weight, value * gain[step][index])
                for other in range(PLANES):
                    for mate in range(QUARTERS):
                        block = (other % per_chunk) * 32 + step * ROWS + index
                        start = pl.multiple_of(block * ROWS, ROWS)
                        send[other // per_chunk][mate][pl.ds(start, ROWS), :] = tile[
                            index, row_offset(other, mate, plane, quarter), :
                        ]

        for mate in range(QUARTERS):
            send[0][mate][pl.ds(512, ROWS), :] = square_ref[...]


def column_kernel(chunk, place, *refs):
    refs = list(refs)

    def take(count):
        head = refs[:count]
        del refs[:count]
        return head

    plane, quarter, group = place[0], place[1], place[2]
    per_chunk = PLANES // CHUNKS
    came = take(QUARTERS)
    weights = [take(1 if chunk * per_chunk + n == 0 else 2) for n in range(per_chunk)]
    send = take(QUARTERS)
    value, tile = take(2)
    for n in range(per_chunk):

        @pl.loop(0, ROWS)
        def _(index, n=n):
            for step in range(PLANES):
                for mate in range(QUARTERS):
                    start = (n * 32 + step * ROWS) * ROWS + index
                    value[index, row_offset(step, mate, plane, quarter), :] = came[mate][
                        pl.ds(start, ROWS, stride=ROWS), :
                    ]
            tile[index] = product(pick(weights[n], index, group), value[index])
            for step in range(PLANES):
                for mate in range(QUARTERS):
                    start = (n * 32 + step * ROWS) * ROWS + index
                    send[mate][pl.ds(start, ROWS, stride=ROWS), :] = tile[
                        index, row_offset(step, mate, plane, quarter), :
                    ]


SMALL = pl.BlockSpec(memory_space=pltpu.SMEM)
WHOLE = pl.BlockSpec(memory_space=pltpu.VMEM)
PARAMS = pltpu.CompilerParams(vmem_limit_bytes=40 * 1024 * 1024)


def array(*shape):
    return jax.ShapeDtypeStruct(shape, jnp.float32)


def call(kernel, operands, outs, scratch, flops):
    moved = 4 * (sum(a.size for a in operands) + sum(o.size for o in outs))
    return pl.pallas_call(
        kernel,
        out_shape=outs,
        in_specs=[SMALL] + [WHOLE] * (len(operands) - 1),
        out_specs=[WHOLE] * len(outs),
        scratch_shapes=scratch,
        compiler_params=PARAMS,
        cost_estimate=pl.CostEstimate(flops=flops, bytes_accessed=moved, transcendentals=0),
    )(*operands)


PIECE = (ROWS, LANES, LANES)
STAGE_FLOPS = 2 * 32 * LANES * LANES * LANES


def layer_edge(width, place, current, mix=None, following=None):
    operands = [place, *current]
    outs, scratch = [], []
    if mix is not None:
        old_gain, squares, mixed = mix
        operands += [*old_gain, *squares, *mixed[0], *mixed[1]]
        outs += [array(*PIECE)] * PLANES
    if following is not None:
        gain, weights = following
        operands += [*gain, *(part for parts in weights for part in parts)]
        outs += [array(520, LANES)] * QUARTERS + [array(512, LANES)] * QUARTERS
        scratch = [pltpu.VMEM((ROWS, LANES), jnp.float32), pltpu.VMEM(PIECE, jnp.float32)]
    kernel = functools.partial(layer_edge_kernel, width, mix is not None, following is not None)
    results = list(call(kernel, operands, outs, scratch, 6 * STAGE_FLOPS))
    fresh = current
    if mix is not None:
        fresh, results = results[:PLANES], results[PLANES:]
    return fresh, [results[:QUARTERS], results[QUARTERS:]]


def column_stage(chunk, place, came, weights):
    operands = [place, *came, *(part for parts in weights for part in parts)]
    scratch = [pltpu.VMEM(PIECE, jnp.float32)] * 2
    outs = [array(512, LANES)] * QUARTERS
    return call(functools.partial(column_kernel, chunk), operands, outs, scratch, 3 * STAGE_FLOPS)


def routed(value, to):
    route = []
    for core in range(2):
        for z in range(PLANES):
            for y in range(2):
                there = to(core, z, y)
                route.append((core * 8 + z * 2 + y, there[0] * 8 + there[1] * 2 + there[2]))
    return lax.ppermute(value, ("segment", "block"), route)


def core_swap(value):
    return routed(value, lambda core, z, y: (1 - core, z, y))


def ring(value, distance):
    return routed(value, lambda core, z, y: (core, (z + distance) % PLANES, y))


def to_mate(value, mate):
    return routed(value, lambda core, z, y: (core ^ (mate & 1), z, y ^ (mate >> 1)))


def group_swap(value):
    return lax.ppermute(value, "groups", [(0, 1), (1, 0)])


def exchange(chunk):
    return [chunk[0]] + [to_mate(chunk[mate], mate) for mate in range(1, QUARTERS)]


def plane_body(tokens, gains, right_factors, left_factors):
    core = lax.axis_index("segment")
    block = lax.axis_index("block")
    group = lax.axis_index("groups")
    z, y = block // 2, block % 2
    place = jnp.stack([z, y * 2 + core, group]).astype(jnp.int32)
    rounds = right_factors.shape[1]
    layers = 2 * rounds
    width = right_factors.shape[3] * 8 * right_factors.shape[2]

    folded = tokens.reshape(2, LANES, 2, ROWS, LANES).transpose(2, 0, 3, 4, 1)
    mine = lax.dynamic_index_in_dim(folded, core, 0, keepdims=False)
    theirs = core_swap(lax.dynamic_index_in_dim(folded, 1 - core, 0, keepdims=False))
    four = jnp.stack([mine, theirs]).reshape((4,) + PIECE)
    current = []
    for step in range(PLANES):
        plane = (z - step) % PLANES
        slot = (plane // 2 ^ core) * 2 + plane % 2
        piece = lax.dynamic_index_in_dim(four, slot, 0, keepdims=False)
        current.append(piece if step == 0 else ring(piece, -step))

    mine = lax.dynamic_slice_in_dim(gains[0].reshape(rounds, 2 * ROWS, LANES), core * ROWS, ROWS, 1)
    theirs = core_swap(lax.dynamic_slice_in_dim(gains[0].reshape(rounds, 2 * ROWS, LANES), (1 - core) * ROWS, ROWS, 1))
    first = jnp.where(core == 0, mine, theirs)
    second = jnp.where(core == 0, theirs, mine)
    held = jnp.stack([first, second], axis=1).reshape(layers, ROWS, LANES)
    gain_pieces = []
    for step in range(PLANES):
        gain_pieces.append(held)
        if step < PLANES - 1:
            held = ring(held, -1)
    gain = [
        [jnp.broadcast_to(piece[layer][:, :, None], PIECE) for piece in gain_pieces] for layer in range(layers)
    ]

    def gathered(factors):
        found = [None] * layers
        for r in range(rounds):
            mine = lax.dynamic_slice_in_dim(factors[0, r], core * ROWS, ROWS, 0)
            theirs = core_swap(lax.dynamic_slice_in_dim(factors[0, r], (1 - core) * ROWS, ROWS, 0))
            found[2 * r] = jnp.where(core == 0, mine, theirs)
            found[2 * r + 1] = jnp.where(core == 0, theirs, mine)
        pieces = []
        for layer in range(layers):
            parts = [(found[layer],)]
            half = lax.dynamic_slice_in_dim(found[layer], group * 4, 4, 0)
            for _ in range(PLANES - 1):
                half = ring(half, -1)
                parts.append((half, group_swap(half)))
            pieces.append(parts)
        return pieces

    right = gathered(right_factors)
    left = gathered(left_factors)

    _, sends = layer_edge(width, place, current, None, (gain[0], right[0]))
    for layer in range(layers):
        came = [exchange(sends[0]), exchange(sends[1])]
        mixed = []
        for chunk in range(CHUNKS):
            weights = left[layer][chunk * 2 : chunk * 2 + 2]
            mixed.append(exchange(column_stage(chunk, place, came[chunk], weights)))
        following = (gain[layer + 1], right[layer + 1]) if layer + 1 < layers else None
        current, sends = layer_edge(width, place, current, (gain[layer], came[0], mixed), following)

    back = [None] * PLANES
    for step in range(PLANES):
        back[step] = current[step] if step == 0 else ring(current[step], step)
    stacked = jnp.stack(back)
    ordered = jnp.stack([lax.dynamic_index_in_dim(stacked, (z - p) % PLANES, 0, keepdims=False) for p in range(PLANES)])
    ordered = ordered.reshape((2, 2) + PIECE)
    mine = lax.dynamic_index_in_dim(ordered, core, 0, keepdims=False)
    theirs = core_swap(lax.dynamic_index_in_dim(ordered, 1 - core, 0, keepdims=False))
    both = jnp.stack([jnp.where(core == 0, mine, theirs), jnp.where(core == 0, theirs, mine)])
    return both.transpose(1, 4, 0, 2, 3).reshape(tokens.shape)


def wide_body(tokens, gains, right_factors, left_factors):
    blocks_here, block_size = right_factors.shape[2:4]
    token_count, width_here = tokens.shape
    width = width_here * lax.axis_size("block")
    rounds = right_factors.shape[1]
    core = lax.axis_index("segment")
    count = lax.axis_size("segment")

    def gathered(value):
        return lax.all_gather(value[0], "segment", axis=0)

    gains, right_factors, left_factors = gathered(gains), gathered(right_factors), gathered(left_factors)
    current = tokens.T
    for layer in range(count * rounds):
        s, r = layer % count, layer // count
        sum_squares = lax.psum(jnp.sum(current * current, axis=0), "block")
        normed = current * lax.rsqrt(sum_squares / width + epsilon)[None, :] * gains[s, r][:, None]
        inner = jnp.einsum(
            "bit,bij->bjt",
            normed.reshape(blocks_here, block_size, token_count),
            right_factors[s, r],
            precision=exact,
        )
        combined = jnp.einsum(
            "bjt,jbc->cjt",
            lax.all_to_all(inner, "block", split_axis=1, concat_axis=0, tiled=True),
            left_factors[s, r],
            precision=exact,
        )
        mixed = lax.all_to_all(combined, "block", split_axis=0, concat_axis=1, tiled=True)
        current = current + mixed.reshape(width_here, token_count) * jax.nn.silu(normed)
    return current.T


def solution(mesh):
    placed = (
        P(("groups", "segment"), "block"),
        P("segment", None, "block"),
        P("segment", None, "block", None, None),
        P("segment", None, "block", None, None),
    )
    planes = dict(mesh.shape) == {"groups": 2, "segment": 2, "block": 8}

    def body(tokens, gains, right_factors, left_factors):
        fits = planes and tokens.shape == (256, 2048) and right_factors.shape[2:] == (16, 128, 128)
        return (plane_body if fits else wide_body)(tokens, gains, right_factors, left_factors)

    return jax.shard_map(
        body,
        mesh=mesh,
        in_specs=placed,
        out_specs=P(("groups", "segment"), "block"),
        check_vma=False,
    )
```

time: 706 us -> 488 us (0.69)
  blocking collectives: 338 us -> 0 us
  starting transfers between devices: 22 us -> 159 us
  Pallas kernels: 0 us -> 91.3 us
  waiting for transfers between devices: 250 us -> 190 us
  local copies, waits for them, and re-layouts: 48.9 us -> 27.8 us
  matrix products: 20.2 us -> 0 us
  other arithmetic: 18.4 us -> 8.92 us
    all_to_all x5 -> x0, blocking collectives: 237 us -> none  [apply_layer(): lax.all_to_all(inner, 'block', split_axis=1, concat_axis=0, tiled=True)]
    all_to_all x5 -> x0, waiting for transfers between devices: 233 us -> none  [apply_layer(): lax.all_to_all(combined, 'block', split_axis=0, concat_axis=1, tiled=True)]
    ppermute x4 -> x112, waiting for transfers between devices: 16.6 us -> 190 us  [the longest x88 190 us: routed(): return lax.ppermute(value, ('segment', 'block'), route)]
    ppermute x4 -> x112, starting transfers between devices: 0.28 us -> 159 us  [the longest x88 133 us: routed(): return lax.ppermute(value, ('segment', 'block'), route)]
    psum x5 -> x0, blocking collectives: 101 us -> none  [apply_layer(): sum_squares = lax.psum(partial_squares, 'block')]
    pallas_call x0 -> x13, Pallas kernels: none -> 91.3 us  [call(): pl.pallas_call(kernel, out_shape=outs, in_specs=[SMALL] + [WHOLE] * (len(...]
    all_to_all x5 -> x0, starting transfers between devices: 21.7 us -> none  [apply_layer(): lax.all_to_all(combined, 'block', split_axis=0, concat_axis=1, tiled=True)]
    dot_general x10 -> x0, matrix products: 20.2 us -> none  [the longest x5 10.3 us: apply_layer(): jnp.einsum('bjt,jbc->cjt', lax.all_to_all(inner, 'block', split_axis=1, c...]
  transfers between devices with their start and end apart: 9 -> 112, of which waited for: 9 -> 42; matrix products, arithmetic and copies ran while one was open for 0% -> 5% of each run, Pallas kernels for 0% -> 19%
where the time goes in v1:
time: 488 us; the launch traced here: 478 us
  waiting for transfers between devices  190 us (39%)
  starting transfers between devices  159 us (33%)
  Pallas kernels  91.3 us (19%)
  local copies, waits for them, and re-layouts  27.8 us (6%)
  other arithmetic  8.92 us (2%)
    ppermute x88, waiting for transfers between devices, routed(): return lax.ppermute(value, ('segment', 'block'), route)  190 us
    ppermute x88, starting transfers between devices, routed(): return lax.ppermute(value, ('segment', 'block'), route)  133 us
    pallas_call x13, Pallas kernels, call(): pl.pallas_call(kernel, out_shape=outs, in_specs=[SMALL] + [WHOLE] * (len(...  91.3 us
    ppermute x24, starting transfers between devices, group_swap(): return lax.ppermute(value, 'groups', [(0, 1), (1, 0)])  26 us
  transfers between devices with their start and end apart: 112, of which 42 were waited for; matrix products, arithmetic and copies ran while one was open for 5% of the time, Pallas kernels for 19%

profile of v1, /device:TPU:0, one launch (start us, length us, event | category | flops | bytes accessed | tf_op | source)
XLA Modules:
  0.0 478.0 jit_solution(12645756036129865271)
XLA Ops:
  8.8 5.0 %collective-permute-start.5 = (f32[4,8,128]{2,1,0:T(8,128)S(1)}, f32[4,8,128]{2,1,0:T(8,128)S(1)}, u32[]{:S(2)}, u32[]{:S(2)}) collective-permute-start(f32[4,8,128]{2,1,0:T(8,128)S(1)} %bitcast.116), channel_id=1, source_target_pairs={{0,6},{1,7},{2,0},{3,1},{4,2},{5,3},{6,4},{7,5},{8,14},{9,15},{10,... | collective-permute-start | bytes 49160 | tf_op jit(solution)/shard_map/ppermute | solution.py:194
  15.3 4.1 collective-permute-start.6
  20.8 4.1 collective-permute-start.7
  30.1 4.1 collective-permute-start.43
  37.3 3.8 collective-permute-done.19.refs_5_
  42.9 3.7 collective-permute-done.34.refs_25_
  49.2 3.2 collective-permute-done.43.refs_5_
  54.2 3.7 collective-permute-done.59.refs_25_
  59.7 3.8 collective-permute-done.69.refs_5_
  65.0 4.1 collective-permute-done.84.refs_25_
  70.9 3.8 collective-permute-done.93.refs_5_
  78.1 2.4 collective-permute-done.11.refs_11_
  83.8 2.3 collective-permute-done.27.refs_4_
  87.6 3.0 pad_maximum_fusion
  90.6 2.9 copy.13
  99.7 3.2 collective-permute-done.13.refs_13_
  103.0 3.8 collective-permute-start.29
  107.3 32.6 %collective-permute-done.29.refs_6_ = f32[4,128,128]{2,1,0:T(8,128)S(1)} collective-permute-done((f32[4,128,128]{2,1,0:T(8,128)}, f32[4,128,128]{2,1,0:T(8,128)S(1)}, u32[]{:S(2)}, u32[]{:S(2)}) %collective-permute-start.29) | collective-permute-done | bytes 262176 | tf_op jit(solution)/shard_map/ppermute | solution.py:194
  139.8 4.2 collective-permute-start.61
  147.4 5.8 %collective-permute-start.38 = (f32[4,128,128]{2,1,0:T(8,128)}, f32[4,128,128]{2,1,0:T(8,128)S(1)}, u32[]{:S(2)}, u32[]{:S(2)}) collective-permute-start(f32[4,128,128]{2,1,0:T(8,128)} %collective-permute-done.36.refs_27_), channel_id=1, source_target_pairs={{0,6},{1,7},{2,0},{3,1},{4,2},{5,3},{6,4},{7,5},{8,14},{9,15},{10,... | collective-permute-start | bytes 786440 | tf_op jit(solution)/shard_map/ppermute | solution.py:194
  155.5 10.2 %shard_map.46 = (f32[520,128]{1,0:T(8,128)S(1)}, f32[520,128]{1,0:T(8,128)S(1)}, f32[520,128]{1,0:T(8,128)S(1)}, f32[520,128]{1,0:T(8,128)S(1)}, f32[512,128]{1,...) custom-call(s32[3]{0:T(128)S(1)} %pad_add_fusion.place, ...), custom_call_target="tpu_custom_call" | custom-call | flops 805306368 | bytes 8405004 | tf_op jit(solution)/shard_map/pallas_call | solution.py:145
  167.7 2.5 collective-permute-done.38.refs_29_
  172.1 2.9 collective-permute-done.25.refs_2_
  175.6 4.2 collective-permute-done.26.refs_3_
  179.8 13.4 %collective-permute-start.53 = (f32[4,128,128]{2,1,0:T(8,128)}, f32[4,128,128]{2,1,0:T(8,128)S(1)}, u32[]{:S(2)}, u32[]{:S(2)}) collective-permute-start(f32[4,128,128]{2,1,0:T(8,128)} %collective-permute-done.51.refs_4_), channel_id=1, source_target_pairs={{0,6},{1,7},{2,0},{3,1},{4,2},{5,3},{6,4},{7,5},{8,14},{9,15},{10,... | collective-permute-start | bytes 786440 | tf_op jit(solution)/shard_map/ppermute | solution.py:194
  193.2 5.5 %shard_map.48 = (f32[512,128]{1,0:T(8,128)S(1)}, f32[512,128]{1,0:T(8,128)S(1)}, f32[512,128]{1,0:T(8,128)S(1)}, f32[512,128]{1,0:T(8,128)S(1)}) custom-call(s32[3]{0:T(128)S(1)} %pad_add_fusion.place, f32[512,128]{1,0:T(8,128)S(1)} %get-tuple-element.93.refs_0_, f32[512,128]{1,0:T(8,128)S(1)} %collective-permute-done.24.refs_1_, ...), custom_call_target="tpu_custom_call" | custom-call | flops 402653184 | bytes 3145740 | tf_op jit(solution)/shard_map/pallas_call | solution.py:145
  201.6 5.6 %shard_map.47 = (f32[512,128]{1,0:T(8,128)S(1)}, f32[512,128]{1,0:T(8,128)S(1)}, f32[512,128]{1,0:T(8,128)S(1)}, f32[512,128]{1,0:T(8,128)S(1)}) custom-call(s32[3]{0:T(128)S(1)} %pad_add_fusion.place, f32[520,128]{1,0:T(8,128)S(1)} %get-tuple-element.85.refs_0_.refs_8_, f32[520,128]{1,0:T(8,128)S(1)} %collective-permute-done.15.refs_1_.refs_9_, ...), custom_call_target="tpu_custom_call" | custom-call | flops 402653184 | bytes 3162124 | tf_op jit(solution)/shard_map/pallas_call | solution.py:145
  209.5 4.7 collective-permute-start.77
  215.9 4.2 collective-permute-start.86
  221.5 5.0 %collective-permute-start.63 = (f32[4,128,128]{2,1,0:T(8,128)S(1)}, f32[4,128,128]{2,1,0:T(8,128)S(1)}, u32[]{:S(2)}, u32[]{:S(2)}) collective-permute-start(f32[4,128,128]{2,1,0:T(8,128)S(1)} %collective-permute-done.61.refs_27_), channel_id=1, source_target_pairs={{0,6},{1,7},{2,0},{3,1},{4,2},{5,3},{6,4},{7,5},{8,14},{9,15},{10,... | collective-permute-start | bytes 786440 | tf_op jit(solution)/shard_map/ppermute | solution.py:194
  230.7 12.2 %shard_map.49 = (f32[8,128,128]{2,1,0:T(8,128)S(1)}, f32[8,128,128]{2,1,0:T(8,128)S(1)}, f32[8,128,128]{2,1,0:T(8,128)S(1)}, f32[8,128,128]{2,1,0:T(8,128)S(1)},...) custom-call(s32[3]{0:T(128)S(1)} %pad_add_fusion.place, ...), custom_call_target="tpu_custom_call" | custom-call | flops 805306368 | bytes 15761420 | tf_op jit(solution)/shard_map/pallas_call | solution.py:145
  246.7 5.4 %collective-permute-done.49.refs_2_ = f32[512,128]{1,0:T(8,128)S(1)} collective-permute-done((f32[512,128]{1,0:T(8,128)S(1)}, f32[512,128]{1,0:T(8,128)S(1)}, u32[]{:S(2)}, u32[]{:S(2)}) %collective-permute-start.49) | collective-permute-done | bytes 262176 | tf_op jit(solution)/shard_map/ppermute | solution.py:194
  253.0 3.9 collective-permute-done.50.refs_3_
  256.9 3.8 collective-permute-start.79
  260.7 5.5 %shard_map.51 = (f32[512,128]{1,0:T(8,128)S(1)}, f32[512,128]{1,0:T(8,128)S(1)}, f32[512,128]{1,0:T(8,128)S(1)}, f32[512,128]{1,0:T(8,128)S(1)}) custom-call(s32[3]{0:T(128)S(1)} %pad_add_fusion.place, f32[512,128]{1,0:T(8,128)S(1)} %get-tuple-element.113.refs_0_, f32[512,128]{1,0:T(8,128)S(1)} %collective-permute-done.48.refs_1_, ...), custom_call_target="tpu_custom_call" | custom-call | flops 402653184 | bytes 3145740 | tf_op jit(solution)/shard_map/pallas_call | solution.py:145
  268.7 5.6 %shard_map.50 = (f32[512,128]{1,0:T(8,128)S(1)}, f32[512,128]{1,0:T(8,128)S(1)}, f32[512,128]{1,0:T(8,128)S(1)}, f32[512,128]{1,0:T(8,128)S(1)}) custom-call(s32[3]{0:T(128)S(1)} %pad_add_fusion.place, f32[520,128]{1,0:T(8,128)S(1)} %get-tuple-element.105.refs_0_.refs_8_, f32[520,128]{1,0:T(8,128)S(1)} %collective-permute-done.40.refs_1_.refs_9_, ...), custom_call_target="tpu_custom_call" | custom-call | flops 402653184 | bytes 3162124 | tf_op jit(solution)/shard_map/pallas_call | solution.py:145
  278.4 4.4 collective-permute-done.57.refs_19_
  282.8 3.8 collective-permute-start.101
  288.8 4.2 collective-permute-start.88
  297.3 12.1 %shard_map.52 = (f32[8,128,128]{2,1,0:T(8,128)S(1)}, f32[8,128,128]{2,1,0:T(8,128)S(1)}, f32[8,128,128]{2,1,0:T(8,128)S(1)}, f32[8,128,128]{2,1,0:T(8,128)S(1)},...) custom-call(s32[3]{0:T(128)S(1)} %pad_add_fusion.place, ...), custom_call_target="tpu_custom_call" | custom-call | flops 805306368 | bytes 15761420 | tf_op jit(solution)/shard_map/pallas_call | solution.py:145
  313.5 5.7 %collective-permute-done.75.refs_2_ = f32[512,128]{1,0:T(8,128)S(1)} collective-permute-done((f32[512,128]{1,0:T(8,128)S(1)}, f32[512,128]{1,0:T(8,128)S(1)}, u32[]{:S(2)}, u32[]{:S(2)}) %collective-permute-start.75) | collective-permute-done | bytes 262176 | tf_op jit(solution)/shard_map/ppermute | solution.py:194
  320.3 3.5 collective-permute-done.76.refs_3_
  325.1 3.7 collective-permute-start.103
  328.8 5.1 %shard_map.54 = (f32[512,128]{1,0:T(8,128)S(1)}, f32[512,128]{1,0:T(8,128)S(1)}, f32[512,128]{1,0:T(8,128)S(1)}, f32[512,128]{1,0:T(8,128)S(1)}) custom-call(s32[3]{0:T(128)S(1)} %pad_add_fusion.place, f32[512,128]{1,0:T(8,128)S(1)} %get-tuple-element.133.refs_0_, f32[512,128]{1,0:T(8,128)S(1)} %collective-permute-done.74.refs_1_, ...), custom_call_target="tpu_custom_call" | custom-call | flops 402653184 | bytes 3145740 | tf_op jit(solution)/shard_map/pallas_call | solution.py:145
  335.4 5.1 %shard_map.53 = (f32[512,128]{1,0:T(8,128)S(1)}, f32[512,128]{1,0:T(8,128)S(1)}, f32[512,128]{1,0:T(8,128)S(1)}, f32[512,128]{1,0:T(8,128)S(1)}) custom-call(s32[3]{0:T(128)S(1)} %pad_add_fusion.place, f32[520,128]{1,0:T(8,128)S(1)} %get-tuple-element.125.refs_0_.refs_8_, f32[520,128]{1,0:T(8,128)S(1)} %collective-permute-done.65.refs_1_.refs_9_, ...), custom_call_target="tpu_custom_call" | custom-call | flops 402653184 | bytes 3162124 | tf_op jit(solution)/shard_map/pallas_call | solution.py:145
  344.3 5.4 %collective-permute-done.82.refs_18_ = f32[512,128]{1,0:T(8,128)S(1)} collective-permute-done((f32[512,128]{1,0:T(8,128)S(1)}, f32[512,128]{1,0:T(8,128)S(1)}, u32[]{:S(2)}, u32[]{:S(2)}) %collective-permute-start.82) | collective-permute-done | bytes 262176 | tf_op jit(solution)/shard_map/ppermute | solution.py:194
  350.6 3.8 collective-permute-done.83.refs_19_
  355.4 5.5 %collective-permute-done.72.refs_14_ = f32[512,128]{1,0:T(8,128)S(1)} collective-permute-done((f32[512,128]{1,0:T(8,128)S(1)}, f32[512,128]{1,0:T(8,128)S(1)}, u32[]{:S(2)}, u32[]{:S(2)}) %collective-permute-start.72) | collective-permute-done | bytes 262176 | tf_op jit(solution)/shard_map/ppermute | solution.py:194
  360.9 4.3 collective-permute-done.73.refs_15_
  367.7 12.1 %shard_map.55 = (f32[8,128,128]{2,1,0:T(8,128)S(1)}, f32[8,128,128]{2,1,0:T(8,128)S(1)}, f32[8,128,128]{2,1,0:T(8,128)S(1)}, f32[8,128,128]{2,1,0:T(8,128)S(1)},...) custom-call(s32[3]{0:T(128)S(1)} %pad_add_fusion.place, ...), custom_call_target="tpu_custom_call" | custom-call | flops 805306368 | bytes 15761420 | tf_op jit(solution)/shard_map/pallas_call | solution.py:145
  383.5 4.4 collective-permute-done.100.refs_3_
  390.8 3.9 collective-permute-done.99.refs_2_
  394.7 5.1 %shard_map.57 = (f32[512,128]{1,0:T(8,128)S(1)}, f32[512,128]{1,0:T(8,128)S(1)}, f32[512,128]{1,0:T(8,128)S(1)}, f32[512,128]{1,0:T(8,128)S(1)}) custom-call(s32[3]{0:T(128)S(1)} %pad_add_fusion.place, f32[512,128]{1,0:T(8,128)S(1)} %get-tuple-element.153.refs_0_, f32[512,128]{1,0:T(8,128)S(1)} %collective-permute-done.98.refs_1_, ...), custom_call_target="tpu_custom_call" | custom-call | flops 402653184 | bytes 3145740 | tf_op jit(solution)/shard_map/pallas_call | solution.py:145
  401.7 3.2 collective-permute-done.92.refs_3_.refs_11_
  404.9 5.1 %shard_map.56 = (f32[512,128]{1,0:T(8,128)S(1)}, f32[512,128]{1,0:T(8,128)S(1)}, f32[512,128]{1,0:T(8,128)S(1)}, f32[512,128]{1,0:T(8,128)S(1)}) custom-call(s32[3]{0:T(128)S(1)} %pad_add_fusion.place, f32[520,128]{1,0:T(8,128)S(1)} %get-tuple-element.145.refs_0_.refs_8_, f32[520,128]{1,0:T(8,128)S(1)} %collective-permute-done.90.refs_1_.refs_9_, ...), custom_call_target="tpu_custom_call" | custom-call | flops 402653184 | bytes 3162124 | tf_op jit(solution)/shard_map/pallas_call | solution.py:145
  412.5 3.7 collective-permute-done.107.refs_19_
  416.2 6.8 %collective-permute-done.96.refs_14_ = f32[512,128]{1,0:T(8,128)S(1)} collective-permute-done((f32[512,128]{1,0:T(8,128)S(1)}, f32[512,128]{1,0:T(8,128)S(1)}, u32[]{:S(2)}, u32[]{:S(2)}) %collective-permute-start.96) | collective-permute-done | bytes 262176 | tf_op jit(solution)/shard_map/ppermute | solution.py:194
  422.9 4.4 collective-permute-done.97.refs_15_
  427.4 2.2 shard_map.58
  429.6 4.3 collective-permute-start.109
  434.5 11.9 %collective-permute-done.108 = f32[8,128,128]{2,1,0:T(8,128)S(1)} collective-permute-done((f32[8,128,128]{2,1,0:T(8,128)S(1)}, f32[8,128,128]{2,1,0:T(8,128)S(1)}, u32[]{:S(2)}, u32[]{:S(2)}) %collective-permute-start.108) | collective-permute-done | bytes 524320 | tf_op jit(solution)/shard_map/ppermute | solution.py:194
  446.3 22.2 %collective-permute-done.109 = f32[8,128,128]{2,1,0:T(8,128)S(1)} collective-permute-done((f32[8,128,128]{2,1,0:T(8,128)S(1)}, f32[8,128,128]{2,1,0:T(8,128)S(1)}, u32[]{:S(2)}, u32[]{:S(2)}) %collective-permute-start.109) | collective-permute-done | bytes 524320 | tf_op jit(solution)/shard_map/ppermute | solution.py:194
  470.3 2.6 collective-permute-done.111
  475.3 2.7 reshape.43
  (272 shorter events, 117.5 us)
Async XLA Ops:
  3.4 72.8 %collective-permute-start = (f32[2,8,128,128]{2,1,3,0:T(8,128)}, f32[2,8,128,128]{2,1,3,0:T(8,128)}, u32[]{:S(2)}, u32[]{:S(2)}) collective-permute-start(f32[2,8,128,128]{2,1,3,0:T(8,128)} %get-tuple-element.180), channel_id=1, source_target_pairs={{0,8},{1,9},{2,10},{3,11},{4,12},{5,13},{6,14},{7,15},{8,0},{9,1},... | collective-permute-start | bytes 3145736 | tf_op jit(solution)/shard_map/ppermute | solution.py:194
  8.6 17.6 %collective-permute-start.18 = (f32[8,128,128]{2,1,0:T(8,128)S(1)}, f32[8,128,128]{2,1,0:T(8,128)}, u32[]{:S(2)}, u32[]{:S(2)}) collective-permute-start(f32[8,128,128]{2,1,0:T(8,128)S(1)} %dynamic-slice_bitcast_fusion.5), channel_id=1, source_target_pairs={{0,8},{1,9},{2,10},{3,11},{4,12},{5,13},{6,14},{7,15},{8,0},{9,1},... | collective-permute-start | bytes 1572872 | tf_op jit(solution)/shard_map/ppermute | solution.py:194
  29.4 17.3 %collective-permute-start.34 = (f32[4,128,128]{2,1,0:T(8,128)S(1)}, f32[4,128,128]{2,1,0:T(8,128)S(1)}, u32[]{:S(2)}, u32[]{:S(2)}) collective-permute-start(f32[4,128,128]{2,1,0:T(8,128)S(1)} %constant_dynamic-slice_fusion.9), channel_id=1, source_target_pairs={{0,6},{1,7},{2,0},{3,1},{4,2},{5,3},{6,4},{7,5},{8,14},{9,15},{10,... | collective-permute-start | bytes 786440 | tf_op jit(solution)/shard_map/ppermute | solution.py:194
  30.1 22.4 %collective-permute-start.43 = (f32[4,128,128]{2,1,0:T(8,128)S(1)}, f32[4,128,128]{2,1,0:T(8,128)}, u32[]{:S(2)}, u32[]{:S(2)}) collective-permute-start(f32[4,128,128]{2,1,0:T(8,128)S(1)} %constant_dynamic-slice_fusion.8), channel_id=1, source_target_pairs={{0,6},{1,7},{2,0},{3,1},{4,2},{5,3},{6,4},{7,5},{8,14},{9,15},{10,... | collective-permute-start | bytes 786440 | tf_op jit(solution)/shard_map/ppermute | solution.py:194
  35.6 22.4 %collective-permute-start.59 = (f32[4,128,128]{2,1,0:T(8,128)S(1)}, f32[4,128,128]{2,1,0:T(8,128)S(1)}, u32[]{:S(2)}, u32[]{:S(2)}) collective-permute-start(f32[4,128,128]{2,1,0:T(8,128)S(1)} %constant_dynamic-slice_fusion.7), channel_id=1, source_target_pairs={{0,6},{1,7},{2,0},{3,1},{4,2},{5,3},{6,4},{7,5},{8,14},{9,15},{10,... | collective-permute-start | bytes 786440 | tf_op jit(solution)/shard_map/ppermute | solution.py:194
  41.2 22.4 %collective-permute-start.69 = (f32[4,128,128]{2,1,0:T(8,128)S(1)}, f32[4,128,128]{2,1,0:T(8,128)S(1)}, u32[]{:S(2)}, u32[]{:S(2)}) collective-permute-start(f32[4,128,128]{2,1,0:T(8,128)S(1)} %constant_dynamic-slice_fusion.6), channel_id=1, source_target_pairs={{0,6},{1,7},{2,0},{3,1},{4,2},{5,3},{6,4},{7,5},{8,14},{9,15},{10,... | collective-permute-start | bytes 786440 | tf_op jit(solution)/shard_map/ppermute | solution.py:194
  46.7 22.5 %collective-permute-start.84 = (f32[4,128,128]{2,1,0:T(8,128)S(1)}, f32[4,128,128]{2,1,0:T(8,128)S(1)}, u32[]{:S(2)}, u32[]{:S(2)}) collective-permute-start(f32[4,128,128]{2,1,0:T(8,128)S(1)} %constant_dynamic-slice_fusion.5), channel_id=1, source_target_pairs={{0,6},{1,7},{2,0},{3,1},{4,2},{5,3},{6,4},{7,5},{8,14},{9,15},{10,... | collective-permute-start | bytes 786440 | tf_op jit(solution)/shard_map/ppermute | solution.py:194
  52.4 22.4 %collective-permute-start.93 = (f32[4,128,128]{2,1,0:T(8,128)}, f32[4,128,128]{2,1,0:T(8,128)S(1)}, u32[]{:S(2)}, u32[]{:S(2)}) collective-permute-start(f32[4,128,128]{2,1,0:T(8,128)} %constant_dynamic-slice_fusion.4), channel_id=1, source_target_pairs={{0,6},{1,7},{2,0},{3,1},{4,2},{5,3},{6,4},{7,5},{8,14},{9,15},{10,... | collective-permute-start | bytes 786440 | tf_op jit(solution)/shard_map/ppermute | solution.py:194
  57.9 22.6 %collective-permute-start.11 = (f32[4,128,128]{2,1,0:T(8,128)}, f32[4,128,128]{2,1,0:T(8,128)}, u32[]{:S(2)}, u32[]{:S(2)}) collective-permute-start(f32[4,128,128]{2,1,0:T(8,128)} %collective-permute-done.9.refs_9_), channel_id=1, source_target_pairs={{0,6},{1,7},{2,0},{3,1},{4,2},{5,3},{6,4},{7,5},{8,14},{9,15},{10,... | collective-permute-start | bytes 786440 | tf_op jit(solution)/shard_map/ppermute | solution.py:194
  63.5 18.5 %collective-permute-start.10 = (f32[4,128,128]{2,1,0:T(8,128)}, f32[4,128,128]{2,1,0:T(8,128)}, u32[]{:S(2)}, u32[]{:S(2)}) collective-permute-start(f32[4,128,128]{2,1,0:T(8,128)} %collective-permute-done.9.refs_9_), channel_id=1, source_target_pairs={{0,16},{16,0},{1,17},{17,1},{2,18},{18,2},{3,19},{19,3},{4,20},{20... | collective-permute-start | bytes 786440 | tf_op jit(solution)/shard_map/ppermute | solution.py:210
  69.2 17.0 %collective-permute-start.27 = (f32[4,128,128]{2,1,0:T(8,128)}, f32[4,128,128]{2,1,0:T(8,128)}, u32[]{:S(2)}, u32[]{:S(2)}) collective-permute-start(f32[4,128,128]{2,1,0:T(8,128)} %collective-permute-done.19.refs_5_), channel_id=1, source_target_pairs={{0,6},{1,7},{2,0},{3,1},{4,2},{5,3},{6,4},{7,5},{8,14},{9,15},{10,... | collective-permute-start | bytes 786440 | tf_op jit(solution)/shard_map/ppermute | solution.py:194
  74.8 18.7 %collective-permute-start.20 = (f32[4,128,128]{2,1,0:T(8,128)}, f32[4,128,128]{2,1,0:T(8,128)}, u32[]{:S(2)}, u32[]{:S(2)}) collective-permute-start(f32[4,128,128]{2,1,0:T(8,128)} %collective-permute-done.19.refs_5_), channel_id=1, source_target_pairs={{0,16},{16,0},{1,17},{17,1},{2,18},{18,2},{3,19},{19,3},{4,20},{20... | collective-permute-start | bytes 786440 | tf_op jit(solution)/shard_map/ppermute | solution.py:210
  76.3 19.0 %collective-permute-start.36 = (f32[4,128,128]{2,1,0:T(8,128)}, f32[4,128,128]{2,1,0:T(8,128)}, u32[]{:S(2)}, u32[]{:S(2)}) collective-permute-start(f32[4,128,128]{2,1,0:T(8,128)} %copy-done.8), channel_id=1, source_target_pairs={{0,6},{1,7},{2,0},{3,1},{4,2},{5,3},{6,4},{7,5},{8,14},{9,15},{10,... | collective-permute-start | bytes 786440 | tf_op jit(solution)/shard_map/ppermute | solution.py:194
  80.5 17.1 %collective-permute-start.35 = (f32[4,128,128]{2,1,0:T(8,128)}, f32[4,128,128]{2,1,0:T(8,128)}, u32[]{:S(2)}, u32[]{:S(2)}) collective-permute-start(f32[4,128,128]{2,1,0:T(8,128)} %copy-done.8), channel_id=1, source_target_pairs={{0,16},{16,0},{1,17},{17,1},{2,18},{18,2},{3,19},{19,3},{4,20},{20... | collective-permute-start | bytes 786440 | tf_op jit(solution)/shard_map/ppermute | solution.py:210
  82.0 15.7 %collective-permute-start.51 = (f32[4,128,128]{2,1,0:T(8,128)}, f32[4,128,128]{2,1,0:T(8,128)}, u32[]{:S(2)}, u32[]{:S(2)}) collective-permute-start(f32[4,128,128]{2,1,0:T(8,128)} %collective-permute-done.43.refs_5_), channel_id=1, source_target_pairs={{0,6},{1,7},{2,0},{3,1},{4,2},{5,3},{6,4},{7,5},{8,14},{9,15},{10,... | collective-permute-start | bytes 786440 | tf_op jit(solution)/shard_map/ppermute | solution.py:194
  97.6 46.5 %collective-permute-start.1 = (f32[8,128,128]{2,1,0:T(8,128)S(1)}, f32[8,128,128]{2,1,0:T(8,128)S(1)}, u32[]{:S(2)}, u32[]{:S(2)}) collective-permute-start(f32[8,128,128]{2,1,0:T(8,128)S(1)} %get-tuple-element.177), channel_id=1, source_target_pairs={{0,6},{1,7},{2,0},{3,1},{4,2},{5,3},{6,4},{7,5},{8,14},{9,15},{10,... | collective-permute-start | bytes 1572872 | tf_op jit(solution)/shard_map/ppermute | solution.py:194
  97.7 48.4 %collective-permute-start.2 = (f32[8,128,128]{2,1,0:T(8,128)S(1)}, f32[8,128,128]{2,1,0:T(8,128)S(1)}, u32[]{:S(2)}, u32[]{:S(2)}) collective-permute-start(f32[8,128,128]{2,1,0:T(8,128)S(1)} %get-tuple-element.176), channel_id=1, source_target_pairs={{0,4},{1,5},{2,6},{3,7},{4,0},{5,1},{6,2},{7,3},{8,12},{9,13},{10,... | collective-permute-start | bytes 1572872 | tf_op jit(solution)/shard_map/ppermute | solution.py:194
  99.4 48.0 %collective-permute-start.3 = (f32[8,128,128]{2,1,0:T(8,128)S(1)}, f32[8,128,128]{2,1,0:T(8,128)S(1)}, u32[]{:S(2)}, u32[]{:S(2)}) collective-permute-start(f32[8,128,128]{2,1,0:T(8,128)S(1)} %get-tuple-element.175), channel_id=1, source_target_pairs={{0,2},{1,3},{2,4},{3,5},{4,6},{5,7},{6,0},{7,1},{8,10},{9,11},{10,... | collective-permute-start | bytes 1572872 | tf_op jit(solution)/shard_map/ppermute | solution.py:194
  103.0 36.9 %collective-permute-start.29 = (f32[4,128,128]{2,1,0:T(8,128)}, f32[4,128,128]{2,1,0:T(8,128)S(1)}, u32[]{:S(2)}, u32[]{:S(2)}) collective-permute-start(f32[4,128,128]{2,1,0:T(8,128)} %collective-permute-done.27.refs_4_), channel_id=1, source_target_pairs={{0,6},{1,7},{2,0},{3,1},{4,2},{5,3},{6,4},{7,5},{8,14},{9,15},{10,... | collective-permute-start | bytes 786440 | tf_op jit(solution)/shard_map/ppermute | solution.py:194
  106.7 46.5 %collective-permute-start.14 = (f32[4,128,128]{2,1,0:T(8,128)S(1)}, f32[4,128,128]{2,1,0:T(8,128)S(1)}, u32[]{:S(2)}, u32[]{:S(2)}) collective-permute-start(f32[4,128,128]{2,1,0:T(8,128)S(1)} %collective-permute-done.13.refs_13_), channel_id=1, source_target_pairs={{0,16},{16,0},{1,17},{17,1},{2,18},{18,2},{3,19},{19,3},{4,20},{20... | collective-permute-start | bytes 786440 | tf_op jit(solution)/shard_map/ppermute | solution.py:210
  139.8 26.0 %collective-permute-start.61 = (f32[4,128,128]{2,1,0:T(8,128)S(1)}, f32[4,128,128]{2,1,0:T(8,128)S(1)}, u32[]{:S(2)}, u32[]{:S(2)}) collective-permute-start(f32[4,128,128]{2,1,0:T(8,128)S(1)} %copy-done.7), channel_id=1, source_target_pairs={{0,6},{1,7},{2,0},{3,1},{4,2},{5,3},{6,4},{7,5},{8,14},{9,15},{10,... | collective-permute-start | bytes 786440 | tf_op jit(solution)/shard_map/ppermute | solution.py:194
  144.1 21.8 %collective-permute-start.60 = (f32[4,128,128]{2,1,0:T(8,128)S(1)}, f32[4,128,128]{2,1,0:T(8,128)S(1)}, u32[]{:S(2)}, u32[]{:S(2)}) collective-permute-start(f32[4,128,128]{2,1,0:T(8,128)S(1)} %copy-done.7), channel_id=1, source_target_pairs={{0,16},{16,0},{1,17},{17,1},{2,18},{18,2},{3,19},{19,3},{4,20},{20... | collective-permute-start | bytes 786440 | tf_op jit(solution)/shard_map/ppermute | solution.py:210
  146.1 21.3 %collective-permute-start.28 = (f32[4,128,128]{2,1,0:T(8,128)}, f32[4,128,128]{2,1,0:T(8,128)S(1)}, u32[]{:S(2)}, u32[]{:S(2)}) collective-permute-start(f32[4,128,128]{2,1,0:T(8,128)} %collective-permute-done.27.refs_4_), channel_id=1, source_target_pairs={{0,16},{16,0},{1,17},{17,1},{2,18},{18,2},{3,19},{19,3},{4,20},{20... | collective-permute-start | bytes 786440 | tf_op jit(solution)/shard_map/ppermute | solution.py:210
  147.4 22.8 %collective-permute-start.38 = (f32[4,128,128]{2,1,0:T(8,128)}, f32[4,128,128]{2,1,0:T(8,128)S(1)}, u32[]{:S(2)}, u32[]{:S(2)}) collective-permute-start(f32[4,128,128]{2,1,0:T(8,128)} %collective-permute-done.36.refs_27_), channel_id=1, source_target_pairs={{0,6},{1,7},{2,0},{3,1},{4,2},{5,3},{6,4},{7,5},{8,14},{9,15},{10,... | collective-permute-start | bytes 786440 | tf_op jit(solution)/shard_map/ppermute | solution.py:194
  153.2 17.0 %collective-permute-start.30 = (f32[4,128,128]{2,1,0:T(8,128)S(1)}, f32[4,128,128]{2,1,0:T(8,128)S(1)}, u32[]{:S(2)}, u32[]{:S(2)}) collective-permute-start(f32[4,128,128]{2,1,0:T(8,128)S(1)} %collective-permute-done.29.refs_6_), channel_id=1, source_target_pairs={{0,16},{16,0},{1,17},{17,1},{2,18},{18,2},{3,19},{19,3},{4,20},{20... | collective-permute-start | bytes 786440 | tf_op jit(solution)/shard_map/ppermute | solution.py:210
  170.3 28.4 %collective-permute-start.15 = (f32[520,128]{1,0:T(8,128)S(1)}, f32[520,128]{1,0:T(8,128)S(1)}, u32[]{:S(2)}, u32[]{:S(2)}) collective-permute-start(f32[520,128]{1,0:T(8,128)S(1)} %get-tuple-element.86), channel_id=1, source_target_pairs={{0,8},{1,9},{2,10},{3,11},{4,12},{5,13},{6,14},{7,15},{8,0},{9,1},... | collective-permute-start | bytes 798728 | tf_op jit(solution)/shard_map/ppermute | solution.py:194
  170.3 29.3 %collective-permute-start.16 = (f32[520,128]{1,0:T(8,128)S(1)}, f32[520,128]{1,0:T(8,128)S(1)}, u32[]{:S(2)}, u32[]{:S(2)}) collective-permute-start(f32[520,128]{1,0:T(8,128)S(1)} %get-tuple-element.87), channel_id=1, source_target_pairs={{0,1},{1,0},{2,3},{3,2},{4,5},{5,4},{6,7},{7,6},{8,9},{9,8},{10,11... | collective-permute-start | bytes 798728 | tf_op jit(solution)/shard_map/ppermute | solution.py:194
  171.8 28.3 %collective-permute-start.17 = (f32[520,128]{1,0:T(8,128)S(1)}, f32[520,128]{1,0:T(8,128)S(1)}, u32[]{:S(2)}, u32[]{:S(2)}) collective-permute-start(f32[520,128]{1,0:T(8,128)S(1)} %get-tuple-element.88), channel_id=1, source_target_pairs={{0,9},{1,8},{2,11},{3,10},{4,13},{5,12},{6,15},{7,14},{8,1},{9,0},... | collective-permute-start | bytes 798728 | tf_op jit(solution)/shard_map/ppermute | solution.py:194
  175.1 32.2 %collective-permute-start.37 = (f32[4,128,128]{2,1,0:T(8,128)}, f32[4,128,128]{2,1,0:T(8,128)S(1)}, u32[]{:S(2)}, u32[]{:S(2)}) collective-permute-start(f32[4,128,128]{2,1,0:T(8,128)} %collective-permute-done.36.refs_27_), channel_id=1, source_target_pairs={{0,16},{16,0},{1,17},{17,1},{2,18},{18,2},{3,19},{19,3},{4,20},{20... | collective-permute-start | bytes 786440 | tf_op jit(solution)/shard_map/ppermute | solution.py:210
  179.8 27.6 %collective-permute-start.53 = (f32[4,128,128]{2,1,0:T(8,128)}, f32[4,128,128]{2,1,0:T(8,128)S(1)}, u32[]{:S(2)}, u32[]{:S(2)}) collective-permute-start(f32[4,128,128]{2,1,0:T(8,128)} %collective-permute-done.51.refs_4_), channel_id=1, source_target_pairs={{0,6},{1,7},{2,0},{3,1},{4,2},{5,3},{6,4},{7,5},{8,14},{9,15},{10,... | collective-permute-start | bytes 786440 | tf_op jit(solution)/shard_map/ppermute | solution.py:194
  209.5 17.7 %collective-permute-start.23 = (f32[512,128]{1,0:T(8,128)S(1)}, f32[512,128]{1,0:T(8,128)S(1)}, u32[]{:S(2)}, u32[]{:S(2)}) collective-permute-start(f32[512,128]{1,0:T(8,128)S(1)} %get-tuple-element.92), channel_id=1, source_target_pairs={{0,9},{1,8},{2,11},{3,10},{4,13},{5,12},{6,15},{7,14},{8,1},{9,0},... | collective-permute-start | bytes 786440 | tf_op jit(solution)/shard_map/ppermute | solution.py:194
  209.5 33.4 %collective-permute-start.77 = (f32[4,128,128]{2,1,0:T(8,128)S(1)}, f32[4,128,128]{2,1,0:T(8,128)S(1)}, u32[]{:S(2)}, u32[]{:S(2)}) collective-permute-start(f32[4,128,128]{2,1,0:T(8,128)S(1)} %collective-permute-done.69.refs_5_), channel_id=1, source_target_pairs={{0,6},{1,7},{2,0},{3,1},{4,2},{5,3},{6,4},{7,5},{8,14},{9,15},{10,... | collective-permute-start | bytes 786440 | tf_op jit(solution)/shard_map/ppermute | solution.py:194
  215.9 27.1 %collective-permute-start.86 = (f32[4,128,128]{2,1,0:T(8,128)S(1)}, f32[4,128,128]{2,1,0:T(8,128)S(1)}, u32[]{:S(2)}, u32[]{:S(2)}) collective-permute-start(f32[4,128,128]{2,1,0:T(8,128)S(1)} %collective-permute-done.84.refs_25_), channel_id=1, source_target_pairs={{0,6},{1,7},{2,0},{3,1},{4,2},{5,3},{6,4},{7,5},{8,14},{9,15},{10,... | collective-permute-start | bytes 786440 | tf_op jit(solution)/shard_map/ppermute | solution.py:194
  220.1 23.4 %collective-permute-start.52 = (f32[4,128,128]{2,1,0:T(8,128)}, f32[4,128,128]{2,1,0:T(8,128)S(1)}, u32[]{:S(2)}, u32[]{:S(2)}) collective-permute-start(f32[4,128,128]{2,1,0:T(8,128)} %collective-permute-done.51.refs_4_), channel_id=1, source_target_pairs={{0,16},{16,0},{1,17},{17,1},{2,18},{18,2},{3,19},{19,3},{4,20},{20... | collective-permute-start | bytes 786440 | tf_op jit(solution)/shard_map/ppermute | solution.py:210
  221.5 23.4 %collective-permute-start.63 = (f32[4,128,128]{2,1,0:T(8,128)S(1)}, f32[4,128,128]{2,1,0:T(8,128)S(1)}, u32[]{:S(2)}, u32[]{:S(2)}) collective-permute-start(f32[4,128,128]{2,1,0:T(8,128)S(1)} %collective-permute-done.61.refs_27_), channel_id=1, source_target_pairs={{0,6},{1,7},{2,0},{3,1},{4,2},{5,3},{6,4},{7,5},{8,14},{9,15},{10,... | collective-permute-start | bytes 786440 | tf_op jit(solution)/shard_map/ppermute | solution.py:194
  227.1 18.1 %collective-permute-start.54 = (f32[4,128,128]{2,1,0:T(8,128)S(1)}, f32[4,128,128]{2,1,0:T(8,128)S(1)}, u32[]{:S(2)}, u32[]{:S(2)}) collective-permute-start(f32[4,128,128]{2,1,0:T(8,128)S(1)} %collective-permute-done.53.refs_6_), channel_id=1, source_target_pairs={{0,16},{16,0},{1,17},{17,1},{2,18},{18,2},{3,19},{19,3},{4,20},{20... | collective-permute-start | bytes 786440 | tf_op jit(solution)/shard_map/ppermute | solution.py:210
  244.9 21.4 %collective-permute-start.40 = (f32[520,128]{1,0:T(8,128)S(1)}, f32[520,128]{1,0:T(8,128)S(1)}, u32[]{:S(2)}, u32[]{:S(2)}) collective-permute-start(f32[520,128]{1,0:T(8,128)S(1)} %get-tuple-element.106), channel_id=1, source_target_pairs={{0,8},{1,9},{2,10},{3,11},{4,12},{5,13},{6,14},{7,15},{8,0},{9,1},... | collective-permute-start | bytes 798728 | tf_op jit(solution)/shard_map/ppermute | solution.py:194
  245.2 22.3 %collective-permute-start.41 = (f32[520,128]{1,0:T(8,128)S(1)}, f32[520,128]{1,0:T(8,128)S(1)}, u32[]{:S(2)}, u32[]{:S(2)}) collective-permute-start(f32[520,128]{1,0:T(8,128)S(1)} %get-tuple-element.107), channel_id=1, source_target_pairs={{0,1},{1,0},{2,3},{3,2},{4,5},{5,4},{6,7},{7,6},{8,9},{9,8},{10,11... | collective-permute-start | bytes 798728 | tf_op jit(solution)/shard_map/ppermute | solution.py:194
  245.6 22.6 %collective-permute-start.42 = (f32[520,128]{1,0:T(8,128)S(1)}, f32[520,128]{1,0:T(8,128)S(1)}, u32[]{:S(2)}, u32[]{:S(2)}) collective-permute-start(f32[520,128]{1,0:T(8,128)S(1)} %get-tuple-element.108), channel_id=1, source_target_pairs={{0,9},{1,8},{2,11},{3,10},{4,13},{5,12},{6,15},{7,14},{8,1},{9,0},... | collective-permute-start | bytes 798728 | tf_op jit(solution)/shard_map/ppermute | solution.py:194
  252.2 22.2 %collective-permute-start.62 = (f32[4,128,128]{2,1,0:T(8,128)S(1)}, f32[4,128,128]{2,1,0:T(8,128)S(1)}, u32[]{:S(2)}, u32[]{:S(2)}) collective-permute-start(f32[4,128,128]{2,1,0:T(8,128)S(1)} %collective-permute-done.61.refs_27_), channel_id=1, source_target_pairs={{0,16},{16,0},{1,17},{17,1},{2,18},{18,2},{3,19},{19,3},{4,20},{20... | collective-permute-start | bytes 786440 | tf_op jit(solution)/shard_map/ppermute | solution.py:210
  256.9 18.8 %collective-permute-start.79 = (f32[4,128,128]{2,1,0:T(8,128)S(1)}, f32[4,128,128]{2,1,0:T(8,128)S(1)}, u32[]{:S(2)}, u32[]{:S(2)}) collective-permute-start(f32[4,128,128]{2,1,0:T(8,128)S(1)} %collective-permute-done.77.refs_4_), channel_id=1, source_target_pairs={{0,6},{1,7},{2,0},{3,1},{4,2},{5,3},{6,4},{7,5},{8,14},{9,15},{10,... | collective-permute-start | bytes 786440 | tf_op jit(solution)/shard_map/ppermute | solution.py:194
  276.6 17.5 %collective-permute-start.47 = (f32[512,128]{1,0:T(8,128)S(1)}, f32[512,128]{1,0:T(8,128)S(1)}, u32[]{:S(2)}, u32[]{:S(2)}) collective-permute-start(f32[512,128]{1,0:T(8,128)S(1)} %get-tuple-element.112), channel_id=1, source_target_pairs={{0,9},{1,8},{2,11},{3,10},{4,13},{5,12},{6,15},{7,14},{8,1},{9,0},... | collective-permute-start | bytes 786440 | tf_op jit(solution)/shard_map/ppermute | solution.py:194
  277.6 31.8 %collective-permute-start.70 = (f32[4,128,128]{2,1,0:T(8,128)S(1)}, f32[4,128,128]{2,1,0:T(8,128)S(1)}, u32[]{:S(2)}, u32[]{:S(2)}) collective-permute-start(f32[4,128,128]{2,1,0:T(8,128)S(1)} %collective-permute-done.69.refs_5_), channel_id=1, source_target_pairs={{0,16},{16,0},{1,17},{17,1},{2,18},{18,2},{3,19},{19,3},{4,20},{20... | collective-permute-start | bytes 786440 | tf_op jit(solution)/shard_map/ppermute | solution.py:210
  282.8 26.7 %collective-permute-start.101 = (f32[4,128,128]{2,1,0:T(8,128)S(1)}, f32[4,128,128]{2,1,0:T(8,128)S(1)}, u32[]{:S(2)}, u32[]{:S(2)}) collective-permute-start(f32[4,128,128]{2,1,0:T(8,128)S(1)} %collective-permute-done.93.refs_5_), channel_id=1, source_target_pairs={{0,6},{1,7},{2,0},{3,1},{4,2},{5,3},{6,4},{7,5},{8,14},{9,15},{10,... | collective-permute-start | bytes 786440 | tf_op jit(solution)/shard_map/ppermute | solution.py:194
  286.6 23.4 %collective-permute-start.78 = (f32[4,128,128]{2,1,0:T(8,128)S(1)}, f32[4,128,128]{2,1,0:T(8,128)S(1)}, u32[]{:S(2)}, u32[]{:S(2)}) collective-permute-start(f32[4,128,128]{2,1,0:T(8,128)S(1)} %collective-permute-done.77.refs_4_), channel_id=1, source_target_pairs={{0,16},{16,0},{1,17},{17,1},{2,18},{18,2},{3,19},{19,3},{4,20},{20... | collective-permute-start | bytes 786440 | tf_op jit(solution)/shard_map/ppermute | solution.py:210
  288.8 22.8 %collective-permute-start.88 = (f32[4,128,128]{2,1,0:T(8,128)S(1)}, f32[4,128,128]{2,1,0:T(8,128)S(1)}, u32[]{:S(2)}, u32[]{:S(2)}) collective-permute-start(f32[4,128,128]{2,1,0:T(8,128)S(1)} %collective-permute-done.86.refs_27_), channel_id=1, source_target_pairs={{0,6},{1,7},{2,0},{3,1},{4,2},{5,3},{6,4},{7,5},{8,14},{9,15},{10,... | collective-permute-start | bytes 786440 | tf_op jit(solution)/shard_map/ppermute | solution.py:194
  294.1 17.5 %collective-permute-start.80 = (f32[4,128,128]{2,1,0:T(8,128)S(1)}, f32[4,128,128]{2,1,0:T(8,128)S(1)}, u32[]{:S(2)}, u32[]{:S(2)}) collective-permute-start(f32[4,128,128]{2,1,0:T(8,128)S(1)} %collective-permute-done.79.refs_6_), channel_id=1, source_target_pairs={{0,16},{16,0},{1,17},{17,1},{2,18},{18,2},{3,19},{19,3},{4,20},{20... | collective-permute-start | bytes 786440 | tf_op jit(solution)/shard_map/ppermute | solution.py:210
  309.5 15.6 %collective-permute-start.65 = (f32[520,128]{1,0:T(8,128)S(1)}, f32[520,128]{1,0:T(8,128)S(1)}, u32[]{:S(2)}, u32[]{:S(2)}) collective-permute-start(f32[520,128]{1,0:T(8,128)S(1)} %get-tuple-element.126), channel_id=1, source_target_pairs={{0,8},{1,9},{2,10},{3,11},{4,12},{5,13},{6,14},{7,15},{8,0},{9,1},... | collective-permute-start | bytes 798728 | tf_op jit(solution)/shard_map/ppermute | solution.py:194
  311.6 22.3 %collective-permute-start.66 = (f32[520,128]{1,0:T(8,128)S(1)}, f32[520,128]{1,0:T(8,128)S(1)}, u32[]{:S(2)}, u32[]{:S(2)}) collective-permute-start(f32[520,128]{1,0:T(8,128)S(1)} %get-tuple-element.127), channel_id=1, source_target_pairs={{0,1},{1,0},{2,3},{3,2},{4,5},{5,4},{6,7},{7,6},{8,9},{9,8},{10,11... | collective-permute-start | bytes 798728 | tf_op jit(solution)/shard_map/ppermute | solution.py:194
  313.0 22.2 %collective-permute-start.67 = (f32[520,128]{1,0:T(8,128)S(1)}, f32[520,128]{1,0:T(8,128)S(1)}, u32[]{:S(2)}, u32[]{:S(2)}) collective-permute-start(f32[520,128]{1,0:T(8,128)S(1)} %get-tuple-element.128), channel_id=1, source_target_pairs={{0,9},{1,8},{2,11},{3,10},{4,13},{5,12},{6,15},{7,14},{8,1},{9,0},... | collective-permute-start | bytes 798728 | tf_op jit(solution)/shard_map/ppermute | solution.py:194
  319.2 21.3 %collective-permute-start.85 = (f32[4,128,128]{2,1,0:T(8,128)S(1)}, f32[4,128,128]{2,1,0:T(8,128)S(1)}, u32[]{:S(2)}, u32[]{:S(2)}) collective-permute-start(f32[4,128,128]{2,1,0:T(8,128)S(1)} %collective-permute-done.84.refs_25_), channel_id=1, source_target_pairs={{0,16},{16,0},{1,17},{17,1},{2,18},{18,2},{3,19},{19,3},{4,20},{20... | collective-permute-start | bytes 786440 | tf_op jit(solution)/shard_map/ppermute | solution.py:210
  323.9 18.2 %collective-permute-start.87 = (f32[4,128,128]{2,1,0:T(8,128)S(1)}, f32[4,128,128]{2,1,0:T(8,128)S(1)}, u32[]{:S(2)}, u32[]{:S(2)}) collective-permute-start(f32[4,128,128]{2,1,0:T(8,128)S(1)} %collective-permute-done.86.refs_27_), channel_id=1, source_target_pairs={{0,16},{16,0},{1,17},{17,1},{2,18},{18,2},{3,19},{19,3},{4,20},{20... | collective-permute-start | bytes 786440 | tf_op jit(solution)/shard_map/ppermute | solution.py:210
  325.1 17.1 %collective-permute-start.103 = (f32[4,128,128]{2,1,0:T(8,128)S(1)}, f32[4,128,128]{2,1,0:T(8,128)S(1)}, u32[]{:S(2)}, u32[]{:S(2)}) collective-permute-start(f32[4,128,128]{2,1,0:T(8,128)S(1)} %collective-permute-done.101.refs_4_), channel_id=1, source_target_pairs={{0,6},{1,7},{2,0},{3,1},{4,2},{5,3},{6,4},{7,5},{8,14},{9,15},{10,... | collective-permute-start | bytes 786440 | tf_op jit(solution)/shard_map/ppermute | solution.py:194
  342.7 18.2 %collective-permute-start.72 = (f32[512,128]{1,0:T(8,128)S(1)}, f32[512,128]{1,0:T(8,128)S(1)}, u32[]{:S(2)}, u32[]{:S(2)}) collective-permute-start(f32[512,128]{1,0:T(8,128)S(1)} %get-tuple-element.131), channel_id=1, source_target_pairs={{0,1},{1,0},{2,3},{3,2},{4,5},{5,4},{6,7},{7,6},{8,9},{9,8},{10,11... | collective-permute-start | bytes 786440 | tf_op jit(solution)/shard_map/ppermute | solution.py:194
  344.3 21.0 %collective-permute-start.73 = (f32[512,128]{1,0:T(8,128)S(1)}, f32[512,128]{1,0:T(8,128)S(1)}, u32[]{:S(2)}, u32[]{:S(2)}) collective-permute-start(f32[512,128]{1,0:T(8,128)S(1)} %get-tuple-element.132), channel_id=1, source_target_pairs={{0,9},{1,8},{2,11},{3,10},{4,13},{5,12},{6,15},{7,14},{8,1},{9,0},... | collective-permute-start | bytes 786440 | tf_op jit(solution)/shard_map/ppermute | solution.py:194
  349.7 32.3 %collective-permute-start.102 = (f32[4,128,128]{2,1,0:T(8,128)S(1)}, f32[4,128,128]{2,1,0:T(8,128)S(1)}, u32[]{:S(2)}, u32[]{:S(2)}) collective-permute-start(f32[4,128,128]{2,1,0:T(8,128)S(1)} %collective-permute-done.101.refs_4_), channel_id=1, source_target_pairs={{0,16},{16,0},{1,17},{17,1},{2,18},{18,2},{3,19},{19,3},{4,20},{20... | collective-permute-start | bytes 786440 | tf_op jit(solution)/shard_map/ppermute | solution.py:210
  354.4 27.8 %collective-permute-start.104 = (f32[4,128,128]{2,1,0:T(8,128)S(1)}, f32[4,128,128]{2,1,0:T(8,128)S(1)}, u32[]{:S(2)}, u32[]{:S(2)}) collective-permute-start(f32[4,128,128]{2,1,0:T(8,128)S(1)} %collective-permute-done.103.refs_6_), channel_id=1, source_target_pairs={{0,16},{16,0},{1,17},{17,1},{2,18},{18,2},{3,19},{19,3},{4,20},{20... | collective-permute-start | bytes 786440 | tf_op jit(solution)/shard_map/ppermute | solution.py:210
  382.0 19.3 %collective-permute-start.90 = (f32[520,128]{1,0:T(8,128)S(1)}, f32[520,128]{1,0:T(8,128)S(1)}, u32[]{:S(2)}, u32[]{:S(2)}) collective-permute-start(f32[520,128]{1,0:T(8,128)S(1)} %get-tuple-element.146), channel_id=1, source_target_pairs={{0,8},{1,9},{2,10},{3,11},{4,12},{5,13},{6,14},{7,15},{8,0},{9,1},... | collective-permute-start | bytes 798728 | tf_op jit(solution)/shard_map/ppermute | solution.py:194
  382.2 19.6 %collective-permute-start.91 = (f32[520,128]{1,0:T(8,128)S(1)}, f32[520,128]{1,0:T(8,128)S(1)}, u32[]{:S(2)}, u32[]{:S(2)}) collective-permute-start(f32[520,128]{1,0:T(8,128)S(1)} %get-tuple-element.147), channel_id=1, source_target_pairs={{0,1},{1,0},{2,3},{3,2},{4,5},{5,4},{6,7},{7,6},{8,9},{9,8},{10,11... | collective-permute-start | bytes 798728 | tf_op jit(solution)/shard_map/ppermute | solution.py:194
  387.9 17.0 %collective-permute-start.92 = (f32[520,128]{1,0:T(8,128)S(1)}, f32[520,128]{1,0:T(8,128)S(1)}, u32[]{:S(2)}, u32[]{:S(2)}) collective-permute-start(f32[520,128]{1,0:T(8,128)S(1)} %get-tuple-element.148), channel_id=1, source_target_pairs={{0,9},{1,8},{2,11},{3,10},{4,13},{5,12},{6,15},{7,14},{8,1},{9,0},... | collective-permute-start | bytes 798728 | tf_op jit(solution)/shard_map/ppermute | solution.py:194
  412.3 15.0 %collective-permute-start.97 = (f32[512,128]{1,0:T(8,128)S(1)}, f32[512,128]{1,0:T(8,128)S(1)}, u32[]{:S(2)}, u32[]{:S(2)}) collective-permute-start(f32[512,128]{1,0:T(8,128)S(1)} %get-tuple-element.152), channel_id=1, source_target_pairs={{0,9},{1,8},{2,11},{3,10},{4,13},{5,12},{6,15},{7,14},{8,1},{9,0},... | collective-permute-start | bytes 786440 | tf_op jit(solution)/shard_map/ppermute | solution.py:194
  429.6 16.8 %collective-permute-start.108 = (f32[8,128,128]{2,1,0:T(8,128)S(1)}, f32[8,128,128]{2,1,0:T(8,128)S(1)}, u32[]{:S(2)}, u32[]{:S(2)}) collective-permute-start(f32[8,128,128]{2,1,0:T(8,128)S(1)} %get-tuple-element.162), channel_id=1, source_target_pairs={{0,2},{1,3},{2,4},{3,5},{4,6},{5,7},{6,0},{7,1},{8,10},{9,11},{10,... | collective-permute-start | bytes 1572872 | tf_op jit(solution)/shard_map/ppermute | solution.py:194
  429.6 38.9 %collective-permute-start.109 = (f32[8,128,128]{2,1,0:T(8,128)S(1)}, f32[8,128,128]{2,1,0:T(8,128)S(1)}, u32[]{:S(2)}, u32[]{:S(2)}) collective-permute-start(f32[8,128,128]{2,1,0:T(8,128)S(1)} %get-tuple-element.163), channel_id=1, source_target_pairs={{0,4},{1,5},{2,6},{3,7},{4,0},{5,1},{6,2},{7,3},{8,12},{9,13},{10,... | collective-permute-start | bytes 1572872 | tf_op jit(solution)/shard_map/ppermute | solution.py:194
  433.9 34.6 %collective-permute-start.110 = (f32[8,128,128]{2,1,0:T(8,128)S(1)}, f32[8,128,128]{2,1,0:T(8,128)}, u32[]{:S(2)}, u32[]{:S(2)}) collective-permute-start(f32[8,128,128]{2,1,0:T(8,128)S(1)} %get-tuple-element.164), channel_id=1, source_target_pairs={{0,6},{1,7},{2,0},{3,1},{4,2},{5,3},{6,4},{7,5},{8,14},{9,15},{10,... | collective-permute-start | bytes 1572872 | tf_op jit(solution)/shard_map/ppermute | solution.py:194
  (69 other events, 798.4 us)

commit v2 on v1

v2 whole, which is shorter than its diff:
```python
import functools

import jax
import jax.numpy as jnp
from jax import lax
from jax.experimental import pallas as pl
from jax.experimental.pallas import tpu as pltpu
from jax.sharding import PartitionSpec as P

epsilon = 1e-06
exact = lax.Precision.HIGHEST
LANES = 128
ROWS = 8
PLANES = 4
QUARTERS = 4
CHUNKS = 2


def gray(position):
    return position ^ (position >> 1)


def row_offset(step, mate, position, quarter):
    start = gray((position + step) % PLANES) * (QUARTERS * ROWS) + (quarter ^ mate) * ROWS
    return pl.ds(pl.multiple_of(start, ROWS), ROWS)


def halves(value):
    high = value.astype(jnp.bfloat16)
    return high, (value - high.astype(jnp.float32)).astype(jnp.bfloat16)


def product(weight, value):
    def dot(a, b):
        return lax.dot_general(a, b, (((0,), (0,)), ((), ())), preferred_element_type=jnp.float32)

    weight_high, weight_low = halves(weight)
    value_high, value_low = halves(value)
    return dot(weight_high, value_high) + (dot(weight_high, value_low) + dot(weight_low, value_high))


def pick(parts, index, group):
    if len(parts) == 1:
        return parts[0][index]
    inside = parts[2] + index % 4
    if index < 4:
        return jnp.where(group == 0, parts[0][inside], parts[1][inside])
    return jnp.where(group == 0, parts[1][inside], parts[0][inside])


def sent_tile(step, index, other, by_piece):
    if by_piece:
        return step, (other * ROWS + index) * ROWS
    return other // 2, ((other % 2) * 32 + step * ROWS + index) * ROWS


class Taker:
    def __init__(self, refs):
        self.refs = list(refs)

    def __call__(self, count):
        head, self.refs = self.refs[:count], self.refs[count:]
        return head


def read_place(place):
    return place[0], place[1], place[2]


def take_weights(take, bases):
    return [take(1) if base is None else take(2) + [base] for base in bases]


def first_factor(steps, by_piece, current, gain, weights, send, tile, place):
    position, quarter, group = place
    squares = jnp.zeros((ROWS, LANES), jnp.float32)
    for n, step in enumerate(steps):
        for index in range(ROWS):
            value = current[n][index]
            squares += jnp.sum((value * value).reshape(LANES // ROWS, ROWS, LANES), axis=0)
            tile[index] = product(pick(weights[n], index, group), value * gain[n][index])
        for index in range(ROWS):
            for other in range(PLANES):
                for mate in range(QUARTERS):
                    part, start = sent_tile(step, index, other, by_piece)
                    ref = send[0 if by_piece else part][mate]
                    ref[pl.ds(start, ROWS), :] = tile[index, row_offset(other, mate, position, quarter), :]
    for ref in send[0]:
        ref[pl.ds(ref.shape[0] - ROWS, ROWS), :] = squares


def first_kernel(step, bases, place, *refs):
    take = Taker(refs)
    current, gain = take(1), take(1)
    weights = take_weights(take, bases)
    send, tile = [take(QUARTERS)], take(1)[0]
    first_factor([step], True, current, gain, weights, send, tile, read_place(place))


def edge_kernel(width, squares_count, has_next, bases, place, *refs):
    take = Taker(refs)
    position, quarter, group = read_place(place)
    current, old_gain = take(PLANES), take(PLANES)
    squares_in = take(squares_count)
    mixed = [take(QUARTERS) for _ in range(CHUNKS)]
    if has_next:
        gain = take(PLANES)
        weights = take_weights(take, bases)
    fresh = take(PLANES)
    if has_next:
        send, tile = [take(QUARTERS) for _ in range(CHUNKS)], take(1)[0]

    total = sum(ref[pl.ds(ref.shape[0] - ROWS, ROWS), :] for ref in squares_in)
    scale = lax.rsqrt(jnp.sum(total, axis=0, keepdims=True) / width + epsilon)
    scale = jnp.broadcast_to(scale, (ROWS, LANES))
    for step in range(PLANES):

        def finish(index, carry, step=step):
            for other in range(PLANES):
                for mate in range(QUARTERS):
                    where = row_offset(other, mate, position, quarter)
                    value = current[step][index, where, :]
                    part, start = sent_tile(step, index, other, False)
                    mix = mixed[part][mate][pl.ds(pl.multiple_of(start, ROWS), ROWS), :]
                    normed = value * scale * old_gain[step][index, where, :]
                    value = value + (mix * scale) * (normed / (1.0 + jnp.exp(-normed)))
                    fresh[step][index, where, :] = value
            return carry

        lax.fori_loop(0, ROWS, finish, 0, unroll=2)

    if has_next:
        first_factor(range(PLANES), False, fresh, gain, weights, send, tile, (position, quarter, group))


def column_kernel(chunk, by_piece, bases, has_gain, place, *refs):
    take = Taker(refs)
    position, quarter, group = read_place(place)
    came = [take(QUARTERS) for _ in range(PLANES if by_piece else 1)]
    weights = take_weights(take, bases)
    rows = take(PLANES) if has_gain else []
    send = take(QUARTERS)
    spread = take(PLANES) if has_gain else []
    value, tile = take(2)
    for n in range(2):
        other = chunk * 2 + n
        for index in range(ROWS):
            for step in range(PLANES):
                for mate in range(QUARTERS):
                    part, start = sent_tile(step, 0, other, by_piece)
                    ref = came[part if by_piece else 0][mate]
                    value[index, row_offset(step, mate, position, quarter), :] = ref[
                        pl.ds(start + index, ROWS, stride=ROWS), :
                    ]
            tile[index] = product(pick(weights[n], index, group), value[index])
            for step in range(PLANES):
                for mate in range(QUARTERS):
                    _, start = sent_tile(step, 0, other, False)
                    send[mate][pl.ds(start + index, ROWS, stride=ROWS), :] = tile[
                        index, row_offset(step, mate, position, quarter), :
                    ]
    for step in range(len(rows)):
        columns = rows[step][...].T
        for index in range(ROWS):
            spread[step][index] = jnp.broadcast_to(columns[:, index : index + 1], (LANES, LANES))


SMALL = pl.BlockSpec(memory_space=pltpu.SMEM)
WHOLE = pl.BlockSpec(memory_space=pltpu.VMEM)
PARAMS = pltpu.CompilerParams(vmem_limit_bytes=40 * 1024 * 1024)
PIECE = (ROWS, LANES, LANES)


def array(*shape):
    return jax.ShapeDtypeStruct(shape, jnp.float32)


def call(kernel, operands, outs, scratch, flops):
    moved = 4 * (sum(a.size for a in operands) + sum(o.size for o in outs))
    return pl.pallas_call(
        kernel,
        out_shape=outs,
        in_specs=[SMALL] + [WHOLE] * (len(operands) - 1),
        out_specs=[WHOLE] * len(outs),
        scratch_shapes=[pltpu.VMEM(PIECE, jnp.float32)] * scratch,
        compiler_params=PARAMS,
        cost_estimate=pl.CostEstimate(flops=flops, bytes_accessed=moved, transcendentals=0),
    )(*operands)


STAGE_FLOPS = 6 * 32 * LANES * LANES * LANES


def split_weights(weights):
    return [part for parts in weights for part in parts[:2]], [None if len(p) == 1 else p[2] for p in weights]


def first_piece(step, place, current, gain, weights):
    operands, bases = split_weights([weights])
    kernel = functools.partial(first_kernel, step, bases)
    return call(kernel, [place, current, gain, *operands], [array(264, LANES)] * QUARTERS, 1, STAGE_FLOPS // 4)


def layer_edge(width, place, current, old_gain, squares, mixed, following=None):
    operands = [place, *current, *old_gain, *squares, *mixed[0], *mixed[1]]
    outs, bases = [array(*PIECE)] * PLANES, None
    if following is not None:
        gain, weights = following
        more, bases = split_weights(weights)
        operands += [*gain, *more]
        outs += [array(520, LANES)] * QUARTERS + [array(512, LANES)] * QUARTERS
    kernel = functools.partial(edge_kernel, width, len(squares), following is not None, bases)
    results = list(call(kernel, operands, outs, int(following is not None), 2 * STAGE_FLOPS))
    return results[:PLANES], [results[PLANES : PLANES + QUARTERS], results[PLANES + QUARTERS :]]


def column_stage(chunk, by_piece, place, came, weights, rows=()):
    more, bases = split_weights(weights)
    operands = [place, *(ref for part in came for ref in part), *more, *rows]
    outs = [array(512, LANES)] * QUARTERS + [array(*PIECE)] * len(rows)
    kernel = functools.partial(column_kernel, chunk, by_piece, bases, bool(rows))
    results = list(call(kernel, operands, outs, 2, STAGE_FLOPS))
    return results[:QUARTERS], results[QUARTERS:]


def routed(value, to):
    route = []
    for core in range(2):
        for z in range(PLANES):
            for y in range(2):
                there = to(core, z, y)
                route.append((core * 8 + z * 2 + y, there[0] * 8 + there[1] * 2 + there[2]))
    return lax.ppermute(value, ("segment", "block"), route)


def core_swap(value):
    return routed(value, lambda core, z, y: (1 - core, z, y))


def ring(value, distance):
    return routed(value, lambda core, z, y: (core, gray((gray(z) + distance) % PLANES), y))


def to_mate(value, mate):
    return routed(value, lambda core, z, y: (core ^ (mate & 1), z, y ^ (mate >> 1)))


def group_swap(value):
    return lax.ppermute(value, "groups", [(0, 1), (1, 0)])


def exchange(chunk):
    return [chunk[0]] + [to_mate(chunk[mate], mate) for mate in range(1, QUARTERS)]


def after(value, *earlier):
    return lax.optimization_barrier((value, *earlier))[0]


def plane_body(tokens, gains, right_factors, left_factors):
    core = lax.axis_index("segment")
    block = lax.axis_index("block")
    group = lax.axis_index("groups")
    z, y = block // 2, block % 2
    position = gray(z)
    place = jnp.stack([position, y * 2 + core, group]).astype(jnp.int32)
    rounds = right_factors.shape[1]
    layers = 2 * rounds
    width = right_factors.shape[3] * 8 * right_factors.shape[2]

    def swapped(value):
        mine = lax.dynamic_slice_in_dim(value, core * ROWS, ROWS, 0)
        theirs = core_swap(lax.dynamic_slice_in_dim(value, (1 - core) * ROWS, ROWS, 0))
        return jnp.where(core == 0, mine, theirs), jnp.where(core == 0, theirs, mine)

    folded = tokens.reshape(2, LANES, 2, ROWS, LANES).transpose(2, 0, 3, 4, 1)
    mine = lax.dynamic_index_in_dim(folded, core, 0, keepdims=False)
    theirs = core_swap(lax.dynamic_index_in_dim(folded, 1 - core, 0, keepdims=False))
    four = jnp.stack([mine, theirs]).reshape((4,) + PIECE)
    current = []
    for step in range(PLANES):
        plane = gray((position - step) % PLANES)
        slot = ((plane // 2) ^ core) * 2 + plane % 2
        piece = lax.dynamic_index_in_dim(four, slot, 0, keepdims=False)
        current.append(piece if step == 0 else ring(piece, -step))

    held = jnp.moveaxis(gains[0].reshape(rounds, 2 * ROWS, LANES), 1, 0)
    held = jnp.stack(swapped(held), axis=2).transpose(1, 2, 0, 3).reshape(layers, ROWS, LANES)
    gain_pieces = [held]
    for _ in range(PLANES - 1):
        held = ring(held, -1)
        gain_pieces.append(held)
    gain_rows = [[piece[layer] for piece in gain_pieces] for layer in range(layers)]

    right, left = [None] * layers, [None] * layers
    for r in range(rounds):
        right[2 * r], right[2 * r + 1] = swapped(right_factors[0, r])
        left[2 * r], left[2 * r + 1] = swapped(left_factors[0, r])

    def my_half(value):
        return lax.dynamic_slice_in_dim(value, group * 4, 4, 0)

    def chain(half):
        found = []
        for _ in range(PLANES - 1):
            half = ring(half, -1)
            found.append((half, group_swap(half)))
        return found

    right_parts, left_parts = [], []
    right_chain = chain(my_half(right[0]))
    left_chain = chain(after(my_half(left[0]), right_chain[-1][0]))
    right_parts.append([(right[0],)] + [(*pair, 0) for pair in right_chain])
    left_parts.append([(left[0],)] + [(*pair, 0) for pair in left_chain])
    last = left_chain[-1][0]
    for layer in range(1, layers):
        both = jnp.concatenate([my_half(right[layer]), my_half(left[layer])])
        both_chain = chain(after(both, last))
        last = both_chain[-1][0]
        right_parts.append([(right[layer],)] + [(*pair, 0) for pair in both_chain])
        left_parts.append([(left[layer],)] + [(*pair, 4) for pair in both_chain])

    gain = [jnp.broadcast_to(row[:, :, None], PIECE) for row in gain_rows[0]]
    came = [
        exchange(first_piece(step, place, current[step], gain[step], right_parts[0][step])) for step in range(PLANES)
    ]
    for layer in range(layers):
        by_piece = layer == 0
        squares = [part[mate] for part in (came if by_piece else came[:1]) for mate in range(QUARTERS)]
        mixed, next_gain = [], None
        for chunk in range(CHUNKS):
            rows = gain_rows[layer + 1] if chunk == 0 and layer + 1 < layers else ()
            weights = left_parts[layer][chunk * 2 : chunk * 2 + 2]
            source = came if by_piece else came[chunk : chunk + 1]
            sends, spread = column_stage(chunk, by_piece, place, source, weights, rows)
            mixed.append(exchange(sends))
            next_gain = spread or next_gain
        following = (next_gain, right_parts[layer + 1]) if layer + 1 < layers else None
        current, sends = layer_edge(width, place, current, gain, squares, mixed, following)
        gain = next_gain
        if following is not None:
            came = [exchange(sends[0]), exchange(sends[1])]

    back = [current[step] if step == 0 else ring(current[step], step) for step in range(PLANES)]
    stacked = jnp.stack(back)
    ordered = jnp.stack(
        [
            lax.dynamic_index_in_dim(stacked, (position - gray(plane)) % PLANES, 0, keepdims=False)
            for plane in range(PLANES)
        ]
    ).reshape((2, 2) + PIECE)
    mine = lax.dynamic_index_in_dim(ordered, core, 0, keepdims=False)
    theirs = core_swap(lax.dynamic_index_in_dim(ordered, 1 - core, 0, keepdims=False))
    both = jnp.stack([jnp.where(core == 0, mine, theirs), jnp.where(core == 0, theirs, mine)])
    return both.transpose(1, 4, 0, 2, 3).reshape(tokens.shape)


def wide_body(tokens, gains, right_factors, left_factors):
    blocks_here, block_size = right_factors.shape[2:4]
    token_count, width_here = tokens.shape
    width = width_here * lax.axis_size("block")
    rounds = right_factors.shape[1]
    core = lax.axis_index("segment")
    count = lax.axis_size("segment")

    def gathered(value):
        return lax.all_gather(value[0], "segment", axis=0)

    gains, right_factors, left_factors = gathered(gains), gathered(right_factors), gathered(left_factors)
    current = tokens.T
    for layer in range(count * rounds):
        s, r = layer % count, layer // count
        sum_squares = lax.psum(jnp.sum(current * current, axis=0), "block")
        normed = current * lax.rsqrt(sum_squares / width + epsilon)[None, :] * gains[s, r][:, None]
        inner = jnp.einsum(
            "bit,bij->bjt",
            normed.reshape(blocks_here, block_size, token_count),
            right_factors[s, r],
            precision=exact,
        )
        combined = jnp.einsum(
            "bjt,jbc->cjt",
            lax.all_to_all(inner, "block", split_axis=1, concat_axis=0, tiled=True),
            left_factors[s, r],
            precision=exact,
        )
        mixed = lax.all_to_all(combined, "block", split_axis=0, concat_axis=1, tiled=True)
        current = current + mixed.reshape(width_here, token_count) * jax.nn.silu(normed)
    return current.T


def solution(mesh):
    placed = (
        P(("groups", "segment"), "block"),
        P("segment", None, "block"),
        P("segment", None, "block", None, None),
        P("segment", None, "block", None, None),
    )
    planes = dict(mesh.shape) == {"groups": 2, "segment": 2, "block": 8}

    def body(tokens, gains, right_factors, left_factors):
        fits = planes and tokens.shape == (256, 2048) and right_factors.shape[2:] == (16, 128, 128)
        return (plane_body if fits else wide_body)(tokens, gains, right_factors, left_factors)

    return jax.shard_map(
        body,
        mesh=mesh,
        in_specs=placed,
        out_specs=P(("groups", "segment"), "block"),
        check_vma=False,
    )
```

time: 488 us -> 444 us (0.910); the launches traced: 478 us -> 443 us
  waiting for transfers between devices: 190 us -> 264 us
  starting transfers between devices: 159 us -> 97.3 us
  Pallas kernels: 91.3 us -> 34.9 us
  local copies, waits for them, and re-layouts: 27.8 us -> 35.2 us
    pallas_call x13 -> x16, Pallas kernels: 91.3 us -> 34.9 us  [call(): pl.pallas_call(kernel, out_shape=outs, in_specs=[SMALL] + [WHOLE] * (len(...]
    ppermute x88 -> x85, starting transfers between devices: 133 us -> 78.6 us  [routed(): return lax.ppermute(value, ('segment', 'block'), route)]
    ppermute x88 -> x85, waiting for transfers between devices: 190 us -> 237 us  [routed(): return lax.ppermute(value, ('segment', 'block'), route)]
    ppermute x24 -> x15, waiting for transfers between devices: 0.06 us -> 27 us  [group_swap(): return lax.ppermute(value, 'groups', [(0, 1), (1, 0)])]
    unnamed x44 -> x120, local copies, waits for them, and re-layouts: 4 us -> 13.5 us
    ppermute x24 -> x15, starting transfers between devices: 26 us -> 18.6 us  [group_swap(): return lax.ppermute(value, 'groups', [(0, 1), (1, 0)])]
    broadcast_in_dim x20 -> x4, local copies, waits for them, and re-layouts: 7.94 us -> 0.76 us  [plane_body(): gain = [jnp.broadcast_to(row[:, :, None], PIECE) for row in gain_rows[0]]]
  transfers between devices with their start and end apart: 112 -> 100, of which waited for: 42 -> 49; matrix products, arithmetic and copies ran while one was open for 5% -> 5% of each run, Pallas kernels for 19% -> 6%
where the time goes in v2:
time: 444 us; the launch traced here: 443 us
  waiting for transfers between devices  264 us (59%)
  starting transfers between devices  97.3 us (22%)
  local copies, waits for them, and re-layouts  35.2 us (8%)
  Pallas kernels  34.9 us (8%)
  other arithmetic  10.5 us (2%)
    ppermute x85, waiting for transfers between devices, routed(): return lax.ppermute(value, ('segment', 'block'), route)  237 us
    ppermute x85, starting transfers between devices, routed(): return lax.ppermute(value, ('segment', 'block'), route)  78.6 us
    pallas_call x16, Pallas kernels, call(): pl.pallas_call(kernel, out_shape=outs, in_specs=[SMALL] + [WHOLE] * (len(...  34.9 us
    ppermute x15, waiting for transfers between devices, group_swap(): return lax.ppermute(value, 'groups', [(0, 1), (1, 0)])  27 us
    ppermute x15, starting transfers between devices, group_swap(): return lax.ppermute(value, 'groups', [(0, 1), (1, 0)])  18.6 us
    unnamed x120, local copies, waits for them, and re-layouts  13.5 us
  transfers between devices with their start and end apart: 100, of which 49 were waited for; matrix products, arithmetic and copies ran while one was open for 5% of the time, Pallas kernels for 6%

profile of v2, /device:TPU:0, one launch (start us, length us, event | category | flops | bytes accessed | tf_op | source)
XLA Modules:
  0.0 443.3 jit_solution(5143391162045873819)
XLA Ops:
  0.0 2.7 fusion.5
  3.3 2.7 fusion.4
  6.0 2.0 bitcast_select_fusion.8
  8.1 3.7 collective-permute-start.12
  12.0 5.9 %collective-permute-done.12.refs_2_ = f32[4,128,128]{2,1,0:T(8,128)S(1)} collective-permute-done((f32[4,128,128]{2,1,0:T(8,128)S(1)}, f32[4,128,128]{2,1,0:T(8,128)S(1)}, u32[]{:S(2)}, u32[]{:S(2)}) %collective-permute-start.12) | collective-permute-done | bytes 262176 | tf_op jit(solution)/shard_map/ppermute | solution.py:233
  17.9 3.4 collective-permute-start.17
  21.3 3.3 copy.17
  24.6 3.0 dynamic-slice_bitcast_fusion.2
  27.6 2.5 collective-permute-start.22
  31.3 5.0 %collective-permute-done.22.refs_2_ = f32[4,128,128]{2,1,0:T(8,128)S(1)} collective-permute-done((f32[4,128,128]{2,1,0:T(8,128)S(1)}, f32[4,128,128]{2,1,0:T(8,128)S(1)}, u32[]{:S(2)}, u32[]{:S(2)}) %collective-permute-start.22) | collective-permute-done | bytes 262176 | tf_op jit(solution)/shard_map/ppermute | solution.py:233
  40.3 4.0 collective-permute-done.28.refs_17_
  45.7 5.6 %collective-permute-done.33.refs_16_ = f32[4,128,128]{2,1,0:T(8,128)S(1)} collective-permute-done((f32[4,128,128]{2,1,0:T(8,128)S(1)}, f32[4,128,128]{2,1,0:T(8,128)S(1)}, u32[]{:S(2)}, u32[]{:S(2)}) %collective-permute-start.33) | collective-permute-done | bytes 262176 | tf_op jit(solution)/shard_map/ppermute | solution.py:233
  53.8 4.5 %collective-permute-done.35.refs_18_ = f32[4,128,128]{2,1,0:T(8,128)S(1)} collective-permute-done((f32[4,128,128]{2,1,0:T(8,128)S(1)}, f32[4,128,128]{2,1,0:T(8,128)S(1)}, u32[]{:S(2)}, u32[]{:S(2)}) %collective-permute-start.35) | collective-permute-done | bytes 262176 | tf_op jit(solution)/shard_map/ppermute | solution.py:233
  58.3 2.6 collective-permute-start.40
  60.9 8.6 %collective-permute-done.5 = f32[4,8,128]{2,1,0:T(8,128)S(1)} collective-permute-done((f32[4,8,128]{2,1,0:T(8,128)S(1)}, f32[4,8,128]{2,1,0:T(8,128)S(1)}, u32[]{:S(2)}, u32[]{:S(2)}) %collective-permute-start.5) | collective-permute-done | bytes 16416 | tf_op jit(solution)/shard_map/ppermute | solution.py:233
  69.5 2.3 collective-permute-start.6
  73.4 3.3 collective-permute-start.7
  78.3 2.7 pad_maximum_fusion
  81.0 2.9 copy.13
  86.9 2.1 collective-permute-start.1
  89.0 2.2 collective-permute-start.2
  96.3 14.4 %collective-permute-done.1.refs_0_.refs_1_ = f32[8,128,128]{2,1,0:T(8,128)S(1)} collective-permute-done((f32[8,128,128]{2,1,0:T(8,128)S(1)}, f32[8,128,128]{2,1,0:T(8,128)S(1)}, u32[]{:S(2)}, u32[]{:S(2)}) %collective-permute-start.1) | collective-permute-done | bytes 524320 | tf_op jit(solution)/shard_map/ppermute | solution.py:233
  115.4 7.6 %collective-permute-done.44.refs_41_.refs_6_ = f32[8,128,128]{2,1,0:T(8,128)S(1)} collective-permute-done((f32[8,128,128]{2,1,0:T(8,128)S(1)}, f32[8,128,128]{2,1,0:T(8,128)S(1)}, u32[]{:S(2)}, u32[]{:S(2)}) %collective-permute-start.44) | collective-permute-done | bytes 524320 | tf_op jit(solution)/shard_map/ppermute | solution.py:233
  126.2 15.6 %collective-permute-done.3.refs_0_.refs_3_ = f32[8,128,128]{2,1,0:T(8,128)S(1)} collective-permute-done((f32[8,128,128]{2,1,0:T(8,128)S(1)}, f32[8,128,128]{2,1,0:T(8,128)S(1)}, u32[]{:S(2)}, u32[]{:S(2)}) %collective-permute-start.3) | collective-permute-done | bytes 524320 | tf_op jit(solution)/shard_map/ppermute | solution.py:233
  154.4 5.0 %collective-permute-done.26.refs_15_.refs_23_ = f32[264,128]{1,0:T(8,128)S(1)} collective-permute-done((f32[264,128]{1,0:T(8,128)S(1)}, f32[264,128]{1,0:T(8,128)S(1)}, u32[]{:S(2)}, u32[]{:S(2)}) %collective-permute-start.26) | collective-permute-done | bytes 135200 | tf_op jit(solution)/shard_map/ppermute | solution.py:233
  159.4 2.0 shard_map.50
  164.1 2.9 collective-permute-done.36.refs_19_
  173.1 2.9 collective-permute-done.32.refs_27_
  178.0 4.2 collective-permute-done.38.refs_30_
  183.0 2.8 collective-permute-start.64
  185.8 5.0 %collective-permute-done.39.refs_31_ = f32[512,128]{1,0:T(8,128)S(1)} collective-permute-done((f32[512,128]{1,0:T(8,128)S(1)}, f32[512,128]{1,0:T(8,128)S(1)}, u32[]{:S(2)}, u32[]{:S(2)}) %collective-permute-start.39) | collective-permute-done | bytes 262176 | tf_op jit(solution)/shard_map/ppermute | solution.py:233
  190.8 6.9 %collective-permute-done.43.refs_40_.refs_5_ = f32[8,128,128]{2,1,0:T(8,128)S(1)} collective-permute-done((f32[8,128,128]{2,1,0:T(8,128)S(1)}, f32[8,128,128]{2,1,0:T(8,128)S(1)}, u32[]{:S(2)}, u32[]{:S(2)}) %collective-permute-start.43) | collective-permute-done | bytes 524320 | tf_op jit(solution)/shard_map/ppermute | solution.py:249
  197.7 9.6 %collective-permute-done.45.refs_42_.refs_7_ = f32[8,128,128]{2,1,0:T(8,128)S(1)} collective-permute-done((f32[8,128,128]{2,1,0:T(8,128)S(1)}, f32[8,128,128]{2,1,0:T(8,128)S(1)}, u32[]{:S(2)}, u32[]{:S(2)}) %collective-permute-start.45) | collective-permute-done | bytes 524320 | tf_op jit(solution)/shard_map/ppermute | solution.py:249
  208.1 4.9 %shard_map.52 = (f32[8,128,128]{2,1,0:T(8,128)S(1)}, f32[8,128,128]{2,1,0:T(8,128)S(1)}, f32[8,128,128]{2,1,0:T(8,128)S(1)}, f32[8,128,128]{2,1,0:T(8,128)S(1)},...) custom-call(s32[3]{0:T(128)S(1)} %pad_add_fusion.place, ...), custom_call_target="tpu_custom_call" | custom-call | flops 805306368 | bytes 18432012 | tf_op jit(solution)/shard_map/pallas_call | solution.py:180
  219.1 4.0 collective-permute-done.53.refs_2_
  225.0 8.5 %collective-permute-done.54.refs_3_ = f32[512,128]{1,0:T(8,128)S(1)} collective-permute-done((f32[512,128]{1,0:T(8,128)S(1)}, f32[512,128]{1,0:T(8,128)S(1)}, u32[]{:S(2)}, u32[]{:S(2)}) %collective-permute-start.54) | collective-permute-done | bytes 262176 | tf_op jit(solution)/shard_map/ppermute | solution.py:233
  237.6 4.4 collective-permute-done.48.refs_3_.refs_11_
  243.9 2.1 shard_map.53
  254.9 7.0 %collective-permute-done.50.refs_14_ = f32[512,128]{1,0:T(8,128)S(1)} collective-permute-done((f32[512,128]{1,0:T(8,128)S(1)}, f32[512,128]{1,0:T(8,128)S(1)}, u32[]{:S(2)}, u32[]{:S(2)}) %collective-permute-start.50) | collective-permute-done | bytes 262176 | tf_op jit(solution)/shard_map/ppermute | solution.py:233
  261.9 5.3 %collective-permute-done.51.refs_15_ = f32[512,128]{1,0:T(8,128)S(1)} collective-permute-done((f32[512,128]{1,0:T(8,128)S(1)}, f32[512,128]{1,0:T(8,128)S(1)}, u32[]{:S(2)}, u32[]{:S(2)}) %collective-permute-start.51) | collective-permute-done | bytes 262176 | tf_op jit(solution)/shard_map/ppermute | solution.py:233
  267.3 4.4 collective-permute-done.65.refs_30_.refs_7_
  272.5 4.8 %shard_map.55 = (f32[8,128,128]{2,1,0:T(8,128)S(1)}, f32[8,128,128]{2,1,0:T(8,128)S(1)}, f32[8,128,128]{2,1,0:T(8,128)S(1)}, f32[8,128,128]{2,1,0:T(8,128)S(1)},...) custom-call(s32[3]{0:T(128)S(1)} %pad_add_fusion.place, ...), custom_call_target="tpu_custom_call" | custom-call | flops 805306368 | bytes 17334284 | tf_op jit(solution)/shard_map/pallas_call | solution.py:180
  282.3 4.8 %collective-permute-done.73.refs_2_ = f32[512,128]{1,0:T(8,128)S(1)} collective-permute-done((f32[512,128]{1,0:T(8,128)S(1)}, f32[512,128]{1,0:T(8,128)S(1)}, u32[]{:S(2)}, u32[]{:S(2)}) %collective-permute-start.73) | collective-permute-done | bytes 262176 | tf_op jit(solution)/shard_map/ppermute | solution.py:233
  287.7 4.4 collective-permute-done.74.refs_3_
  299.0 4.4 %collective-permute-done.68.refs_3_.refs_11_ = f32[520,128]{1,0:T(8,128)S(1)} collective-permute-done((f32[520,128]{1,0:T(8,128)S(1)}, f32[520,128]{1,0:T(8,128)S(1)}, u32[]{:S(2)}, u32[]{:S(2)}) %collective-permute-start.68) | collective-permute-done | bytes 266272 | tf_op jit(solution)/shard_map/ppermute | solution.py:233
  306.2 2.1 shard_map.56
  310.3 4.4 collective-permute-done.77.refs_19_
  315.6 5.4 %collective-permute-done.70.refs_14_ = f32[512,128]{1,0:T(8,128)S(1)} collective-permute-done((f32[512,128]{1,0:T(8,128)S(1)}, f32[512,128]{1,0:T(8,128)S(1)}, u32[]{:S(2)}, u32[]{:S(2)}) %collective-permute-start.70) | collective-permute-done | bytes 262176 | tf_op jit(solution)/shard_map/ppermute | solution.py:233
  321.0 4.8 %collective-permute-done.71.refs_15_ = f32[512,128]{1,0:T(8,128)S(1)} collective-permute-done((f32[512,128]{1,0:T(8,128)S(1)}, f32[512,128]{1,0:T(8,128)S(1)}, u32[]{:S(2)}, u32[]{:S(2)}) %collective-permute-start.71) | collective-permute-done | bytes 262176 | tf_op jit(solution)/shard_map/ppermute | solution.py:233
  325.9 3.3 collective-permute-done.83.refs_30_.refs_7_
  330.0 4.7 %shard_map.58 = (f32[8,128,128]{2,1,0:T(8,128)S(1)}, f32[8,128,128]{2,1,0:T(8,128)S(1)}, f32[8,128,128]{2,1,0:T(8,128)S(1)}, f32[8,128,128]{2,1,0:T(8,128)S(1)},...) custom-call(s32[3]{0:T(128)S(1)} %pad_add_fusion.place, ...), custom_call_target="tpu_custom_call" | custom-call | flops 805306368 | bytes 17334284 | tf_op jit(solution)/shard_map/pallas_call | solution.py:180
  338.5 5.4 %collective-permute-done.91.refs_2_ = f32[512,128]{1,0:T(8,128)S(1)} collective-permute-done((f32[512,128]{1,0:T(8,128)S(1)}, f32[512,128]{1,0:T(8,128)S(1)}, u32[]{:S(2)}, u32[]{:S(2)}) %collective-permute-start.91) | collective-permute-done | bytes 262176 | tf_op jit(solution)/shard_map/ppermute | solution.py:233
  343.9 4.7 %collective-permute-done.92.refs_3_ = f32[512,128]{1,0:T(8,128)S(1)} collective-permute-done((f32[512,128]{1,0:T(8,128)S(1)}, f32[512,128]{1,0:T(8,128)S(1)}, u32[]{:S(2)}, u32[]{:S(2)}) %collective-permute-start.92) | collective-permute-done | bytes 262176 | tf_op jit(solution)/shard_map/ppermute | solution.py:233
  355.6 4.4 collective-permute-done.86.refs_3_.refs_11_
  363.8 2.7 collective-permute-done.94.refs_18_
  366.6 4.7 %collective-permute-done.95.refs_19_ = f32[512,128]{1,0:T(8,128)S(1)} collective-permute-done((f32[512,128]{1,0:T(8,128)S(1)}, f32[512,128]{1,0:T(8,128)S(1)}, u32[]{:S(2)}, u32[]{:S(2)}) %collective-permute-start.95) | collective-permute-done | bytes 262176 | tf_op jit(solution)/shard_map/ppermute | solution.py:233
  371.3 6.5 %collective-permute-done.88.refs_14_ = f32[512,128]{1,0:T(8,128)S(1)} collective-permute-done((f32[512,128]{1,0:T(8,128)S(1)}, f32[512,128]{1,0:T(8,128)S(1)}, u32[]{:S(2)}, u32[]{:S(2)}) %collective-permute-start.88) | collective-permute-done | bytes 262176 | tf_op jit(solution)/shard_map/ppermute | solution.py:233
  377.8 4.7 %collective-permute-done.89.refs_15_ = f32[512,128]{1,0:T(8,128)S(1)} collective-permute-done((f32[512,128]{1,0:T(8,128)S(1)}, f32[512,128]{1,0:T(8,128)S(1)}, u32[]{:S(2)}, u32[]{:S(2)}) %collective-permute-start.89) | collective-permute-done | bytes 262176 | tf_op jit(solution)/shard_map/ppermute | solution.py:233
  387.9 10.7 %collective-permute-done.98 = f32[8,128,128]{2,1,0:T(8,128)S(1)} collective-permute-done((f32[8,128,128]{2,1,0:T(8,128)S(1)}, f32[8,128,128]{2,1,0:T(8,128)S(1)}, u32[]{:S(2)}, u32[]{:S(2)}) %collective-permute-start.98) | collective-permute-done | bytes 524320 | tf_op jit(solution)/shard_map/ppermute | solution.py:233
  398.6 13.3 %collective-permute-done.97 = f32[8,128,128]{2,1,0:T(8,128)S(1)} collective-permute-done((f32[8,128,128]{2,1,0:T(8,128)S(1)}, f32[8,128,128]{2,1,0:T(8,128)S(1)}, u32[]{:S(2)}, u32[]{:S(2)}) %collective-permute-start.97) | collective-permute-done | bytes 524320 | tf_op jit(solution)/shard_map/ppermute | solution.py:233
  411.9 21.6 %collective-permute-done.96 = f32[8,128,128]{2,1,0:T(8,128)} collective-permute-done((f32[8,128,128]{2,1,0:T(8,128)S(1)}, f32[8,128,128]{2,1,0:T(8,128)}, u32[]{:S(2)}, u32[]{:S(2)}) %collective-permute-start.96) | collective-permute-done | bytes 524320 | tf_op jit(solution)/shard_map/ppermute | solution.py:233
  435.4 2.6 collective-permute-done.99
  438.6 2.0 copy.15
  440.6 2.7 reshape.31
  (316 shorter events, 118.7 us)
Async XLA Ops:
  11.8 18.4 %collective-permute-start.27 = (f32[8,128,128]{2,1,0:T(8,128)S(1)}, f32[8,128,128]{2,1,0:T(8,128)}, u32[]{:S(2)}, u32[]{:S(2)}) collective-permute-start(f32[8,128,128]{2,1,0:T(8,128)S(1)} %dynamic-slice_bitcast_fusion.5), channel_id=1, source_target_pairs={{0,8},{1,9},{2,10},{3,11},{4,12},{5,13},{6,14},{7,15},{8,0},{9,1},... | collective-permute-start | bytes 1572872 | tf_op jit(solution)/shard_map/ppermute | solution.py:233
  27.6 49.2 %collective-permute-start = (f32[2,8,128,128]{2,1,3,0:T(8,128)}, f32[2,8,128,128]{2,1,3,0:T(8,128)}, u32[]{:S(2)}, u32[]{:S(2)}) collective-permute-start(f32[2,8,128,128]{2,1,3,0:T(8,128)} %get-tuple-element.228), channel_id=1, source_target_pairs={{0,8},{1,9},{2,10},{3,11},{4,12},{5,13},{6,14},{7,15},{8,0},{9,1},... | collective-permute-start | bytes 3145736 | tf_op jit(solution)/shard_map/ppermute | solution.py:233
  38.9 50.1 %collective-permute-start.58 = (f32[8,128,128]{2,1,0:T(8,128)}, f32[8,128,128]{2,1,0:T(8,128)}, u32[]{:S(2)}, u32[]{:S(2)}) collective-permute-start(f32[8,128,128]{2,1,0:T(8,128)} %dynamic-slice_bitcast_fusion.4), channel_id=1, source_target_pairs={{0,8},{1,9},{2,10},{3,11},{4,12},{5,13},{6,14},{7,15},{8,0},{9,1},... | collective-permute-start | bytes 1572872 | tf_op jit(solution)/shard_map/ppermute | solution.py:233
  40.3 51.0 %collective-permute-start.59 = (f32[8,128,128]{2,1,0:T(8,128)}, f32[8,128,128]{2,1,0:T(8,128)}, u32[]{:S(2)}, u32[]{:S(2)}) collective-permute-start(f32[8,128,128]{2,1,0:T(8,128)} %dynamic-slice_bitcast_fusion.3), channel_id=1, source_target_pairs={{0,8},{1,9},{2,10},{3,11},{4,12},{5,13},{6,14},{7,15},{8,0},{9,1},... | collective-permute-start | bytes 1572872 | tf_op jit(solution)/shard_map/ppermute | solution.py:233
  58.3 18.4 %collective-permute-start.40 = (f32[8,128,128]{2,1,0:T(8,128)S(1)}, f32[8,128,128]{2,1,0:T(8,128)S(1)}, u32[]{:S(2)}, u32[]{:S(2)}) collective-permute-start(f32[8,128,128]{2,1,0:T(8,128)S(1)} %pad_maximum_fusion.3), channel_id=1, source_target_pairs={{0,4},{1,5},{2,0},{3,1},{4,6},{5,7},{6,2},{7,3},{8,12},{9,13},{10,... | collective-permute-start | bytes 1572872 | tf_op jit(solution)/shard_map/ppermute | solution.py:233
  73.4 13.5 %collective-permute-start.7 = (f32[4,8,128]{2,1,0:T(8,128)S(1)}, f32[4,8,128]{2,1,0:T(8,128)S(1)}, u32[]{:S(2)}, u32[]{:S(2)}) collective-permute-start(f32[4,8,128]{2,1,0:T(8,128)S(1)} %collective-permute-done.6), channel_id=1, source_target_pairs={{0,4},{1,5},{2,0},{3,1},{4,6},{5,7},{6,2},{7,3},{8,12},{9,13},{10,... | collective-permute-start | bytes 49160 | tf_op jit(solution)/shard_map/ppermute | solution.py:233
  76.7 14.6 %collective-permute-start.42 = (f32[8,128,128]{2,1,0:T(8,128)S(1)}, f32[8,128,128]{2,1,0:T(8,128)S(1)}, u32[]{:S(2)}, u32[]{:S(2)}) collective-permute-start(f32[8,128,128]{2,1,0:T(8,128)S(1)} %collective-permute-done.40.refs_37_.refs_5_), channel_id=1, source_target_pairs={{0,4},{1,5},{2,0},{3,1},{4,6},{5,7},{6,2},{7,3},{8,12},{9,13},{10,... | collective-permute-start | bytes 1572872 | tf_op jit(solution)/shard_map/ppermute | solution.py:233
  76.8 15.9 %collective-permute-start.13 = (f32[4,128,128]{2,1,0:T(8,128)S(1)}, f32[4,128,128]{2,1,0:T(8,128)}, u32[]{:S(2)}, u32[]{:S(2)}) collective-permute-start(f32[4,128,128]{2,1,0:T(8,128)S(1)} %collective-permute-done.12.refs_2_), channel_id=1, source_target_pairs={{0,16},{16,0},{1,17},{17,1},{2,18},{18,2},{3,19},{19,3},{4,20},{20... | collective-permute-start | bytes 786440 | tf_op jit(solution)/shard_map/ppermute | solution.py:249
  86.9 23.8 %collective-permute-start.1 = (f32[8,128,128]{2,1,0:T(8,128)S(1)}, f32[8,128,128]{2,1,0:T(8,128)S(1)}, u32[]{:S(2)}, u32[]{:S(2)}) collective-permute-start(f32[8,128,128]{2,1,0:T(8,128)S(1)} %get-tuple-element.225), channel_id=1, source_target_pairs={{0,4},{1,5},{2,0},{3,1},{4,6},{5,7},{6,2},{7,3},{8,12},{9,13},{10,... | collective-permute-start | bytes 1572872 | tf_op jit(solution)/shard_map/ppermute | solution.py:233
  89.0 26.3 %collective-permute-start.2 = (f32[8,128,128]{2,1,0:T(8,128)S(1)}, f32[8,128,128]{2,1,0:T(8,128)S(1)}, u32[]{:S(2)}, u32[]{:S(2)}) collective-permute-start(f32[8,128,128]{2,1,0:T(8,128)S(1)} %get-tuple-element.224), channel_id=1, source_target_pairs={{0,6},{1,7},{2,4},{3,5},{4,2},{5,3},{6,0},{7,1},{8,14},{9,15},{10,... | collective-permute-start | bytes 1572872 | tf_op jit(solution)/shard_map/ppermute | solution.py:233
  91.3 31.7 %collective-permute-start.44 = (f32[8,128,128]{2,1,0:T(8,128)S(1)}, f32[8,128,128]{2,1,0:T(8,128)S(1)}, u32[]{:S(2)}, u32[]{:S(2)}) collective-permute-start(f32[8,128,128]{2,1,0:T(8,128)S(1)} %collective-permute-done.42.refs_39_.refs_4_), channel_id=1, source_target_pairs={{0,4},{1,5},{2,0},{3,1},{4,6},{5,7},{6,2},{7,3},{8,12},{9,13},{10,... | collective-permute-start | bytes 1572872 | tf_op jit(solution)/shard_map/ppermute | solution.py:233
  92.6 49.2 %collective-permute-start.3 = (f32[8,128,128]{2,1,0:T(8,128)S(1)}, f32[8,128,128]{2,1,0:T(8,128)S(1)}, u32[]{:S(2)}, u32[]{:S(2)}) collective-permute-start(f32[8,128,128]{2,1,0:T(8,128)S(1)} %get-tuple-element.223), channel_id=1, source_target_pairs={{0,2},{1,3},{2,6},{3,7},{4,0},{5,1},{6,4},{7,5},{8,10},{9,11},{10,... | collective-permute-start | bytes 1572872 | tf_op jit(solution)/shard_map/ppermute | solution.py:233
  94.6 19.2 %collective-permute-start.18 = (f32[4,128,128]{2,1,0:T(8,128)S(1)}, f32[4,128,128]{2,1,0:T(8,128)S(1)}, u32[]{:S(2)}, u32[]{:S(2)}) collective-permute-start(f32[4,128,128]{2,1,0:T(8,128)S(1)} %collective-permute-done.17.refs_2_), channel_id=1, source_target_pairs={{0,16},{16,0},{1,17},{17,1},{2,18},{18,2},{3,19},{19,3},{4,20},{20... | collective-permute-start | bytes 786440 | tf_op jit(solution)/shard_map/ppermute | solution.py:249
  110.7 31.2 %collective-permute-start.23 = (f32[4,128,128]{2,1,0:T(8,128)S(1)}, f32[4,128,128]{2,1,0:T(8,128)S(1)}, u32[]{:S(2)}, u32[]{:S(2)}) collective-permute-start(f32[4,128,128]{2,1,0:T(8,128)S(1)} %collective-permute-done.22.refs_2_), channel_id=1, source_target_pairs={{0,16},{16,0},{1,17},{17,1},{2,18},{18,2},{3,19},{19,3},{4,20},{20... | collective-permute-start | bytes 786440 | tf_op jit(solution)/shard_map/ppermute | solution.py:249
  115.4 10.5 %collective-permute-start.11 = (f32[264,128]{1,0:T(8,128)S(1)}, f32[264,128]{1,0:T(8,128)S(1)}, u32[]{:S(2)}, u32[]{:S(2)}) collective-permute-start(f32[264,128]{1,0:T(8,128)S(1)} %get-tuple-element.112), channel_id=1, source_target_pairs={{0,9},{1,8},{2,11},{3,10},{4,13},{5,12},{6,15},{7,14},{8,1},{9,0},... | collective-permute-start | bytes 405512 | tf_op jit(solution)/shard_map/ppermute | solution.py:233
  123.0 20.4 %collective-permute-start.14 = (f32[264,128]{1,0:T(8,128)S(1)}, f32[264,128]{1,0:T(8,128)S(1)}, u32[]{:S(2)}, u32[]{:S(2)}) collective-permute-start(f32[264,128]{1,0:T(8,128)S(1)} %get-tuple-element.114), channel_id=1, source_target_pairs={{0,8},{1,9},{2,10},{3,11},{4,12},{5,13},{6,14},{7,15},{8,0},{9,1},... | collective-permute-start | bytes 405512 | tf_op jit(solution)/shard_map/ppermute | solution.py:233
  124.3 20.3 %collective-permute-start.15 = (f32[264,128]{1,0:T(8,128)S(1)}, f32[264,128]{1,0:T(8,128)S(1)}, u32[]{:S(2)}, u32[]{:S(2)}) collective-permute-start(f32[264,128]{1,0:T(8,128)S(1)} %get-tuple-element.115), channel_id=1, source_target_pairs={{0,1},{1,0},{2,3},{3,2},{4,5},{5,4},{6,7},{7,6},{8,9},{9,8},{10,11... | collective-permute-start | bytes 405512 | tf_op jit(solution)/shard_map/ppermute | solution.py:233
  125.9 19.1 %collective-permute-start.16 = (f32[264,128]{1,0:T(8,128)S(1)}, f32[264,128]{1,0:T(8,128)S(1)}, u32[]{:S(2)}, u32[]{:S(2)}) collective-permute-start(f32[264,128]{1,0:T(8,128)S(1)} %get-tuple-element.116), channel_id=1, source_target_pairs={{0,9},{1,8},{2,11},{3,10},{4,13},{5,12},{6,15},{7,14},{8,1},{9,0},... | collective-permute-start | bytes 405512 | tf_op jit(solution)/shard_map/ppermute | solution.py:233
  143.3 25.3 %collective-permute-start.60 = (f32[8,128,128]{2,1,0:T(8,128)S(1)}, f32[8,128,128]{2,1,0:T(8,128)S(1)}, u32[]{:S(2)}, u32[]{:S(2)}) collective-permute-start(f32[8,128,128]{2,1,0:T(8,128)S(1)} %pad_maximum_fusion.4), channel_id=1, source_target_pairs={{0,4},{1,5},{2,0},{3,1},{4,6},{5,7},{6,2},{7,3},{8,12},{9,13},{10,... | collective-permute-start | bytes 1572872 | tf_op jit(solution)/shard_map/ppermute | solution.py:233
  147.9 11.5 %collective-permute-start.29 = (f32[4,128,128]{2,1,0:T(8,128)S(1)}, f32[4,128,128]{2,1,0:T(8,128)S(1)}, u32[]{:S(2)}, u32[]{:S(2)}) collective-permute-start(f32[4,128,128]{2,1,0:T(8,128)S(1)} %copy-done.48), channel_id=1, source_target_pairs={{0,16},{16,0},{1,17},{17,1},{2,18},{18,2},{3,19},{19,3},{4,20},{20... | collective-permute-start | bytes 786440 | tf_op jit(solution)/shard_map/ppermute | solution.py:249
  150.4 13.3 %collective-permute-start.34 = (f32[4,128,128]{2,1,0:T(8,128)S(1)}, f32[4,128,128]{2,1,0:T(8,128)S(1)}, u32[]{:S(2)}, u32[]{:S(2)}) collective-permute-start(f32[4,128,128]{2,1,0:T(8,128)S(1)} %copy-done.50), channel_id=1, source_target_pairs={{0,16},{16,0},{1,17},{17,1},{2,18},{18,2},{3,19},{19,3},{4,20},{20... | collective-permute-start | bytes 786440 | tf_op jit(solution)/shard_map/ppermute | solution.py:249
  151.9 15.0 %collective-permute-start.36 = (f32[4,128,128]{2,1,0:T(8,128)S(1)}, f32[4,128,128]{2,1,0:T(8,128)S(1)}, u32[]{:S(2)}, u32[]{:S(2)}) collective-permute-start(f32[4,128,128]{2,1,0:T(8,128)S(1)} %copy-done.52), channel_id=1, source_target_pairs={{0,16},{16,0},{1,17},{17,1},{2,18},{18,2},{3,19},{19,3},{4,20},{20... | collective-permute-start | bytes 786440 | tf_op jit(solution)/shard_map/ppermute | solution.py:249
  163.7 12.2 %collective-permute-start.32 = (f32[512,128]{1,0:T(8,128)S(1)}, f32[512,128]{1,0:T(8,128)S(1)}, u32[]{:S(2)}, u32[]{:S(2)}) collective-permute-start(f32[512,128]{1,0:T(8,128)S(1)} %get-tuple-element.129), channel_id=1, source_target_pairs={{0,9},{1,8},{2,11},{3,10},{4,13},{5,12},{6,15},{7,14},{8,1},{9,0},... | collective-permute-start | bytes 786440 | tf_op jit(solution)/shard_map/ppermute | solution.py:233
  168.7 14.3 %collective-permute-start.62 = (f32[8,128,128]{2,1,0:T(8,128)S(1)}, f32[8,128,128]{2,1,0:T(8,128)S(1)}, u32[]{:S(2)}, u32[]{:S(2)}) collective-permute-start(f32[8,128,128]{2,1,0:T(8,128)S(1)} %collective-permute-done.60.refs_25_.refs_5_), channel_id=1, source_target_pairs={{0,4},{1,5},{2,0},{3,1},{4,6},{5,7},{6,2},{7,3},{8,12},{9,13},{10,... | collective-permute-start | bytes 1572872 | tf_op jit(solution)/shard_map/ppermute | solution.py:233
  170.6 11.6 %collective-permute-start.38 = (f32[512,128]{1,0:T(8,128)S(1)}, f32[512,128]{1,0:T(8,128)S(1)}, u32[]{:S(2)}, u32[]{:S(2)}) collective-permute-start(f32[512,128]{1,0:T(8,128)S(1)} %get-tuple-element.132), channel_id=1, source_target_pairs={{0,1},{1,0},{2,3},{3,2},{4,5},{5,4},{6,7},{7,6},{8,9},{9,8},{10,11... | collective-permute-start | bytes 786440 | tf_op jit(solution)/shard_map/ppermute | solution.py:233
  171.6 19.2 %collective-permute-start.41 = (f32[8,128,128]{2,1,0:T(8,128)S(1)}, f32[8,128,128]{2,1,0:T(8,128)S(1)}, u32[]{:S(2)}, u32[]{:S(2)}) collective-permute-start(f32[8,128,128]{2,1,0:T(8,128)S(1)} %collective-permute-done.40.refs_37_.refs_5_), channel_id=1, source_target_pairs={{0,16},{16,0},{1,17},{17,1},{2,18},{18,2},{3,19},{19,3},{4,20},{20... | collective-permute-start | bytes 1572872 | tf_op jit(solution)/shard_map/ppermute | solution.py:249
  176.0 21.7 %collective-permute-start.43 = (f32[8,128,128]{2,1,0:T(8,128)S(1)}, f32[8,128,128]{2,1,0:T(8,128)S(1)}, u32[]{:S(2)}, u32[]{:S(2)}) collective-permute-start(f32[8,128,128]{2,1,0:T(8,128)S(1)} %collective-permute-done.42.refs_39_.refs_4_), channel_id=1, source_target_pairs={{0,16},{16,0},{1,17},{17,1},{2,18},{18,2},{3,19},{19,3},{4,20},{20... | collective-permute-start | bytes 1572872 | tf_op jit(solution)/shard_map/ppermute | solution.py:249
  177.5 29.8 %collective-permute-start.45 = (f32[8,128,128]{2,1,0:T(8,128)S(1)}, f32[8,128,128]{2,1,0:T(8,128)S(1)}, u32[]{:S(2)}, u32[]{:S(2)}) collective-permute-start(f32[8,128,128]{2,1,0:T(8,128)S(1)} %collective-permute-done.44.refs_41_.refs_6_), channel_id=1, source_target_pairs={{0,16},{16,0},{1,17},{17,1},{2,18},{18,2},{3,19},{19,3},{4,20},{20... | collective-permute-start | bytes 1572872 | tf_op jit(solution)/shard_map/ppermute | solution.py:249
  183.0 34.5 %collective-permute-start.64 = (f32[8,128,128]{2,1,0:T(8,128)S(1)}, f32[8,128,128]{2,1,0:T(8,128)S(1)}, u32[]{:S(2)}, u32[]{:S(2)}) collective-permute-start(f32[8,128,128]{2,1,0:T(8,128)S(1)} %collective-permute-done.62.refs_27_.refs_4_), channel_id=1, source_target_pairs={{0,4},{1,5},{2,0},{3,1},{4,6},{5,7},{6,2},{7,3},{8,12},{9,13},{10,... | collective-permute-start | bytes 1572872 | tf_op jit(solution)/shard_map/ppermute | solution.py:233
  215.6 21.3 %collective-permute-start.46 = (f32[520,128]{1,0:T(8,128)S(1)}, f32[520,128]{1,0:T(8,128)S(1)}, u32[]{:S(2)}, u32[]{:S(2)}) collective-permute-start(f32[520,128]{1,0:T(8,128)S(1)} %get-tuple-element.144), channel_id=1, source_target_pairs={{0,8},{1,9},{2,10},{3,11},{4,12},{5,13},{6,14},{7,15},{8,0},{9,1},... | collective-permute-start | bytes 798728 | tf_op jit(solution)/shard_map/ppermute | solution.py:233
  215.8 21.2 %collective-permute-start.47 = (f32[520,128]{1,0:T(8,128)S(1)}, f32[520,128]{1,0:T(8,128)S(1)}, u32[]{:S(2)}, u32[]{:S(2)}) collective-permute-start(f32[520,128]{1,0:T(8,128)S(1)} %get-tuple-element.145), channel_id=1, source_target_pairs={{0,1},{1,0},{2,3},{3,2},{4,5},{5,4},{6,7},{7,6},{8,9},{9,8},{10,11... | collective-permute-start | bytes 798728 | tf_op jit(solution)/shard_map/ppermute | solution.py:233
  216.3 17.2 %collective-permute-start.54 = (f32[512,128]{1,0:T(8,128)S(1)}, f32[512,128]{1,0:T(8,128)S(1)}, u32[]{:S(2)}, u32[]{:S(2)}) collective-permute-start(f32[512,128]{1,0:T(8,128)S(1)} %get-tuple-element.154), channel_id=1, source_target_pairs={{0,9},{1,8},{2,11},{3,10},{4,13},{5,12},{6,15},{7,14},{8,1},{9,0},... | collective-permute-start | bytes 786440 | tf_op jit(solution)/shard_map/ppermute | solution.py:233
  217.5 28.4 %collective-permute-start.61 = (f32[8,128,128]{2,1,0:T(8,128)S(1)}, f32[8,128,128]{2,1,0:T(8,128)S(1)}, u32[]{:S(2)}, u32[]{:S(2)}) collective-permute-start(f32[8,128,128]{2,1,0:T(8,128)S(1)} %collective-permute-done.60.refs_25_.refs_5_), channel_id=1, source_target_pairs={{0,16},{16,0},{1,17},{17,1},{2,18},{18,2},{3,19},{19,3},{4,20},{20... | collective-permute-start | bytes 1572872 | tf_op jit(solution)/shard_map/ppermute | solution.py:249
  223.1 26.9 %collective-permute-start.78 = (f32[8,128,128]{2,1,0:T(8,128)S(1)}, f32[8,128,128]{2,1,0:T(8,128)S(1)}, u32[]{:S(2)}, u32[]{:S(2)}) collective-permute-start(f32[8,128,128]{2,1,0:T(8,128)S(1)} %pad_maximum_fusion.5), channel_id=1, source_target_pairs={{0,4},{1,5},{2,0},{3,1},{4,6},{5,7},{6,2},{7,3},{8,12},{9,13},{10,... | collective-permute-start | bytes 1572872 | tf_op jit(solution)/shard_map/ppermute | solution.py:233
  237.0 11.5 %collective-permute-start.56 = (f32[512,128]{1,0:T(8,128)S(1)}, f32[512,128]{1,0:T(8,128)S(1)}, u32[]{:S(2)}, u32[]{:S(2)}) collective-permute-start(f32[512,128]{1,0:T(8,128)S(1)} %get-tuple-element.157), channel_id=1, source_target_pairs={{0,1},{1,0},{2,3},{3,2},{4,5},{5,4},{6,7},{7,6},{8,9},{9,8},{10,11... | collective-permute-start | bytes 786440 | tf_op jit(solution)/shard_map/ppermute | solution.py:233
  242.0 10.8 %collective-permute-start.57 = (f32[512,128]{1,0:T(8,128)S(1)}, f32[512,128]{1,0:T(8,128)S(1)}, u32[]{:S(2)}, u32[]{:S(2)}) collective-permute-start(f32[512,128]{1,0:T(8,128)S(1)} %get-tuple-element.158), channel_id=1, source_target_pairs={{0,9},{1,8},{2,11},{3,10},{4,13},{5,12},{6,15},{7,14},{8,1},{9,0},... | collective-permute-start | bytes 786440 | tf_op jit(solution)/shard_map/ppermute | solution.py:233
  246.1 21.2 %collective-permute-start.63 = (f32[8,128,128]{2,1,0:T(8,128)S(1)}, f32[8,128,128]{2,1,0:T(8,128)S(1)}, u32[]{:S(2)}, u32[]{:S(2)}) collective-permute-start(f32[8,128,128]{2,1,0:T(8,128)S(1)} %collective-permute-done.62.refs_27_.refs_4_), channel_id=1, source_target_pairs={{0,16},{16,0},{1,17},{17,1},{2,18},{18,2},{3,19},{19,3},{4,20},{20... | collective-permute-start | bytes 1572872 | tf_op jit(solution)/shard_map/ppermute | solution.py:249
  248.6 23.1 %collective-permute-start.65 = (f32[8,128,128]{2,1,0:T(8,128)S(1)}, f32[8,128,128]{2,1,0:T(8,128)S(1)}, u32[]{:S(2)}, u32[]{:S(2)}) collective-permute-start(f32[8,128,128]{2,1,0:T(8,128)S(1)} %copy-done.15), channel_id=1, source_target_pairs={{0,16},{16,0},{1,17},{17,1},{2,18},{18,2},{3,19},{19,3},{4,20},{20... | collective-permute-start | bytes 1572872 | tf_op jit(solution)/shard_map/ppermute | solution.py:249
  250.1 31.3 %collective-permute-start.80 = (f32[8,128,128]{2,1,0:T(8,128)S(1)}, f32[8,128,128]{2,1,0:T(8,128)S(1)}, u32[]{:S(2)}, u32[]{:S(2)}) collective-permute-start(f32[8,128,128]{2,1,0:T(8,128)S(1)} %collective-permute-done.78.refs_25_.refs_5_), channel_id=1, source_target_pairs={{0,4},{1,5},{2,0},{3,1},{4,6},{5,7},{6,2},{7,3},{8,12},{9,13},{10,... | collective-permute-start | bytes 1572872 | tf_op jit(solution)/shard_map/ppermute | solution.py:233
  254.3 13.0 %collective-permute-start.51 = (f32[512,128]{1,0:T(8,128)S(1)}, f32[512,128]{1,0:T(8,128)S(1)}, u32[]{:S(2)}, u32[]{:S(2)}) collective-permute-start(f32[512,128]{1,0:T(8,128)S(1)} %get-tuple-element.150), channel_id=1, source_target_pairs={{0,9},{1,8},{2,11},{3,10},{4,13},{5,12},{6,15},{7,14},{8,1},{9,0},... | collective-permute-start | bytes 786440 | tf_op jit(solution)/shard_map/ppermute | solution.py:233
  278.6 13.5 %collective-permute-start.74 = (f32[512,128]{1,0:T(8,128)S(1)}, f32[512,128]{1,0:T(8,128)S(1)}, u32[]{:S(2)}, u32[]{:S(2)}) collective-permute-start(f32[512,128]{1,0:T(8,128)S(1)} %get-tuple-element.179), channel_id=1, source_target_pairs={{0,9},{1,8},{2,11},{3,10},{4,13},{5,12},{6,15},{7,14},{8,1},{9,0},... | collective-permute-start | bytes 786440 | tf_op jit(solution)/shard_map/ppermute | solution.py:233
  279.9 24.2 %collective-permute-start.79 = (f32[8,128,128]{2,1,0:T(8,128)S(1)}, f32[8,128,128]{2,1,0:T(8,128)S(1)}, u32[]{:S(2)}, u32[]{:S(2)}) collective-permute-start(f32[8,128,128]{2,1,0:T(8,128)S(1)} %collective-permute-done.78.refs_25_.refs_5_), channel_id=1, source_target_pairs={{0,16},{16,0},{1,17},{17,1},{2,18},{18,2},{3,19},{19,3},{4,20},{20... | collective-permute-start | bytes 1572872 | tf_op jit(solution)/shard_map/ppermute | solution.py:249
  281.4 24.2 %collective-permute-start.82 = (f32[8,128,128]{2,1,0:T(8,128)S(1)}, f32[8,128,128]{2,1,0:T(8,128)S(1)}, u32[]{:S(2)}, u32[]{:S(2)}) collective-permute-start(f32[8,128,128]{2,1,0:T(8,128)S(1)} %collective-permute-done.80.refs_27_.refs_4_), channel_id=1, source_target_pairs={{0,4},{1,5},{2,0},{3,1},{4,6},{5,7},{6,2},{7,3},{8,12},{9,13},{10,... | collective-permute-start | bytes 1572872 | tf_op jit(solution)/shard_map/ppermute | solution.py:233
  282.3 14.4 %collective-permute-start.66 = (f32[520,128]{1,0:T(8,128)S(1)}, f32[520,128]{1,0:T(8,128)S(1)}, u32[]{:S(2)}, u32[]{:S(2)}) collective-permute-start(f32[520,128]{1,0:T(8,128)S(1)} %get-tuple-element.169), channel_id=1, source_target_pairs={{0,8},{1,9},{2,10},{3,11},{4,12},{5,13},{6,14},{7,15},{8,0},{9,1},... | collective-permute-start | bytes 798728 | tf_op jit(solution)/shard_map/ppermute | solution.py:233
  287.2 11.3 %collective-permute-start.67 = (f32[520,128]{1,0:T(8,128)S(1)}, f32[520,128]{1,0:T(8,128)S(1)}, u32[]{:S(2)}, u32[]{:S(2)}) collective-permute-start(f32[520,128]{1,0:T(8,128)S(1)} %get-tuple-element.170), channel_id=1, source_target_pairs={{0,1},{1,0},{2,3},{3,2},{4,5},{5,4},{6,7},{7,6},{8,9},{9,8},{10,11... | collective-permute-start | bytes 798728 | tf_op jit(solution)/shard_map/ppermute | solution.py:233
  292.0 11.4 %collective-permute-start.68 = (f32[520,128]{1,0:T(8,128)S(1)}, f32[520,128]{1,0:T(8,128)S(1)}, u32[]{:S(2)}, u32[]{:S(2)}) collective-permute-start(f32[520,128]{1,0:T(8,128)S(1)} %get-tuple-element.171), channel_id=1, source_target_pairs={{0,9},{1,8},{2,11},{3,10},{4,13},{5,12},{6,15},{7,14},{8,1},{9,0},... | collective-permute-start | bytes 798728 | tf_op jit(solution)/shard_map/ppermute | solution.py:233
  296.7 11.5 %collective-permute-start.75 = (f32[512,128]{1,0:T(8,128)S(1)}, f32[512,128]{1,0:T(8,128)S(1)}, u32[]{:S(2)}, u32[]{:S(2)}) collective-permute-start(f32[512,128]{1,0:T(8,128)S(1)} %get-tuple-element.181), channel_id=1, source_target_pairs={{0,8},{1,9},{2,10},{3,11},{4,12},{5,13},{6,14},{7,15},{8,0},{9,1},... | collective-permute-start | bytes 786440 | tf_op jit(solution)/shard_map/ppermute | solution.py:233
  298.5 11.3 %collective-permute-start.76 = (f32[512,128]{1,0:T(8,128)S(1)}, f32[512,128]{1,0:T(8,128)S(1)}, u32[]{:S(2)}, u32[]{:S(2)}) collective-permute-start(f32[512,128]{1,0:T(8,128)S(1)} %get-tuple-element.182), channel_id=1, source_target_pairs={{0,1},{1,0},{2,3},{3,2},{4,5},{5,4},{6,7},{7,6},{8,9},{9,8},{10,11... | collective-permute-start | bytes 786440 | tf_op jit(solution)/shard_map/ppermute | solution.py:233
  303.4 11.2 %collective-permute-start.77 = (f32[512,128]{1,0:T(8,128)S(1)}, f32[512,128]{1,0:T(8,128)S(1)}, u32[]{:S(2)}, u32[]{:S(2)}) collective-permute-start(f32[512,128]{1,0:T(8,128)S(1)} %get-tuple-element.183), channel_id=1, source_target_pairs={{0,9},{1,8},{2,11},{3,10},{4,13},{5,12},{6,15},{7,14},{8,1},{9,0},... | collective-permute-start | bytes 786440 | tf_op jit(solution)/shard_map/ppermute | solution.py:233
  304.1 21.8 %collective-permute-start.81 = (f32[8,128,128]{2,1,0:T(8,128)S(1)}, f32[8,128,128]{2,1,0:T(8,128)S(1)}, u32[]{:S(2)}, u32[]{:S(2)}) collective-permute-start(f32[8,128,128]{2,1,0:T(8,128)S(1)} %collective-permute-done.80.refs_27_.refs_4_), channel_id=1, source_target_pairs={{0,16},{16,0},{1,17},{17,1},{2,18},{18,2},{3,19},{19,3},{4,20},{20... | collective-permute-start | bytes 1572872 | tf_op jit(solution)/shard_map/ppermute | solution.py:249
  305.6 23.5 %collective-permute-start.83 = (f32[8,128,128]{2,1,0:T(8,128)S(1)}, f32[8,128,128]{2,1,0:T(8,128)S(1)}, u32[]{:S(2)}, u32[]{:S(2)}) collective-permute-start(f32[8,128,128]{2,1,0:T(8,128)S(1)} %collective-permute-done.82.refs_29_.refs_6_), channel_id=1, source_target_pairs={{0,16},{16,0},{1,17},{17,1},{2,18},{18,2},{3,19},{19,3},{4,20},{20... | collective-permute-start | bytes 1572872 | tf_op jit(solution)/shard_map/ppermute | solution.py:249
  309.8 11.2 %collective-permute-start.70 = (f32[512,128]{1,0:T(8,128)S(1)}, f32[512,128]{1,0:T(8,128)S(1)}, u32[]{:S(2)}, u32[]{:S(2)}) collective-permute-start(f32[512,128]{1,0:T(8,128)S(1)} %get-tuple-element.174), channel_id=1, source_target_pairs={{0,1},{1,0},{2,3},{3,2},{4,5},{5,4},{6,7},{7,6},{8,9},{9,8},{10,11... | collective-permute-start | bytes 786440 | tf_op jit(solution)/shard_map/ppermute | solution.py:233
  314.7 11.2 %collective-permute-start.71 = (f32[512,128]{1,0:T(8,128)S(1)}, f32[512,128]{1,0:T(8,128)S(1)}, u32[]{:S(2)}, u32[]{:S(2)}) collective-permute-start(f32[512,128]{1,0:T(8,128)S(1)} %get-tuple-element.175), channel_id=1, source_target_pairs={{0,9},{1,8},{2,11},{3,10},{4,13},{5,12},{6,15},{7,14},{8,1},{9,0},... | collective-permute-start | bytes 786440 | tf_op jit(solution)/shard_map/ppermute | solution.py:233
  336.3 12.3 %collective-permute-start.92 = (f32[512,128]{1,0:T(8,128)S(1)}, f32[512,128]{1,0:T(8,128)S(1)}, u32[]{:S(2)}, u32[]{:S(2)}) collective-permute-start(f32[512,128]{1,0:T(8,128)S(1)} %get-tuple-element.204), channel_id=1, source_target_pairs={{0,9},{1,8},{2,11},{3,10},{4,13},{5,12},{6,15},{7,14},{8,1},{9,0},... | collective-permute-start | bytes 786440 | tf_op jit(solution)/shard_map/ppermute | solution.py:233
  336.6 19.0 %collective-permute-start.84 = (f32[520,128]{1,0:T(8,128)S(1)}, f32[520,128]{1,0:T(8,128)S(1)}, u32[]{:S(2)}, u32[]{:S(2)}) collective-permute-start(f32[520,128]{1,0:T(8,128)S(1)} %get-tuple-element.194), channel_id=1, source_target_pairs={{0,8},{1,9},{2,10},{3,11},{4,12},{5,13},{6,14},{7,15},{8,0},{9,1},... | collective-permute-start | bytes 798728 | tf_op jit(solution)/shard_map/ppermute | solution.py:233
  337.0 18.7 %collective-permute-start.85 = (f32[520,128]{1,0:T(8,128)S(1)}, f32[520,128]{1,0:T(8,128)S(1)}, u32[]{:S(2)}, u32[]{:S(2)}) collective-permute-start(f32[520,128]{1,0:T(8,128)S(1)} %get-tuple-element.195), channel_id=1, source_target_pairs={{0,1},{1,0},{2,3},{3,2},{4,5},{5,4},{6,7},{7,6},{8,9},{9,8},{10,11... | collective-permute-start | bytes 798728 | tf_op jit(solution)/shard_map/ppermute | solution.py:233
  338.4 21.6 %collective-permute-start.86 = (f32[520,128]{1,0:T(8,128)S(1)}, f32[520,128]{1,0:T(8,128)S(1)}, u32[]{:S(2)}, u32[]{:S(2)}) collective-permute-start(f32[520,128]{1,0:T(8,128)S(1)} %get-tuple-element.196), channel_id=1, source_target_pairs={{0,9},{1,8},{2,11},{3,10},{4,13},{5,12},{6,15},{7,14},{8,1},{9,0},... | collective-permute-start | bytes 798728 | tf_op jit(solution)/shard_map/ppermute | solution.py:233
  354.1 12.4 %collective-permute-start.94 = (f32[512,128]{1,0:T(8,128)S(1)}, f32[512,128]{1,0:T(8,128)S(1)}, u32[]{:S(2)}, u32[]{:S(2)}) collective-permute-start(f32[512,128]{1,0:T(8,128)S(1)} %get-tuple-element.207), channel_id=1, source_target_pairs={{0,1},{1,0},{2,3},{3,2},{4,5},{5,4},{6,7},{7,6},{8,9},{9,8},{10,11... | collective-permute-start | bytes 786440 | tf_op jit(solution)/shard_map/ppermute | solution.py:233
  355.6 15.7 %collective-permute-start.95 = (f32[512,128]{1,0:T(8,128)S(1)}, f32[512,128]{1,0:T(8,128)S(1)}, u32[]{:S(2)}, u32[]{:S(2)}) collective-permute-start(f32[512,128]{1,0:T(8,128)S(1)} %get-tuple-element.208), channel_id=1, source_target_pairs={{0,9},{1,8},{2,11},{3,10},{4,13},{5,12},{6,15},{7,14},{8,1},{9,0},... | collective-permute-start | bytes 786440 | tf_op jit(solution)/shard_map/ppermute | solution.py:233
  362.4 15.4 %collective-permute-start.88 = (f32[512,128]{1,0:T(8,128)S(1)}, f32[512,128]{1,0:T(8,128)S(1)}, u32[]{:S(2)}, u32[]{:S(2)}) collective-permute-start(f32[512,128]{1,0:T(8,128)S(1)} %get-tuple-element.199), channel_id=1, source_target_pairs={{0,1},{1,0},{2,3},{3,2},{4,5},{5,4},{6,7},{7,6},{8,9},{9,8},{10,11... | collective-permute-start | bytes 786440 | tf_op jit(solution)/shard_map/ppermute | solution.py:233
  363.8 18.7 %collective-permute-start.89 = (f32[512,128]{1,0:T(8,128)S(1)}, f32[512,128]{1,0:T(8,128)S(1)}, u32[]{:S(2)}, u32[]{:S(2)}) collective-permute-start(f32[512,128]{1,0:T(8,128)S(1)} %get-tuple-element.200), channel_id=1, source_target_pairs={{0,9},{1,8},{2,11},{3,10},{4,13},{5,12},{6,15},{7,14},{8,1},{9,0},... | collective-permute-start | bytes 786440 | tf_op jit(solution)/shard_map/ppermute | solution.py:233
  384.4 14.2 %collective-permute-start.98 = (f32[8,128,128]{2,1,0:T(8,128)S(1)}, f32[8,128,128]{2,1,0:T(8,128)S(1)}, u32[]{:S(2)}, u32[]{:S(2)}) collective-permute-start(f32[8,128,128]{2,1,0:T(8,128)S(1)} %get-tuple-element.212), channel_id=1, source_target_pairs={{0,4},{1,5},{2,0},{3,1},{4,6},{5,7},{6,2},{7,3},{8,12},{9,13},{10,... | collective-permute-start | bytes 1572872 | tf_op jit(solution)/shard_map/ppermute | solution.py:233
  386.3 25.6 %collective-permute-start.97 = (f32[8,128,128]{2,1,0:T(8,128)S(1)}, f32[8,128,128]{2,1,0:T(8,128)S(1)}, u32[]{:S(2)}, u32[]{:S(2)}) collective-permute-start(f32[8,128,128]{2,1,0:T(8,128)S(1)} %get-tuple-element.211), channel_id=1, source_target_pairs={{0,6},{1,7},{2,4},{3,5},{4,2},{5,3},{6,0},{7,1},{8,14},{9,15},{10,... | collective-permute-start | bytes 1572872 | tf_op jit(solution)/shard_map/ppermute | solution.py:233
  387.9 45.6 %collective-permute-start.96 = (f32[8,128,128]{2,1,0:T(8,128)S(1)}, f32[8,128,128]{2,1,0:T(8,128)}, u32[]{:S(2)}, u32[]{:S(2)}) collective-permute-start(f32[8,128,128]{2,1,0:T(8,128)S(1)} %get-tuple-element.210), channel_id=1, source_target_pairs={{0,2},{1,3},{2,6},{3,7},{4,0},{5,1},{6,4},{7,5},{8,10},{9,11},{10,... | collective-permute-start | bytes 1572872 | tf_op jit(solution)/shard_map/ppermute | solution.py:233
  (95 other events, 1509.8 us)

commit v3 on v2

--- a/solution.py
+++ b/solution.py
@@ -39,13 +39,17 @@
     return dot(weight_high, value_high) + (dot(weight_high, value_low) + dot(weight_low, value_high))
 
 
-def pick(parts, index, group):
-    if len(parts) == 1:
-        return parts[0][index]
-    inside = parts[2] + index % 4
-    if index < 4:
-        return jnp.where(group == 0, parts[0][inside], parts[1][inside])
-    return jnp.where(group == 0, parts[1][inside], parts[0][inside])
+def pick(piece, index, group):
+    kind, base, refs = piece
+    if kind == "whole":
+        return refs[0][base + index]
+    if kind == "halves":
+        inside = base + index % 4
+        owner = index // 4
+    else:
+        inside = base + index
+        owner = 0 if kind == "next" else 1
+    return jnp.where(group == owner, refs[0][inside], refs[1][inside])
 
 
 def sent_tile(step, index, other, by_piece):
@@ -67,8 +71,8 @@
     return place[0], place[1], place[2]
 
 
-def take_weights(take, bases):
-    return [take(1) if base is None else take(2) + [base] for base in bases]
+def take_weights(take, kinds):
+    return [(kind, base, take(1 if kind == "whole" else 2)) for kind, base in kinds]
 
 
 def first_factor(steps, by_piece, current, gain, weights, send, tile, place):
@@ -89,30 +93,54 @@
         ref[pl.ds(ref.shape[0] - ROWS, ROWS), :] = squares
 
 
-def first_kernel(step, bases, place, *refs):
+def first_kernel(step, kinds, place, *refs):
     take = Taker(refs)
-    current, gain = take(1), take(1)
-    weights = take_weights(take, bases)
-    send, tile = [take(QUARTERS)], take(1)[0]
+    tokens, gain = take(1)[0], take(1)
+    weights = take_weights(take, kinds)
+    current, send, tile = take(1), [take(QUARTERS)], take(1)[0]
+    for index in range(ROWS):
+        current[0][index] = tokens[:, pl.ds(index * LANES, LANES)].T
     first_factor([step], True, current, gain, weights, send, tile, read_place(place))
 
 
-def edge_kernel(width, squares_count, has_next, bases, place, *refs):
+def last_kernel(width, step, squares_count, place, *refs):
+    take = Taker(refs)
+    position, quarter, _ = read_place(place)
+    current, old_gain, squares_in, mixed = take(1)[0], take(1)[0], take(squares_count), take(QUARTERS)
+    result, tile = take(2)
+    scale = token_scale(width, squares_in)
+    for index in range(ROWS):
+        for other in range(PLANES):
+            for mate in range(QUARTERS):
+                where = row_offset(other, mate, position, quarter)
+                _, start = sent_tile(step, index, other, True)
+                mix = mixed[mate][pl.ds(start, ROWS), :]
+                tile[index, where, :] = residual(current[index, where, :], mix, scale, old_gain[index, where, :])
+        result[:, pl.ds(index * LANES, LANES)] = tile[index].T
+
+
+def token_scale(width, squares):
+    total = sum(ref[pl.ds(ref.shape[0] - ROWS, ROWS), :] for ref in squares)
+    scale = lax.rsqrt(jnp.sum(total, axis=0, keepdims=True) / width + epsilon)
+    return jnp.broadcast_to(scale, (ROWS, LANES))
+
+
+def residual(value, mix, scale, gain):
+    normed = value * scale * gain
+    return value + (mix * scale) * (normed / (1.0 + jnp.exp(-normed)))
+
+
+def edge_kernel(width, squares_count, kinds, place, *refs):
     take = Taker(refs)
     position, quarter, group = read_place(place)
     current, old_gain = take(PLANES), take(PLANES)
     squares_in = take(squares_count)
     mixed = [take(QUARTERS) for _ in range(CHUNKS)]
-    if has_next:
-        gain = take(PLANES)
-        weights = take_weights(take, bases)
+    gain = take(PLANES)
+    weights = take_weights(take, kinds)
     fresh = take(PLANES)
-    if has_next:
-        send, tile = [take(QUARTERS) for _ in range(CHUNKS)], take(1)[0]
-
-    total = sum(ref[pl.ds(ref.shape[0] - ROWS, ROWS), :] for ref in squares_in)
-    scale = lax.rsqrt(jnp.sum(total, axis=0, keepdims=True) / width + epsilon)
-    scale = jnp.broadcast_to(scale, (ROWS, LANES))
+    send, tile = [take(QUARTERS) for _ in range(CHUNKS)], take(1)[0]
+    scale = token_scale(width, squares_in)
     for step in range(PLANES):
 
         def finish(index, carry, step=step):
@@ -122,41 +150,38 @@
                     value = current[step][index, where, :]
                     part, start = sent_tile(step, index, other, False)
                     mix = mixed[part][mate][pl.ds(pl.multiple_of(start, ROWS), ROWS), :]
-                    normed = value * scale * old_gain[step][index, where, :]
-                    value = value + (mix * scale) * (normed / (1.0 + jnp.exp(-normed)))
-                    fresh[step][index, where, :] = value
+                    gained = old_gain[step][index, where, :]
+                    fresh[step][index, where, :] = residual(value, mix, scale, gained)
             return carry
 
         lax.fori_loop(0, ROWS, finish, 0, unroll=2)
 
-    if has_next:
-        first_factor(range(PLANES), False, fresh, gain, weights, send, tile, (position, quarter, group))
-
-
-def column_kernel(chunk, by_piece, bases, has_gain, place, *refs):
+    first_factor(range(PLANES), False, fresh, gain, weights, send, tile, (position, quarter, group))
+
+
+def column_kernel(others, in_pieces, out_pieces, kinds, has_gain, place, *refs):
     take = Taker(refs)
     position, quarter, group = read_place(place)
-    came = [take(QUARTERS) for _ in range(PLANES if by_piece else 1)]
-    weights = take_weights(take, bases)
+    came = [take(QUARTERS) for _ in range(PLANES if in_pieces else len(others) // 2)]
+    weights = take_weights(take, kinds)
     rows = take(PLANES) if has_gain else []
-    send = take(QUARTERS)
+    send = [take(QUARTERS) for _ in range(PLANES if out_pieces else len(others) // 2)]
     spread = take(PLANES) if has_gain else []
     value, tile = take(2)
-    for n in range(2):
-        other = chunk * 2 + n
+    for n, other in enumerate(others):
         for index in range(ROWS):
             for step in range(PLANES):
                 for mate in range(QUARTERS):
-                    part, start = sent_tile(step, 0, other, by_piece)
-                    ref = came[part if by_piece else 0][mate]
+                    part, start = sent_tile(step, 0, other, in_pieces)
+                    ref = came[part if in_pieces else n // 2][mate]
                     value[index, row_offset(step, mate, position, quarter), :] = ref[
                         pl.ds(start + index, ROWS, stride=ROWS), :
                     ]
             tile[index] = product(pick(weights[n], index, group), value[index])
             for step in range(PLANES):
                 for mate in range(QUARTERS):
-                    _, start = sent_tile(step, 0, other, False)
-                    send[mate][pl.ds(start + index, ROWS, stride=ROWS), :] = tile[
+                    part, start = sent_tile(step, 0, other, out_pieces)
+                    send[part if out_pieces else n // 2][mate][pl.ds(start + index, ROWS, stride=ROWS), :] = tile[
                         index, row_offset(step, mate, position, quarter), :
                     ]
     for step in range(len(rows)):
@@ -192,35 +217,41 @@
 
 
 def split_weights(weights):
-    return [part for parts in weights for part in parts[:2]], [None if len(p) == 1 else p[2] for p in weights]
-
-
-def first_piece(step, place, current, gain, weights):
-    operands, bases = split_weights([weights])
-    kernel = functools.partial(first_kernel, step, bases)
-    return call(kernel, [place, current, gain, *operands], [array(264, LANES)] * QUARTERS, 1, STAGE_FLOPS // 4)
-
-
-def layer_edge(width, place, current, old_gain, squares, mixed, following=None):
-    operands = [place, *current, *old_gain, *squares, *mixed[0], *mixed[1]]
-    outs, bases = [array(*PIECE)] * PLANES, None
-    if following is not None:
-        gain, weights = following
-        more, bases = split_weights(weights)
-        operands += [*gain, *more]
-        outs += [array(520, LANES)] * QUARTERS + [array(512, LANES)] * QUARTERS
-    kernel = functools.partial(edge_kernel, width, len(squares), following is not None, bases)
-    results = list(call(kernel, operands, outs, int(following is not None), 2 * STAGE_FLOPS))
+    return [array for piece in weights for array in piece[2]], [piece[:2] for piece in weights]
+
+
+def first_piece(step, place, tokens, gain, weights):
+    operands, kinds = split_weights([weights])
+    kernel = functools.partial(first_kernel, step, kinds)
+    outs = [array(*PIECE)] + [array(264, LANES)] * QUARTERS
+    results = list(call(kernel, [place, tokens, gain, *operands], outs, 1, STAGE_FLOPS // 4))
+    return results[0], results[1:]
+
+
+def last_piece(width, step, place, current, old_gain, squares, mixed):
+    kernel = functools.partial(last_kernel, width, step, len(squares))
+    operands = [place, current, old_gain, *squares, *mixed]
+    return call(kernel, operands, [array(LANES, ROWS * LANES)], 1, STAGE_FLOPS // 4)[0]
+
+
+def layer_edge(width, place, current, old_gain, squares, mixed, gain, weights):
+    more, kinds = split_weights(weights)
+    operands = [place, *current, *old_gain, *squares, *mixed[0], *mixed[1], *gain, *more]
+    outs = [array(*PIECE)] * PLANES + [array(520, LANES)] * QUARTERS + [array(512, LANES)] * QUARTERS
+    kernel = functools.partial(edge_kernel, width, len(squares), kinds)
+    results = list(call(kernel, operands, outs, 1, 2 * STAGE_FLOPS))
     return results[:PLANES], [results[PLANES : PLANES + QUARTERS], results[PLANES + QUARTERS :]]
 
 
-def column_stage(chunk, by_piece, place, came, weights, rows=()):
-    more, bases = split_weights(weights)
+def column_stage(others, in_pieces, out_pieces, place, came, weights, rows=()):
+    more, kinds = split_weights(weights)
     operands = [place, *(ref for part in came for ref in part), *more, *rows]
-    outs = [array(512, LANES)] * QUARTERS + [array(*PIECE)] * len(rows)
-    kernel = functools.partial(column_kernel, chunk, by_piece, bases, bool(rows))
+    outs = [array(256, LANES)] * (QUARTERS * PLANES) if out_pieces else [array(512, LANES)] * QUARTERS
+    count = len(outs)
+    outs = outs + [array(*PIECE)] * len(rows)
+    kernel = functools.partial(column_kernel, others, in_pieces, out_pieces, kinds, bool(rows))
     results = list(call(kernel, operands, outs, 2, STAGE_FLOPS))
-    return results[:QUARTERS], results[QUARTERS:]
+    return [results[n : n + QUARTERS] for n in range(0, count, QUARTERS)], results[count:]
 
 
 def routed(value, to):
@@ -239,6 +270,18 @@
 
 def ring(value, distance):
     return routed(value, lambda core, z, y: (core, gray((gray(z) + distance) % PLANES), y))
+
+
+def group_ring(value):
+    route = []
+    for group in range(2):
+        for core in range(2):
+            for z in range(PLANES):
+                for y in range(2):
+                    there = gray((gray(z) + (1 if group else -1)) % PLANES)
+                    start = group * 16 + core * 8 + y
+                    route.append((start + z * 2, start + there * 2))
+    return lax.ppermute(value, ("groups", "segment", "block"), route)
 
 
 def to_mate(value, mate):
@@ -273,16 +316,17 @@
         theirs = core_swap(lax.dynamic_slice_in_dim(value, (1 - core) * ROWS, ROWS, 0))
         return jnp.where(core == 0, mine, theirs), jnp.where(core == 0, theirs, mine)
 
-    folded = tokens.reshape(2, LANES, 2, ROWS, LANES).transpose(2, 0, 3, 4, 1)
-    mine = lax.dynamic_index_in_dim(folded, core, 0, keepdims=False)
-    theirs = core_swap(lax.dynamic_index_in_dim(folded, 1 - core, 0, keepdims=False))
-    four = jnp.stack([mine, theirs]).reshape((4,) + PIECE)
-    current = []
+    half = tokens.shape[1] // 2
+    mine = lax.dynamic_slice_in_dim(tokens, core * half, half, 1)
+    theirs = core_swap(lax.dynamic_slice_in_dim(tokens, (1 - core) * half, half, 1))
+    pieces = []
     for step in range(PLANES):
         plane = gray((position - step) % PLANES)
-        slot = ((plane // 2) ^ core) * 2 + plane % 2
-        piece = lax.dynamic_index_in_dim(four, slot, 0, keepdims=False)
-        current.append(piece if step == 0 else ring(piece, -step))
+        start = (plane % 2) * LANES
+        kept = lax.dynamic_slice_in_dim(mine, start, LANES, 0)
+        other = lax.dynamic_slice_in_dim(theirs, start, LANES, 0)
+        pieces.append(jnp.where(plane // 2 == core, kept, other))
+    arrived = [piece if step == 0 else ring(piece, -step) for step, piece in enumerate(pieces)]
 
     held = jnp.moveaxis(gains[0].reshape(rounds, 2 * ROWS, LANES), 1, 0)
     held = jnp.stack(swapped(held), axis=2).transpose(1, 2, 0, 3).reshape(layers, ROWS, LANES)
@@ -297,62 +341,76 @@
         right[2 * r], right[2 * r + 1] = swapped(right_factors[0, r])
         left[2 * r], left[2 * r + 1] = swapped(left_factors[0, r])
 
-    def my_half(value):
-        return lax.dynamic_slice_in_dim(value, group * 4, 4, 0)
-
-    def chain(half):
+    def fetched(parts, earlier):
+        together = parts[0] if len(parts) == 1 else jnp.concatenate(parts)
+        near = group_ring(after(together, *earlier))
+        folded = near.reshape(len(parts), 2, 4, LANES, LANES)
+        far = group_ring(lax.dynamic_index_in_dim(folded, group, 1, keepdims=False).reshape(-1, LANES, LANES))
+        near_pair, far_pair = (near, group_swap(near)), (far, group_swap(far))
         found = []
-        for _ in range(PLANES - 1):
-            half = ring(half, -1)
-            found.append((half, group_swap(half)))
-        return found
+        for n, part in enumerate(parts):
+            found.append(
+                [
+                    ("whole", 0, (part,)),
+                    ("next", n * ROWS, near_pair),
+                    ("halves", n * 4, far_pair),
+                    ("previous", n * ROWS, near_pair),
+                ]
+            )
+        return found, far
 
     right_parts, left_parts = [], []
-    right_chain = chain(my_half(right[0]))
-    left_chain = chain(after(my_half(left[0]), right_chain[-1][0]))
-    right_parts.append([(right[0],)] + [(*pair, 0) for pair in right_chain])
-    left_parts.append([(left[0],)] + [(*pair, 0) for pair in left_chain])
-    last = left_chain[-1][0]
+    (found,), last = fetched([right[0]], [pieces[1]])
+    right_parts.append(found)
+    (found,), last = fetched([left[0]], [last])
+    left_parts.append(found)
     for layer in range(1, layers):
-        both = jnp.concatenate([my_half(right[layer]), my_half(left[layer])])
-        both_chain = chain(after(both, last))
-        last = both_chain[-1][0]
-        right_parts.append([(right[layer],)] + [(*pair, 0) for pair in both_chain])
-        left_parts.append([(left[layer],)] + [(*pair, 4) for pair in both_chain])
+        (found, more), last = fetched([right[layer], left[layer]], [last])
+        right_parts.append(found)
+        left_parts.append(more)
 
     gain = [jnp.broadcast_to(row[:, :, None], PIECE) for row in gain_rows[0]]
-    came = [
-        exchange(first_piece(step, place, current[step], gain[step], right_parts[0][step])) for step in range(PLANES)
-    ]
-    for layer in range(layers):
-        by_piece = layer == 0
-        squares = [part[mate] for part in (came if by_piece else came[:1]) for mate in range(QUARTERS)]
-        mixed, next_gain = [], None
+    current, came = [], []
+    for step in range(PLANES):
+        turned, sends = first_piece(step, place, arrived[step], gain[step], right_parts[0][step])
+        current.append(turned)
+        came.append(exchange(sends))
+    for layer in range(layers - 1):
+        in_pieces = layer == 0
+        squares = [part[mate] for part in (came if in_pieces else came[:1]) for mate in range(QUARTERS)]
+        mixed = []
         for chunk in range(CHUNKS):
-            rows = gain_rows[layer + 1] if chunk == 0 and layer + 1 < layers else ()
-            weights = left_parts[layer][chunk * 2 : chunk * 2 + 2]
-            source = came if by_piece else came[chunk : chunk + 1]
-            sends, spread = column_stage(chunk, by_piece, place, source, weights, rows)
+            others = (chunk * 2, chunk * 2 + 1)
+            rows = gain_rows[layer + 1] if chunk == 0 else ()
+            weights = left_parts[layer][others[0] : others[1] + 1]
+            source = came if in_pieces else came[chunk : chunk + 1]
+            (sends,), spread = column_stage(others, in_pieces, False, place, source, weights, rows)
             mixed.append(exchange(sends))
             next_gain = spread or next_gain
-        following = (next_gain, right_parts[layer + 1]) if layer + 1 < layers else None
-        current, sends = layer_edge(width, place, current, gain, squares, mixed, following)
+        current, sends = layer_edge(
+            width, place, current, gain, squares, mixed, next_gain, right_parts[layer + 1]
+        )
         gain = next_gain
-        if following is not None:
-            came = [exchange(sends[0]), exchange(sends[1])]
-
-    back = [current[step] if step == 0 else ring(current[step], step) for step in range(PLANES)]
+        came = [exchange(sends[0]), exchange(sends[1])]
+
+    squares = came[0]
+    sends, _ = column_stage(tuple(range(PLANES)), False, True, place, came, left_parts[-1])
+    back = [None] * PLANES
+    for step in (2, 1, 3, 0):
+        mixed = exchange(sends[step])
+        done = last_piece(width, step, place, current[step], gain[step], squares, mixed)
+        back[step] = done if step == 0 else ring(done, step)
     stacked = jnp.stack(back)
-    ordered = jnp.stack(
-        [
-            lax.dynamic_index_in_dim(stacked, (position - gray(plane)) % PLANES, 0, keepdims=False)
-            for plane in range(PLANES)
-        ]
-    ).reshape((2, 2) + PIECE)
-    mine = lax.dynamic_index_in_dim(ordered, core, 0, keepdims=False)
-    theirs = core_swap(lax.dynamic_index_in_dim(ordered, 1 - core, 0, keepdims=False))
-    both = jnp.stack([jnp.where(core == 0, mine, theirs), jnp.where(core == 0, theirs, mine)])
-    return both.transpose(1, 4, 0, 2, 3).reshape(tokens.shape)
+
+    def found_for(half_index):
+        planes = [half_index * 2 + n for n in range(2)]
+        return jnp.stack(
+            [lax.dynamic_index_in_dim(stacked, (position - gray(p)) % PLANES, 0, keepdims=False) for p in planes]
+        ).reshape(tokens.shape[0], half)
+
+    mine = found_for(core)
+    theirs = core_swap(found_for(1 - core))
+    return jnp.where(core == 0, jnp.concatenate([mine, theirs], 1), jnp.concatenate([theirs, mine], 1))
 
 
 def wide_body(tokens, gains, right_factors, left_factors):

time: 444 us -> 435 us (0.980)
  waiting for transfers between devices: 264 us -> 245 us
  starting transfers between devices: 97.3 us -> 106 us
  local copies, waits for them, and re-layouts: 35.2 us -> 29.6 us
  Pallas kernels: 34.9 us -> 40.4 us
    ppermute x85 -> x76, waiting for transfers between devices: 237 us -> 178 us  [routed(): return lax.ppermute(value, ('segment', 'block'), route)]
    ppermute x0 -> x10, waiting for transfers between devices: none -> 37.4 us  [group_ring(): return lax.ppermute(value, ('groups', 'segment', 'block'), route)]
    ppermute x85 -> x76, starting transfers between devices: 78.6 us -> 59 us  [routed(): return lax.ppermute(value, ('segment', 'block'), route)]
    ppermute x0 -> x10, starting transfers between devices: none -> 18.7 us  [group_ring(): return lax.ppermute(value, ('groups', 'segment', 'block'), route)]
    ppermute x15 -> x10, starting transfers between devices: 18.6 us -> 27.9 us  [group_swap(): return lax.ppermute(value, 'groups', [(0, 1), (1, 0)])]
    unnamed x120 -> x125, local copies, waits for them, and re-layouts: 13.5 us -> 20.4 us
    pallas_call x16 -> x18, Pallas kernels: 34.9 us -> 40.4 us  [call(): pl.pallas_call(kernel, out_shape=outs, in_specs=[SMALL] + [WHOLE] * (len(...]
    ppermute x15 -> x10, waiting for transfers between devices: 27 us -> 29.6 us  [group_swap(): return lax.ppermute(value, 'groups', [(0, 1), (1, 0)])]
  transfers between devices with their start and end apart: 100 -> 96, of which waited for: 49 -> 46; matrix products, arithmetic and copies ran while one was open for 5% -> 3% of each run, Pallas kernels for 6% -> 7%
where the time goes in v3:
time: 435 us; the launch traced here: 434 us
  waiting for transfers between devices  245 us (56%)
  starting transfers between devices  106 us (24%)
  Pallas kernels  40.4 us (9%)
  local copies, waits for them, and re-layouts  29.6 us (7%)
  other arithmetic  12.7 us (3%)
    ppermute x76, waiting for transfers between devices, routed(): return lax.ppermute(value, ('segment', 'block'), route)  178 us
    ppermute x76, starting transfers between devices, routed(): return lax.ppermute(value, ('segment', 'block'), route)  59 us
    pallas_call x18, Pallas kernels, call(): pl.pallas_call(kernel, out_shape=outs, in_specs=[SMALL] + [WHOLE] * (len(...  40.4 us
    ppermute x10, waiting for transfers between devices, group_ring(): return lax.ppermute(value, ('groups', 'segment', 'block'), route)  37.4 us
    ppermute x10, waiting for transfers between devices, group_swap(): return lax.ppermute(value, 'groups', [(0, 1), (1, 0)])  29.6 us
    ppermute x10, starting transfers between devices, group_swap(): return lax.ppermute(value, 'groups', [(0, 1), (1, 0)])  27.9 us
    unnamed x125, local copies, waits for them, and re-layouts  20.4 us
    ppermute x10, starting transfers between devices, group_ring(): return lax.ppermute(value, ('groups', 'segment', 'block'), route)  18.7 us
  transfers between devices with their start and end apart: 96, of which 46 were waited for; matrix products, arithmetic and copies ran while one was open for 3% of the time, Pallas kernels for 7%

profile of v3, /device:TPU:0, one launch (start us, length us, event | category | flops | bytes accessed | tf_op | source)
XLA Modules:
  0.0 434.2 jit_solution(367983214442426719)
XLA Ops:
  0.0 2.5 constant_dynamic-slice_fusion.7
  4.4 2.7 fusion.2
  9.3 2.0 dynamic-slice_select_fusion
  11.3 3.8 collective-permute-start.5
  15.2 11.5 %collective-permute-done.5.refs_2_ = f32[8,128,128]{2,1,0:T(8,128)S(1)} collective-permute-done((f32[8,128,128]{2,1,0:T(8,128)S(1)}, f32[8,128,128]{2,1,0:T(8,128)S(1)}, u32[]{:S(2)}, u32[]{:S(2)}) %collective-permute-start.5) | collective-permute-done | bytes 524320 | tf_op jit(solution)/shard_map/ppermute | solution.py:284
  26.7 3.4 collective-permute-start.9
  31.5 3.9 collective-permute-done.9.refs_2_
  36.1 3.4 collective-permute-start.26
  40.3 9.1 %collective-permute-done.26.refs_17_.refs_18_ = f32[8,128,128]{2,1,0:T(8,128)S(1)} collective-permute-done((f32[8,128,128]{2,1,0:T(8,128)S(1)}, f32[8,128,128]{2,1,0:T(8,128)S(1)}, u32[]{:S(2)}, u32[]{:S(2)}) %collective-permute-start.26) | collective-permute-done | bytes 524320 | tf_op jit(solution)/shard_map/ppermute | solution.py:284
  49.3 3.4 collective-permute-start.31
  53.8 2.8 collective-permute-done.31.refs_16_
  56.7 3.4 collective-permute-start.36
  62.4 17.7 %collective-permute-done.4 = f32[4,8,128]{2,1,0:T(8,128)S(1)} collective-permute-done((f32[4,8,128]{2,1,0:T(8,128)S(1)}, f32[4,8,128]{2,1,0:T(8,128)S(1)}, u32[]{:S(2)}, u32[]{:S(2)}) %collective-permute-start.4) | collective-permute-done | bytes 16416 | tf_op jit(solution)/shard_map/ppermute | solution.py:264
  80.1 3.2 collective-permute-start.8
  88.4 6.5 %collective-permute-done.12 = f32[4,8,128]{2,1,0:T(8,128)S(1)} collective-permute-done((f32[4,8,128]{2,1,0:T(8,128)S(1)}, f32[4,8,128]{2,1,0:T(8,128)S(1)}, u32[]{:S(2)}, u32[]{:S(2)}) %collective-permute-start.12) | collective-permute-done | bytes 16416 | tf_op jit(solution)/shard_map/ppermute | solution.py:264
  96.9 3.5 collective-permute-start.6
  104.5 13.2 %collective-permute-done.10.refs_3_ = f32[4,128,128]{2,1,0:T(8,128)S(1)} collective-permute-done((f32[4,128,128]{2,1,0:T(8,128)S(1)}, f32[4,128,128]{2,1,0:T(8,128)S(1)}, u32[]{:S(2)}, u32[]{:S(2)}) %collective-permute-start.10) | collective-permute-done | bytes 262176 | tf_op jit(solution)/shard_map/ppermute | solution.py:292
  119.2 10.2 %collective-permute-done.38.refs_39_.refs_4_ = f32[8,128,128]{2,1,0:T(8,128)S(1)} collective-permute-done((f32[8,128,128]{2,1,0:T(8,128)S(1)}, f32[8,128,128]{2,1,0:T(8,128)S(1)}, u32[]{:S(2)}, u32[]{:S(2)}) %collective-permute-start.38) | collective-permute-done | bytes 524320 | tf_op jit(solution)/shard_map/ppermute | solution.py:284
  132.6 2.6 collective-permute-done.15.refs_3_.refs_11_
  138.3 11.6 %collective-permute-start.27 = (f32[8,128,128]{2,1,0:T(8,128)S(1)}, f32[8,128,128]{2,1,0:T(8,128)S(1)}, u32[]{:S(2)}, u32[]{:S(2)}) collective-permute-start(f32[8,128,128]{2,1,0:T(8,128)S(1)} %collective-permute-done.26.refs_17_.refs_18_), channel_id=1, source_target_pairs={{0,16},{16,0},{1,17},{17,1},{2,18},{18,2},{3,19},{19,3},{4,20},{20... | collective-permute-start | bytes 1572872 | tf_op jit(solution)/shard_map/ppermute | solution.py:292
  157.0 2.0 collective-permute-done.17.refs_6_.refs_14_
  162.6 4.4 %collective-permute-done.23.refs_14_.refs_22_ = f32[264,128]{1,0:T(8,128)S(1)} collective-permute-done((f32[264,128]{1,0:T(8,128)S(1)}, f32[264,128]{1,0:T(8,128)S(1)}, u32[]{:S(2)}, u32[]{:S(2)}) %collective-permute-start.23) | collective-permute-done | bytes 135200 | tf_op jit(solution)/shard_map/ppermute | solution.py:264
  169.4 2.0 shard_map.50
  174.4 16.4 %collective-permute-done.32.refs_17_ = f32[4,128,128]{2,1,0:T(8,128)S(1)} collective-permute-done((f32[4,128,128]{2,1,0:T(8,128)S(1)}, f32[4,128,128]{2,1,0:T(8,128)S(1)}, u32[]{:S(2)}, u32[]{:S(2)}) %collective-permute-start.32) | collective-permute-done | bytes 262176 | tf_op jit(solution)/shard_map/ppermute | solution.py:292
  190.8 2.3 collective-permute-start.39
  195.0 4.1 collective-permute-done.30.refs_27_
  201.2 7.1 %collective-permute-done.34.refs_30_ = f32[512,128]{1,0:T(8,128)S(1)} collective-permute-done((f32[512,128]{1,0:T(8,128)S(1)}, f32[512,128]{1,0:T(8,128)S(1)}, u32[]{:S(2)}, u32[]{:S(2)}) %collective-permute-start.34) | collective-permute-done | bytes 262176 | tf_op jit(solution)/shard_map/ppermute | solution.py:264
  208.3 4.5 %collective-permute-done.35.refs_31_ = f32[512,128]{1,0:T(8,128)S(1)} collective-permute-done((f32[512,128]{1,0:T(8,128)S(1)}, f32[512,128]{1,0:T(8,128)S(1)}, u32[]{:S(2)}, u32[]{:S(2)}) %collective-permute-start.35) | collective-permute-done | bytes 262176 | tf_op jit(solution)/shard_map/ppermute | solution.py:264
  216.1 5.6 %shard_map.52 = (f32[8,128,128]{2,1,0:T(8,128)S(1)}, f32[8,128,128]{2,1,0:T(8,128)S(1)}, f32[8,128,128]{2,1,0:T(8,128)S(1)}, f32[8,128,128]{2,1,0:T(8,128)S(1)},...) custom-call(s32[3]{0:T(128)S(1)} %pad_add_fusion.place, ...), custom_call_target="tpu_custom_call" | custom-call | flops 805306368 | bytes 20529164 | tf_op jit(solution)/shard_map/pallas_call | solution.py:205
  224.9 2.3 collective-permute-start.55
  228.2 3.4 collective-permute-done.47.refs_2_
  231.7 9.6 %collective-permute-done.48.refs_3_ = f32[512,128]{1,0:T(8,128)S(1)} collective-permute-done((f32[512,128]{1,0:T(8,128)S(1)}, f32[512,128]{1,0:T(8,128)S(1)}, u32[]{:S(2)}, u32[]{:S(2)}) %collective-permute-start.48) | collective-permute-done | bytes 262176 | tf_op jit(solution)/shard_map/ppermute | solution.py:264
  246.8 2.3 collective-permute-done.42.refs_3_.refs_11_
  249.1 2.2 collective-permute-start.51
  251.3 2.1 shard_map.53
  253.5 3.3 collective-permute-done.50.refs_18_
  256.8 1.6 collective-permute-start.57
  262.7 6.2 %collective-permute-done.44.refs_14_ = f32[512,128]{1,0:T(8,128)S(1)} collective-permute-done((f32[512,128]{1,0:T(8,128)S(1)}, f32[512,128]{1,0:T(8,128)S(1)}, u32[]{:S(2)}, u32[]{:S(2)}) %collective-permute-start.44) | collective-permute-done | bytes 262176 | tf_op jit(solution)/shard_map/ppermute | solution.py:264
  268.8 6.0 %collective-permute-done.45.refs_15_ = f32[512,128]{1,0:T(8,128)S(1)} collective-permute-done((f32[512,128]{1,0:T(8,128)S(1)}, f32[512,128]{1,0:T(8,128)S(1)}, u32[]{:S(2)}, u32[]{:S(2)}) %collective-permute-start.45) | collective-permute-done | bytes 262176 | tf_op jit(solution)/shard_map/ppermute | solution.py:264
  277.0 5.4 %shard_map.55 = (f32[8,128,128]{2,1,0:T(8,128)S(1)}, f32[8,128,128]{2,1,0:T(8,128)S(1)}, f32[8,128,128]{2,1,0:T(8,128)S(1)}, f32[8,128,128]{2,1,0:T(8,128)S(1)},...) custom-call(s32[3]{0:T(128)S(1)} %pad_add_fusion.place, ...), custom_call_target="tpu_custom_call" | custom-call | flops 805306368 | bytes 19431436 | tf_op jit(solution)/shard_map/pallas_call | solution.py:205
  285.1 1.9 collective-permute-start.71
  287.0 5.3 %collective-permute-done.65.refs_2_ = f32[512,128]{1,0:T(8,128)S(1)} collective-permute-done((f32[512,128]{1,0:T(8,128)S(1)}, f32[512,128]{1,0:T(8,128)S(1)}, u32[]{:S(2)}, u32[]{:S(2)}) %collective-permute-start.65) | collective-permute-done | bytes 262176 | tf_op jit(solution)/shard_map/ppermute | solution.py:264
  293.6 3.6 collective-permute-done.66.refs_3_
  297.2 1.8 collective-permute-start.60
  304.9 3.6 collective-permute-done.60.refs_3_.refs_11_
  308.6 1.8 collective-permute-start.69
  312.0 2.1 shard_map.56
  316.2 3.6 collective-permute-done.69.refs_19_
  319.8 1.8 collective-permute-start.63
  321.6 4.6 %collective-permute-done.62.refs_14_ = f32[512,128]{1,0:T(8,128)S(1)} collective-permute-done((f32[512,128]{1,0:T(8,128)S(1)}, f32[512,128]{1,0:T(8,128)S(1)}, u32[]{:S(2)}, u32[]{:S(2)}) %collective-permute-start.62) | collective-permute-done | bytes 262176 | tf_op jit(solution)/shard_map/ppermute | solution.py:264
  326.2 4.8 %collective-permute-done.63.refs_15_ = f32[512,128]{1,0:T(8,128)S(1)} collective-permute-done((f32[512,128]{1,0:T(8,128)S(1)}, f32[512,128]{1,0:T(8,128)S(1)}, u32[]{:S(2)}, u32[]{:S(2)}) %collective-permute-start.63) | collective-permute-done | bytes 262176 | tf_op jit(solution)/shard_map/ppermute | solution.py:264
  332.2 5.3 %shard_map.58 = (f32[8,128,128]{2,1,0:T(8,128)S(1)}, f32[8,128,128]{2,1,0:T(8,128)S(1)}, f32[8,128,128]{2,1,0:T(8,128)S(1)}, f32[8,128,128]{2,1,0:T(8,128)S(1)},...) custom-call(s32[3]{0:T(128)S(1)} %pad_add_fusion.place, ...), custom_call_target="tpu_custom_call" | custom-call | flops 805306368 | bytes 19431436 | tf_op jit(solution)/shard_map/pallas_call | solution.py:205
  341.6 17.1 %collective-permute-done.78.refs_6_ = f32[512,128]{1,0:T(8,128)S(1)} collective-permute-done((f32[512,128]{1,0:T(8,128)S(1)}, f32[512,128]{1,0:T(8,128)S(1)}, u32[]{:S(2)}, u32[]{:S(2)}) %collective-permute-start.78) | collective-permute-done | bytes 262176 | tf_op jit(solution)/shard_map/ppermute | solution.py:264
  358.7 4.2 collective-permute-done.79.refs_7_
  366.2 3.2 shard_map.59
  373.4 2.9 collective-permute-done.92.refs_8_
  378.6 1.6 collective-permute-start.85
  385.6 1.9 collective-permute-done.84.refs_8_
  388.4 1.8 shard_map.61
  393.5 4.5 %collective-permute-done.81.refs_8_ = f32[256,128]{1,0:T(8,128)} collective-permute-done((f32[256,128]{1,0:T(8,128)}, f32[256,128]{1,0:T(8,128)}, u32[]{:S(2)}, u32[]{:S(2)}) %collective-permute-start.81) | collective-permute-done | bytes 131104 | tf_op jit(solution)/shard_map/ppermute | solution.py:264
  400.3 4.4 %collective-permute-done.94 = f32[128,1024]{1,0:T(8,128)} collective-permute-done((f32[128,1024]{1,0:T(8,128)S(1)}, f32[128,1024]{1,0:T(8,128)}, u32[]{:S(2)}, u32[]{:S(2)}) %collective-permute-start.94) | collective-permute-done | bytes 524320 | tf_op jit(solution)/shard_map/ppermute | solution.py:264
  404.6 2.9 collective-permute-done.90
  407.6 20.4 %collective-permute-done.86 = f32[128,1024]{1,0:T(8,128)} collective-permute-done((f32[128,1024]{1,0:T(8,128)}, f32[128,1024]{1,0:T(8,128)}, u32[]{:S(2)}, u32[]{:S(2)}) %collective-permute-start.86) | collective-permute-done | bytes 524320 | tf_op jit(solution)/shard_map/ppermute | solution.py:264
  430.1 2.5 collective-permute-done.95
  (308 shorter events, 112.6 us)
Async XLA Ops:
  11.3 15.4 %collective-permute-start.5 = (f32[8,128,128]{2,1,0:T(8,128)S(1)}, f32[8,128,128]{2,1,0:T(8,128)S(1)}, u32[]{:S(2)}, u32[]{:S(2)}) collective-permute-start(f32[8,128,128]{2,1,0:T(8,128)S(1)} %get-tuple-element.119.refs_2_), channel_id=1, source_target_pairs={{0,4},{1,5},{2,0},{3,1},{4,6},{5,7},{6,2},{7,3},{8,12},{9,13},{10,... | collective-permute-start | bytes 1572872 | tf_op jit(solution)/shard_map/ppermute | solution.py:284
  15.1 15.0 %collective-permute-start.25 = (f32[8,128,128]{2,1,0:T(8,128)S(1)}, f32[8,128,128]{2,1,0:T(8,128)}, u32[]{:S(2)}, u32[]{:S(2)}) collective-permute-start(f32[8,128,128]{2,1,0:T(8,128)S(1)} %dynamic-slice_bitcast_fusion.2), channel_id=1, source_target_pairs={{0,8},{1,9},{2,10},{3,11},{4,12},{5,13},{6,14},{7,15},{8,0},{9,1},... | collective-permute-start | bytes 1572872 | tf_op jit(solution)/shard_map/ppermute | solution.py:264
  36.1 13.3 %collective-permute-start.26 = (f32[8,128,128]{2,1,0:T(8,128)S(1)}, f32[8,128,128]{2,1,0:T(8,128)S(1)}, u32[]{:S(2)}, u32[]{:S(2)}) collective-permute-start(f32[8,128,128]{2,1,0:T(8,128)S(1)} %get-tuple-element.139.refs_16_), channel_id=1, source_target_pairs={{0,4},{1,5},{2,0},{3,1},{4,6},{5,7},{6,2},{7,3},{8,12},{9,13},{10,... | collective-permute-start | bytes 1572872 | tf_op jit(solution)/shard_map/ppermute | solution.py:284
  52.8 9.4 %collective-permute-start.1 = (f32[8,2,128]{2,0,1:T(8,128)S(1)}, f32[8,2,128]{2,0,1:T(8,128)S(1)}, u32[]{:S(2)}, u32[]{:S(2)}) collective-permute-start(f32[8,2,128]{2,0,1:T(8,128)S(1)} %dynamic-slice_bitcast_fusion.6), channel_id=1, source_target_pairs={{0,8},{1,9},{2,10},{3,11},{4,12},{5,13},{6,14},{7,15},{8,0},{9,1},... | collective-permute-start | bytes 24584 | tf_op jit(solution)/shard_map/ppermute | solution.py:264
  56.7 30.6 %collective-permute-start.36 = (f32[16,128,128]{2,1,0:T(8,128)}, f32[16,128,128]{2,1,0:T(8,128)S(1)}, u32[]{:S(2)}, u32[]{:S(2)}) collective-permute-start(f32[16,128,128]{2,1,0:T(8,128)} %pad_maximum_fusion.1), channel_id=1, source_target_pairs={{0,4},{1,5},{2,0},{3,1},{4,6},{5,7},{6,2},{7,3},{8,12},{9,13},{10,... | collective-permute-start | bytes 3145736 | tf_op jit(solution)/shard_map/ppermute | solution.py:284
  60.9 34.5 %collective-permute-start.52 = (f32[8,128,128]{2,1,0:T(8,128)}, f32[8,128,128]{2,1,0:T(8,128)}, u32[]{:S(2)}, u32[]{:S(2)}) collective-permute-start(f32[8,128,128]{2,1,0:T(8,128)} %dynamic-slice_bitcast_fusion.1), channel_id=1, source_target_pairs={{0,8},{1,9},{2,10},{3,11},{4,12},{5,13},{6,14},{7,15},{8,0},{9,1},... | collective-permute-start | bytes 1572872 | tf_op jit(solution)/shard_map/ppermute | solution.py:264
  61.7 35.2 %collective-permute-start.53 = (f32[8,128,128]{2,1,0:T(8,128)}, f32[8,128,128]{2,1,0:T(8,128)}, u32[]{:S(2)}, u32[]{:S(2)}) collective-permute-start(f32[8,128,128]{2,1,0:T(8,128)} %dynamic-slice_bitcast_fusion), channel_id=1, source_target_pairs={{0,8},{1,9},{2,10},{3,11},{4,12},{5,13},{6,14},{7,15},{8,0},{9,1},... | collective-permute-start | bytes 1572872 | tf_op jit(solution)/shard_map/ppermute | solution.py:264
  62.3 17.9 %collective-permute-start.4 = (f32[4,8,128]{2,1,0:T(8,128)S(1)}, f32[4,8,128]{2,1,0:T(8,128)S(1)}, u32[]{:S(2)}, u32[]{:S(2)}) collective-permute-start(f32[4,8,128]{2,1,0:T(8,128)S(1)} %bitcast.107), channel_id=1, source_target_pairs={{0,4},{1,5},{2,0},{3,1},{4,6},{5,7},{6,2},{7,3},{8,12},{9,13},{10,... | collective-permute-start | bytes 49160 | tf_op jit(solution)/shard_map/ppermute | solution.py:264
  83.3 19.3 %collective-permute-start.7 = (f32[128,1024]{1,0:T(8,128)}, f32[128,1024]{1,0:T(8,128)S(1)}, u32[]{:S(2)}, u32[]{:S(2)}) collective-permute-start(f32[128,1024]{1,0:T(8,128)} %get-tuple-element.232), channel_id=1, source_target_pairs={{0,6},{1,7},{2,4},{3,5},{4,2},{5,3},{6,0},{7,1},{8,14},{9,15},{10,... | collective-permute-start | bytes 1572872 | tf_op jit(solution)/shard_map/ppermute | solution.py:264
  87.1 13.3 %collective-permute-start.13 = (f32[264,128]{1,0:T(8,128)S(1)}, f32[264,128]{1,0:T(8,128)S(1)}, u32[]{:S(2)}, u32[]{:S(2)}) collective-permute-start(f32[264,128]{1,0:T(8,128)S(1)} %get-tuple-element.124), channel_id=1, source_target_pairs={{0,8},{1,9},{2,10},{3,11},{4,12},{5,13},{6,14},{7,15},{8,0},{9,1},... | collective-permute-start | bytes 405512 | tf_op jit(solution)/shard_map/ppermute | solution.py:264
  94.9 41.1 %collective-permute-start.3 = (f32[128,1024]{1,0:T(8,128)}, f32[128,1024]{1,0:T(8,128)S(1)}, u32[]{:S(2)}, u32[]{:S(2)}) collective-permute-start(f32[128,1024]{1,0:T(8,128)} %get-tuple-element.233), channel_id=1, source_target_pairs={{0,4},{1,5},{2,0},{3,1},{4,6},{5,7},{6,2},{7,3},{8,12},{9,13},{10,... | collective-permute-start | bytes 1572872 | tf_op jit(solution)/shard_map/ppermute | solution.py:264
  95.4 43.0 %collective-permute-start.11 = (f32[128,1024]{1,0:T(8,128)S(1)}, f32[128,1024]{1,0:T(8,128)S(1)}, u32[]{:S(2)}, u32[]{:S(2)}) collective-permute-start(f32[128,1024]{1,0:T(8,128)S(1)} %copy-done.60), channel_id=1, source_target_pairs={{0,2},{1,3},{2,6},{3,7},{4,0},{5,1},{6,4},{7,5},{8,10},{9,11},{10,... | collective-permute-start | bytes 1572872 | tf_op jit(solution)/shard_map/ppermute | solution.py:264
  96.9 53.0 %collective-permute-start.6 = (f32[8,128,128]{2,1,0:T(8,128)S(1)}, f32[8,128,128]{2,1,0:T(8,128)S(1)}, u32[]{:S(2)}, u32[]{:S(2)}) collective-permute-start(f32[8,128,128]{2,1,0:T(8,128)S(1)} %collective-permute-done.5.refs_2_), channel_id=1, source_target_pairs={{0,16},{16,0},{1,17},{17,1},{2,18},{18,2},{3,19},{19,3},{4,20},{20... | collective-permute-start | bytes 1572872 | tf_op jit(solution)/shard_map/ppermute | solution.py:292
  100.5 28.9 %collective-permute-start.38 = (f32[8,128,128]{2,1,0:T(8,128)S(1)}, f32[8,128,128]{2,1,0:T(8,128)S(1)}, u32[]{:S(2)}, u32[]{:S(2)}) collective-permute-start(f32[8,128,128]{2,1,0:T(8,128)S(1)} %bitcast.106), channel_id=1, source_target_pairs={{0,4},{1,5},{2,0},{3,1},{4,6},{5,7},{6,2},{7,3},{8,12},{9,13},{10,... | collective-permute-start | bytes 1572872 | tf_op jit(solution)/shard_map/ppermute | solution.py:284
  102.6 15.1 %collective-permute-start.10 = (f32[4,128,128]{2,1,0:T(8,128)S(1)}, f32[4,128,128]{2,1,0:T(8,128)S(1)}, u32[]{:S(2)}, u32[]{:S(2)}) collective-permute-start(f32[4,128,128]{2,1,0:T(8,128)S(1)} %copy-done.51), channel_id=1, source_target_pairs={{0,16},{16,0},{1,17},{17,1},{2,18},{18,2},{3,19},{19,3},{4,20},{20... | collective-permute-start | bytes 786440 | tf_op jit(solution)/shard_map/ppermute | solution.py:292
  117.7 13.4 %collective-permute-start.14 = (f32[264,128]{1,0:T(8,128)S(1)}, f32[264,128]{1,0:T(8,128)S(1)}, u32[]{:S(2)}, u32[]{:S(2)}) collective-permute-start(f32[264,128]{1,0:T(8,128)S(1)} %get-tuple-element.125), channel_id=1, source_target_pairs={{0,1},{1,0},{2,3},{3,2},{4,5},{5,4},{6,7},{7,6},{8,9},{9,8},{10,11... | collective-permute-start | bytes 405512 | tf_op jit(solution)/shard_map/ppermute | solution.py:264
  131.1 21.1 %collective-permute-start.19 = (f32[264,128]{1,0:T(8,128)S(1)}, f32[264,128]{1,0:T(8,128)S(1)}, u32[]{:S(2)}, u32[]{:S(2)}) collective-permute-start(f32[264,128]{1,0:T(8,128)S(1)} %get-tuple-element.132), channel_id=1, source_target_pairs={{0,8},{1,9},{2,10},{3,11},{4,12},{5,13},{6,14},{7,15},{8,0},{9,1},... | collective-permute-start | bytes 405512 | tf_op jit(solution)/shard_map/ppermute | solution.py:264
  135.2 17.4 %collective-permute-start.20 = (f32[264,128]{1,0:T(8,128)S(1)}, f32[264,128]{1,0:T(8,128)S(1)}, u32[]{:S(2)}, u32[]{:S(2)}) collective-permute-start(f32[264,128]{1,0:T(8,128)S(1)} %get-tuple-element.133), channel_id=1, source_target_pairs={{0,1},{1,0},{2,3},{3,2},{4,5},{5,4},{6,7},{7,6},{8,9},{9,8},{10,11... | collective-permute-start | bytes 405512 | tf_op jit(solution)/shard_map/ppermute | solution.py:264
  136.1 17.7 %collective-permute-start.21 = (f32[264,128]{1,0:T(8,128)S(1)}, f32[264,128]{1,0:T(8,128)S(1)}, u32[]{:S(2)}, u32[]{:S(2)}) collective-permute-start(f32[264,128]{1,0:T(8,128)S(1)} %get-tuple-element.134), channel_id=1, source_target_pairs={{0,9},{1,8},{2,11},{3,10},{4,13},{5,12},{6,15},{7,14},{8,1},{9,0},... | collective-permute-start | bytes 405512 | tf_op jit(solution)/shard_map/ppermute | solution.py:264
  138.3 31.0 %collective-permute-start.27 = (f32[8,128,128]{2,1,0:T(8,128)S(1)}, f32[8,128,128]{2,1,0:T(8,128)S(1)}, u32[]{:S(2)}, u32[]{:S(2)}) collective-permute-start(f32[8,128,128]{2,1,0:T(8,128)S(1)} %collective-permute-done.26.refs_17_.refs_18_), channel_id=1, source_target_pairs={{0,16},{16,0},{1,17},{17,1},{2,18},{18,2},{3,19},{19,3},{4,20},{20... | collective-permute-start | bytes 1572872 | tf_op jit(solution)/shard_map/ppermute | solution.py:292
  149.9 50.1 %collective-permute-start.54 = (f32[16,128,128]{2,1,0:T(8,128)S(1)}, f32[16,128,128]{2,1,0:T(8,128)S(1)}, u32[]{:S(2)}, u32[]{:S(2)}) collective-permute-start(f32[16,128,128]{2,1,0:T(8,128)S(1)} %pad_maximum_fusion.2), channel_id=1, source_target_pairs={{0,4},{1,5},{2,0},{3,1},{4,6},{5,7},{6,2},{7,3},{8,12},{9,13},{10,... | collective-permute-start | bytes 3145736 | tf_op jit(solution)/shard_map/ppermute | solution.py:284
  159.0 53.8 %collective-permute-start.37 = (f32[16,128,128]{2,1,0:T(8,128)S(1)}, f32[16,128,128]{2,1,0:T(8,128)S(1)}, u32[]{:S(2)}, u32[]{:S(2)}) collective-permute-start(f32[16,128,128]{2,1,0:T(8,128)S(1)} %collective-permute-done.36.refs_37_.refs_41_.refs_5_.refs_6_), channel_id=1, source_target_pairs={{0,16},{16,0},{1,17},{17,1},{2,18},{18,2},{3,19},{19,3},{4,20},{20... | collective-permute-start | bytes 3145736 | tf_op jit(solution)/shard_map/ppermute | solution.py:292
  167.0 23.8 %collective-permute-start.32 = (f32[4,128,128]{2,1,0:T(8,128)S(1)}, f32[4,128,128]{2,1,0:T(8,128)S(1)}, u32[]{:S(2)}, u32[]{:S(2)}) collective-permute-start(f32[4,128,128]{2,1,0:T(8,128)S(1)} %collective-permute-done.31.refs_16_), channel_id=1, source_target_pairs={{0,16},{16,0},{1,17},{17,1},{2,18},{18,2},{3,19},{19,3},{4,20},{20... | collective-permute-start | bytes 786440 | tf_op jit(solution)/shard_map/ppermute | solution.py:292
  173.0 17.9 %collective-permute-start.28 = (f32[512,128]{1,0:T(8,128)S(1)}, f32[512,128]{1,0:T(8,128)S(1)}, u32[]{:S(2)}, u32[]{:S(2)}) collective-permute-start(f32[512,128]{1,0:T(8,128)S(1)} %get-tuple-element.141), channel_id=1, source_target_pairs={{0,8},{1,9},{2,10},{3,11},{4,12},{5,13},{6,14},{7,15},{8,0},{9,1},... | collective-permute-start | bytes 786440 | tf_op jit(solution)/shard_map/ppermute | solution.py:264
  173.3 21.4 %collective-permute-start.29 = (f32[512,128]{1,0:T(8,128)S(1)}, f32[512,128]{1,0:T(8,128)S(1)}, u32[]{:S(2)}, u32[]{:S(2)}) collective-permute-start(f32[512,128]{1,0:T(8,128)S(1)} %get-tuple-element.142), channel_id=1, source_target_pairs={{0,1},{1,0},{2,3},{3,2},{4,5},{5,4},{6,7},{7,6},{8,9},{9,8},{10,11... | collective-permute-start | bytes 786440 | tf_op jit(solution)/shard_map/ppermute | solution.py:264
  190.8 22.0 %collective-permute-start.39 = (f32[8,128,128]{2,1,0:T(8,128)S(1)}, f32[8,128,128]{2,1,0:T(8,128)S(1)}, u32[]{:S(2)}, u32[]{:S(2)}) collective-permute-start(f32[8,128,128]{2,1,0:T(8,128)S(1)} %collective-permute-done.38.refs_39_.refs_4_), channel_id=1, source_target_pairs={{0,16},{16,0},{1,17},{17,1},{2,18},{18,2},{3,19},{19,3},{4,20},{20... | collective-permute-start | bytes 1572872 | tf_op jit(solution)/shard_map/ppermute | solution.py:292
  199.1 9.2 %collective-permute-start.34 = (f32[512,128]{1,0:T(8,128)S(1)}, f32[512,128]{1,0:T(8,128)S(1)}, u32[]{:S(2)}, u32[]{:S(2)}) collective-permute-start(f32[512,128]{1,0:T(8,128)S(1)} %get-tuple-element.146), channel_id=1, source_target_pairs={{0,1},{1,0},{2,3},{3,2},{4,5},{5,4},{6,7},{7,6},{8,9},{9,8},{10,11... | collective-permute-start | bytes 786440 | tf_op jit(solution)/shard_map/ppermute | solution.py:264
  200.0 12.8 %collective-permute-start.35 = (f32[512,128]{1,0:T(8,128)S(1)}, f32[512,128]{1,0:T(8,128)S(1)}, u32[]{:S(2)}, u32[]{:S(2)}) collective-permute-start(f32[512,128]{1,0:T(8,128)S(1)} %get-tuple-element.147), channel_id=1, source_target_pairs={{0,9},{1,8},{2,11},{3,10},{4,13},{5,12},{6,15},{7,14},{8,1},{9,0},... | collective-permute-start | bytes 786440 | tf_op jit(solution)/shard_map/ppermute | solution.py:264
  200.9 24.0 %collective-permute-start.56 = (f32[8,128,128]{2,1,0:T(8,128)S(1)}, f32[8,128,128]{2,1,0:T(8,128)S(1)}, u32[]{:S(2)}, u32[]{:S(2)}) collective-permute-start(f32[8,128,128]{2,1,0:T(8,128)S(1)} %bitcast.104), channel_id=1, source_target_pairs={{0,4},{1,5},{2,0},{3,1},{4,6},{5,7},{6,2},{7,3},{8,12},{9,13},{10,... | collective-permute-start | bytes 1572872 | tf_op jit(solution)/shard_map/ppermute | solution.py:284
  222.5 9.2 %collective-permute-start.47 = (f32[512,128]{1,0:T(8,128)S(1)}, f32[512,128]{1,0:T(8,128)S(1)}, u32[]{:S(2)}, u32[]{:S(2)}) collective-permute-start(f32[512,128]{1,0:T(8,128)S(1)} %get-tuple-element.167), channel_id=1, source_target_pairs={{0,1},{1,0},{2,3},{3,2},{4,5},{5,4},{6,7},{7,6},{8,9},{9,8},{10,11... | collective-permute-start | bytes 786440 | tf_op jit(solution)/shard_map/ppermute | solution.py:264
  223.0 22.1 %collective-permute-start.40 = (f32[520,128]{1,0:T(8,128)S(1)}, f32[520,128]{1,0:T(8,128)S(1)}, u32[]{:S(2)}, u32[]{:S(2)}) collective-permute-start(f32[520,128]{1,0:T(8,128)S(1)} %get-tuple-element.158), channel_id=1, source_target_pairs={{0,8},{1,9},{2,10},{3,11},{4,12},{5,13},{6,14},{7,15},{8,0},{9,1},... | collective-permute-start | bytes 798728 | tf_op jit(solution)/shard_map/ppermute | solution.py:264
  223.0 22.2 %collective-permute-start.41 = (f32[520,128]{1,0:T(8,128)S(1)}, f32[520,128]{1,0:T(8,128)S(1)}, u32[]{:S(2)}, u32[]{:S(2)}) collective-permute-start(f32[520,128]{1,0:T(8,128)S(1)} %get-tuple-element.159), channel_id=1, source_target_pairs={{0,1},{1,0},{2,3},{3,2},{4,5},{5,4},{6,7},{7,6},{8,9},{9,8},{10,11... | collective-permute-start | bytes 798728 | tf_op jit(solution)/shard_map/ppermute | solution.py:264
  224.6 16.7 %collective-permute-start.48 = (f32[512,128]{1,0:T(8,128)S(1)}, f32[512,128]{1,0:T(8,128)S(1)}, u32[]{:S(2)}, u32[]{:S(2)}) collective-permute-start(f32[512,128]{1,0:T(8,128)S(1)} %get-tuple-element.168), channel_id=1, source_target_pairs={{0,9},{1,8},{2,11},{3,10},{4,13},{5,12},{6,15},{7,14},{8,1},{9,0},... | collective-permute-start | bytes 786440 | tf_op jit(solution)/shard_map/ppermute | solution.py:264
  224.9 49.9 %collective-permute-start.55 = (f32[16,128,128]{2,1,0:T(8,128)S(1)}, f32[16,128,128]{2,1,0:T(8,128)S(1)}, u32[]{:S(2)}, u32[]{:S(2)}) collective-permute-start(f32[16,128,128]{2,1,0:T(8,128)S(1)} %collective-permute-done.54.refs_25_.refs_29_.refs_5_.refs_6_), channel_id=1, source_target_pairs={{0,16},{16,0},{1,17},{17,1},{2,18},{18,2},{3,19},{19,3},{4,20},{20... | collective-permute-start | bytes 3145736 | tf_op jit(solution)/shard_map/ppermute | solution.py:292
  231.7 53.4 %collective-permute-start.70 = (f32[16,128,128]{2,1,0:T(8,128)}, f32[16,128,128]{2,1,0:T(8,128)S(1)}, u32[]{:S(2)}, u32[]{:S(2)}) collective-permute-start(f32[16,128,128]{2,1,0:T(8,128)} %pad_maximum_fusion.3), channel_id=1, source_target_pairs={{0,4},{1,5},{2,0},{3,1},{4,6},{5,7},{6,2},{7,3},{8,12},{9,13},{10,... | collective-permute-start | bytes 3145736 | tf_op jit(solution)/shard_map/ppermute | solution.py:284
  245.2 11.5 %collective-permute-start.50 = (f32[512,128]{1,0:T(8,128)S(1)}, f32[512,128]{1,0:T(8,128)S(1)}, u32[]{:S(2)}, u32[]{:S(2)}) collective-permute-start(f32[512,128]{1,0:T(8,128)S(1)} %get-tuple-element.171), channel_id=1, source_target_pairs={{0,1},{1,0},{2,3},{3,2},{4,5},{5,4},{6,7},{7,6},{8,9},{9,8},{10,11... | collective-permute-start | bytes 786440 | tf_op jit(solution)/shard_map/ppermute | solution.py:264
  249.1 10.9 %collective-permute-start.51 = (f32[512,128]{1,0:T(8,128)S(1)}, f32[512,128]{1,0:T(8,128)S(1)}, u32[]{:S(2)}, u32[]{:S(2)}) collective-permute-start(f32[512,128]{1,0:T(8,128)S(1)} %get-tuple-element.172), channel_id=1, source_target_pairs={{0,9},{1,8},{2,11},{3,10},{4,13},{5,12},{6,15},{7,14},{8,1},{9,0},... | collective-permute-start | bytes 786440 | tf_op jit(solution)/shard_map/ppermute | solution.py:264
  256.8 18.0 %collective-permute-start.57 = (f32[8,128,128]{2,1,0:T(8,128)S(1)}, f32[8,128,128]{2,1,0:T(8,128)S(1)}, u32[]{:S(2)}, u32[]{:S(2)}) collective-permute-start(f32[8,128,128]{2,1,0:T(8,128)S(1)} %collective-permute-done.56.refs_27_.refs_4_), channel_id=1, source_target_pairs={{0,16},{16,0},{1,17},{17,1},{2,18},{18,2},{3,19},{19,3},{4,20},{20... | collective-permute-start | bytes 1572872 | tf_op jit(solution)/shard_map/ppermute | solution.py:292
  261.3 13.5 %collective-permute-start.45 = (f32[512,128]{1,0:T(8,128)S(1)}, f32[512,128]{1,0:T(8,128)S(1)}, u32[]{:S(2)}, u32[]{:S(2)}) collective-permute-start(f32[512,128]{1,0:T(8,128)S(1)} %get-tuple-element.164), channel_id=1, source_target_pairs={{0,9},{1,8},{2,11},{3,10},{4,13},{5,12},{6,15},{7,14},{8,1},{9,0},... | collective-permute-start | bytes 786440 | tf_op jit(solution)/shard_map/ppermute | solution.py:264
  284.5 12.7 %collective-permute-start.66 = (f32[512,128]{1,0:T(8,128)S(1)}, f32[512,128]{1,0:T(8,128)S(1)}, u32[]{:S(2)}, u32[]{:S(2)}) collective-permute-start(f32[512,128]{1,0:T(8,128)S(1)} %get-tuple-element.193), channel_id=1, source_target_pairs={{0,9},{1,8},{2,11},{3,10},{4,13},{5,12},{6,15},{7,14},{8,1},{9,0},... | collective-permute-start | bytes 786440 | tf_op jit(solution)/shard_map/ppermute | solution.py:264
  285.1 45.9 %collective-permute-start.71 = (f32[16,128,128]{2,1,0:T(8,128)S(1)}, f32[16,128,128]{2,1,0:T(8,128)S(1)}, u32[]{:S(2)}, u32[]{:S(2)}) collective-permute-start(f32[16,128,128]{2,1,0:T(8,128)S(1)} %collective-permute-done.70.refs_25_.refs_29_.refs_9_.refs_13_), channel_id=1, source_target_pairs={{0,16},{16,0},{1,17},{17,1},{2,18},{18,2},{3,19},{19,3},{4,20},{20... | collective-permute-start | bytes 3145736 | tf_op jit(solution)/shard_map/ppermute | solution.py:292
  287.0 23.3 %collective-permute-start.72 = (f32[8,128,128]{2,1,0:T(8,128)S(1)}, f32[8,128,128]{2,1,0:T(8,128)S(1)}, u32[]{:S(2)}, u32[]{:S(2)}) collective-permute-start(f32[8,128,128]{2,1,0:T(8,128)S(1)} %bitcast.105), channel_id=1, source_target_pairs={{0,4},{1,5},{2,0},{3,1},{4,6},{5,7},{6,2},{7,3},{8,12},{9,13},{10,... | collective-permute-start | bytes 1572872 | tf_op jit(solution)/shard_map/ppermute | solution.py:284
  287.0 15.8 %collective-permute-start.58 = (f32[520,128]{1,0:T(8,128)S(1)}, f32[520,128]{1,0:T(8,128)S(1)}, u32[]{:S(2)}, u32[]{:S(2)}) collective-permute-start(f32[520,128]{1,0:T(8,128)S(1)} %get-tuple-element.183), channel_id=1, source_target_pairs={{0,8},{1,9},{2,10},{3,11},{4,12},{5,13},{6,14},{7,15},{8,0},{9,1},... | collective-permute-start | bytes 798728 | tf_op jit(solution)/shard_map/ppermute | solution.py:264
  292.3 11.3 %collective-permute-start.59 = (f32[520,128]{1,0:T(8,128)S(1)}, f32[520,128]{1,0:T(8,128)S(1)}, u32[]{:S(2)}, u32[]{:S(2)}) collective-permute-start(f32[520,128]{1,0:T(8,128)S(1)} %get-tuple-element.184), channel_id=1, source_target_pairs={{0,1},{1,0},{2,3},{3,2},{4,5},{5,4},{6,7},{7,6},{8,9},{9,8},{10,11... | collective-permute-start | bytes 798728 | tf_op jit(solution)/shard_map/ppermute | solution.py:264
  297.2 11.4 %collective-permute-start.60 = (f32[520,128]{1,0:T(8,128)S(1)}, f32[520,128]{1,0:T(8,128)S(1)}, u32[]{:S(2)}, u32[]{:S(2)}) collective-permute-start(f32[520,128]{1,0:T(8,128)S(1)} %get-tuple-element.185), channel_id=1, source_target_pairs={{0,9},{1,8},{2,11},{3,10},{4,13},{5,12},{6,15},{7,14},{8,1},{9,0},... | collective-permute-start | bytes 798728 | tf_op jit(solution)/shard_map/ppermute | solution.py:264
  302.8 11.2 %collective-permute-start.67 = (f32[512,128]{1,0:T(8,128)S(1)}, f32[512,128]{1,0:T(8,128)S(1)}, u32[]{:S(2)}, u32[]{:S(2)}) collective-permute-start(f32[512,128]{1,0:T(8,128)S(1)} %get-tuple-element.195), channel_id=1, source_target_pairs={{0,8},{1,9},{2,10},{3,11},{4,12},{5,13},{6,14},{7,15},{8,0},{9,1},... | collective-permute-start | bytes 786440 | tf_op jit(solution)/shard_map/ppermute | solution.py:264
  303.6 11.3 %collective-permute-start.68 = (f32[512,128]{1,0:T(8,128)S(1)}, f32[512,128]{1,0:T(8,128)S(1)}, u32[]{:S(2)}, u32[]{:S(2)}) collective-permute-start(f32[512,128]{1,0:T(8,128)S(1)} %get-tuple-element.196), channel_id=1, source_target_pairs={{0,1},{1,0},{2,3},{3,2},{4,5},{5,4},{6,7},{7,6},{8,9},{9,8},{10,11... | collective-permute-start | bytes 786440 | tf_op jit(solution)/shard_map/ppermute | solution.py:264
  308.6 11.2 %collective-permute-start.69 = (f32[512,128]{1,0:T(8,128)S(1)}, f32[512,128]{1,0:T(8,128)S(1)}, u32[]{:S(2)}, u32[]{:S(2)}) collective-permute-start(f32[512,128]{1,0:T(8,128)S(1)} %get-tuple-element.197), channel_id=1, source_target_pairs={{0,9},{1,8},{2,11},{3,10},{4,13},{5,12},{6,15},{7,14},{8,1},{9,0},... | collective-permute-start | bytes 786440 | tf_op jit(solution)/shard_map/ppermute | solution.py:264
  310.4 20.7 %collective-permute-start.73 = (f32[8,128,128]{2,1,0:T(8,128)S(1)}, f32[8,128,128]{2,1,0:T(8,128)S(1)}, u32[]{:S(2)}, u32[]{:S(2)}) collective-permute-start(f32[8,128,128]{2,1,0:T(8,128)S(1)} %collective-permute-done.72.refs_27_.refs_11_), channel_id=1, source_target_pairs={{0,16},{16,0},{1,17},{17,1},{2,18},{18,2},{3,19},{19,3},{4,20},{20... | collective-permute-start | bytes 1572872 | tf_op jit(solution)/shard_map/ppermute | solution.py:292
  315.0 11.2 %collective-permute-start.62 = (f32[512,128]{1,0:T(8,128)S(1)}, f32[512,128]{1,0:T(8,128)S(1)}, u32[]{:S(2)}, u32[]{:S(2)}) collective-permute-start(f32[512,128]{1,0:T(8,128)S(1)} %get-tuple-element.188), channel_id=1, source_target_pairs={{0,1},{1,0},{2,3},{3,2},{4,5},{5,4},{6,7},{7,6},{8,9},{9,8},{10,11... | collective-permute-start | bytes 786440 | tf_op jit(solution)/shard_map/ppermute | solution.py:264
  319.8 11.2 %collective-permute-start.63 = (f32[512,128]{1,0:T(8,128)S(1)}, f32[512,128]{1,0:T(8,128)S(1)}, u32[]{:S(2)}, u32[]{:S(2)}) collective-permute-start(f32[512,128]{1,0:T(8,128)S(1)} %get-tuple-element.189), channel_id=1, source_target_pairs={{0,9},{1,8},{2,11},{3,10},{4,13},{5,12},{6,15},{7,14},{8,1},{9,0},... | collective-permute-start | bytes 786440 | tf_op jit(solution)/shard_map/ppermute | solution.py:264
  337.8 25.0 %collective-permute-start.74 = (f32[520,128]{1,0:T(8,128)S(1)}, f32[520,128]{1,0:T(8,128)S(1)}, u32[]{:S(2)}, u32[]{:S(2)}) collective-permute-start(f32[520,128]{1,0:T(8,128)S(1)} %get-tuple-element.205), channel_id=1, source_target_pairs={{0,8},{1,9},{2,10},{3,11},{4,12},{5,13},{6,14},{7,15},{8,0},{9,1},... | collective-permute-start | bytes 798728 | tf_op jit(solution)/shard_map/ppermute | solution.py:264
  338.1 24.7 %collective-permute-start.75 = (f32[520,128]{1,0:T(8,128)S(1)}, f32[520,128]{1,0:T(8,128)S(1)}, u32[]{:S(2)}, u32[]{:S(2)}) collective-permute-start(f32[520,128]{1,0:T(8,128)S(1)} %get-tuple-element.206), channel_id=1, source_target_pairs={{0,1},{1,0},{2,3},{3,2},{4,5},{5,4},{6,7},{7,6},{8,9},{9,8},{10,11... | collective-permute-start | bytes 798728 | tf_op jit(solution)/shard_map/ppermute | solution.py:264
  339.2 23.6 %collective-permute-start.76 = (f32[520,128]{1,0:T(8,128)S(1)}, f32[520,128]{1,0:T(8,128)S(1)}, u32[]{:S(2)}, u32[]{:S(2)}) collective-permute-start(f32[520,128]{1,0:T(8,128)S(1)} %get-tuple-element.207), channel_id=1, source_target_pairs={{0,9},{1,8},{2,11},{3,10},{4,13},{5,12},{6,15},{7,14},{8,1},{9,0},... | collective-permute-start | bytes 798728 | tf_op jit(solution)/shard_map/ppermute | solution.py:264
  339.7 19.0 %collective-permute-start.78 = (f32[512,128]{1,0:T(8,128)S(1)}, f32[512,128]{1,0:T(8,128)S(1)}, u32[]{:S(2)}, u32[]{:S(2)}) collective-permute-start(f32[512,128]{1,0:T(8,128)S(1)} %get-tuple-element.210), channel_id=1, source_target_pairs={{0,1},{1,0},{2,3},{3,2},{4,5},{5,4},{6,7},{7,6},{8,9},{9,8},{10,11... | collective-permute-start | bytes 786440 | tf_op jit(solution)/shard_map/ppermute | solution.py:264
  340.9 22.0 %collective-permute-start.79 = (f32[512,128]{1,0:T(8,128)S(1)}, f32[512,128]{1,0:T(8,128)S(1)}, u32[]{:S(2)}, u32[]{:S(2)}) collective-permute-start(f32[512,128]{1,0:T(8,128)S(1)} %get-tuple-element.211), channel_id=1, source_target_pairs={{0,9},{1,8},{2,11},{3,10},{4,13},{5,12},{6,15},{7,14},{8,1},{9,0},... | collective-permute-start | bytes 786440 | tf_op jit(solution)/shard_map/ppermute | solution.py:264
  372.0 9.8 %collective-permute-start.88 = (f32[256,128]{1,0:T(8,128)S(1)}, f32[256,128]{1,0:T(8,128)S(1)}, u32[]{:S(2)}, u32[]{:S(2)}) collective-permute-start(f32[256,128]{1,0:T(8,128)S(1)} %get-tuple-element.224), channel_id=1, source_target_pairs={{0,1},{1,0},{2,3},{3,2},{4,5},{5,4},{6,7},{7,6},{8,9},{9,8},{10,11... | collective-permute-start | bytes 393224 | tf_op jit(solution)/shard_map/ppermute | solution.py:264
  373.2 10.2 %collective-permute-start.89 = (f32[256,128]{1,0:T(8,128)S(1)}, f32[256,128]{1,0:T(8,128)S(1)}, u32[]{:S(2)}, u32[]{:S(2)}) collective-permute-start(f32[256,128]{1,0:T(8,128)S(1)} %get-tuple-element.225), channel_id=1, source_target_pairs={{0,9},{1,8},{2,11},{3,10},{4,13},{5,12},{6,15},{7,14},{8,1},{9,0},... | collective-permute-start | bytes 393224 | tf_op jit(solution)/shard_map/ppermute | solution.py:264
  376.3 9.3 %collective-permute-start.83 = (f32[256,128]{1,0:T(8,128)S(1)}, f32[256,128]{1,0:T(8,128)S(1)}, u32[]{:S(2)}, u32[]{:S(2)}) collective-permute-start(f32[256,128]{1,0:T(8,128)S(1)} %get-tuple-element.218), channel_id=1, source_target_pairs={{0,8},{1,9},{2,10},{3,11},{4,12},{5,13},{6,14},{7,15},{8,0},{9,1},... | collective-permute-start | bytes 393224 | tf_op jit(solution)/shard_map/ppermute | solution.py:264
  377.8 9.7 %collective-permute-start.84 = (f32[256,128]{1,0:T(8,128)S(1)}, f32[256,128]{1,0:T(8,128)S(1)}, u32[]{:S(2)}, u32[]{:S(2)}) collective-permute-start(f32[256,128]{1,0:T(8,128)S(1)} %get-tuple-element.219), channel_id=1, source_target_pairs={{0,1},{1,0},{2,3},{3,2},{4,5},{5,4},{6,7},{7,6},{8,9},{9,8},{10,11... | collective-permute-start | bytes 393224 | tf_op jit(solution)/shard_map/ppermute | solution.py:264
  378.6 9.8 %collective-permute-start.85 = (f32[256,128]{1,0:T(8,128)S(1)}, f32[256,128]{1,0:T(8,128)S(1)}, u32[]{:S(2)}, u32[]{:S(2)}) collective-permute-start(f32[256,128]{1,0:T(8,128)S(1)} %get-tuple-element.220), channel_id=1, source_target_pairs={{0,9},{1,8},{2,11},{3,10},{4,13},{5,12},{6,15},{7,14},{8,1},{9,0},... | collective-permute-start | bytes 393224 | tf_op jit(solution)/shard_map/ppermute | solution.py:264
  381.9 22.8 %collective-permute-start.94 = (f32[128,1024]{1,0:T(8,128)S(1)}, f32[128,1024]{1,0:T(8,128)}, u32[]{:S(2)}, u32[]{:S(2)}) collective-permute-start(f32[128,1024]{1,0:T(8,128)S(1)} %shard_map.63), channel_id=1, source_target_pairs={{0,4},{1,5},{2,0},{3,1},{4,6},{5,7},{6,2},{7,3},{8,12},{9,13},{10,... | collective-permute-start | bytes 1572872 | tf_op jit(solution)/shard_map/ppermute | solution.py:264
  384.4 23.2 %collective-permute-start.90 = (f32[128,1024]{1,0:T(8,128)S(1)}, f32[128,1024]{1,0:T(8,128)}, u32[]{:S(2)}, u32[]{:S(2)}) collective-permute-start(f32[128,1024]{1,0:T(8,128)S(1)} %shard_map.62), channel_id=1, source_target_pairs={{0,6},{1,7},{2,4},{3,5},{4,2},{5,3},{6,0},{7,1},{8,14},{9,15},{10,... | collective-permute-start | bytes 1572872 | tf_op jit(solution)/shard_map/ppermute | solution.py:264
  390.1 37.9 %collective-permute-start.86 = (f32[128,1024]{1,0:T(8,128)}, f32[128,1024]{1,0:T(8,128)}, u32[]{:S(2)}, u32[]{:S(2)}) collective-permute-start(f32[128,1024]{1,0:T(8,128)} %shard_map.61), channel_id=1, source_target_pairs={{0,2},{1,3},{2,6},{3,7},{4,0},{5,1},{6,4},{7,5},{8,10},{9,11},{10,... | collective-permute-start | bytes 1572872 | tf_op jit(solution)/shard_map/ppermute | solution.py:264
  (94 other events, 1269.6 us)

commit v4 on v3

--- a/solution.py
+++ b/solution.py
@@ -95,12 +95,45 @@
 
 def first_kernel(step, kinds, place, *refs):
     take = Taker(refs)
-    tokens, gain = take(1)[0], take(1)
+    tokens = take(1)[0]
     weights = take_weights(take, kinds)
-    current, send, tile = take(1), [take(QUARTERS)], take(1)[0]
+    current, gain, rows, send, tile = take(1), take(1), take(1)[0], [take(QUARTERS)], take(1)[0]
     for index in range(ROWS):
-        current[0][index] = tokens[:, pl.ds(index * LANES, LANES)].T
+        current[0][index] = tokens[pl.ds(0, LANES), pl.ds(index * LANES, LANES)].T
+    rows[...] = tokens[pl.ds(LANES, ROWS), :]
+    spread_gain(0, rows, gain[0])
     first_factor([step], True, current, gain, weights, send, tile, read_place(place))
+
+
+def spread_gain(layer, rows, spread):
+    for index in range(ROWS):
+        columns = rows[:, pl.ds(index * LANES, LANES)].T
+        spread[index] = jnp.broadcast_to(columns[:, layer : layer + 1], (LANES, LANES))
+
+
+def deal_kernel(rounds, place, tokens, gains, their_tokens, their_gains, *pieces):
+    position, core = place[0], place[1] % 2
+    half = their_tokens.shape[1]
+    columns = pl.ds(pl.multiple_of(core * half, half), half)
+    rows = []
+    for r in range(rounds):
+        mine, other = gains[pl.ds(r, 1), columns], their_gains[pl.ds(r, 1), :]
+        rows += [jnp.where(core == 0, mine, other), jnp.where(core == 0, other, mine)]
+    rows.append(jnp.zeros((ROWS - 2 * rounds, half), jnp.float32))
+    rows = jnp.concatenate(rows)
+    for step in range(PLANES):
+        plane = gray((position + PLANES - step) % PLANES)
+        base = (plane % 2) * LANES
+
+        def move(n, carry, step=step, plane=plane, base=base):
+            start = pl.multiple_of(base + n * ROWS, ROWS)
+            kept, other = tokens[pl.ds(start, ROWS), columns], their_tokens[pl.ds(start, ROWS), :]
+            there = pl.ds(pl.multiple_of(n * ROWS, ROWS), ROWS)
+            pieces[step][there, :] = jnp.where(plane // 2 == core, kept, other)
+            return carry
+
+        lax.fori_loop(0, LANES // ROWS, move, 0, unroll=4)
+        pieces[step][pl.ds(LANES, ROWS), :] = rows
 
 
 def last_kernel(width, step, squares_count, place, *refs):
@@ -159,14 +192,14 @@
     first_factor(range(PLANES), False, fresh, gain, weights, send, tile, (position, quarter, group))
 
 
-def column_kernel(others, in_pieces, out_pieces, kinds, has_gain, place, *refs):
+def column_kernel(others, in_pieces, out_pieces, kinds, gain_layer, place, *refs):
     take = Taker(refs)
     position, quarter, group = read_place(place)
     came = [take(QUARTERS) for _ in range(PLANES if in_pieces else len(others) // 2)]
     weights = take_weights(take, kinds)
-    rows = take(PLANES) if has_gain else []
+    rows = take(PLANES) if gain_layer else []
     send = [take(QUARTERS) for _ in range(PLANES if out_pieces else len(others) // 2)]
-    spread = take(PLANES) if has_gain else []
+    spread = take(PLANES) if gain_layer else []
     value, tile = take(2)
     for n, other in enumerate(others):
         for index in range(ROWS):
@@ -185,32 +218,63 @@
                         index, row_offset(step, mate, position, quarter), :
                     ]
     for step in range(len(rows)):
-        columns = rows[step][...].T
-        for index in range(ROWS):
-            spread[step][index] = jnp.broadcast_to(columns[:, index : index + 1], (LANES, LANES))
+        spread_gain(gain_layer, rows[step], spread[step])
 
 
 SMALL = pl.BlockSpec(memory_space=pltpu.SMEM)
 WHOLE = pl.BlockSpec(memory_space=pltpu.VMEM)
-PARAMS = pltpu.CompilerParams(vmem_limit_bytes=40 * 1024 * 1024)
+PARAMS = pltpu.CompilerParams(vmem_limit_bytes=8 * 1024 * 1024)
 PIECE = (ROWS, LANES, LANES)
+COST_PART = 16
 
 
 def array(*shape):
     return jax.ShapeDtypeStruct(shape, jnp.float32)
 
 
-def call(kernel, operands, outs, scratch, flops):
+def marked(kernel, operand_count, wait_count, *refs):
+    outs = refs[operand_count + wait_count :]
+    outs[0][0] = 0
+    kernel(*refs[:operand_count], *outs[1:])
+
+
+def call(kernel, operands, outs, scratch, flops, waits=(), specs=None, out_spec=WHOLE):
     moved = 4 * (sum(a.size for a in operands) + sum(o.size for o in outs))
-    return pl.pallas_call(
-        kernel,
-        out_shape=outs,
-        in_specs=[SMALL] + [WHOLE] * (len(operands) - 1),
-        out_specs=[WHOLE] * len(outs),
-        scratch_shapes=[pltpu.VMEM(PIECE, jnp.float32)] * scratch,
+    results = pl.pallas_call(
+        functools.partial(marked, kernel, len(operands), len(waits)),
+        out_shape=[jax.ShapeDtypeStruct((1,), jnp.int32), *outs],
+        in_specs=[SMALL] + (specs or [WHOLE] * (len(operands) - 1)) + [WHOLE if w.ndim > 1 else SMALL for w in waits],
+        out_specs=[SMALL] + [out_spec] * len(outs),
+        scratch_shapes=scratch if isinstance(scratch, list) else [pltpu.VMEM(PIECE, jnp.float32)] * scratch,
         compiler_params=PARAMS,
-        cost_estimate=pl.CostEstimate(flops=flops, bytes_accessed=moved, transcendentals=0),
-    )(*operands)
+        cost_estimate=pl.CostEstimate(flops=flops // COST_PART, bytes_accessed=moved // COST_PART, transcendentals=0),
+    )(*operands, *waits)
+    return list(results[1:]), results[0]
+
+
+def copies_kernel(moves, in_count, out_count, place, *refs):
+    sems = refs[-1]
+    copies = []
+    for n, (source, at, target, there, when) in enumerate(moves):
+        copy = pltpu.make_async_copy(refs[source].at[at(place)], refs[in_count + target].at[there], sems.at[n])
+        copies.append((copy, when))
+    for act in ("start", "wait"):
+        for copy, when in copies:
+            if when is None:
+                getattr(copy, act)()
+            else:
+                pl.when(when(place))(getattr(copy, act))
+
+
+def copied(place, operands, outs, moves, waits=(), anywhere=True):
+    specs = [pl.BlockSpec(memory_space=pl.ANY) if anywhere else WHOLE] * len(operands)
+    kernel = functools.partial(copies_kernel, moves, len(operands), len(outs))
+    sems = [pltpu.SemaphoreType.DMA((len(moves),))]
+    return call(kernel, [place, *operands], outs, sems, 0, waits, specs)[0]
+
+
+def core_of(place):
+    return place[1] % 2
 
 
 STAGE_FLOPS = 6 * 32 * LANES * LANES * LANES
@@ -220,18 +284,24 @@
     return [array for piece in weights for array in piece[2]], [piece[:2] for piece in weights]
 
 
-def first_piece(step, place, tokens, gain, weights):
+def deal(place, tokens, gains, their_tokens, their_gains):
+    outs = [array(LANES + ROWS, their_tokens.shape[1])] * PLANES
+    operands = [place, tokens, gains, their_tokens, their_gains]
+    return call(functools.partial(deal_kernel, gains.shape[0]), operands, outs, 0, 0)
+
+
+def first_piece(step, place, tokens, weights, waits):
     operands, kinds = split_weights([weights])
     kernel = functools.partial(first_kernel, step, kinds)
-    outs = [array(*PIECE)] + [array(264, LANES)] * QUARTERS
-    results = list(call(kernel, [place, tokens, gain, *operands], outs, 1, STAGE_FLOPS // 4))
-    return results[0], results[1:]
+    outs = [array(*PIECE)] * 2 + [array(ROWS, ROWS * LANES)] + [array(264, LANES)] * QUARTERS
+    results, mark = call(kernel, [place, tokens, *operands], outs, 1, STAGE_FLOPS // 4, waits)
+    return results[:3], results[3:], mark
 
 
 def last_piece(width, step, place, current, old_gain, squares, mixed):
     kernel = functools.partial(last_kernel, width, step, len(squares))
     operands = [place, current, old_gain, *squares, *mixed]
-    return call(kernel, operands, [array(LANES, ROWS * LANES)], 1, STAGE_FLOPS // 4)[0]
+    return call(kernel, operands, [array(LANES, ROWS * LANES)], 1, STAGE_FLOPS // 4)[0][0]
 
 
 def layer_edge(width, place, current, old_gain, squares, mixed, gain, weights):
@@ -239,19 +309,19 @@
     operands = [place, *current, *old_gain, *squares, *mixed[0], *mixed[1], *gain, *more]
     outs = [array(*PIECE)] * PLANES + [array(520, LANES)] * QUARTERS + [array(512, LANES)] * QUARTERS
     kernel = functools.partial(edge_kernel, width, len(squares), kinds)
-    results = list(call(kernel, operands, outs, 1, 2 * STAGE_FLOPS))
+    results, _ = call(kernel, operands, outs, 1, 2 * STAGE_FLOPS)
     return results[:PLANES], [results[PLANES : PLANES + QUARTERS], results[PLANES + QUARTERS :]]
 
 
-def column_stage(others, in_pieces, out_pieces, place, came, weights, rows=()):
+def column_stage(others, in_pieces, out_pieces, place, came, weights, rows=(), gain_layer=0):
     more, kinds = split_weights(weights)
     operands = [place, *(ref for part in came for ref in part), *more, *rows]
     outs = [array(256, LANES)] * (QUARTERS * PLANES) if out_pieces else [array(512, LANES)] * QUARTERS
     count = len(outs)
     outs = outs + [array(*PIECE)] * len(rows)
-    kernel = functools.partial(column_kernel, others, in_pieces, out_pieces, kinds, bool(rows))
-    results = list(call(kernel, operands, outs, 2, STAGE_FLOPS))
-    return [results[n : n + QUARTERS] for n in range(0, count, QUARTERS)], results[count:]
+    kernel = functools.partial(column_kernel, others, in_pieces, out_pieces, kinds, gain_layer)
+    results, mark = call(kernel, operands, outs, 2, STAGE_FLOPS)
+    return [results[n : n + QUARTERS] for n in range(0, count, QUARTERS)], results[count:], mark
 
 
 def routed(value, to):
@@ -296,10 +366,6 @@
     return [chunk[0]] + [to_mate(chunk[mate], mate) for mate in range(1, QUARTERS)]
 
 
-def after(value, *earlier):
-    return lax.optimization_barrier((value, *earlier))[0]
-
-
 def plane_body(tokens, gains, right_factors, left_factors):
     core = lax.axis_index("segment")
     block = lax.axis_index("block")
@@ -311,82 +377,83 @@
     layers = 2 * rounds
     width = right_factors.shape[3] * 8 * right_factors.shape[2]
 
-    def swapped(value):
-        mine = lax.dynamic_slice_in_dim(value, core * ROWS, ROWS, 0)
-        theirs = core_swap(lax.dynamic_slice_in_dim(value, (1 - core) * ROWS, ROWS, 0))
-        return jnp.where(core == 0, mine, theirs), jnp.where(core == 0, theirs, mine)
-
-    half = tokens.shape[1] // 2
-    mine = lax.dynamic_slice_in_dim(tokens, core * half, half, 1)
-    theirs = core_swap(lax.dynamic_slice_in_dim(tokens, (1 - core) * half, half, 1))
-    pieces = []
-    for step in range(PLANES):
-        plane = gray((position - step) % PLANES)
-        start = (plane % 2) * LANES
-        kept = lax.dynamic_slice_in_dim(mine, start, LANES, 0)
-        other = lax.dynamic_slice_in_dim(theirs, start, LANES, 0)
-        pieces.append(jnp.where(plane // 2 == core, kept, other))
+    count, half = tokens.shape[0], tokens.shape[1] // 2
+    their_tokens = core_swap(lax.dynamic_slice_in_dim(tokens, (1 - core) * half, half, 1))
+    their_gains = core_swap(lax.dynamic_slice_in_dim(gains[0], (1 - core) * half, half, 1))
+
+    pieces, dealt = deal(place, tokens, gains[0], their_tokens, their_gains)
     arrived = [piece if step == 0 else ring(piece, -step) for step, piece in enumerate(pieces)]
 
-    held = jnp.moveaxis(gains[0].reshape(rounds, 2 * ROWS, LANES), 1, 0)
-    held = jnp.stack(swapped(held), axis=2).transpose(1, 2, 0, 3).reshape(layers, ROWS, LANES)
-    gain_pieces = [held]
-    for _ in range(PLANES - 1):
-        held = ring(held, -1)
-        gain_pieces.append(held)
-    gain_rows = [[piece[layer] for piece in gain_pieces] for layer in range(layers)]
-
-    right, left = [None] * layers, [None] * layers
-    for r in range(rounds):
-        right[2 * r], right[2 * r + 1] = swapped(right_factors[0, r])
-        left[2 * r], left[2 * r + 1] = swapped(left_factors[0, r])
-
-    def fetched(parts, earlier):
-        together = parts[0] if len(parts) == 1 else jnp.concatenate(parts)
-        near = group_ring(after(together, *earlier))
-        folded = near.reshape(len(parts), 2, 4, LANES, LANES)
-        far = group_ring(lax.dynamic_index_in_dim(folded, group, 1, keepdims=False).reshape(-1, LANES, LANES))
+    def swapped(factors, r, waits):
+        move = (0, lambda p: (0, r, pl.ds((1 - core_of(p)) * ROWS, ROWS)), 0, pl.ds(0, ROWS), None)
+        return factors, r, core_swap(copied(place, [factors], [array(*PIECE)], [move], waits)[0])
+
+    def own(pairs, section, waits):
+        operands, moves = [], []
+        for n, (factors, r, theirs) in enumerate(pairs):
+            there = pl.ds(n * ROWS, ROWS)
+            operands += [factors, theirs]
+            mine = lambda p, r=r: (0, r, pl.ds(core_of(p) * ROWS, ROWS))
+            moves.append((2 * n, mine, 0, there, lambda p: core_of(p) == section))
+            moves.append((2 * n + 1, lambda p: pl.ds(0, ROWS), 0, there, lambda p: core_of(p) != section))
+        return copied(place, operands, [array(len(pairs) * ROWS, LANES, LANES)], moves, waits)[0]
+
+    def near_half(near, waits=()):
+        count = near.shape[0] // ROWS
+        moves = [
+            (0, lambda p, n=n: pl.ds(n * ROWS + p[2] * 4, 4), 0, pl.ds(n * 4, 4), None) for n in range(count)
+        ]
+        return group_ring(copied(place, [near], [array(count * 4, LANES, LANES)], moves, waits, False)[0])
+
+    def four_pieces(part, near, far):
         near_pair, far_pair = (near, group_swap(near)), (far, group_swap(far))
-        found = []
-        for n, part in enumerate(parts):
-            found.append(
-                [
-                    ("whole", 0, (part,)),
-                    ("next", n * ROWS, near_pair),
-                    ("halves", n * 4, far_pair),
-                    ("previous", n * ROWS, near_pair),
-                ]
-            )
-        return found, far
-
-    right_parts, left_parts = [], []
-    (found,), last = fetched([right[0]], [pieces[1]])
-    right_parts.append(found)
-    (found,), last = fetched([left[0]], [last])
-    left_parts.append(found)
-    for layer in range(1, layers):
-        (found, more), last = fetched([right[layer], left[layer]], [last])
-        right_parts.append(found)
-        left_parts.append(more)
-
-    gain = [jnp.broadcast_to(row[:, :, None], PIECE) for row in gain_rows[0]]
-    current, came = [], []
-    for step in range(PLANES):
-        turned, sends = first_piece(step, place, arrived[step], gain[step], right_parts[0][step])
-        current.append(turned)
-        came.append(exchange(sends))
+        return [
+            [
+                ("whole", n * ROWS, (part,)),
+                ("next", n * ROWS, near_pair),
+                ("halves", n * 4, far_pair),
+                ("previous", n * ROWS, near_pair),
+            ]
+            for n in range(part.shape[0] // ROWS)
+        ]
+
+    right_parts, left_parts = [None] * layers, [None] * layers
+    pairs = [swapped(right_factors, 0, ())]
+    part = own(pairs, 0, ())
+    near = group_ring(part)
+    far = near_half(near, arrived[1:4:2])
+    (right_parts[0],) = four_pieces(part, near, far)
+    pairs.append(swapped(left_factors, 0, [dealt]))
+
+    current, gain, rows, came = [None] * PLANES, [None] * PLANES, [None] * PLANES, [None] * PLANES
+    waits = []
+    for step in (0, 1, 3, 2):
+        results, sends, mark = first_piece(step, place, arrived[step], right_parts[0][step], waits)
+        waits = [mark]
+        current[step], gain[step], rows[step] = results
+        came[step] = exchange(sends)
+    part = own(pairs[1:], 0, [arrived[2], far])
+    near = group_ring(part)
+    far = near_half(near)
+    (left_parts[0],) = four_pieces(part, near, far)
     for layer in range(layers - 1):
+        part = own(pairs, (layer + 1) % 2, [far, mark])
+        near = group_ring(part)
+        far = near_half(near)
+        right_parts[layer + 1], left_parts[layer + 1] = four_pieces(part, near, far)
         in_pieces = layer == 0
         squares = [part[mate] for part in (came if in_pieces else came[:1]) for mate in range(QUARTERS)]
         mixed = []
         for chunk in range(CHUNKS):
             others = (chunk * 2, chunk * 2 + 1)
-            rows = gain_rows[layer + 1] if chunk == 0 else ()
+            extra = (rows, layer + 1) if chunk == 0 else ()
             weights = left_parts[layer][others[0] : others[1] + 1]
             source = came if in_pieces else came[chunk : chunk + 1]
-            (sends,), spread = column_stage(others, in_pieces, False, place, source, weights, rows)
-            mixed.append(exchange(sends))
+            (half_sends,), spread, mark = column_stage(others, in_pieces, False, place, source, weights, *extra)
+            mixed.append(exchange(half_sends))
             next_gain = spread or next_gain
+        if layer % 2 == 0 and layer + 2 < layers:
+            pairs = [swapped(factors, (layer + 2) // 2, [mark]) for factors in (right_factors, left_factors)]
         current, sends = layer_edge(
             width, place, current, gain, squares, mixed, next_gain, right_parts[layer + 1]
         )
@@ -394,7 +461,7 @@
         came = [exchange(sends[0]), exchange(sends[1])]
 
     squares = came[0]
-    sends, _ = column_stage(tuple(range(PLANES)), False, True, place, came, left_parts[-1])
+    sends, _, _ = column_stage(tuple(range(PLANES)), False, True, place, came, left_parts[-1])
     back = [None] * PLANES
     for step in (2, 1, 3, 0):
         mixed = exchange(sends[step])

time: 435 us -> 405 us (0.931)
  local copies, waits for them, and re-layouts: 29.6 us -> 2.72 us
  Pallas kernels: 40.4 us -> 63.1 us
  waiting for transfers between devices: 245 us -> 229 us
  other arithmetic: 12.7 us -> 3.35 us
    ppermute x10, waiting for transfers between devices: 29.6 us -> 3.73 us  [group_swap(): return lax.ppermute(value, 'groups', [(0, 1), (1, 0)])]
    pallas_call x18 -> x33, Pallas kernels: 40.4 us -> 63.1 us  [call(): pl.pallas_call(functools.partial(marked, kernel, len(operands), len(waits...]
    ppermute x10, waiting for transfers between devices: 37.4 us -> 59.4 us  [group_ring(): return lax.ppermute(value, ('groups', 'segment', 'block'), route)]
    unnamed x125 -> x8, local copies, waits for them, and re-layouts: 20.4 us -> 0.02 us
    ppermute x10, starting transfers between devices: 27.9 us -> 12.3 us  [group_swap(): return lax.ppermute(value, 'groups', [(0, 1), (1, 0)])]
    ppermute x10, starting transfers between devices: 18.7 us -> 34.1 us  [group_ring(): return lax.ppermute(value, ('groups', 'segment', 'block'), route)]
    ppermute x76 -> x73, waiting for transfers between devices: 178 us -> 166 us  [routed(): return lax.ppermute(value, ('segment', 'block'), route)]
    select_n x5 -> x0, other arithmetic: 7.13 us -> none  [the longest x4 5.15 us: swapped(): jnp.where(core == 0, theirs, mine)]
  transfers between devices with their start and end apart: 96 -> 93, of which waited for: 46 -> 44; matrix products, arithmetic and copies ran while one was open for 3% -> 0% of each run, Pallas kernels for 7% -> 13%
where the time goes in v4:
time: 405 us
  waiting for transfers between devices  229 us (57%)
  starting transfers between devices  107 us (26%)
  Pallas kernels  63.1 us (16%)
    ppermute x73, waiting for transfers between devices, routed(): return lax.ppermute(value, ('segment', 'block'), route)  166 us
    pallas_call x33, Pallas kernels, call(): pl.pallas_call(functools.partial(marked, kernel, len(operands), len(waits...  63.1 us
    ppermute x73, starting transfers between devices, routed(): return lax.ppermute(value, ('segment', 'block'), route)  60.2 us
    ppermute x10, waiting for transfers between devices, group_ring(): return lax.ppermute(value, ('groups', 'segment', 'block'), route)  59.4 us
    ppermute x10, starting transfers between devices, group_ring(): return lax.ppermute(value, ('groups', 'segment', 'block'), route)  34.1 us
    ppermute x10, starting transfers between devices, group_swap(): return lax.ppermute(value, 'groups', [(0, 1), (1, 0)])  12.3 us
  transfers between devices with their start and end apart: 93, of which 44 were waited for; matrix products, arithmetic and copies ran while one was open for 0% of the time, Pallas kernels for 13%

profile of v4, /device:TPU:0, one launch (start us, length us, event | category | flops | bytes accessed | tf_op | source)
XLA Modules:
  0.0 405.1 jit_solution(1373848321729841229)
XLA Ops:
  0.0 2.5 constant_dynamic-slice_fusion.4
  7.6 3.9 collective-permute-start.3
  12.7 3.0 collective-permute-start.4
  18.8 28.9 %collective-permute-done.4.refs_2_.refs_1_ = f32[8,128,128]{2,1,0:T(8,128)S(1)} collective-permute-done((f32[8,128,128]{2,1,0:T(8,128)S(1)}, f32[8,128,128]{2,1,0:T(8,128)S(1)}, u32[]{:S(2)}, u32[]{:S(2)}) %collective-permute-start.4) | collective-permute-done | bytes 524320 | tf_op jit(solution)/shard_map/ppermute | solution.py:354
  48.8 3.5 collective-permute-start.8
  52.3 9.2 %collective-permute-done.6.refs_1_.refs_3_ = f32[136,1024]{1,0:T(8,128)S(1)} collective-permute-done((f32[136,1024]{1,0:T(8,128)S(1)}, f32[136,1024]{1,0:T(8,128)S(1)}, u32[]{:S(2)}, u32[]{:S(2)}) %collective-permute-start.6) | collective-permute-done | bytes 557088 | tf_op jit(solution)/shard_map/ppermute | solution.py:334
  61.6 4.9 %collective-permute-done.8.refs_2_.refs_4_ = f32[4,128,128]{2,1,0:T(8,128)S(1)} collective-permute-done((f32[4,128,128]{2,1,0:T(8,128)S(1)}, f32[4,128,128]{2,1,0:T(8,128)S(1)}, u32[]{:S(2)}, u32[]{:S(2)}) %collective-permute-start.8) | collective-permute-done | bytes 262176 | tf_op jit(solution)/shard_map/ppermute | solution.py:354
  67.7 13.5 %collective-permute-start.23 = (f32[8,128,128]{2,1,0:T(8,128)S(1)}, f32[8,128,128]{2,1,0:T(8,128)S(1)}, u32[]{:S(2)}, u32[]{:S(2)}) collective-permute-start(f32[8,128,128]{2,1,0:T(8,128)S(1)} %get-tuple-element.186.refs_17_), channel_id=1, source_target_pairs={{0,4},{1,5},{2,0},{3,1},{4,6},{5,7},{6,2},{7,3},{8,12},{9,13},{10,... | collective-permute-start | bytes 1572872 | tf_op jit(solution)/shard_map/ppermute | solution.py:354
  81.1 2.0 collective-permute-start.9
  83.2 9.3 %collective-permute-done.23.refs_18_.refs_1_.refs_19_ = f32[8,128,128]{2,1,0:T(8,128)S(1)} collective-permute-done((f32[8,128,128]{2,1,0:T(8,128)S(1)}, f32[8,128,128]{2,1,0:T(8,128)S(1)}, u32[]{:S(2)}, u32[]{:S(2)}) %collective-permute-start.23) | collective-permute-done | bytes 524320 | tf_op jit(solution)/shard_map/ppermute | solution.py:354
  93.6 3.4 collective-permute-start.28
  98.8 2.4 shard_map.50
  101.3 2.3 shard_map.52
  103.6 2.4 shard_map.53
  111.7 2.7 collective-permute-done.11.refs_3_.refs_11_
  114.5 2.7 collective-permute-start.24
  122.7 2.0 collective-permute-start.21
  126.0 2.4 collective-permute-start.29
  128.4 2.2 collective-permute-start.17
  130.6 4.4 %collective-permute-done.17.refs_11_.refs_19_ = f32[264,128]{1,0:T(8,128)S(1)} collective-permute-done((f32[264,128]{1,0:T(8,128)S(1)}, f32[264,128]{1,0:T(8,128)S(1)}, u32[]{:S(2)}, u32[]{:S(2)}) %collective-permute-start.17) | collective-permute-done | bytes 135200 | tf_op jit(solution)/shard_map/ppermute | solution.py:334
  134.9 2.0 collective-permute-done.18.refs_12_.refs_20_
  136.9 2.0 shard_map.58
  144.2 1.9 collective-permute-start.35
  146.1 12.3 %collective-permute-done.35.refs_40_.refs_5_ = f32[8,128,128]{2,1,0:T(8,128)S(1)} collective-permute-done((f32[8,128,128]{2,1,0:T(8,128)S(1)}, f32[8,128,128]{2,1,0:T(8,128)S(1)}, u32[]{:S(2)}, u32[]{:S(2)}) %collective-permute-start.35) | collective-permute-done | bytes 524320 | tf_op jit(solution)/shard_map/ppermute | solution.py:354
  160.3 2.6 collective-permute-start.51
  164.0 2.5 shard_map.56
  169.4 6.3 %collective-permute-done.26.refs_27_ = f32[512,128]{1,0:T(8,128)S(1)} collective-permute-done((f32[512,128]{1,0:T(8,128)S(1)}, f32[512,128]{1,0:T(8,128)S(1)}, u32[]{:S(2)}, u32[]{:S(2)}) %collective-permute-start.26) | collective-permute-done | bytes 262176 | tf_op jit(solution)/shard_map/ppermute | solution.py:334
  175.7 4.7 %collective-permute-done.27.refs_28_ = f32[512,128]{1,0:T(8,128)S(1)} collective-permute-done((f32[512,128]{1,0:T(8,128)S(1)}, f32[512,128]{1,0:T(8,128)S(1)}, u32[]{:S(2)}, u32[]{:S(2)}) %collective-permute-start.27) | collective-permute-done | bytes 262176 | tf_op jit(solution)/shard_map/ppermute | solution.py:334
  181.8 3.8 collective-permute-done.51.refs_1_.refs_26_.refs_30_.refs_6_.refs_7_
  186.8 2.8 collective-permute-start.53
  189.5 5.0 %collective-permute-done.32.refs_32_ = f32[512,128]{1,0:T(8,128)S(1)} collective-permute-done((f32[512,128]{1,0:T(8,128)S(1)}, f32[512,128]{1,0:T(8,128)S(1)}, u32[]{:S(2)}, u32[]{:S(2)}) %collective-permute-start.32) | collective-permute-done | bytes 262176 | tf_op jit(solution)/shard_map/ppermute | solution.py:334
  194.5 3.7 collective-permute-done.36.refs_41_.refs_6_
  198.2 3.3 shard_map.61
  205.2 5.6 %collective-permute-done.44.refs_3_ = f32[512,128]{1,0:T(8,128)S(1)} collective-permute-done((f32[512,128]{1,0:T(8,128)S(1)}, f32[512,128]{1,0:T(8,128)S(1)}, u32[]{:S(2)}, u32[]{:S(2)}) %collective-permute-start.44) | collective-permute-done | bytes 262176 | tf_op jit(solution)/shard_map/ppermute | solution.py:334
  212.1 3.4 collective-permute-done.45.refs_4_
  215.5 1.9 shard_map.63
  219.4 2.2 collective-permute-start.67
  224.0 6.0 %collective-permute-done.39.refs_4_.refs_12_ = f32[520,128]{1,0:T(8,128)S(1)} collective-permute-done((f32[520,128]{1,0:T(8,128)S(1)}, f32[520,128]{1,0:T(8,128)S(1)}, u32[]{:S(2)}, u32[]{:S(2)}) %collective-permute-start.39) | collective-permute-done | bytes 266272 | tf_op jit(solution)/shard_map/ppermute | solution.py:334
  230.0 2.2 collective-permute-start.48
  232.2 2.4 shard_map.62
  234.8 2.0 collective-permute-done.47.refs_19_
  237.6 3.1 collective-permute-done.48.refs_20_
  243.0 6.8 %collective-permute-done.41.refs_15_ = f32[512,128]{1,0:T(8,128)S(1)} collective-permute-done((f32[512,128]{1,0:T(8,128)S(1)}, f32[512,128]{1,0:T(8,128)S(1)}, u32[]{:S(2)}, u32[]{:S(2)}) %collective-permute-start.41) | collective-permute-done | bytes 262176 | tf_op jit(solution)/shard_map/ppermute | solution.py:334
  249.8 5.7 %collective-permute-done.42.refs_16_ = f32[512,128]{1,0:T(8,128)S(1)} collective-permute-done((f32[512,128]{1,0:T(8,128)S(1)}, f32[512,128]{1,0:T(8,128)S(1)}, u32[]{:S(2)}, u32[]{:S(2)}) %collective-permute-start.42) | collective-permute-done | bytes 262176 | tf_op jit(solution)/shard_map/ppermute | solution.py:334
  255.4 3.3 shard_map.68
  263.3 4.8 %collective-permute-done.62.refs_3_ = f32[512,128]{1,0:T(8,128)S(1)} collective-permute-done((f32[512,128]{1,0:T(8,128)S(1)}, f32[512,128]{1,0:T(8,128)S(1)}, u32[]{:S(2)}, u32[]{:S(2)}) %collective-permute-start.62) | collective-permute-done | bytes 262176 | tf_op jit(solution)/shard_map/ppermute | solution.py:334
  269.3 3.4 collective-permute-done.63.refs_4_
  274.7 2.0 shard_map.70
  276.7 2.6 collective-permute-done.56.refs_3_.refs_11_
  280.7 3.5 collective-permute-done.57.refs_4_.refs_12_
  284.2 1.9 collective-permute-start.66
  286.8 2.4 shard_map.69
  292.0 3.4 collective-permute-done.66.refs_20_
  297.3 4.6 %collective-permute-done.59.refs_15_ = f32[512,128]{1,0:T(8,128)S(1)} collective-permute-done((f32[512,128]{1,0:T(8,128)S(1)}, f32[512,128]{1,0:T(8,128)S(1)}, u32[]{:S(2)}, u32[]{:S(2)}) %collective-permute-start.59) | collective-permute-done | bytes 262176 | tf_op jit(solution)/shard_map/ppermute | solution.py:334
  301.9 4.7 %collective-permute-done.60.refs_16_ = f32[512,128]{1,0:T(8,128)S(1)} collective-permute-done((f32[512,128]{1,0:T(8,128)S(1)}, f32[512,128]{1,0:T(8,128)S(1)}, u32[]{:S(2)}, u32[]{:S(2)}) %collective-permute-start.60) | collective-permute-done | bytes 262176 | tf_op jit(solution)/shard_map/ppermute | solution.py:334
  306.6 3.3 shard_map.73
  314.0 17.0 %collective-permute-done.75.refs_7_ = f32[512,128]{1,0:T(8,128)S(1)} collective-permute-done((f32[512,128]{1,0:T(8,128)S(1)}, f32[512,128]{1,0:T(8,128)S(1)}, u32[]{:S(2)}, u32[]{:S(2)}) %collective-permute-start.75) | collective-permute-done | bytes 262176 | tf_op jit(solution)/shard_map/ppermute | solution.py:334
  331.0 4.3 %collective-permute-done.76.refs_8_ = f32[512,128]{1,0:T(8,128)S(1)} collective-permute-done((f32[512,128]{1,0:T(8,128)S(1)}, f32[512,128]{1,0:T(8,128)S(1)}, u32[]{:S(2)}, u32[]{:S(2)}) %collective-permute-start.76) | collective-permute-done | bytes 262176 | tf_op jit(solution)/shard_map/ppermute | solution.py:334
  335.4 3.0 shard_map.74
  342.4 2.8 collective-permute-done.89.refs_9_
  362.8 4.1 %collective-permute-done.78.refs_9_ = f32[256,128]{1,0:T(8,128)S(1)} collective-permute-done((f32[256,128]{1,0:T(8,128)S(1)}, f32[256,128]{1,0:T(8,128)S(1)}, u32[]{:S(2)}, u32[]{:S(2)}) %collective-permute-start.78) | collective-permute-done | bytes 131104 | tf_op jit(solution)/shard_map/ppermute | solution.py:334
  369.4 8.3 %collective-permute-done.87 = f32[128,1024]{1,0:T(8,128)} collective-permute-done((f32[128,1024]{1,0:T(8,128)}, f32[128,1024]{1,0:T(8,128)}, u32[]{:S(2)}, u32[]{:S(2)}) %collective-permute-start.87) | collective-permute-done | bytes 524320 | tf_op jit(solution)/shard_map/ppermute | solution.py:334
  377.7 21.3 %collective-permute-done.83 = f32[128,1024]{1,0:T(8,128)} collective-permute-done((f32[128,1024]{1,0:T(8,128)}, f32[128,1024]{1,0:T(8,128)}, u32[]{:S(2)}, u32[]{:S(2)}) %collective-permute-start.83) | collective-permute-done | bytes 524320 | tf_op jit(solution)/shard_map/ppermute | solution.py:334
  401.0 2.5 collective-permute-done.92
  (171 shorter events, 99.3 us)
Async XLA Ops:
  7.6 40.1 %collective-permute-start.3 = (f32[136,1024]{1,0:T(8,128)S(1)}, f32[136,1024]{1,0:T(8,128)S(1)}, u32[]{:S(2)}, u32[]{:S(2)}) collective-permute-start(f32[136,1024]{1,0:T(8,128)S(1)} %get-tuple-element.154), channel_id=1, source_target_pairs={{0,4},{1,5},{2,0},{3,1},{4,6},{5,7},{6,2},{7,3},{8,12},{9,13},{10,... | collective-permute-start | bytes 1671176 | tf_op jit(solution)/shard_map/ppermute | solution.py:334
  11.5 36.2 %collective-permute-start.7 = (f32[136,1024]{1,0:T(8,128)S(1)}, f32[136,1024]{1,0:T(8,128)S(1)}, u32[]{:S(2)}, u32[]{:S(2)}) collective-permute-start(f32[136,1024]{1,0:T(8,128)S(1)} %get-tuple-element.158), channel_id=1, source_target_pairs={{0,2},{1,3},{2,6},{3,7},{4,0},{5,1},{6,4},{7,5},{8,10},{9,11},{10,... | collective-permute-start | bytes 1671176 | tf_op jit(solution)/shard_map/ppermute | solution.py:334
  12.7 35.1 %collective-permute-start.4 = (f32[8,128,128]{2,1,0:T(8,128)S(1)}, f32[8,128,128]{2,1,0:T(8,128)S(1)}, u32[]{:S(2)}, u32[]{:S(2)}) collective-permute-start(f32[8,128,128]{2,1,0:T(8,128)S(1)} %get-tuple-element.152.refs_2_), channel_id=1, source_target_pairs={{0,4},{1,5},{2,0},{3,1},{4,6},{5,7},{6,2},{7,3},{8,12},{9,13},{10,... | collective-permute-start | bytes 1572872 | tf_op jit(solution)/shard_map/ppermute | solution.py:354
  15.6 45.9 %collective-permute-start.6 = (f32[136,1024]{1,0:T(8,128)S(1)}, f32[136,1024]{1,0:T(8,128)S(1)}, u32[]{:S(2)}, u32[]{:S(2)}) collective-permute-start(f32[136,1024]{1,0:T(8,128)S(1)} %get-tuple-element.157), channel_id=1, source_target_pairs={{0,6},{1,7},{2,4},{3,5},{4,2},{5,3},{6,0},{7,1},{8,14},{9,15},{10,... | collective-permute-start | bytes 1671176 | tf_op jit(solution)/shard_map/ppermute | solution.py:334
  18.7 33.6 %collective-permute-start.22 = (f32[8,128,128]{2,1,0:T(8,128)S(1)}, f32[8,128,128]{2,1,0:T(8,128)S(1)}, u32[]{:S(2)}, u32[]{:S(2)}) collective-permute-start(f32[8,128,128]{2,1,0:T(8,128)S(1)} %get-tuple-element.185), channel_id=1, source_target_pairs={{0,8},{1,9},{2,10},{3,11},{4,12},{5,13},{6,14},{7,15},{8,0},{9,1},... | collective-permute-start | bytes 1572872 | tf_op jit(solution)/shard_map/ppermute | solution.py:334
  48.8 17.7 %collective-permute-start.8 = (f32[4,128,128]{2,1,0:T(8,128)S(1)}, f32[4,128,128]{2,1,0:T(8,128)S(1)}, u32[]{:S(2)}, u32[]{:S(2)}) collective-permute-start(f32[4,128,128]{2,1,0:T(8,128)S(1)} %get-tuple-element.159), channel_id=1, source_target_pairs={{0,4},{1,5},{2,0},{3,1},{4,6},{5,7},{6,2},{7,3},{8,12},{9,13},{10,... | collective-permute-start | bytes 786440 | tf_op jit(solution)/shard_map/ppermute | solution.py:354
  67.7 24.8 %collective-permute-start.23 = (f32[8,128,128]{2,1,0:T(8,128)S(1)}, f32[8,128,128]{2,1,0:T(8,128)S(1)}, u32[]{:S(2)}, u32[]{:S(2)}) collective-permute-start(f32[8,128,128]{2,1,0:T(8,128)S(1)} %get-tuple-element.186.refs_17_), channel_id=1, source_target_pairs={{0,4},{1,5},{2,0},{3,1},{4,6},{5,7},{6,2},{7,3},{8,12},{9,13},{10,... | collective-permute-start | bytes 1572872 | tf_op jit(solution)/shard_map/ppermute | solution.py:354
  81.1 17.7 %collective-permute-start.5 = (f32[8,128,128]{2,1,0:T(8,128)S(1)}, f32[8,128,128]{2,1,0:T(8,128)S(1)}, u32[]{:S(2)}, u32[]{:S(2)}) collective-permute-start(f32[8,128,128]{2,1,0:T(8,128)S(1)} %collective-permute-done.4.refs_2_.refs_1_), channel_id=1, source_target_pairs={{0,16},{16,0},{1,17},{17,1},{2,18},{18,2},{3,19},{19,3},{4,20},{20... | collective-permute-start | bytes 1572872 | tf_op jit(solution)/shard_map/ppermute | solution.py:362
  81.1 22.5 %collective-permute-start.9 = (f32[4,128,128]{2,1,0:T(8,128)S(1)}, f32[4,128,128]{2,1,0:T(8,128)S(1)}, u32[]{:S(2)}, u32[]{:S(2)}) collective-permute-start(f32[4,128,128]{2,1,0:T(8,128)S(1)} %collective-permute-done.8.refs_2_.refs_4_), channel_id=1, source_target_pairs={{0,16},{16,0},{1,17},{17,1},{2,18},{18,2},{3,19},{19,3},{4,20},{20... | collective-permute-start | bytes 786440 | tf_op jit(solution)/shard_map/ppermute | solution.py:362
  93.6 12.5 %collective-permute-start.28 = (f32[4,128,128]{2,1,0:T(8,128)S(1)}, f32[4,128,128]{2,1,0:T(8,128)S(1)}, u32[]{:S(2)}, u32[]{:S(2)}) collective-permute-start(f32[4,128,128]{2,1,0:T(8,128)S(1)} %get-tuple-element.195), channel_id=1, source_target_pairs={{0,4},{1,5},{2,0},{3,1},{4,6},{5,7},{6,2},{7,3},{8,12},{9,13},{10,... | collective-permute-start | bytes 786440 | tf_op jit(solution)/shard_map/ppermute | solution.py:354
  107.9 35.2 %collective-permute-start.33 = (f32[16,128,128]{2,1,0:T(8,128)S(1)}, f32[16,128,128]{2,1,0:T(8,128)S(1)}, u32[]{:S(2)}, u32[]{:S(2)}) collective-permute-start(f32[16,128,128]{2,1,0:T(8,128)S(1)} %get-tuple-element.205.refs_37_.refs_5_), channel_id=1, source_target_pairs={{0,4},{1,5},{2,0},{3,1},{4,6},{5,7},{6,2},{7,3},{8,12},{9,13},{10,... | collective-permute-start | bytes 3145736 | tf_op jit(solution)/shard_map/ppermute | solution.py:354
  109.9 8.7 %collective-permute-start.13 = (f32[264,128]{1,0:T(8,128)S(1)}, f32[264,128]{1,0:T(8,128)S(1)}, u32[]{:S(2)}, u32[]{:S(2)}) collective-permute-start(f32[264,128]{1,0:T(8,128)S(1)} %get-tuple-element.173), channel_id=1, source_target_pairs={{0,8},{1,9},{2,10},{3,11},{4,12},{5,13},{6,14},{7,15},{8,0},{9,1},... | collective-permute-start | bytes 405512 | tf_op jit(solution)/shard_map/ppermute | solution.py:334
  110.2 9.6 %collective-permute-start.14 = (f32[264,128]{1,0:T(8,128)S(1)}, f32[264,128]{1,0:T(8,128)S(1)}, u32[]{:S(2)}, u32[]{:S(2)}) collective-permute-start(f32[264,128]{1,0:T(8,128)S(1)} %get-tuple-element.174), channel_id=1, source_target_pairs={{0,1},{1,0},{2,3},{3,2},{4,5},{5,4},{6,7},{7,6},{8,9},{9,8},{10,11... | collective-permute-start | bytes 405512 | tf_op jit(solution)/shard_map/ppermute | solution.py:334
  114.5 22.5 %collective-permute-start.24 = (f32[8,128,128]{2,1,0:T(8,128)S(1)}, f32[8,128,128]{2,1,0:T(8,128)S(1)}, u32[]{:S(2)}, u32[]{:S(2)}) collective-permute-start(f32[8,128,128]{2,1,0:T(8,128)S(1)} %collective-permute-done.23.refs_18_.refs_1_.refs_19_), channel_id=1, source_target_pairs={{0,16},{16,0},{1,17},{17,1},{2,18},{18,2},{3,19},{19,3},{4,20},{20... | collective-permute-start | bytes 1572872 | tf_op jit(solution)/shard_map/ppermute | solution.py:362
  126.0 11.0 %collective-permute-start.29 = (f32[4,128,128]{2,1,0:T(8,128)S(1)}, f32[4,128,128]{2,1,0:T(8,128)S(1)}, u32[]{:S(2)}, u32[]{:S(2)}) collective-permute-start(f32[4,128,128]{2,1,0:T(8,128)S(1)} %collective-permute-done.28.refs_17_.refs_5_), channel_id=1, source_target_pairs={{0,16},{16,0},{1,17},{17,1},{2,18},{18,2},{3,19},{19,3},{4,20},{20... | collective-permute-start | bytes 786440 | tf_op jit(solution)/shard_map/ppermute | solution.py:362
  144.2 14.3 %collective-permute-start.35 = (f32[8,128,128]{2,1,0:T(8,128)S(1)}, f32[8,128,128]{2,1,0:T(8,128)S(1)}, u32[]{:S(2)}, u32[]{:S(2)}) collective-permute-start(f32[8,128,128]{2,1,0:T(8,128)S(1)} %get-tuple-element.206), channel_id=1, source_target_pairs={{0,4},{1,5},{2,0},{3,1},{4,6},{5,7},{6,2},{7,3},{8,12},{9,13},{10,... | collective-permute-start | bytes 1572872 | tf_op jit(solution)/shard_map/ppermute | solution.py:354
  160.3 25.3 %collective-permute-start.51 = (f32[16,128,128]{2,1,0:T(8,128)S(1)}, f32[16,128,128]{2,1,0:T(8,128)S(1)}, u32[]{:S(2)}, u32[]{:S(2)}) collective-permute-start(f32[16,128,128]{2,1,0:T(8,128)S(1)} %get-tuple-element.234.refs_25_.refs_5_), channel_id=1, source_target_pairs={{0,4},{1,5},{2,0},{3,1},{4,6},{5,7},{6,2},{7,3},{8,12},{9,13},{10,... | collective-permute-start | bytes 3145736 | tf_op jit(solution)/shard_map/ppermute | solution.py:354
  162.9 35.3 %collective-permute-start.34 = (f32[16,128,128]{2,1,0:T(8,128)S(1)}, f32[16,128,128]{2,1,0:T(8,128)S(1)}, u32[]{:S(2)}, u32[]{:S(2)}) collective-permute-start(f32[16,128,128]{2,1,0:T(8,128)S(1)} %collective-permute-done.33.refs_1_.refs_38_.refs_42_.refs_6_.refs_7_), channel_id=1, source_target_pairs={{0,16},{16,0},{1,17},{17,1},{2,18},{18,2},{3,19},{19,3},{4,20},{20... | collective-permute-start | bytes 3145736 | tf_op jit(solution)/shard_map/ppermute | solution.py:362
  166.5 9.2 %collective-permute-start.26 = (f32[512,128]{1,0:T(8,128)S(1)}, f32[512,128]{1,0:T(8,128)S(1)}, u32[]{:S(2)}, u32[]{:S(2)}) collective-permute-start(f32[512,128]{1,0:T(8,128)S(1)} %get-tuple-element.193), channel_id=1, source_target_pairs={{0,1},{1,0},{2,3},{3,2},{4,5},{5,4},{6,7},{7,6},{8,9},{9,8},{10,11... | collective-permute-start | bytes 786440 | tf_op jit(solution)/shard_map/ppermute | solution.py:334
  168.0 12.5 %collective-permute-start.27 = (f32[512,128]{1,0:T(8,128)S(1)}, f32[512,128]{1,0:T(8,128)S(1)}, u32[]{:S(2)}, u32[]{:S(2)}) collective-permute-start(f32[512,128]{1,0:T(8,128)S(1)} %get-tuple-element.194), channel_id=1, source_target_pairs={{0,9},{1,8},{2,11},{3,10},{4,13},{5,12},{6,15},{7,14},{8,1},{9,0},... | collective-permute-start | bytes 786440 | tf_op jit(solution)/shard_map/ppermute | solution.py:334
  168.4 29.8 %collective-permute-start.36 = (f32[8,128,128]{2,1,0:T(8,128)S(1)}, f32[8,128,128]{2,1,0:T(8,128)S(1)}, u32[]{:S(2)}, u32[]{:S(2)}) collective-permute-start(f32[8,128,128]{2,1,0:T(8,128)S(1)} %collective-permute-done.35.refs_40_.refs_5_), channel_id=1, source_target_pairs={{0,16},{16,0},{1,17},{17,1},{2,18},{18,2},{3,19},{19,3},{4,20},{20... | collective-permute-start | bytes 1572872 | tf_op jit(solution)/shard_map/ppermute | solution.py:362
  175.7 11.1 %collective-permute-start.30 = (f32[512,128]{1,0:T(8,128)S(1)}, f32[512,128]{1,0:T(8,128)S(1)}, u32[]{:S(2)}, u32[]{:S(2)}) collective-permute-start(f32[512,128]{1,0:T(8,128)S(1)} %get-tuple-element.197), channel_id=1, source_target_pairs={{0,8},{1,9},{2,10},{3,11},{4,12},{5,13},{6,14},{7,15},{8,0},{9,1},... | collective-permute-start | bytes 786440 | tf_op jit(solution)/shard_map/ppermute | solution.py:334
  180.4 9.1 %collective-permute-start.31 = (f32[512,128]{1,0:T(8,128)S(1)}, f32[512,128]{1,0:T(8,128)S(1)}, u32[]{:S(2)}, u32[]{:S(2)}) collective-permute-start(f32[512,128]{1,0:T(8,128)S(1)} %get-tuple-element.198), channel_id=1, source_target_pairs={{0,1},{1,0},{2,3},{3,2},{4,5},{5,4},{6,7},{7,6},{8,9},{9,8},{10,11... | collective-permute-start | bytes 786440 | tf_op jit(solution)/shard_map/ppermute | solution.py:334
  185.6 8.9 %collective-permute-start.32 = (f32[512,128]{1,0:T(8,128)S(1)}, f32[512,128]{1,0:T(8,128)S(1)}, u32[]{:S(2)}, u32[]{:S(2)}) collective-permute-start(f32[512,128]{1,0:T(8,128)S(1)} %get-tuple-element.199), channel_id=1, source_target_pairs={{0,9},{1,8},{2,11},{3,10},{4,13},{5,12},{6,15},{7,14},{8,1},{9,0},... | collective-permute-start | bytes 786440 | tf_op jit(solution)/shard_map/ppermute | solution.py:334
  186.8 30.7 %collective-permute-start.53 = (f32[8,128,128]{2,1,0:T(8,128)S(1)}, f32[8,128,128]{2,1,0:T(8,128)S(1)}, u32[]{:S(2)}, u32[]{:S(2)}) collective-permute-start(f32[8,128,128]{2,1,0:T(8,128)S(1)} %get-tuple-element.235), channel_id=1, source_target_pairs={{0,4},{1,5},{2,0},{3,1},{4,6},{5,7},{6,2},{7,3},{8,12},{9,13},{10,... | collective-permute-start | bytes 1572872 | tf_op jit(solution)/shard_map/ppermute | solution.py:354
  201.6 9.2 %collective-permute-start.44 = (f32[512,128]{1,0:T(8,128)S(1)}, f32[512,128]{1,0:T(8,128)S(1)}, u32[]{:S(2)}, u32[]{:S(2)}) collective-permute-start(f32[512,128]{1,0:T(8,128)S(1)} %get-tuple-element.221), channel_id=1, source_target_pairs={{0,1},{1,0},{2,3},{3,2},{4,5},{5,4},{6,7},{7,6},{8,9},{9,8},{10,11... | collective-permute-start | bytes 786440 | tf_op jit(solution)/shard_map/ppermute | solution.py:334
  203.0 12.5 %collective-permute-start.45 = (f32[512,128]{1,0:T(8,128)S(1)}, f32[512,128]{1,0:T(8,128)S(1)}, u32[]{:S(2)}, u32[]{:S(2)}) collective-permute-start(f32[512,128]{1,0:T(8,128)S(1)} %get-tuple-element.222), channel_id=1, source_target_pairs={{0,9},{1,8},{2,11},{3,10},{4,13},{5,12},{6,15},{7,14},{8,1},{9,0},... | collective-permute-start | bytes 786440 | tf_op jit(solution)/shard_map/ppermute | solution.py:334
  203.5 19.8 %collective-permute-start.37 = (f32[520,128]{1,0:T(8,128)S(1)}, f32[520,128]{1,0:T(8,128)S(1)}, u32[]{:S(2)}, u32[]{:S(2)}) collective-permute-start(f32[520,128]{1,0:T(8,128)S(1)} %get-tuple-element.212), channel_id=1, source_target_pairs={{0,8},{1,9},{2,10},{3,11},{4,12},{5,13},{6,14},{7,15},{8,0},{9,1},... | collective-permute-start | bytes 798728 | tf_op jit(solution)/shard_map/ppermute | solution.py:334
  203.8 19.4 %collective-permute-start.38 = (f32[520,128]{1,0:T(8,128)S(1)}, f32[520,128]{1,0:T(8,128)S(1)}, u32[]{:S(2)}, u32[]{:S(2)}) collective-permute-start(f32[520,128]{1,0:T(8,128)S(1)} %get-tuple-element.213), channel_id=1, source_target_pairs={{0,1},{1,0},{2,3},{3,2},{4,5},{5,4},{6,7},{7,6},{8,9},{9,8},{10,11... | collective-permute-start | bytes 798728 | tf_op jit(solution)/shard_map/ppermute | solution.py:334
  210.8 44.6 %collective-permute-start.52 = (f32[16,128,128]{2,1,0:T(8,128)S(1)}, f32[16,128,128]{2,1,0:T(8,128)S(1)}, u32[]{:S(2)}, u32[]{:S(2)}) collective-permute-start(f32[16,128,128]{2,1,0:T(8,128)S(1)} %collective-permute-done.51.refs_1_.refs_26_.refs_30_.refs_6_.refs_7_), channel_id=1, source_target_pairs={{0,16},{16,0},{1,17},{17,1},{2,18},{18,2},{3,19},{19,3},{4,20},{20... | collective-permute-start | bytes 3145736 | tf_op jit(solution)/shard_map/ppermute | solution.py:362
  219.4 41.4 %collective-permute-start.67 = (f32[16,128,128]{2,1,0:T(8,128)S(1)}, f32[16,128,128]{2,1,0:T(8,128)S(1)}, u32[]{:S(2)}, u32[]{:S(2)}) collective-permute-start(f32[16,128,128]{2,1,0:T(8,128)S(1)} %get-tuple-element.261.refs_25_.refs_9_), channel_id=1, source_target_pairs={{0,4},{1,5},{2,0},{3,1},{4,6},{5,7},{6,2},{7,3},{8,12},{9,13},{10,... | collective-permute-start | bytes 3145736 | tf_op jit(solution)/shard_map/ppermute | solution.py:354
  221.6 8.4 %collective-permute-start.39 = (f32[520,128]{1,0:T(8,128)S(1)}, f32[520,128]{1,0:T(8,128)S(1)}, u32[]{:S(2)}, u32[]{:S(2)}) collective-permute-start(f32[520,128]{1,0:T(8,128)S(1)} %get-tuple-element.214), channel_id=1, source_target_pairs={{0,9},{1,8},{2,11},{3,10},{4,13},{5,12},{6,15},{7,14},{8,1},{9,0},... | collective-permute-start | bytes 798728 | tf_op jit(solution)/shard_map/ppermute | solution.py:334
  223.3 11.4 %collective-permute-start.46 = (f32[512,128]{1,0:T(8,128)S(1)}, f32[512,128]{1,0:T(8,128)S(1)}, u32[]{:S(2)}, u32[]{:S(2)}) collective-permute-start(f32[512,128]{1,0:T(8,128)S(1)} %get-tuple-element.224), channel_id=1, source_target_pairs={{0,8},{1,9},{2,10},{3,11},{4,12},{5,13},{6,14},{7,15},{8,0},{9,1},... | collective-permute-start | bytes 786440 | tf_op jit(solution)/shard_map/ppermute | solution.py:334
  223.3 13.5 %collective-permute-start.47 = (f32[512,128]{1,0:T(8,128)S(1)}, f32[512,128]{1,0:T(8,128)S(1)}, u32[]{:S(2)}, u32[]{:S(2)}) collective-permute-start(f32[512,128]{1,0:T(8,128)S(1)} %get-tuple-element.225), channel_id=1, source_target_pairs={{0,1},{1,0},{2,3},{3,2},{4,5},{5,4},{6,7},{7,6},{8,9},{9,8},{10,11... | collective-permute-start | bytes 786440 | tf_op jit(solution)/shard_map/ppermute | solution.py:334
  230.0 10.6 %collective-permute-start.48 = (f32[512,128]{1,0:T(8,128)S(1)}, f32[512,128]{1,0:T(8,128)S(1)}, u32[]{:S(2)}, u32[]{:S(2)}) collective-permute-start(f32[512,128]{1,0:T(8,128)S(1)} %get-tuple-element.226), channel_id=1, source_target_pairs={{0,9},{1,8},{2,11},{3,10},{4,13},{5,12},{6,15},{7,14},{8,1},{9,0},... | collective-permute-start | bytes 786440 | tf_op jit(solution)/shard_map/ppermute | solution.py:334
  236.8 18.6 %collective-permute-start.54 = (f32[8,128,128]{2,1,0:T(8,128)S(1)}, f32[8,128,128]{2,1,0:T(8,128)S(1)}, u32[]{:S(2)}, u32[]{:S(2)}) collective-permute-start(f32[8,128,128]{2,1,0:T(8,128)S(1)} %collective-permute-done.53.refs_28_.refs_5_), channel_id=1, source_target_pairs={{0,16},{16,0},{1,17},{17,1},{2,18},{18,2},{3,19},{19,3},{4,20},{20... | collective-permute-start | bytes 1572872 | tf_op jit(solution)/shard_map/ppermute | solution.py:362
  240.6 9.1 %collective-permute-start.41 = (f32[512,128]{1,0:T(8,128)S(1)}, f32[512,128]{1,0:T(8,128)S(1)}, u32[]{:S(2)}, u32[]{:S(2)}) collective-permute-start(f32[512,128]{1,0:T(8,128)S(1)} %get-tuple-element.217), channel_id=1, source_target_pairs={{0,1},{1,0},{2,3},{3,2},{4,5},{5,4},{6,7},{7,6},{8,9},{9,8},{10,11... | collective-permute-start | bytes 786440 | tf_op jit(solution)/shard_map/ppermute | solution.py:334
  241.9 13.5 %collective-permute-start.42 = (f32[512,128]{1,0:T(8,128)S(1)}, f32[512,128]{1,0:T(8,128)S(1)}, u32[]{:S(2)}, u32[]{:S(2)}) collective-permute-start(f32[512,128]{1,0:T(8,128)S(1)} %get-tuple-element.218), channel_id=1, source_target_pairs={{0,9},{1,8},{2,11},{3,10},{4,13},{5,12},{6,15},{7,14},{8,1},{9,0},... | collective-permute-start | bytes 786440 | tf_op jit(solution)/shard_map/ppermute | solution.py:334
  258.9 9.1 %collective-permute-start.62 = (f32[512,128]{1,0:T(8,128)S(1)}, f32[512,128]{1,0:T(8,128)S(1)}, u32[]{:S(2)}, u32[]{:S(2)}) collective-permute-start(f32[512,128]{1,0:T(8,128)S(1)} %get-tuple-element.250), channel_id=1, source_target_pairs={{0,1},{1,0},{2,3},{3,2},{4,5},{5,4},{6,7},{7,6},{8,9},{9,8},{10,11... | collective-permute-start | bytes 786440 | tf_op jit(solution)/shard_map/ppermute | solution.py:334
  260.2 12.5 %collective-permute-start.63 = (f32[512,128]{1,0:T(8,128)S(1)}, f32[512,128]{1,0:T(8,128)S(1)}, u32[]{:S(2)}, u32[]{:S(2)}) collective-permute-start(f32[512,128]{1,0:T(8,128)S(1)} %get-tuple-element.251), channel_id=1, source_target_pairs={{0,9},{1,8},{2,11},{3,10},{4,13},{5,12},{6,15},{7,14},{8,1},{9,0},... | collective-permute-start | bytes 786440 | tf_op jit(solution)/shard_map/ppermute | solution.py:334
  261.9 24.2 %collective-permute-start.69 = (f32[8,128,128]{2,1,0:T(8,128)S(1)}, f32[8,128,128]{2,1,0:T(8,128)S(1)}, u32[]{:S(2)}, u32[]{:S(2)}) collective-permute-start(f32[8,128,128]{2,1,0:T(8,128)S(1)} %get-tuple-element.262), channel_id=1, source_target_pairs={{0,4},{1,5},{2,0},{3,1},{4,6},{5,7},{6,2},{7,3},{8,12},{9,13},{10,... | collective-permute-start | bytes 1572872 | tf_op jit(solution)/shard_map/ppermute | solution.py:354
  263.0 43.6 %collective-permute-start.68 = (f32[16,128,128]{2,1,0:T(8,128)S(1)}, f32[16,128,128]{2,1,0:T(8,128)S(1)}, u32[]{:S(2)}, u32[]{:S(2)}) collective-permute-start(f32[16,128,128]{2,1,0:T(8,128)S(1)} %collective-permute-done.67.refs_1_.refs_26_.refs_30_.refs_10_.refs_14_), channel_id=1, source_target_pairs={{0,16},{16,0},{1,17},{17,1},{2,18},{18,2},{3,19},{19,3},{4,20},{20... | collective-permute-start | bytes 3145736 | tf_op jit(solution)/shard_map/ppermute | solution.py:362
  263.3 13.4 %collective-permute-start.55 = (f32[520,128]{1,0:T(8,128)S(1)}, f32[520,128]{1,0:T(8,128)S(1)}, u32[]{:S(2)}, u32[]{:S(2)}) collective-permute-start(f32[520,128]{1,0:T(8,128)S(1)} %get-tuple-element.241), channel_id=1, source_target_pairs={{0,8},{1,9},{2,10},{3,11},{4,12},{5,13},{6,14},{7,15},{8,0},{9,1},... | collective-permute-start | bytes 798728 | tf_op jit(solution)/shard_map/ppermute | solution.py:334
  268.0 11.3 %collective-permute-start.56 = (f32[520,128]{1,0:T(8,128)S(1)}, f32[520,128]{1,0:T(8,128)S(1)}, u32[]{:S(2)}, u32[]{:S(2)}) collective-permute-start(f32[520,128]{1,0:T(8,128)S(1)} %get-tuple-element.242), channel_id=1, source_target_pairs={{0,1},{1,0},{2,3},{3,2},{4,5},{5,4},{6,7},{7,6},{8,9},{9,8},{10,11... | collective-permute-start | bytes 798728 | tf_op jit(solution)/shard_map/ppermute | solution.py:334
  272.7 11.4 %collective-permute-start.57 = (f32[520,128]{1,0:T(8,128)S(1)}, f32[520,128]{1,0:T(8,128)S(1)}, u32[]{:S(2)}, u32[]{:S(2)}) collective-permute-start(f32[520,128]{1,0:T(8,128)S(1)} %get-tuple-element.243), channel_id=1, source_target_pairs={{0,9},{1,8},{2,11},{3,10},{4,13},{5,12},{6,15},{7,14},{8,1},{9,0},... | collective-permute-start | bytes 798728 | tf_op jit(solution)/shard_map/ppermute | solution.py:334
  276.7 12.6 %collective-permute-start.64 = (f32[512,128]{1,0:T(8,128)S(1)}, f32[512,128]{1,0:T(8,128)S(1)}, u32[]{:S(2)}, u32[]{:S(2)}) collective-permute-start(f32[512,128]{1,0:T(8,128)S(1)} %get-tuple-element.253), channel_id=1, source_target_pairs={{0,8},{1,9},{2,10},{3,11},{4,12},{5,13},{6,14},{7,15},{8,0},{9,1},... | collective-permute-start | bytes 786440 | tf_op jit(solution)/shard_map/ppermute | solution.py:334
  279.4 11.3 %collective-permute-start.65 = (f32[512,128]{1,0:T(8,128)S(1)}, f32[512,128]{1,0:T(8,128)S(1)}, u32[]{:S(2)}, u32[]{:S(2)}) collective-permute-start(f32[512,128]{1,0:T(8,128)S(1)} %get-tuple-element.254), channel_id=1, source_target_pairs={{0,1},{1,0},{2,3},{3,2},{4,5},{5,4},{6,7},{7,6},{8,9},{9,8},{10,11... | collective-permute-start | bytes 786440 | tf_op jit(solution)/shard_map/ppermute | solution.py:334
  284.2 11.2 %collective-permute-start.66 = (f32[512,128]{1,0:T(8,128)S(1)}, f32[512,128]{1,0:T(8,128)S(1)}, u32[]{:S(2)}, u32[]{:S(2)}) collective-permute-start(f32[512,128]{1,0:T(8,128)S(1)} %get-tuple-element.255), channel_id=1, source_target_pairs={{0,9},{1,8},{2,11},{3,10},{4,13},{5,12},{6,15},{7,14},{8,1},{9,0},... | collective-permute-start | bytes 786440 | tf_op jit(solution)/shard_map/ppermute | solution.py:334
  286.1 20.5 %collective-permute-start.70 = (f32[8,128,128]{2,1,0:T(8,128)S(1)}, f32[8,128,128]{2,1,0:T(8,128)S(1)}, u32[]{:S(2)}, u32[]{:S(2)}) collective-permute-start(f32[8,128,128]{2,1,0:T(8,128)S(1)} %collective-permute-done.69.refs_28_.refs_12_), channel_id=1, source_target_pairs={{0,16},{16,0},{1,17},{17,1},{2,18},{18,2},{3,19},{19,3},{4,20},{20... | collective-permute-start | bytes 1572872 | tf_op jit(solution)/shard_map/ppermute | solution.py:362
  290.7 11.2 %collective-permute-start.59 = (f32[512,128]{1,0:T(8,128)S(1)}, f32[512,128]{1,0:T(8,128)S(1)}, u32[]{:S(2)}, u32[]{:S(2)}) collective-permute-start(f32[512,128]{1,0:T(8,128)S(1)} %get-tuple-element.246), channel_id=1, source_target_pairs={{0,1},{1,0},{2,3},{3,2},{4,5},{5,4},{6,7},{7,6},{8,9},{9,8},{10,11... | collective-permute-start | bytes 786440 | tf_op jit(solution)/shard_map/ppermute | solution.py:334
  295.4 11.2 %collective-permute-start.60 = (f32[512,128]{1,0:T(8,128)S(1)}, f32[512,128]{1,0:T(8,128)S(1)}, u32[]{:S(2)}, u32[]{:S(2)}) collective-permute-start(f32[512,128]{1,0:T(8,128)S(1)} %get-tuple-element.247), channel_id=1, source_target_pairs={{0,9},{1,8},{2,11},{3,10},{4,13},{5,12},{6,15},{7,14},{8,1},{9,0},... | collective-permute-start | bytes 786440 | tf_op jit(solution)/shard_map/ppermute | solution.py:334
  310.3 25.1 %collective-permute-start.71 = (f32[520,128]{1,0:T(8,128)S(1)}, f32[520,128]{1,0:T(8,128)S(1)}, u32[]{:S(2)}, u32[]{:S(2)}) collective-permute-start(f32[520,128]{1,0:T(8,128)S(1)} %get-tuple-element.265), channel_id=1, source_target_pairs={{0,8},{1,9},{2,10},{3,11},{4,12},{5,13},{6,14},{7,15},{8,0},{9,1},... | collective-permute-start | bytes 798728 | tf_op jit(solution)/shard_map/ppermute | solution.py:334
  310.5 24.9 %collective-permute-start.72 = (f32[520,128]{1,0:T(8,128)S(1)}, f32[520,128]{1,0:T(8,128)S(1)}, u32[]{:S(2)}, u32[]{:S(2)}) collective-permute-start(f32[520,128]{1,0:T(8,128)S(1)} %get-tuple-element.266), channel_id=1, source_target_pairs={{0,1},{1,0},{2,3},{3,2},{4,5},{5,4},{6,7},{7,6},{8,9},{9,8},{10,11... | collective-permute-start | bytes 798728 | tf_op jit(solution)/shard_map/ppermute | solution.py:334
  311.8 23.5 %collective-permute-start.73 = (f32[520,128]{1,0:T(8,128)S(1)}, f32[520,128]{1,0:T(8,128)S(1)}, u32[]{:S(2)}, u32[]{:S(2)}) collective-permute-start(f32[520,128]{1,0:T(8,128)S(1)} %get-tuple-element.267), channel_id=1, source_target_pairs={{0,9},{1,8},{2,11},{3,10},{4,13},{5,12},{6,15},{7,14},{8,1},{9,0},... | collective-permute-start | bytes 798728 | tf_op jit(solution)/shard_map/ppermute | solution.py:334
  312.1 18.9 %collective-permute-start.75 = (f32[512,128]{1,0:T(8,128)S(1)}, f32[512,128]{1,0:T(8,128)S(1)}, u32[]{:S(2)}, u32[]{:S(2)}) collective-permute-start(f32[512,128]{1,0:T(8,128)S(1)} %get-tuple-element.270), channel_id=1, source_target_pairs={{0,1},{1,0},{2,3},{3,2},{4,5},{5,4},{6,7},{7,6},{8,9},{9,8},{10,11... | collective-permute-start | bytes 786440 | tf_op jit(solution)/shard_map/ppermute | solution.py:334
  313.4 21.9 %collective-permute-start.76 = (f32[512,128]{1,0:T(8,128)S(1)}, f32[512,128]{1,0:T(8,128)S(1)}, u32[]{:S(2)}, u32[]{:S(2)}) collective-permute-start(f32[512,128]{1,0:T(8,128)S(1)} %get-tuple-element.271), channel_id=1, source_target_pairs={{0,9},{1,8},{2,11},{3,10},{4,13},{5,12},{6,15},{7,14},{8,1},{9,0},... | collective-permute-start | bytes 786440 | tf_op jit(solution)/shard_map/ppermute | solution.py:334
  341.0 10.0 %collective-permute-start.85 = (f32[256,128]{1,0:T(8,128)S(1)}, f32[256,128]{1,0:T(8,128)S(1)}, u32[]{:S(2)}, u32[]{:S(2)}) collective-permute-start(f32[256,128]{1,0:T(8,128)S(1)} %get-tuple-element.286), channel_id=1, source_target_pairs={{0,1},{1,0},{2,3},{3,2},{4,5},{5,4},{6,7},{7,6},{8,9},{9,8},{10,11... | collective-permute-start | bytes 393224 | tf_op jit(solution)/shard_map/ppermute | solution.py:334
  342.4 10.2 %collective-permute-start.86 = (f32[256,128]{1,0:T(8,128)S(1)}, f32[256,128]{1,0:T(8,128)S(1)}, u32[]{:S(2)}, u32[]{:S(2)}) collective-permute-start(f32[256,128]{1,0:T(8,128)S(1)} %get-tuple-element.287), channel_id=1, source_target_pairs={{0,9},{1,8},{2,11},{3,10},{4,13},{5,12},{6,15},{7,14},{8,1},{9,0},... | collective-permute-start | bytes 393224 | tf_op jit(solution)/shard_map/ppermute | solution.py:334
  345.3 10.5 %collective-permute-start.80 = (f32[256,128]{1,0:T(8,128)S(1)}, f32[256,128]{1,0:T(8,128)S(1)}, u32[]{:S(2)}, u32[]{:S(2)}) collective-permute-start(f32[256,128]{1,0:T(8,128)S(1)} %get-tuple-element.279), channel_id=1, source_target_pairs={{0,8},{1,9},{2,10},{3,11},{4,12},{5,13},{6,14},{7,15},{8,0},{9,1},... | collective-permute-start | bytes 393224 | tf_op jit(solution)/shard_map/ppermute | solution.py:334
  346.9 9.6 %collective-permute-start.81 = (f32[256,128]{1,0:T(8,128)S(1)}, f32[256,128]{1,0:T(8,128)S(1)}, u32[]{:S(2)}, u32[]{:S(2)}) collective-permute-start(f32[256,128]{1,0:T(8,128)S(1)} %get-tuple-element.280), channel_id=1, source_target_pairs={{0,1},{1,0},{2,3},{3,2},{4,5},{5,4},{6,7},{7,6},{8,9},{9,8},{10,11... | collective-permute-start | bytes 393224 | tf_op jit(solution)/shard_map/ppermute | solution.py:334
  347.6 9.9 %collective-permute-start.82 = (f32[256,128]{1,0:T(8,128)S(1)}, f32[256,128]{1,0:T(8,128)S(1)}, u32[]{:S(2)}, u32[]{:S(2)}) collective-permute-start(f32[256,128]{1,0:T(8,128)S(1)} %get-tuple-element.281), channel_id=1, source_target_pairs={{0,9},{1,8},{2,11},{3,10},{4,13},{5,12},{6,15},{7,14},{8,1},{9,0},... | collective-permute-start | bytes 393224 | tf_op jit(solution)/shard_map/ppermute | solution.py:334
  351.0 18.3 %collective-permute-start.91 = (f32[128,1024]{1,0:T(8,128)}, f32[128,1024]{1,0:T(8,128)}, u32[]{:S(2)}, u32[]{:S(2)}) collective-permute-start(f32[128,1024]{1,0:T(8,128)} %get-tuple-element.294), channel_id=1, source_target_pairs={{0,4},{1,5},{2,0},{3,1},{4,6},{5,7},{6,2},{7,3},{8,12},{9,13},{10,... | collective-permute-start | bytes 1572872 | tf_op jit(solution)/shard_map/ppermute | solution.py:334
  354.3 23.4 %collective-permute-start.87 = (f32[128,1024]{1,0:T(8,128)}, f32[128,1024]{1,0:T(8,128)}, u32[]{:S(2)}, u32[]{:S(2)}) collective-permute-start(f32[128,1024]{1,0:T(8,128)} %get-tuple-element.288), channel_id=1, source_target_pairs={{0,6},{1,7},{2,4},{3,5},{4,2},{5,3},{6,0},{7,1},{8,14},{9,15},{10,... | collective-permute-start | bytes 1572872 | tf_op jit(solution)/shard_map/ppermute | solution.py:334
  359.3 39.6 %collective-permute-start.83 = (f32[128,1024]{1,0:T(8,128)}, f32[128,1024]{1,0:T(8,128)}, u32[]{:S(2)}, u32[]{:S(2)}) collective-permute-start(f32[128,1024]{1,0:T(8,128)} %get-tuple-element.282), channel_id=1, source_target_pairs={{0,2},{1,3},{2,6},{3,7},{4,0},{5,1},{6,4},{7,5},{8,10},{9,11},{10,... | collective-permute-start | bytes 1572872 | tf_op jit(solution)/shard_map/ppermute | solution.py:334
  (33 other events, 167.8 us)

commit v5 on v4

--- a/solution.py
+++ b/solution.py
@@ -309,18 +309,18 @@
     operands = [place, *current, *old_gain, *squares, *mixed[0], *mixed[1], *gain, *more]
     outs = [array(*PIECE)] * PLANES + [array(520, LANES)] * QUARTERS + [array(512, LANES)] * QUARTERS
     kernel = functools.partial(edge_kernel, width, len(squares), kinds)
-    results, _ = call(kernel, operands, outs, 1, 2 * STAGE_FLOPS)
-    return results[:PLANES], [results[PLANES : PLANES + QUARTERS], results[PLANES + QUARTERS :]]
-
-
-def column_stage(others, in_pieces, out_pieces, place, came, weights, rows=(), gain_layer=0):
+    results, mark = call(kernel, operands, outs, 1, 2 * STAGE_FLOPS)
+    return results[:PLANES], [results[PLANES : PLANES + QUARTERS], results[PLANES + QUARTERS :]], mark
+
+
+def column_stage(others, in_pieces, out_pieces, place, came, weights, waits, rows=(), gain_layer=0):
     more, kinds = split_weights(weights)
     operands = [place, *(ref for part in came for ref in part), *more, *rows]
     outs = [array(256, LANES)] * (QUARTERS * PLANES) if out_pieces else [array(512, LANES)] * QUARTERS
     count = len(outs)
     outs = outs + [array(*PIECE)] * len(rows)
     kernel = functools.partial(column_kernel, others, in_pieces, out_pieces, kinds, gain_layer)
-    results, mark = call(kernel, operands, outs, 2, STAGE_FLOPS)
+    results, mark = call(kernel, operands, outs, 2, STAGE_FLOPS, waits)
     return [results[n : n + QUARTERS] for n in range(0, count, QUARTERS)], results[count:], mark
 
 
@@ -403,9 +403,12 @@
         moves = [
             (0, lambda p, n=n: pl.ds(n * ROWS + p[2] * 4, 4), 0, pl.ds(n * 4, 4), None) for n in range(count)
         ]
-        return group_ring(copied(place, [near], [array(count * 4, LANES, LANES)], moves, waits, False)[0])
-
-    def four_pieces(part, near, far):
+        moves.append((0, lambda p: pl.ds(0, count * ROWS), 1, pl.ds(0, count * ROWS), None))
+        outs = [array(count * 4, LANES, LANES), array(count * ROWS, LANES, LANES)]
+        passed, kept = copied(place, [near], outs, moves, waits, False)
+        return group_ring(passed), kept
+
+    def four_pieces(part, far, near):
         near_pair, far_pair = (near, group_swap(near)), (far, group_swap(far))
         return [
             [
@@ -421,47 +424,70 @@
     pairs = [swapped(right_factors, 0, ())]
     part = own(pairs, 0, ())
     near = group_ring(part)
-    far = near_half(near, arrived[1:4:2])
-    (right_parts[0],) = four_pieces(part, near, far)
     pairs.append(swapped(left_factors, 0, [dealt]))
 
     current, gain, rows, came = [None] * PLANES, [None] * PLANES, [None] * PLANES, [None] * PLANES
     waits = []
     for step in (0, 1, 3, 2):
-        results, sends, mark = first_piece(step, place, arrived[step], right_parts[0][step], waits)
+        if step == 1:
+            far, near = near_half(near, [*arrived[1:4:2], mark])
+            (right_parts[0],) = four_pieces(part, far, near)
+        weights = right_parts[0][step] if step else ("whole", 0, (part,))
+        results, sends, mark = first_piece(step, place, arrived[step], weights, waits)
         waits = [mark]
         current[step], gain[step], rows[step] = results
         came[step] = exchange(sends)
-    part = own(pairs[1:], 0, [arrived[2], far])
-    near = group_ring(part)
-    far = near_half(near)
-    (left_parts[0],) = four_pieces(part, near, far)
+        if step == 3:
+            left = own(pairs[1:], 0, [arrived[2], far, mark, *came[0][2:], *came[1][2:]])
+            left_near = group_ring(left)
+    far, near = near_half(left_near, [mark, *came[3][2:]])
+    (left_parts[0],) = four_pieces(left, far, near)
+    right = own(pairs[:1], 1, [far, *came[2][2:], left_parts[0][1][2][1]])
+    right_near = group_ring(right)
+    left = own(pairs[1:], 1, [right])
+    left_near = group_ring(left)
     for layer in range(layers - 1):
-        part = own(pairs, (layer + 1) % 2, [far, mark])
-        near = group_ring(part)
-        far = near_half(near)
-        right_parts[layer + 1], left_parts[layer + 1] = four_pieces(part, near, far)
         in_pieces = layer == 0
         squares = [part[mate] for part in (came if in_pieces else came[:1]) for mate in range(QUARTERS)]
-        mixed = []
+        mixed, marks = [], []
         for chunk in range(CHUNKS):
             others = (chunk * 2, chunk * 2 + 1)
             extra = (rows, layer + 1) if chunk == 0 else ()
             weights = left_parts[layer][others[0] : others[1] + 1]
             source = came if in_pieces else came[chunk : chunk + 1]
-            (half_sends,), spread, mark = column_stage(others, in_pieces, False, place, source, weights, *extra)
+            (half_sends,), spread, mark = column_stage(
+                others, in_pieces, False, place, source, weights, marks, *extra
+            )
             mixed.append(exchange(half_sends))
+            marks = [mark]
             next_gain = spread or next_gain
-        if layer % 2 == 0 and layer + 2 < layers:
-            pairs = [swapped(factors, (layer + 2) // 2, [mark]) for factors in (right_factors, left_factors)]
-        current, sends = layer_edge(
+        if layer == 0:
+            far, near = near_half(right_near, marks)
+            (right_parts[1],) = four_pieces(right, far, near)
+            right_last = right_parts[1][2][2][1]
+            far, near = near_half(left_near, [far, right_parts[1][1][2][1], *mixed[0][2:]])
+            (left_parts[1],) = four_pieces(left, far, near)
+            pairs = [swapped(factors, 1, marks) for factors in (right_factors, left_factors)]
+        if layer + 2 < layers:
+            waits = [far, mark if layer else right_last, *mixed[0][2:], *mixed[1][2:]]
+            part = own(pairs, layer % 2, waits)
+            near = group_ring(part)
+        current, sends, mark = layer_edge(
             width, place, current, gain, squares, mixed, next_gain, right_parts[layer + 1]
         )
         gain = next_gain
         came = [exchange(sends[0]), exchange(sends[1])]
+        if layer + 2 < layers:
+            waits = ()
+            if layer == 0:
+                swaps = left_parts[1][1][2][1], left_parts[1][2][2][1]
+                waits = [mark, *came[0][2:], *swaps]
+            far, kept = near_half(near, waits)
+            near = near if layer else kept
+            right_parts[layer + 2], left_parts[layer + 2] = four_pieces(part, far, near)
 
     squares = came[0]
-    sends, _, _ = column_stage(tuple(range(PLANES)), False, True, place, came, left_parts[-1])
+    sends, _, _ = column_stage(tuple(range(PLANES)), False, True, place, came, left_parts[-1], ())
     back = [None] * PLANES
     for step in (2, 1, 3, 0):
         mixed = exchange(sends[step])

time: 405 us -> 383 us (0.946)
  waiting for transfers between devices: 229 us -> 209 us
  starting transfers between devices: 107 us -> 97 us
  Pallas kernels: 63.1 us -> 70.2 us
    ppermute x73, waiting for transfers between devices: 166 us -> 134 us  [routed(): return lax.ppermute(value, ('segment', 'block'), route)]
    ppermute x10 -> x12, waiting for transfers between devices: 3.73 us -> 27.3 us  [group_swap(): return lax.ppermute(value, 'groups', [(0, 1), (1, 0)])]
    ppermute x10 -> x12, waiting for transfers between devices: 59.4 us -> 47.6 us  [group_ring(): return lax.ppermute(value, ('groups', 'segment', 'block'), route)]
    ppermute x10 -> x12, starting transfers between devices: 34.1 us -> 26.8 us  [group_ring(): return lax.ppermute(value, ('groups', 'segment', 'block'), route)]
    pallas_call x33 -> x35, Pallas kernels: 63.1 us -> 70.2 us  [call(): pl.pallas_call(functools.partial(marked, kernel, len(operands), len(waits...]
    ppermute x73, starting transfers between devices: 60.2 us -> 56 us  [routed(): return lax.ppermute(value, ('segment', 'block'), route)]
    ppermute x10 -> x12, starting transfers between devices: 12.3 us -> 14.1 us  [group_swap(): return lax.ppermute(value, 'groups', [(0, 1), (1, 0)])]
  transfers between devices with their start and end apart: 93 -> 97, of which waited for: 44 -> 52; matrix products, arithmetic and copies ran while one was open for 0% -> 0% of each run, Pallas kernels for 13% -> 15%
where the time goes in v5:
time: 383 us; the launch traced here: 382 us
  waiting for transfers between devices  209 us (55%)
  starting transfers between devices  97 us (25%)
  Pallas kernels  70.2 us (18%)
    ppermute x73, waiting for transfers between devices, routed(): return lax.ppermute(value, ('segment', 'block'), route)  134 us
    pallas_call x35, Pallas kernels, call(): pl.pallas_call(functools.partial(marked, kernel, len(operands), len(waits...  70.2 us
    ppermute x73, starting transfers between devices, routed(): return lax.ppermute(value, ('segment', 'block'), route)  56 us
    ppermute x12, waiting for transfers between devices, group_ring(): return lax.ppermute(value, ('groups', 'segment', 'block'), route)  47.6 us
    ppermute x12, waiting for transfers between devices, group_swap(): return lax.ppermute(value, 'groups', [(0, 1), (1, 0)])  27.3 us
    ppermute x12, starting transfers between devices, group_ring(): return lax.ppermute(value, ('groups', 'segment', 'block'), route)  26.8 us
    ppermute x12, starting transfers between devices, group_swap(): return lax.ppermute(value, 'groups', [(0, 1), (1, 0)])  14.1 us
  transfers between devices with their start and end apart: 97, of which 52 were waited for; matrix products, arithmetic and copies ran while one was open for 0% of the time, Pallas kernels for 15%

profile of v5, /device:TPU:0, one launch (start us, length us, event | category | flops | bytes accessed | tf_op | source)
XLA Modules:
  0.0 382.4 jit_solution(6462353450761412848)
XLA Ops:
  0.0 2.5 constant_dynamic-slice_fusion.4
  7.6 3.9 %collective-permute-start.3 = (f32[136,1024]{1,0:T(8,128)S(1)}, f32[136,1024]{1,0:T(8,128)S(1)}, u32[]{:S(2)}, u32[]{:S(2)}) collective-permute-start(f32[136,1024]{1,0:T(8,128)S(1)} %get-tuple-element.165), channel_id=1, source_target_pairs={{0,4},{1,5},{2,0},{3,1},{4,6},{5,7},{6,2},{7,3},{8,12},{9,13},{10,... | collective-permute-start | bytes 1671176 | tf_op jit(solution)/shard_map/ppermute | solution.py:334
  12.6 3.0 collective-permute-start.4
  17.4 29.6 %collective-permute-done.4.refs_1_ = f32[8,128,128]{2,1,0:T(8,128)S(1)} collective-permute-done((f32[8,128,128]{2,1,0:T(8,128)S(1)}, f32[8,128,128]{2,1,0:T(8,128)S(1)}, u32[]{:S(2)}, u32[]{:S(2)}) %collective-permute-start.4) | collective-permute-done | bytes 524320 | tf_op jit(solution)/shard_map/ppermute | solution.py:354
  48.8 3.3 collective-permute-start.6
  52.1 2.5 collective-permute-start.7
  58.3 5.9 %collective-permute-done.6.refs_3_ = f32[8,128,128]{2,1,0:T(8,128)S(1)} collective-permute-done((f32[8,128,128]{2,1,0:T(8,128)S(1)}, f32[8,128,128]{2,1,0:T(8,128)S(1)}, u32[]{:S(2)}, u32[]{:S(2)}) %collective-permute-start.6) | collective-permute-done | bytes 524320 | tf_op jit(solution)/shard_map/ppermute | solution.py:362
  65.5 2.4 shard_map.51
  69.6 2.4 shard_map.52
  72.0 1.9 collective-permute-done.8.refs_2_.refs_4_
  77.2 8.6 %collective-permute-start.23 = (f32[8,128,128]{2,1,0:T(8,128)S(1)}, f32[8,128,128]{2,1,0:T(8,128)S(1)}, u32[]{:S(2)}, u32[]{:S(2)}) collective-permute-start(f32[8,128,128]{2,1,0:T(8,128)S(1)} %get-tuple-element.198.refs_17_), channel_id=1, source_target_pairs={{0,4},{1,5},{2,0},{3,1},{4,6},{5,7},{6,2},{7,3},{8,12},{9,13},{10,... | collective-permute-start | bytes 1572872 | tf_op jit(solution)/shard_map/ppermute | solution.py:354
  87.4 4.8 %collective-permute-done.9.refs_3_ = f32[4,128,128]{2,1,0:T(8,128)S(1)} collective-permute-done((f32[4,128,128]{2,1,0:T(8,128)S(1)}, f32[4,128,128]{2,1,0:T(8,128)S(1)}, u32[]{:S(2)}, u32[]{:S(2)}) %collective-permute-start.9) | collective-permute-done | bytes 262176 | tf_op jit(solution)/shard_map/ppermute | solution.py:362
  92.2 2.4 shard_map.53
  98.1 2.6 collective-permute-start.24
  102.6 4.0 %collective-permute-done.17.refs_11_.refs_4_.refs_19_ = f32[264,128]{1,0:T(8,128)S(1)} collective-permute-done((f32[264,128]{1,0:T(8,128)S(1)}, f32[264,128]{1,0:T(8,128)S(1)}, u32[]{:S(2)}, u32[]{:S(2)}) %collective-permute-start.17) | collective-permute-done | bytes 135200 | tf_op jit(solution)/shard_map/ppermute | solution.py:334
  106.6 1.9 collective-permute-done.18.refs_12_.refs_5_.refs_20_
  111.2 2.4 collective-permute-start.33
  115.7 1.9 collective-permute-start.40
  119.2 2.5 shard_map.57
  123.5 2.7 shard_map.58
  128.4 2.2 collective-permute-start.34
  136.8 5.3 %collective-permute-done.35.refs_40_.refs_2_ = f32[4,128,128]{2,1,0:T(8,128)S(1)} collective-permute-done((f32[4,128,128]{2,1,0:T(8,128)S(1)}, f32[4,128,128]{2,1,0:T(8,128)S(1)}, u32[]{:S(2)}, u32[]{:S(2)}) %collective-permute-start.35) | collective-permute-done | bytes 262176 | tf_op jit(solution)/shard_map/ppermute | solution.py:354
  142.3 1.8 collective-permute-start.36
  146.2 3.8 collective-permute-done.32.refs_32_.refs_10_
  151.2 3.1 collective-permute-done.48.refs_5_
  155.6 1.9 collective-permute-start.55
  159.5 3.4 shard_map.61
  165.0 7.1 %collective-permute-done.38.refs_3_.refs_11_ = f32[520,128]{1,0:T(8,128)S(1)} collective-permute-done((f32[520,128]{1,0:T(8,128)S(1)}, f32[520,128]{1,0:T(8,128)S(1)}, u32[]{:S(2)}, u32[]{:S(2)}) %collective-permute-start.38) | collective-permute-done | bytes 266272 | tf_op jit(solution)/shard_map/ppermute | solution.py:334
  172.1 4.1 %collective-permute-done.39.refs_4_.refs_12_ = f32[520,128]{1,0:T(8,128)S(1)} collective-permute-done((f32[520,128]{1,0:T(8,128)S(1)}, f32[520,128]{1,0:T(8,128)S(1)}, u32[]{:S(2)}, u32[]{:S(2)}) %collective-permute-start.39) | collective-permute-done | bytes 266272 | tf_op jit(solution)/shard_map/ppermute | solution.py:334
  178.5 2.4 collective-permute-done.55.refs_1_
  180.9 1.8 shard_map.69
  182.7 2.8 collective-permute-start.57
  185.5 2.5 shard_map.64
  188.7 1.8 collective-permute-done.47.refs_4_
  190.6 2.6 shard_map.65
  194.2 1.9 collective-permute-start.52
  198.2 3.6 collective-permute-done.44.refs_16_.refs_8_
  201.8 7.0 %collective-permute-done.51.refs_19_.refs_9_ = f32[512,128]{1,0:T(8,128)S(1)} collective-permute-done((f32[512,128]{1,0:T(8,128)S(1)}, f32[512,128]{1,0:T(8,128)S(1)}, u32[]{:S(2)}, u32[]{:S(2)}) %collective-permute-start.51) | collective-permute-done | bytes 262176 | tf_op jit(solution)/shard_map/ppermute | solution.py:334
  208.8 3.7 collective-permute-done.52.refs_20_.refs_10_
  212.5 1.9 shard_map.73
  218.5 4.3 %collective-permute-done.56.refs_27_.refs_31_.refs_7_.refs_8_ = f32[16,128,128]{2,1,0:T(8,128)S(1)} collective-permute-done((f32[16,128,128]{2,1,0:T(8,128)S(1)}, f32[16,128,128]{2,1,0:T(8,128)S(1)}, u32[]{:S(2)}, u32[]{:S(2)}) %collective-permute-start.56) | collective-permute-done | bytes 1048608 | tf_op jit(solution)/shard_map/ppermute | solution.py:362
  222.8 9.2 %collective-permute-done.58.refs_29_.refs_6_ = f32[8,128,128]{2,1,0:T(8,128)S(1)} collective-permute-done((f32[8,128,128]{2,1,0:T(8,128)S(1)}, f32[8,128,128]{2,1,0:T(8,128)S(1)}, u32[]{:S(2)}, u32[]{:S(2)}) %collective-permute-start.58) | collective-permute-done | bytes 524320 | tf_op jit(solution)/shard_map/ppermute | solution.py:362
  232.0 3.3 shard_map.70
  237.3 3.0 collective-permute-done.71.refs_1_.refs_26_.refs_30_.refs_10_.refs_14_
  242.0 2.1 collective-permute-start.73
  245.9 3.6 collective-permute-done.61.refs_4_.refs_12_
  251.2 2.4 shard_map.71
  253.8 2.3 collective-permute-done.66.refs_3_
  257.1 3.6 collective-permute-done.67.refs_4_
  262.8 2.6 shard_map.72
  268.4 3.6 collective-permute-done.64.refs_16_
  273.7 4.8 %collective-permute-done.69.refs_19_ = f32[512,128]{1,0:T(8,128)S(1)} collective-permute-done((f32[512,128]{1,0:T(8,128)S(1)}, f32[512,128]{1,0:T(8,128)S(1)}, u32[]{:S(2)}, u32[]{:S(2)}) %collective-permute-start.69) | collective-permute-done | bytes 262176 | tf_op jit(solution)/shard_map/ppermute | solution.py:334
  278.5 4.7 %collective-permute-done.70.refs_20_ = f32[512,128]{1,0:T(8,128)S(1)} collective-permute-done((f32[512,128]{1,0:T(8,128)S(1)}, f32[512,128]{1,0:T(8,128)S(1)}, u32[]{:S(2)}, u32[]{:S(2)}) %collective-permute-start.70) | collective-permute-done | bytes 262176 | tf_op jit(solution)/shard_map/ppermute | solution.py:334
  283.2 3.3 shard_map.75
  290.6 17.0 %collective-permute-done.79.refs_7_ = f32[512,128]{1,0:T(8,128)S(1)} collective-permute-done((f32[512,128]{1,0:T(8,128)S(1)}, f32[512,128]{1,0:T(8,128)S(1)}, u32[]{:S(2)}, u32[]{:S(2)}) %collective-permute-start.79) | collective-permute-done | bytes 262176 | tf_op jit(solution)/shard_map/ppermute | solution.py:334
  307.7 4.3 %collective-permute-done.80.refs_8_ = f32[512,128]{1,0:T(8,128)S(1)} collective-permute-done((f32[512,128]{1,0:T(8,128)S(1)}, f32[512,128]{1,0:T(8,128)S(1)}, u32[]{:S(2)}, u32[]{:S(2)}) %collective-permute-start.80) | collective-permute-done | bytes 262176 | tf_op jit(solution)/shard_map/ppermute | solution.py:334
  312.0 3.0 shard_map.76
  319.0 2.9 collective-permute-done.93.refs_9_
  330.7 2.6 collective-permute-start.91
  334.2 1.8 shard_map.78
  339.7 4.1 %collective-permute-done.82.refs_9_ = f32[256,128]{1,0:T(8,128)S(1)} collective-permute-done((f32[256,128]{1,0:T(8,128)S(1)}, f32[256,128]{1,0:T(8,128)S(1)}, u32[]{:S(2)}, u32[]{:S(2)}) %collective-permute-start.82) | collective-permute-done | bytes 131104 | tf_op jit(solution)/shard_map/ppermute | solution.py:334
  346.1 9.0 %collective-permute-done.91 = f32[128,1024]{1,0:T(8,128)} collective-permute-done((f32[128,1024]{1,0:T(8,128)}, f32[128,1024]{1,0:T(8,128)}, u32[]{:S(2)}, u32[]{:S(2)}) %collective-permute-start.91) | collective-permute-done | bytes 524320 | tf_op jit(solution)/shard_map/ppermute | solution.py:334
  355.1 21.2 %collective-permute-done.87 = f32[128,1024]{1,0:T(8,128)} collective-permute-done((f32[128,1024]{1,0:T(8,128)}, f32[128,1024]{1,0:T(8,128)}, u32[]{:S(2)}, u32[]{:S(2)}) %collective-permute-start.87) | collective-permute-done | bytes 524320 | tf_op jit(solution)/shard_map/ppermute | solution.py:334
  378.4 2.4 collective-permute-done.96
  (181 shorter events, 104.9 us)
Async XLA Ops:
  7.6 39.4 %collective-permute-start.3 = (f32[136,1024]{1,0:T(8,128)S(1)}, f32[136,1024]{1,0:T(8,128)S(1)}, u32[]{:S(2)}, u32[]{:S(2)}) collective-permute-start(f32[136,1024]{1,0:T(8,128)S(1)} %get-tuple-element.165), channel_id=1, source_target_pairs={{0,4},{1,5},{2,0},{3,1},{4,6},{5,7},{6,2},{7,3},{8,12},{9,13},{10,... | collective-permute-start | bytes 1671176 | tf_op jit(solution)/shard_map/ppermute | solution.py:334
  11.5 35.5 %collective-permute-start.5 = (f32[136,1024]{1,0:T(8,128)S(1)}, f32[136,1024]{1,0:T(8,128)S(1)}, u32[]{:S(2)}, u32[]{:S(2)}) collective-permute-start(f32[136,1024]{1,0:T(8,128)S(1)} %get-tuple-element.166), channel_id=1, source_target_pairs={{0,2},{1,3},{2,6},{3,7},{4,0},{5,1},{6,4},{7,5},{8,10},{9,11},{10,... | collective-permute-start | bytes 1671176 | tf_op jit(solution)/shard_map/ppermute | solution.py:334
  12.6 34.4 %collective-permute-start.4 = (f32[8,128,128]{2,1,0:T(8,128)S(1)}, f32[8,128,128]{2,1,0:T(8,128)S(1)}, u32[]{:S(2)}, u32[]{:S(2)}) collective-permute-start(f32[8,128,128]{2,1,0:T(8,128)S(1)} %get-tuple-element.163.refs_2_), channel_id=1, source_target_pairs={{0,4},{1,5},{2,0},{3,1},{4,6},{5,7},{6,2},{7,3},{8,12},{9,13},{10,... | collective-permute-start | bytes 1572872 | tf_op jit(solution)/shard_map/ppermute | solution.py:354
  48.8 15.4 %collective-permute-start.6 = (f32[8,128,128]{2,1,0:T(8,128)S(1)}, f32[8,128,128]{2,1,0:T(8,128)S(1)}, u32[]{:S(2)}, u32[]{:S(2)}) collective-permute-start(f32[8,128,128]{2,1,0:T(8,128)S(1)} %get-tuple-element.168.refs_2_), channel_id=1, source_target_pairs={{0,16},{16,0},{1,17},{17,1},{2,18},{18,2},{3,19},{19,3},{4,20},{20... | collective-permute-start | bytes 1572872 | tf_op jit(solution)/shard_map/ppermute | solution.py:362
  52.1 19.9 %collective-permute-start.7 = (f32[136,1024]{1,0:T(8,128)S(1)}, f32[136,1024]{1,0:T(8,128)S(1)}, u32[]{:S(2)}, u32[]{:S(2)}) collective-permute-start(f32[136,1024]{1,0:T(8,128)S(1)} %get-tuple-element.170), channel_id=1, source_target_pairs={{0,6},{1,7},{2,4},{3,5},{4,2},{5,3},{6,0},{7,1},{8,14},{9,15},{10,... | collective-permute-start | bytes 1671176 | tf_op jit(solution)/shard_map/ppermute | solution.py:334
  56.4 15.7 %collective-permute-start.22 = (f32[8,128,128]{2,1,0:T(8,128)S(1)}, f32[8,128,128]{2,1,0:T(8,128)S(1)}, u32[]{:S(2)}, u32[]{:S(2)}) collective-permute-start(f32[8,128,128]{2,1,0:T(8,128)S(1)} %get-tuple-element.197), channel_id=1, source_target_pairs={{0,8},{1,9},{2,10},{3,11},{4,12},{5,13},{6,14},{7,15},{8,0},{9,1},... | collective-permute-start | bytes 1572872 | tf_op jit(solution)/shard_map/ppermute | solution.py:334
  56.4 11.5 %collective-permute-start.11 = (f32[264,128]{1,0:T(8,128)S(1)}, f32[264,128]{1,0:T(8,128)S(1)}, u32[]{:S(2)}, u32[]{:S(2)}) collective-permute-start(f32[264,128]{1,0:T(8,128)S(1)} %get-tuple-element.182), channel_id=1, source_target_pairs={{0,1},{1,0},{2,3},{3,2},{4,5},{5,4},{6,7},{7,6},{8,9},{9,8},{10,11... | collective-permute-start | bytes 405512 | tf_op jit(solution)/shard_map/ppermute | solution.py:334
  58.0 11.5 %collective-permute-start.12 = (f32[264,128]{1,0:T(8,128)S(1)}, f32[264,128]{1,0:T(8,128)S(1)}, u32[]{:S(2)}, u32[]{:S(2)}) collective-permute-start(f32[264,128]{1,0:T(8,128)S(1)} %get-tuple-element.183), channel_id=1, source_target_pairs={{0,9},{1,8},{2,11},{3,10},{4,13},{5,12},{6,15},{7,14},{8,1},{9,0},... | collective-permute-start | bytes 405512 | tf_op jit(solution)/shard_map/ppermute | solution.py:334
  64.2 9.7 %collective-permute-start.8 = (f32[4,128,128]{2,1,0:T(8,128)S(1)}, f32[4,128,128]{2,1,0:T(8,128)S(1)}, u32[]{:S(2)}, u32[]{:S(2)}) collective-permute-start(f32[4,128,128]{2,1,0:T(8,128)S(1)} %get-tuple-element.171), channel_id=1, source_target_pairs={{0,4},{1,5},{2,0},{3,1},{4,6},{5,7},{6,2},{7,3},{8,12},{9,13},{10,... | collective-permute-start | bytes 786440 | tf_op jit(solution)/shard_map/ppermute | solution.py:354
  77.2 19.1 %collective-permute-start.23 = (f32[8,128,128]{2,1,0:T(8,128)S(1)}, f32[8,128,128]{2,1,0:T(8,128)S(1)}, u32[]{:S(2)}, u32[]{:S(2)}) collective-permute-start(f32[8,128,128]{2,1,0:T(8,128)S(1)} %get-tuple-element.198.refs_17_), channel_id=1, source_target_pairs={{0,4},{1,5},{2,0},{3,1},{4,6},{5,7},{6,2},{7,3},{8,12},{9,13},{10,... | collective-permute-start | bytes 1572872 | tf_op jit(solution)/shard_map/ppermute | solution.py:354
  98.1 12.0 %collective-permute-start.24 = (f32[8,128,128]{2,1,0:T(8,128)S(1)}, f32[8,128,128]{2,1,0:T(8,128)S(1)}, u32[]{:S(2)}, u32[]{:S(2)}) collective-permute-start(f32[8,128,128]{2,1,0:T(8,128)S(1)} %get-tuple-element.200.refs_18_.refs_19_), channel_id=1, source_target_pairs={{0,16},{16,0},{1,17},{17,1},{2,18},{18,2},{3,19},{19,3},{4,20},{20... | collective-permute-start | bytes 1572872 | tf_op jit(solution)/shard_map/ppermute | solution.py:362
  111.2 15.4 %collective-permute-start.33 = (f32[8,128,128]{2,1,0:T(8,128)S(1)}, f32[8,128,128]{2,1,0:T(8,128)S(1)}, u32[]{:S(2)}, u32[]{:S(2)}) collective-permute-start(f32[8,128,128]{2,1,0:T(8,128)S(1)} %get-tuple-element.219.refs_37_.refs_3_), channel_id=1, source_target_pairs={{0,4},{1,5},{2,0},{3,1},{4,6},{5,7},{6,2},{7,3},{8,12},{9,13},{10,... | collective-permute-start | bytes 1572872 | tf_op jit(solution)/shard_map/ppermute | solution.py:354
  114.2 9.3 %collective-permute-start.29 = (f32[4,128,128]{2,1,0:T(8,128)S(1)}, f32[4,128,128]{2,1,0:T(8,128)S(1)}, u32[]{:S(2)}, u32[]{:S(2)}) collective-permute-start(f32[4,128,128]{2,1,0:T(8,128)S(1)} %collective-permute-done.28.refs_17_.refs_3_), channel_id=1, source_target_pairs={{0,16},{16,0},{1,17},{17,1},{2,18},{18,2},{3,19},{19,3},{4,20},{20... | collective-permute-start | bytes 786440 | tf_op jit(solution)/shard_map/ppermute | solution.py:362
  115.7 20.9 %collective-permute-start.40 = (f32[8,128,128]{2,1,0:T(8,128)S(1)}, f32[8,128,128]{2,1,0:T(8,128)S(1)}, u32[]{:S(2)}, u32[]{:S(2)}) collective-permute-start(f32[8,128,128]{2,1,0:T(8,128)S(1)} %get-tuple-element.231.refs_5_), channel_id=1, source_target_pairs={{0,4},{1,5},{2,0},{3,1},{4,6},{5,7},{6,2},{7,3},{8,12},{9,13},{10,... | collective-permute-start | bytes 1572872 | tf_op jit(solution)/shard_map/ppermute | solution.py:354
  121.7 14.0 %collective-permute-start.26 = (f32[512,128]{1,0:T(8,128)S(1)}, f32[512,128]{1,0:T(8,128)S(1)}, u32[]{:S(2)}, u32[]{:S(2)}) collective-permute-start(f32[512,128]{1,0:T(8,128)S(1)} %get-tuple-element.207), channel_id=1, source_target_pairs={{0,1},{1,0},{2,3},{3,2},{4,5},{5,4},{6,7},{7,6},{8,9},{9,8},{10,11... | collective-permute-start | bytes 786440 | tf_op jit(solution)/shard_map/ppermute | solution.py:334
  123.3 13.0 %collective-permute-start.27 = (f32[512,128]{1,0:T(8,128)S(1)}, f32[512,128]{1,0:T(8,128)S(1)}, u32[]{:S(2)}, u32[]{:S(2)}) collective-permute-start(f32[512,128]{1,0:T(8,128)S(1)} %get-tuple-element.208), channel_id=1, source_target_pairs={{0,9},{1,8},{2,11},{3,10},{4,13},{5,12},{6,15},{7,14},{8,1},{9,0},... | collective-permute-start | bytes 786440 | tf_op jit(solution)/shard_map/ppermute | solution.py:334
  128.4 13.9 %collective-permute-start.34 = (f32[8,128,128]{2,1,0:T(8,128)S(1)}, f32[8,128,128]{2,1,0:T(8,128)S(1)}, u32[]{:S(2)}, u32[]{:S(2)}) collective-permute-start(f32[8,128,128]{2,1,0:T(8,128)S(1)} %get-tuple-element.221.refs_38_.refs_42_), channel_id=1, source_target_pairs={{0,16},{16,0},{1,17},{17,1},{2,18},{18,2},{3,19},{19,3},{4,20},{20... | collective-permute-start | bytes 1572872 | tf_op jit(solution)/shard_map/ppermute | solution.py:362
  134.1 11.1 %collective-permute-start.31 = (f32[512,128]{1,0:T(8,128)S(1)}, f32[512,128]{1,0:T(8,128)S(1)}, u32[]{:S(2)}, u32[]{:S(2)}) collective-permute-start(f32[512,128]{1,0:T(8,128)S(1)} %get-tuple-element.213), channel_id=1, source_target_pairs={{0,1},{1,0},{2,3},{3,2},{4,5},{5,4},{6,7},{7,6},{8,9},{9,8},{10,11... | collective-permute-start | bytes 786440 | tf_op jit(solution)/shard_map/ppermute | solution.py:334
  136.3 13.6 %collective-permute-start.53 = (f32[8,128,128]{2,1,0:T(8,128)S(1)}, f32[8,128,128]{2,1,0:T(8,128)S(1)}, u32[]{:S(2)}, u32[]{:S(2)}) collective-permute-start(f32[8,128,128]{2,1,0:T(8,128)S(1)} %get-tuple-element.251), channel_id=1, source_target_pairs={{0,8},{1,9},{2,10},{3,11},{4,12},{5,13},{6,14},{7,15},{8,0},{9,1},... | collective-permute-start | bytes 1572872 | tf_op jit(solution)/shard_map/ppermute | solution.py:334
  136.7 13.3 %collective-permute-start.54 = (f32[8,128,128]{2,1,0:T(8,128)S(1)}, f32[8,128,128]{2,1,0:T(8,128)S(1)}, u32[]{:S(2)}, u32[]{:S(2)}) collective-permute-start(f32[8,128,128]{2,1,0:T(8,128)S(1)} %get-tuple-element.252), channel_id=1, source_target_pairs={{0,8},{1,9},{2,10},{3,11},{4,12},{5,13},{6,14},{7,15},{8,0},{9,1},... | collective-permute-start | bytes 1572872 | tf_op jit(solution)/shard_map/ppermute | solution.py:334
  145.3 9.1 %collective-permute-start.48 = (f32[4,128,128]{2,1,0:T(8,128)S(1)}, f32[4,128,128]{2,1,0:T(8,128)S(1)}, u32[]{:S(2)}, u32[]{:S(2)}) collective-permute-start(f32[4,128,128]{2,1,0:T(8,128)S(1)} %get-tuple-element.241), channel_id=1, source_target_pairs={{0,4},{1,5},{2,0},{3,1},{4,6},{5,7},{6,2},{7,3},{8,12},{9,13},{10,... | collective-permute-start | bytes 786440 | tf_op jit(solution)/shard_map/ppermute | solution.py:354
  155.6 25.3 %collective-permute-start.55 = (f32[16,128,128]{2,1,0:T(8,128)S(1)}, f32[16,128,128]{2,1,0:T(8,128)S(1)}, u32[]{:S(2)}, u32[]{:S(2)}) collective-permute-start(f32[16,128,128]{2,1,0:T(8,128)S(1)} %get-tuple-element.253.refs_25_.refs_5_), channel_id=1, source_target_pairs={{0,4},{1,5},{2,0},{3,1},{4,6},{5,7},{6,2},{7,3},{8,12},{9,13},{10,... | collective-permute-start | bytes 3145736 | tf_op jit(solution)/shard_map/ppermute | solution.py:354
  158.1 19.1 %collective-permute-start.41 = (f32[8,128,128]{2,1,0:T(8,128)S(1)}, f32[8,128,128]{2,1,0:T(8,128)S(1)}, u32[]{:S(2)}, u32[]{:S(2)}) collective-permute-start(f32[8,128,128]{2,1,0:T(8,128)S(1)} %get-tuple-element.232.refs_6_.refs_7_), channel_id=1, source_target_pairs={{0,16},{16,0},{1,17},{17,1},{2,18},{18,2},{3,19},{19,3},{4,20},{20... | collective-permute-start | bytes 1572872 | tf_op jit(solution)/shard_map/ppermute | solution.py:362
  162.8 9.3 %collective-permute-start.38 = (f32[520,128]{1,0:T(8,128)S(1)}, f32[520,128]{1,0:T(8,128)S(1)}, u32[]{:S(2)}, u32[]{:S(2)}) collective-permute-start(f32[520,128]{1,0:T(8,128)S(1)} %get-tuple-element.229), channel_id=1, source_target_pairs={{0,1},{1,0},{2,3},{3,2},{4,5},{5,4},{6,7},{7,6},{8,9},{9,8},{10,11... | collective-permute-start | bytes 798728 | tf_op jit(solution)/shard_map/ppermute | solution.py:334
  164.0 12.2 %collective-permute-start.39 = (f32[520,128]{1,0:T(8,128)S(1)}, f32[520,128]{1,0:T(8,128)S(1)}, u32[]{:S(2)}, u32[]{:S(2)}) collective-permute-start(f32[520,128]{1,0:T(8,128)S(1)} %get-tuple-element.230), channel_id=1, source_target_pairs={{0,9},{1,8},{2,11},{3,10},{4,13},{5,12},{6,15},{7,14},{8,1},{9,0},... | collective-permute-start | bytes 798728 | tf_op jit(solution)/shard_map/ppermute | solution.py:334
  164.4 13.9 %collective-permute-start.49 = (f32[4,128,128]{2,1,0:T(8,128)S(1)}, f32[4,128,128]{2,1,0:T(8,128)S(1)}, u32[]{:S(2)}, u32[]{:S(2)}) collective-permute-start(f32[4,128,128]{2,1,0:T(8,128)S(1)} %collective-permute-done.48.refs_5_), channel_id=1, source_target_pairs={{0,16},{16,0},{1,17},{17,1},{2,18},{18,2},{3,19},{19,3},{4,20},{20... | collective-permute-start | bytes 786440 | tf_op jit(solution)/shard_map/ppermute | solution.py:362
  172.1 13.4 %collective-permute-start.37 = (f32[520,128]{1,0:T(8,128)S(1)}, f32[520,128]{1,0:T(8,128)S(1)}, u32[]{:S(2)}, u32[]{:S(2)}) collective-permute-start(f32[520,128]{1,0:T(8,128)S(1)} %get-tuple-element.228), channel_id=1, source_target_pairs={{0,8},{1,9},{2,10},{3,11},{4,12},{5,13},{6,14},{7,15},{8,0},{9,1},... | collective-permute-start | bytes 798728 | tf_op jit(solution)/shard_map/ppermute | solution.py:334
  176.2 12.5 %collective-permute-start.45 = (f32[512,128]{1,0:T(8,128)S(1)}, f32[512,128]{1,0:T(8,128)S(1)}, u32[]{:S(2)}, u32[]{:S(2)}) collective-permute-start(f32[512,128]{1,0:T(8,128)S(1)} %get-tuple-element.238), channel_id=1, source_target_pairs={{0,8},{1,9},{2,10},{3,11},{4,12},{5,13},{6,14},{7,15},{8,0},{9,1},... | collective-permute-start | bytes 786440 | tf_op jit(solution)/shard_map/ppermute | solution.py:334
  177.1 11.6 %collective-permute-start.46 = (f32[512,128]{1,0:T(8,128)S(1)}, f32[512,128]{1,0:T(8,128)S(1)}, u32[]{:S(2)}, u32[]{:S(2)}) collective-permute-start(f32[512,128]{1,0:T(8,128)S(1)} %get-tuple-element.239), channel_id=1, source_target_pairs={{0,1},{1,0},{2,3},{3,2},{4,5},{5,4},{6,7},{7,6},{8,9},{9,8},{10,11... | collective-permute-start | bytes 786440 | tf_op jit(solution)/shard_map/ppermute | solution.py:334
  178.2 12.3 %collective-permute-start.47 = (f32[512,128]{1,0:T(8,128)S(1)}, f32[512,128]{1,0:T(8,128)S(1)}, u32[]{:S(2)}, u32[]{:S(2)}) collective-permute-start(f32[512,128]{1,0:T(8,128)S(1)} %get-tuple-element.240), channel_id=1, source_target_pairs={{0,9},{1,8},{2,11},{3,10},{4,13},{5,12},{6,15},{7,14},{8,1},{9,0},... | collective-permute-start | bytes 786440 | tf_op jit(solution)/shard_map/ppermute | solution.py:334
  182.7 29.7 %collective-permute-start.57 = (f32[8,128,128]{2,1,0:T(8,128)S(1)}, f32[8,128,128]{2,1,0:T(8,128)S(1)}, u32[]{:S(2)}, u32[]{:S(2)}) collective-permute-start(f32[8,128,128]{2,1,0:T(8,128)S(1)} %get-tuple-element.256), channel_id=1, source_target_pairs={{0,4},{1,5},{2,0},{3,1},{4,6},{5,7},{6,2},{7,3},{8,12},{9,13},{10,... | collective-permute-start | bytes 1572872 | tf_op jit(solution)/shard_map/ppermute | solution.py:354
  188.0 9.5 %collective-permute-start.43 = (f32[512,128]{1,0:T(8,128)S(1)}, f32[512,128]{1,0:T(8,128)S(1)}, u32[]{:S(2)}, u32[]{:S(2)}) collective-permute-start(f32[512,128]{1,0:T(8,128)S(1)} %get-tuple-element.235), channel_id=1, source_target_pairs={{0,1},{1,0},{2,3},{3,2},{4,5},{5,4},{6,7},{7,6},{8,9},{9,8},{10,11... | collective-permute-start | bytes 786440 | tf_op jit(solution)/shard_map/ppermute | solution.py:334
  188.7 13.1 %collective-permute-start.44 = (f32[512,128]{1,0:T(8,128)S(1)}, f32[512,128]{1,0:T(8,128)S(1)}, u32[]{:S(2)}, u32[]{:S(2)}) collective-permute-start(f32[512,128]{1,0:T(8,128)S(1)} %get-tuple-element.236), channel_id=1, source_target_pairs={{0,9},{1,8},{2,11},{3,10},{4,13},{5,12},{6,15},{7,14},{8,1},{9,0},... | collective-permute-start | bytes 786440 | tf_op jit(solution)/shard_map/ppermute | solution.py:334
  193.2 15.6 %collective-permute-start.51 = (f32[512,128]{1,0:T(8,128)S(1)}, f32[512,128]{1,0:T(8,128)S(1)}, u32[]{:S(2)}, u32[]{:S(2)}) collective-permute-start(f32[512,128]{1,0:T(8,128)S(1)} %get-tuple-element.245), channel_id=1, source_target_pairs={{0,1},{1,0},{2,3},{3,2},{4,5},{5,4},{6,7},{7,6},{8,9},{9,8},{10,11... | collective-permute-start | bytes 786440 | tf_op jit(solution)/shard_map/ppermute | solution.py:334
  194.2 18.3 %collective-permute-start.52 = (f32[512,128]{1,0:T(8,128)S(1)}, f32[512,128]{1,0:T(8,128)S(1)}, u32[]{:S(2)}, u32[]{:S(2)}) collective-permute-start(f32[512,128]{1,0:T(8,128)S(1)} %get-tuple-element.246), channel_id=1, source_target_pairs={{0,9},{1,8},{2,11},{3,10},{4,13},{5,12},{6,15},{7,14},{8,1},{9,0},... | collective-permute-start | bytes 786440 | tf_op jit(solution)/shard_map/ppermute | solution.py:334
  197.5 25.3 %collective-permute-start.56 = (f32[16,128,128]{2,1,0:T(8,128)S(1)}, f32[16,128,128]{2,1,0:T(8,128)S(1)}, u32[]{:S(2)}, u32[]{:S(2)}) collective-permute-start(f32[16,128,128]{2,1,0:T(8,128)S(1)} %get-tuple-element.255.refs_26_.refs_30_.refs_6_.refs_7_), channel_id=1, source_target_pairs={{0,16},{16,0},{1,17},{17,1},{2,18},{18,2},{3,19},{19,3},{4,20},{20... | collective-permute-start | bytes 3145736 | tf_op jit(solution)/shard_map/ppermute | solution.py:362
  214.4 26.0 %collective-permute-start.71 = (f32[16,128,128]{2,1,0:T(8,128)S(1)}, f32[16,128,128]{2,1,0:T(8,128)S(1)}, u32[]{:S(2)}, u32[]{:S(2)}) collective-permute-start(f32[16,128,128]{2,1,0:T(8,128)S(1)} %get-tuple-element.283.refs_25_.refs_9_), channel_id=1, source_target_pairs={{0,4},{1,5},{2,0},{3,1},{4,6},{5,7},{6,2},{7,3},{8,12},{9,13},{10,... | collective-permute-start | bytes 3145736 | tf_op jit(solution)/shard_map/ppermute | solution.py:354
  215.3 16.7 %collective-permute-start.58 = (f32[8,128,128]{2,1,0:T(8,128)S(1)}, f32[8,128,128]{2,1,0:T(8,128)S(1)}, u32[]{:S(2)}, u32[]{:S(2)}) collective-permute-start(f32[8,128,128]{2,1,0:T(8,128)S(1)} %collective-permute-done.57.refs_28_.refs_5_), channel_id=1, source_target_pairs={{0,16},{16,0},{1,17},{17,1},{2,18},{18,2},{3,19},{19,3},{4,20},{20... | collective-permute-start | bytes 1572872 | tf_op jit(solution)/shard_map/ppermute | solution.py:362
  235.4 9.3 %collective-permute-start.60 = (f32[520,128]{1,0:T(8,128)S(1)}, f32[520,128]{1,0:T(8,128)S(1)}, u32[]{:S(2)}, u32[]{:S(2)}) collective-permute-start(f32[520,128]{1,0:T(8,128)S(1)} %get-tuple-element.263), channel_id=1, source_target_pairs={{0,1},{1,0},{2,3},{3,2},{4,5},{5,4},{6,7},{7,6},{8,9},{9,8},{10,11... | collective-permute-start | bytes 798728 | tf_op jit(solution)/shard_map/ppermute | solution.py:334
  236.6 12.9 %collective-permute-start.61 = (f32[520,128]{1,0:T(8,128)S(1)}, f32[520,128]{1,0:T(8,128)S(1)}, u32[]{:S(2)}, u32[]{:S(2)}) collective-permute-start(f32[520,128]{1,0:T(8,128)S(1)} %get-tuple-element.264), channel_id=1, source_target_pairs={{0,9},{1,8},{2,11},{3,10},{4,13},{5,12},{6,15},{7,14},{8,1},{9,0},... | collective-permute-start | bytes 798728 | tf_op jit(solution)/shard_map/ppermute | solution.py:334
  242.0 20.5 %collective-permute-start.73 = (f32[8,128,128]{2,1,0:T(8,128)S(1)}, f32[8,128,128]{2,1,0:T(8,128)S(1)}, u32[]{:S(2)}, u32[]{:S(2)}) collective-permute-start(f32[8,128,128]{2,1,0:T(8,128)S(1)} %get-tuple-element.284), channel_id=1, source_target_pairs={{0,4},{1,5},{2,0},{3,1},{4,6},{5,7},{6,2},{7,3},{8,12},{9,13},{10,... | collective-permute-start | bytes 1572872 | tf_op jit(solution)/shard_map/ppermute | solution.py:354
  244.1 39.1 %collective-permute-start.72 = (f32[16,128,128]{2,1,0:T(8,128)S(1)}, f32[16,128,128]{2,1,0:T(8,128)S(1)}, u32[]{:S(2)}, u32[]{:S(2)}) collective-permute-start(f32[16,128,128]{2,1,0:T(8,128)S(1)} %collective-permute-done.71.refs_1_.refs_26_.refs_30_.refs_10_.refs_14_), channel_id=1, source_target_pairs={{0,16},{16,0},{1,17},{17,1},{2,18},{18,2},{3,19},{19,3},{4,20},{20... | collective-permute-start | bytes 3145736 | tf_op jit(solution)/shard_map/ppermute | solution.py:362
  244.4 9.3 %collective-permute-start.65 = (f32[512,128]{1,0:T(8,128)S(1)}, f32[512,128]{1,0:T(8,128)S(1)}, u32[]{:S(2)}, u32[]{:S(2)}) collective-permute-start(f32[512,128]{1,0:T(8,128)S(1)} %get-tuple-element.270), channel_id=1, source_target_pairs={{0,8},{1,9},{2,10},{3,11},{4,12},{5,13},{6,14},{7,15},{8,0},{9,1},... | collective-permute-start | bytes 786440 | tf_op jit(solution)/shard_map/ppermute | solution.py:334
  244.7 11.3 %collective-permute-start.66 = (f32[512,128]{1,0:T(8,128)S(1)}, f32[512,128]{1,0:T(8,128)S(1)}, u32[]{:S(2)}, u32[]{:S(2)}) collective-permute-start(f32[512,128]{1,0:T(8,128)S(1)} %get-tuple-element.271), channel_id=1, source_target_pairs={{0,1},{1,0},{2,3},{3,2},{4,5},{5,4},{6,7},{7,6},{8,9},{9,8},{10,11... | collective-permute-start | bytes 786440 | tf_op jit(solution)/shard_map/ppermute | solution.py:334
  249.5 11.2 %collective-permute-start.67 = (f32[512,128]{1,0:T(8,128)S(1)}, f32[512,128]{1,0:T(8,128)S(1)}, u32[]{:S(2)}, u32[]{:S(2)}) collective-permute-start(f32[512,128]{1,0:T(8,128)S(1)} %get-tuple-element.272), channel_id=1, source_target_pairs={{0,9},{1,8},{2,11},{3,10},{4,13},{5,12},{6,15},{7,14},{8,1},{9,0},... | collective-permute-start | bytes 786440 | tf_op jit(solution)/shard_map/ppermute | solution.py:334
  253.7 11.8 %collective-permute-start.62 = (f32[512,128]{1,0:T(8,128)S(1)}, f32[512,128]{1,0:T(8,128)S(1)}, u32[]{:S(2)}, u32[]{:S(2)}) collective-permute-start(f32[512,128]{1,0:T(8,128)S(1)} %get-tuple-element.266), channel_id=1, source_target_pairs={{0,8},{1,9},{2,10},{3,11},{4,12},{5,13},{6,14},{7,15},{8,0},{9,1},... | collective-permute-start | bytes 786440 | tf_op jit(solution)/shard_map/ppermute | solution.py:334
  256.0 11.2 %collective-permute-start.63 = (f32[512,128]{1,0:T(8,128)S(1)}, f32[512,128]{1,0:T(8,128)S(1)}, u32[]{:S(2)}, u32[]{:S(2)}) collective-permute-start(f32[512,128]{1,0:T(8,128)S(1)} %get-tuple-element.267), channel_id=1, source_target_pairs={{0,1},{1,0},{2,3},{3,2},{4,5},{5,4},{6,7},{7,6},{8,9},{9,8},{10,11... | collective-permute-start | bytes 786440 | tf_op jit(solution)/shard_map/ppermute | solution.py:334
  260.7 11.2 %collective-permute-start.64 = (f32[512,128]{1,0:T(8,128)S(1)}, f32[512,128]{1,0:T(8,128)S(1)}, u32[]{:S(2)}, u32[]{:S(2)}) collective-permute-start(f32[512,128]{1,0:T(8,128)S(1)} %get-tuple-element.268), channel_id=1, source_target_pairs={{0,9},{1,8},{2,11},{3,10},{4,13},{5,12},{6,15},{7,14},{8,1},{9,0},... | collective-permute-start | bytes 786440 | tf_op jit(solution)/shard_map/ppermute | solution.py:334
  262.5 20.7 %collective-permute-start.74 = (f32[8,128,128]{2,1,0:T(8,128)S(1)}, f32[8,128,128]{2,1,0:T(8,128)S(1)}, u32[]{:S(2)}, u32[]{:S(2)}) collective-permute-start(f32[8,128,128]{2,1,0:T(8,128)S(1)} %collective-permute-done.73.refs_28_.refs_12_), channel_id=1, source_target_pairs={{0,16},{16,0},{1,17},{17,1},{2,18},{18,2},{3,19},{19,3},{4,20},{20... | collective-permute-start | bytes 1572872 | tf_op jit(solution)/shard_map/ppermute | solution.py:362
  267.3 11.2 %collective-permute-start.69 = (f32[512,128]{1,0:T(8,128)S(1)}, f32[512,128]{1,0:T(8,128)S(1)}, u32[]{:S(2)}, u32[]{:S(2)}) collective-permute-start(f32[512,128]{1,0:T(8,128)S(1)} %get-tuple-element.276), channel_id=1, source_target_pairs={{0,1},{1,0},{2,3},{3,2},{4,5},{5,4},{6,7},{7,6},{8,9},{9,8},{10,11... | collective-permute-start | bytes 786440 | tf_op jit(solution)/shard_map/ppermute | solution.py:334
  272.0 11.2 %collective-permute-start.70 = (f32[512,128]{1,0:T(8,128)S(1)}, f32[512,128]{1,0:T(8,128)S(1)}, u32[]{:S(2)}, u32[]{:S(2)}) collective-permute-start(f32[512,128]{1,0:T(8,128)S(1)} %get-tuple-element.277), channel_id=1, source_target_pairs={{0,9},{1,8},{2,11},{3,10},{4,13},{5,12},{6,15},{7,14},{8,1},{9,0},... | collective-permute-start | bytes 786440 | tf_op jit(solution)/shard_map/ppermute | solution.py:334
  286.9 25.1 %collective-permute-start.75 = (f32[520,128]{1,0:T(8,128)S(1)}, f32[520,128]{1,0:T(8,128)S(1)}, u32[]{:S(2)}, u32[]{:S(2)}) collective-permute-start(f32[520,128]{1,0:T(8,128)S(1)} %get-tuple-element.287), channel_id=1, source_target_pairs={{0,8},{1,9},{2,10},{3,11},{4,12},{5,13},{6,14},{7,15},{8,0},{9,1},... | collective-permute-start | bytes 798728 | tf_op jit(solution)/shard_map/ppermute | solution.py:334
  287.1 24.9 %collective-permute-start.76 = (f32[520,128]{1,0:T(8,128)S(1)}, f32[520,128]{1,0:T(8,128)S(1)}, u32[]{:S(2)}, u32[]{:S(2)}) collective-permute-start(f32[520,128]{1,0:T(8,128)S(1)} %get-tuple-element.288), channel_id=1, source_target_pairs={{0,1},{1,0},{2,3},{3,2},{4,5},{5,4},{6,7},{7,6},{8,9},{9,8},{10,11... | collective-permute-start | bytes 798728 | tf_op jit(solution)/shard_map/ppermute | solution.py:334
  288.2 23.8 %collective-permute-start.77 = (f32[520,128]{1,0:T(8,128)S(1)}, f32[520,128]{1,0:T(8,128)S(1)}, u32[]{:S(2)}, u32[]{:S(2)}) collective-permute-start(f32[520,128]{1,0:T(8,128)S(1)} %get-tuple-element.289), channel_id=1, source_target_pairs={{0,9},{1,8},{2,11},{3,10},{4,13},{5,12},{6,15},{7,14},{8,1},{9,0},... | collective-permute-start | bytes 798728 | tf_op jit(solution)/shard_map/ppermute | solution.py:334
  288.7 18.9 %collective-permute-start.79 = (f32[512,128]{1,0:T(8,128)S(1)}, f32[512,128]{1,0:T(8,128)S(1)}, u32[]{:S(2)}, u32[]{:S(2)}) collective-permute-start(f32[512,128]{1,0:T(8,128)S(1)} %get-tuple-element.292), channel_id=1, source_target_pairs={{0,1},{1,0},{2,3},{3,2},{4,5},{5,4},{6,7},{7,6},{8,9},{9,8},{10,11... | collective-permute-start | bytes 786440 | tf_op jit(solution)/shard_map/ppermute | solution.py:334
  289.9 22.1 %collective-permute-start.80 = (f32[512,128]{1,0:T(8,128)S(1)}, f32[512,128]{1,0:T(8,128)S(1)}, u32[]{:S(2)}, u32[]{:S(2)}) collective-permute-start(f32[512,128]{1,0:T(8,128)S(1)} %get-tuple-element.293), channel_id=1, source_target_pairs={{0,9},{1,8},{2,11},{3,10},{4,13},{5,12},{6,15},{7,14},{8,1},{9,0},... | collective-permute-start | bytes 786440 | tf_op jit(solution)/shard_map/ppermute | solution.py:334
  317.7 10.0 %collective-permute-start.89 = (f32[256,128]{1,0:T(8,128)S(1)}, f32[256,128]{1,0:T(8,128)S(1)}, u32[]{:S(2)}, u32[]{:S(2)}) collective-permute-start(f32[256,128]{1,0:T(8,128)S(1)} %get-tuple-element.308), channel_id=1, source_target_pairs={{0,1},{1,0},{2,3},{3,2},{4,5},{5,4},{6,7},{7,6},{8,9},{9,8},{10,11... | collective-permute-start | bytes 393224 | tf_op jit(solution)/shard_map/ppermute | solution.py:334
  318.8 10.2 %collective-permute-start.90 = (f32[256,128]{1,0:T(8,128)S(1)}, f32[256,128]{1,0:T(8,128)S(1)}, u32[]{:S(2)}, u32[]{:S(2)}) collective-permute-start(f32[256,128]{1,0:T(8,128)S(1)} %get-tuple-element.309), channel_id=1, source_target_pairs={{0,9},{1,8},{2,11},{3,10},{4,13},{5,12},{6,15},{7,14},{8,1},{9,0},... | collective-permute-start | bytes 393224 | tf_op jit(solution)/shard_map/ppermute | solution.py:334
  321.9 11.4 %collective-permute-start.84 = (f32[256,128]{1,0:T(8,128)S(1)}, f32[256,128]{1,0:T(8,128)S(1)}, u32[]{:S(2)}, u32[]{:S(2)}) collective-permute-start(f32[256,128]{1,0:T(8,128)S(1)} %get-tuple-element.301), channel_id=1, source_target_pairs={{0,8},{1,9},{2,10},{3,11},{4,12},{5,13},{6,14},{7,15},{8,0},{9,1},... | collective-permute-start | bytes 393224 | tf_op jit(solution)/shard_map/ppermute | solution.py:334
  323.3 10.0 %collective-permute-start.85 = (f32[256,128]{1,0:T(8,128)S(1)}, f32[256,128]{1,0:T(8,128)S(1)}, u32[]{:S(2)}, u32[]{:S(2)}) collective-permute-start(f32[256,128]{1,0:T(8,128)S(1)} %get-tuple-element.302), channel_id=1, source_target_pairs={{0,1},{1,0},{2,3},{3,2},{4,5},{5,4},{6,7},{7,6},{8,9},{9,8},{10,11... | collective-permute-start | bytes 393224 | tf_op jit(solution)/shard_map/ppermute | solution.py:334
  324.2 9.9 %collective-permute-start.86 = (f32[256,128]{1,0:T(8,128)S(1)}, f32[256,128]{1,0:T(8,128)S(1)}, u32[]{:S(2)}, u32[]{:S(2)}) collective-permute-start(f32[256,128]{1,0:T(8,128)S(1)} %get-tuple-element.303), channel_id=1, source_target_pairs={{0,9},{1,8},{2,11},{3,10},{4,13},{5,12},{6,15},{7,14},{8,1},{9,0},... | collective-permute-start | bytes 393224 | tf_op jit(solution)/shard_map/ppermute | solution.py:334
  327.6 18.4 %collective-permute-start.95 = (f32[128,1024]{1,0:T(8,128)}, f32[128,1024]{1,0:T(8,128)}, u32[]{:S(2)}, u32[]{:S(2)}) collective-permute-start(f32[128,1024]{1,0:T(8,128)} %get-tuple-element.316), channel_id=1, source_target_pairs={{0,4},{1,5},{2,0},{3,1},{4,6},{5,7},{6,2},{7,3},{8,12},{9,13},{10,... | collective-permute-start | bytes 1572872 | tf_op jit(solution)/shard_map/ppermute | solution.py:334
  330.7 24.3 %collective-permute-start.91 = (f32[128,1024]{1,0:T(8,128)}, f32[128,1024]{1,0:T(8,128)}, u32[]{:S(2)}, u32[]{:S(2)}) collective-permute-start(f32[128,1024]{1,0:T(8,128)} %get-tuple-element.310), channel_id=1, source_target_pairs={{0,6},{1,7},{2,4},{3,5},{4,2},{5,3},{6,0},{7,1},{8,14},{9,15},{10,... | collective-permute-start | bytes 1572872 | tf_op jit(solution)/shard_map/ppermute | solution.py:334
  336.0 40.3 %collective-permute-start.87 = (f32[128,1024]{1,0:T(8,128)}, f32[128,1024]{1,0:T(8,128)}, u32[]{:S(2)}, u32[]{:S(2)}) collective-permute-start(f32[128,1024]{1,0:T(8,128)} %get-tuple-element.304), channel_id=1, source_target_pairs={{0,2},{1,3},{2,6},{3,7},{4,0},{5,1},{6,4},{7,5},{8,10},{9,11},{10,... | collective-permute-start | bytes 1572872 | tf_op jit(solution)/shard_map/ppermute | solution.py:334
  (37 other events, 222.3 us)

commit v6 on v5

--- a/solution.py
+++ b/solution.py
@@ -408,6 +408,19 @@
         passed, kept = copied(place, [near], outs, moves, waits, False)
         return group_ring(passed), kept
 
+    def near_halves(near, waits):
+        moves, outs = [], []
+        for n in range(2):
+            moves.append((0, lambda p, n=n: pl.ds(n * ROWS + p[2] * 4, 4), 2 * n, pl.ds(0, 4), None))
+            moves.append((0, lambda p, n=n: pl.ds(n * ROWS, ROWS), 2 * n + 1, pl.ds(0, ROWS), None))
+            outs += [array(4, LANES, LANES), array(*PIECE)]
+        passed, kept, left_passed, left_kept = copied(place, [near], outs, moves, waits, False)
+        return (group_ring(passed), kept), (group_ring(left_passed), left_kept)
+
+    def apart(part, n, far, near):
+        near_pair, far_pair = (near, group_swap(near)), (far, group_swap(far))
+        return [("whole", n * ROWS, (part,)), ("next", 0, near_pair), ("halves", 0, far_pair), ("previous", 0, near_pair)]
+
     def four_pieces(part, far, near):
         near_pair, far_pair = (near, group_swap(near)), (far, group_swap(far))
         return [
@@ -428,23 +441,25 @@
 
     current, gain, rows, came = [None] * PLANES, [None] * PLANES, [None] * PLANES, [None] * PLANES
     waits = []
+    near_pair = near, group_swap(near)
     for step in (0, 1, 3, 2):
-        if step == 1:
-            far, near = near_half(near, [*arrived[1:4:2], mark])
-            (right_parts[0],) = four_pieces(part, far, near)
-        weights = right_parts[0][step] if step else ("whole", 0, (part,))
+        weights = [("whole", 0, (part,)), ("next", 0, near_pair), None, ("previous", 0, near_pair)][step]
+        if step == 2:
+            weights = ("halves", 0, (far, group_swap(far)))
         results, sends, mark = first_piece(step, place, arrived[step], weights, waits)
         waits = [mark]
         current[step], gain[step], rows[step] = results
         came[step] = exchange(sends)
+        if step == 1:
+            far, _ = near_half(near, [*arrived[1:], mark])
         if step == 3:
-            left = own(pairs[1:], 0, [arrived[2], far, mark, *came[0][2:], *came[1][2:]])
+            left = own(pairs[1:], 0, [arrived[2], mark, *came[0][2:], *came[1][2:]])
             left_near = group_ring(left)
     far, near = near_half(left_near, [mark, *came[3][2:]])
     (left_parts[0],) = four_pieces(left, far, near)
-    right = own(pairs[:1], 1, [far, *came[2][2:], left_parts[0][1][2][1]])
+    right = own(pairs[:1], 1, [far, *came[2][2:]])
     right_near = group_ring(right)
-    left = own(pairs[1:], 1, [right])
+    left = own(pairs[1:], 1, [right, left_parts[0][1][2][1]])
     left_near = group_ring(left)
     for layer in range(layers - 1):
         in_pieces = layer == 0
@@ -464,12 +479,15 @@
         if layer == 0:
             far, near = near_half(right_near, marks)
             (right_parts[1],) = four_pieces(right, far, near)
-            right_last = right_parts[1][2][2][1]
+            right_last = [right_parts[1][2][2][1]]
             far, near = near_half(left_near, [far, right_parts[1][1][2][1], *mixed[0][2:]])
             (left_parts[1],) = four_pieces(left, far, near)
             pairs = [swapped(factors, 1, marks) for factors in (right_factors, left_factors)]
+        if layer == 2:
+            far, _ = near_half(near, marks)
+            right_parts[3], left_parts[3] = four_pieces(part, far, near)
         if layer + 2 < layers:
-            waits = [far, mark if layer else right_last, *mixed[0][2:], *mixed[1][2:]]
+            waits = [far, *right_last, *mixed[0][2:], *mixed[1][2:]]
             part = own(pairs, layer % 2, waits)
             near = group_ring(part)
         current, sends, mark = layer_edge(
@@ -478,13 +496,11 @@
         gain = next_gain
         came = [exchange(sends[0]), exchange(sends[1])]
         if layer + 2 < layers:
-            waits = ()
             if layer == 0:
                 swaps = left_parts[1][1][2][1], left_parts[1][2][2][1]
-                waits = [mark, *came[0][2:], *swaps]
-            far, kept = near_half(near, waits)
-            near = near if layer else kept
-            right_parts[layer + 2], left_parts[layer + 2] = four_pieces(part, far, near)
+                moved = near_halves(near, [mark, *came[0][2:], *swaps])
+                right_parts[2], left_parts[2] = [apart(part, n, *moved[n]) for n in range(2)]
+                far, right_last = moved[1][0], [right_parts[2][n][2][1] for n in (1, 2)]
 
     squares = came[0]
     sends, _, _ = column_stage(tuple(range(PLANES)), False, True, place, came, left_parts[-1], ())

time: 383 us -> 388 us (1.013)
  waiting for transfers between devices: 209 us -> 222 us
  starting transfers between devices: 97 us -> 87.6 us
    ppermute x73, waiting for transfers between devices: 134 us -> 157 us  [routed(): return lax.ppermute(value, ('segment', 'block'), route)]
    ppermute x12 -> x13, waiting for transfers between devices: 47.6 us -> 29.1 us  [group_ring(): return lax.ppermute(value, ('groups', 'segment', 'block'), route)]
    ppermute x73, starting transfers between devices: 56 us -> 45.4 us  [routed(): return lax.ppermute(value, ('segment', 'block'), route)]
    ppermute x12 -> x14, waiting for transfers between devices: 27.3 us -> 35.7 us  [group_swap(): return lax.ppermute(value, 'groups', [(0, 1), (1, 0)])]
    ppermute x12 -> x14, starting transfers between devices: 14.1 us -> 19.3 us  [group_swap(): return lax.ppermute(value, 'groups', [(0, 1), (1, 0)])]
    ppermute x12 -> x13, starting transfers between devices: 26.8 us -> 22.9 us  [group_ring(): return lax.ppermute(value, ('groups', 'segment', 'block'), route)]
  transfers between devices with their start and end apart: 97 -> 100, of which waited for: 52 -> 50; matrix products, arithmetic and copies ran while one was open for 0% -> 0% of each run, Pallas kernels for 15% -> 15%
where the time goes in v6:
time: 388 us
  waiting for transfers between devices  222 us (57%)
  starting transfers between devices  87.6 us (23%)
  Pallas kernels  70.4 us (18%)
  other arithmetic  4.42 us (1%)
    ppermute x73, waiting for transfers between devices, routed(): return lax.ppermute(value, ('segment', 'block'), route)  157 us
    pallas_call x35, Pallas kernels, call(): pl.pallas_call(functools.partial(marked, kernel, len(operands), len(waits...  70.4 us
    ppermute x73, starting transfers between devices, routed(): return lax.ppermute(value, ('segment', 'block'), route)  45.4 us
    ppermute x14, waiting for transfers between devices, group_swap(): return lax.ppermute(value, 'groups', [(0, 1), (1, 0)])  35.7 us
    ppermute x13, waiting for transfers between devices, group_ring(): return lax.ppermute(value, ('groups', 'segment', 'block'), route)  29.1 us
    ppermute x13, starting transfers between devices, group_ring(): return lax.ppermute(value, ('groups', 'segment', 'block'), route)  22.9 us
    ppermute x14, starting transfers between devices, group_swap(): return lax.ppermute(value, 'groups', [(0, 1), (1, 0)])  19.3 us
  transfers between devices with their start and end apart: 100, of which 50 were waited for; matrix products, arithmetic and copies ran while one was open for 0% of the time, Pallas kernels for 15%

profile of v6, /device:TPU:0, one launch (start us, length us, event | category | flops | bytes accessed | tf_op | source)
XLA Modules:
  0.0 387.7 jit_solution(3174668916258788933)
XLA Ops:
  0.0 2.5 constant_dynamic-slice_fusion.4
  4.2 1.9 collective-permute-done.2.refs_2_
  7.3 3.9 collective-permute-start.4
  16.3 7.1 %collective-permute-done.4.refs_2_.refs_1_ = f32[8,128,128]{2,1,0:T(8,128)S(1)} collective-permute-done((f32[8,128,128]{2,1,0:T(8,128)S(1)}, f32[8,128,128]{2,1,0:T(8,128)S(1)}, u32[]{:S(2)}, u32[]{:S(2)}) %collective-permute-start.4) | collective-permute-done | bytes 524320 | tf_op jit(solution)/shard_map/ppermute | solution.py:354
  23.4 2.5 collective-permute-start.5
  29.6 7.1 %collective-permute-done.5.refs_3_ = f32[8,128,128]{2,1,0:T(8,128)S(1)} collective-permute-done((f32[8,128,128]{2,1,0:T(8,128)S(1)}, f32[8,128,128]{2,1,0:T(8,128)S(1)}, u32[]{:S(2)}, u32[]{:S(2)}) %collective-permute-start.5) | collective-permute-done | bytes 524320 | tf_op jit(solution)/shard_map/ppermute | solution.py:362
  38.2 2.4 shard_map.50
  40.6 8.5 %collective-permute-done.6.refs_3_.refs_1_ = f32[136,1024]{1,0:T(8,128)S(1)} collective-permute-done((f32[136,1024]{1,0:T(8,128)S(1)}, f32[136,1024]{1,0:T(8,128)S(1)}, u32[]{:S(2)}, u32[]{:S(2)}) %collective-permute-start.6) | collective-permute-done | bytes 557088 | tf_op jit(solution)/shard_map/ppermute | solution.py:334
  50.6 21.7 %collective-permute-done.7.refs_4_.refs_1_ = f32[136,1024]{1,0:T(8,128)S(1)} collective-permute-done((f32[136,1024]{1,0:T(8,128)S(1)}, f32[136,1024]{1,0:T(8,128)S(1)}, u32[]{:S(2)}, u32[]{:S(2)}) %collective-permute-start.7) | collective-permute-done | bytes 557088 | tf_op jit(solution)/shard_map/ppermute | solution.py:334
  73.5 2.1 shard_map.51
  75.6 2.4 shard_map.52
  79.9 3.1 collective-permute-start.23
  86.9 5.4 %collective-permute-done.9.refs_3_ = f32[4,128,128]{2,1,0:T(8,128)S(1)} collective-permute-done((f32[4,128,128]{2,1,0:T(8,128)S(1)}, f32[4,128,128]{2,1,0:T(8,128)S(1)}, u32[]{:S(2)}, u32[]{:S(2)}) %collective-permute-start.9) | collective-permute-done | bytes 262176 | tf_op jit(solution)/shard_map/ppermute | solution.py:362
  92.3 2.4 shard_map.53
  97.3 2.4 collective-permute-start.28
  101.4 4.7 %collective-permute-done.17.refs_11_.refs_4_.refs_19_ = f32[264,128]{1,0:T(8,128)S(1)} collective-permute-done((f32[264,128]{1,0:T(8,128)S(1)}, f32[264,128]{1,0:T(8,128)S(1)}, u32[]{:S(2)}, u32[]{:S(2)}) %collective-permute-start.17) | collective-permute-done | bytes 135200 | tf_op jit(solution)/shard_map/ppermute | solution.py:334
  107.3 2.1 collective-permute-start.33
  109.9 2.1 collective-permute-start.29
  114.4 2.5 shard_map.57
  116.9 2.2 collective-permute-start.26
  121.9 2.6 shard_map.58
  126.3 2.2 collective-permute-start.34
  133.1 7.1 %collective-permute-done.35.refs_40_.refs_2_ = f32[4,128,128]{2,1,0:T(8,128)S(1)} collective-permute-done((f32[4,128,128]{2,1,0:T(8,128)S(1)}, f32[4,128,128]{2,1,0:T(8,128)S(1)}, u32[]{:S(2)}, u32[]{:S(2)}) %collective-permute-start.35) | collective-permute-done | bytes 262176 | tf_op jit(solution)/shard_map/ppermute | solution.py:354
  141.5 1.8 collective-permute-start.36
  145.1 3.0 collective-permute-done.32.refs_32_.refs_10_
  148.1 2.0 collective-permute-done.36.refs_41_.refs_6_
  150.1 2.5 collective-permute-done.48.refs_5_
  157.4 3.4 shard_map.61
  164.7 5.5 %collective-permute-done.38.refs_3_.refs_11_ = f32[520,128]{1,0:T(8,128)S(1)} collective-permute-done((f32[520,128]{1,0:T(8,128)S(1)}, f32[520,128]{1,0:T(8,128)S(1)}, u32[]{:S(2)}, u32[]{:S(2)}) %collective-permute-start.38) | collective-permute-done | bytes 266272 | tf_op jit(solution)/shard_map/ppermute | solution.py:334
  170.2 4.6 %collective-permute-done.39.refs_4_.refs_12_ = f32[520,128]{1,0:T(8,128)S(1)} collective-permute-done((f32[520,128]{1,0:T(8,128)S(1)}, f32[520,128]{1,0:T(8,128)S(1)}, u32[]{:S(2)}, u32[]{:S(2)}) %collective-permute-start.39) | collective-permute-done | bytes 266272 | tf_op jit(solution)/shard_map/ppermute | solution.py:334
  177.4 2.5 shard_map.64
  179.9 2.7 collective-permute-done.49.refs_6_
  183.7 1.9 shard_map.69
  189.0 2.6 shard_map.65
  192.8 2.4 collective-permute-done.43.refs_15_.refs_8_
  195.4 4.8 %collective-permute-done.44.refs_16_.refs_9_ = f32[512,128]{1,0:T(8,128)S(1)} collective-permute-done((f32[512,128]{1,0:T(8,128)S(1)}, f32[512,128]{1,0:T(8,128)S(1)}, u32[]{:S(2)}, u32[]{:S(2)}) %collective-permute-start.44) | collective-permute-done | bytes 262176 | tf_op jit(solution)/shard_map/ppermute | solution.py:334
  202.9 3.6 collective-permute-done.51.refs_19_.refs_10_
  206.4 5.0 %collective-permute-done.52.refs_20_.refs_11_ = f32[512,128]{1,0:T(8,128)S(1)} collective-permute-done((f32[512,128]{1,0:T(8,128)S(1)}, f32[512,128]{1,0:T(8,128)S(1)}, u32[]{:S(2)}, u32[]{:S(2)}) %collective-permute-start.52) | collective-permute-done | bytes 262176 | tf_op jit(solution)/shard_map/ppermute | solution.py:334
  216.2 3.3 shard_map.70
  221.4 7.2 %collective-permute-done.62.refs_7_.refs_8_ = f32[8,128,128]{2,1,0:T(8,128)S(1)} collective-permute-done((f32[8,128,128]{2,1,0:T(8,128)S(1)}, f32[8,128,128]{2,1,0:T(8,128)S(1)}, u32[]{:S(2)}, u32[]{:S(2)}) %collective-permute-start.62) | collective-permute-done | bytes 524320 | tf_op jit(solution)/shard_map/ppermute | solution.py:362
  231.0 2.4 collective-permute-done.61.refs_4_.refs_12_
  233.5 2.0 collective-permute-start.68
  235.5 2.5 shard_map.71
  238.0 2.2 collective-permute-done.67.refs_3_
  240.2 4.5 %collective-permute-done.68.refs_4_ = f32[512,128]{1,0:T(8,128)S(1)} collective-permute-done((f32[512,128]{1,0:T(8,128)S(1)}, f32[512,128]{1,0:T(8,128)S(1)}, u32[]{:S(2)}, u32[]{:S(2)}) %collective-permute-start.68) | collective-permute-done | bytes 262176 | tf_op jit(solution)/shard_map/ppermute | solution.py:334
  244.7 2.6 shard_map.72
  247.3 2.3 shard_map.74
  249.6 3.0 collective-permute-start.76
  254.5 9.8 %collective-permute-done.76.refs_28_.refs_12_ = f32[8,128,128]{2,1,0:T(8,128)S(1)} collective-permute-done((f32[8,128,128]{2,1,0:T(8,128)S(1)}, f32[8,128,128]{2,1,0:T(8,128)S(1)}, u32[]{:S(2)}, u32[]{:S(2)}) %collective-permute-start.76) | collective-permute-done | bytes 524320 | tf_op jit(solution)/shard_map/ppermute | solution.py:354
  264.4 1.8 collective-permute-start.77
  268.1 7.3 %collective-permute-done.72.refs_19_ = f32[512,128]{1,0:T(8,128)S(1)} collective-permute-done((f32[512,128]{1,0:T(8,128)S(1)}, f32[512,128]{1,0:T(8,128)S(1)}, u32[]{:S(2)}, u32[]{:S(2)}) %collective-permute-start.72) | collective-permute-done | bytes 262176 | tf_op jit(solution)/shard_map/ppermute | solution.py:334
  275.4 4.7 %collective-permute-done.73.refs_20_ = f32[512,128]{1,0:T(8,128)S(1)} collective-permute-done((f32[512,128]{1,0:T(8,128)S(1)}, f32[512,128]{1,0:T(8,128)S(1)}, u32[]{:S(2)}, u32[]{:S(2)}) %collective-permute-start.73) | collective-permute-done | bytes 262176 | tf_op jit(solution)/shard_map/ppermute | solution.py:334
  280.1 8.9 %collective-permute-done.77.refs_29_.refs_13_ = f32[8,128,128]{2,1,0:T(8,128)S(1)} collective-permute-done((f32[8,128,128]{2,1,0:T(8,128)S(1)}, f32[8,128,128]{2,1,0:T(8,128)S(1)}, u32[]{:S(2)}, u32[]{:S(2)}) %collective-permute-start.77) | collective-permute-done | bytes 524320 | tf_op jit(solution)/shard_map/ppermute | solution.py:362
  289.0 3.2 shard_map.75
  296.3 17.1 %collective-permute-done.82.refs_7_ = f32[512,128]{1,0:T(8,128)S(1)} collective-permute-done((f32[512,128]{1,0:T(8,128)S(1)}, f32[512,128]{1,0:T(8,128)S(1)}, u32[]{:S(2)}, u32[]{:S(2)}) %collective-permute-start.82) | collective-permute-done | bytes 262176 | tf_op jit(solution)/shard_map/ppermute | solution.py:334
  313.4 3.9 collective-permute-done.83.refs_8_
  317.3 3.0 shard_map.76
  324.5 2.9 collective-permute-done.96.refs_9_
  336.7 1.9 collective-permute-done.88.refs_9_
  344.8 4.3 %collective-permute-done.85.refs_9_ = f32[256,128]{1,0:T(8,128)S(1)} collective-permute-done((f32[256,128]{1,0:T(8,128)S(1)}, f32[256,128]{1,0:T(8,128)S(1)}, u32[]{:S(2)}, u32[]{:S(2)}) %collective-permute-start.85) | collective-permute-done | bytes 131104 | tf_op jit(solution)/shard_map/ppermute | solution.py:334
  351.5 5.5 %collective-permute-done.98 = f32[128,1024]{1,0:T(8,128)} collective-permute-done((f32[128,1024]{1,0:T(8,128)}, f32[128,1024]{1,0:T(8,128)}, u32[]{:S(2)}, u32[]{:S(2)}) %collective-permute-start.98) | collective-permute-done | bytes 524320 | tf_op jit(solution)/shard_map/ppermute | solution.py:334
  357.0 2.3 collective-permute-done.94
  359.4 21.1 %collective-permute-done.90 = f32[128,1024]{1,0:T(8,128)} collective-permute-done((f32[128,1024]{1,0:T(8,128)}, f32[128,1024]{1,0:T(8,128)}, u32[]{:S(2)}, u32[]{:S(2)}) %collective-permute-start.90) | collective-permute-done | bytes 524320 | tf_op jit(solution)/shard_map/ppermute | solution.py:334
  383.3 2.8 collective-permute-done.99
  (191 shorter events, 105.6 us)
Async XLA Ops:
  2.5 9.9 %collective-permute-start = (f32[256,1024]{1,0:T(8,128)}, f32[256,1024]{1,0:T(8,128)S(1)}, u32[]{:S(2)}, u32[]{:S(2)}) collective-permute-start(f32[256,1024]{1,0:T(8,128)} %constant_dynamic-slice_fusion.4), channel_id=1, source_target_pairs={{0,8},{1,9},{2,10},{3,11},{4,12},{5,13},{6,14},{7,15},{8,0},{9,1},... | collective-permute-start | bytes 3145736 | tf_op jit(solution)/shard_map/ppermute | solution.py:334
  7.3 16.2 %collective-permute-start.4 = (f32[8,128,128]{2,1,0:T(8,128)S(1)}, f32[8,128,128]{2,1,0:T(8,128)S(1)}, u32[]{:S(2)}, u32[]{:S(2)}) collective-permute-start(f32[8,128,128]{2,1,0:T(8,128)S(1)} %get-tuple-element.164.refs_2_), channel_id=1, source_target_pairs={{0,4},{1,5},{2,0},{3,1},{4,6},{5,7},{6,2},{7,3},{8,12},{9,13},{10,... | collective-permute-start | bytes 1572872 | tf_op jit(solution)/shard_map/ppermute | solution.py:354
  13.8 24.3 %collective-permute-start.3 = (f32[136,1024]{1,0:T(8,128)S(1)}, f32[136,1024]{1,0:T(8,128)S(1)}, u32[]{:S(2)}, u32[]{:S(2)}) collective-permute-start(f32[136,1024]{1,0:T(8,128)S(1)} %get-tuple-element.166), channel_id=1, source_target_pairs={{0,4},{1,5},{2,0},{3,1},{4,6},{5,7},{6,2},{7,3},{8,12},{9,13},{10,... | collective-permute-start | bytes 1671176 | tf_op jit(solution)/shard_map/ppermute | solution.py:334
  15.4 33.7 %collective-permute-start.6 = (f32[136,1024]{1,0:T(8,128)S(1)}, f32[136,1024]{1,0:T(8,128)S(1)}, u32[]{:S(2)}, u32[]{:S(2)}) collective-permute-start(f32[136,1024]{1,0:T(8,128)S(1)} %get-tuple-element.169), channel_id=1, source_target_pairs={{0,6},{1,7},{2,4},{3,5},{4,2},{5,3},{6,0},{7,1},{8,14},{9,15},{10,... | collective-permute-start | bytes 1671176 | tf_op jit(solution)/shard_map/ppermute | solution.py:334
  15.4 56.9 %collective-permute-start.7 = (f32[136,1024]{1,0:T(8,128)S(1)}, f32[136,1024]{1,0:T(8,128)S(1)}, u32[]{:S(2)}, u32[]{:S(2)}) collective-permute-start(f32[136,1024]{1,0:T(8,128)S(1)} %get-tuple-element.170), channel_id=1, source_target_pairs={{0,2},{1,3},{2,6},{3,7},{4,0},{5,1},{6,4},{7,5},{8,10},{9,11},{10,... | collective-permute-start | bytes 1671176 | tf_op jit(solution)/shard_map/ppermute | solution.py:334
  23.4 13.2 %collective-permute-start.5 = (f32[8,128,128]{2,1,0:T(8,128)S(1)}, f32[8,128,128]{2,1,0:T(8,128)S(1)}, u32[]{:S(2)}, u32[]{:S(2)}) collective-permute-start(f32[8,128,128]{2,1,0:T(8,128)S(1)} %collective-permute-done.4.refs_2_.refs_1_), channel_id=1, source_target_pairs={{0,16},{16,0},{1,17},{17,1},{2,18},{18,2},{3,19},{19,3},{4,20},{20... | collective-permute-start | bytes 1572872 | tf_op jit(solution)/shard_map/ppermute | solution.py:362
  27.7 50.3 %collective-permute-start.22 = (f32[8,128,128]{2,1,0:T(8,128)S(1)}, f32[8,128,128]{2,1,0:T(8,128)S(1)}, u32[]{:S(2)}, u32[]{:S(2)}) collective-permute-start(f32[8,128,128]{2,1,0:T(8,128)S(1)} %get-tuple-element.197), channel_id=1, source_target_pairs={{0,8},{1,9},{2,10},{3,11},{4,12},{5,13},{6,14},{7,15},{8,0},{9,1},... | collective-permute-start | bytes 1572872 | tf_op jit(solution)/shard_map/ppermute | solution.py:334
  36.6 38.9 %collective-permute-start.11 = (f32[264,128]{1,0:T(8,128)S(1)}, f32[264,128]{1,0:T(8,128)S(1)}, u32[]{:S(2)}, u32[]{:S(2)}) collective-permute-start(f32[264,128]{1,0:T(8,128)S(1)} %get-tuple-element.182), channel_id=1, source_target_pairs={{0,1},{1,0},{2,3},{3,2},{4,5},{5,4},{6,7},{7,6},{8,9},{9,8},{10,11... | collective-permute-start | bytes 405512 | tf_op jit(solution)/shard_map/ppermute | solution.py:334
  38.2 39.9 %collective-permute-start.12 = (f32[264,128]{1,0:T(8,128)S(1)}, f32[264,128]{1,0:T(8,128)S(1)}, u32[]{:S(2)}, u32[]{:S(2)}) collective-permute-start(f32[264,128]{1,0:T(8,128)S(1)} %get-tuple-element.183), channel_id=1, source_target_pairs={{0,9},{1,8},{2,11},{3,10},{4,13},{5,12},{6,15},{7,14},{8,1},{9,0},... | collective-permute-start | bytes 405512 | tf_op jit(solution)/shard_map/ppermute | solution.py:334
  49.1 28.9 %collective-permute-start.14 = (f32[264,128]{1,0:T(8,128)S(1)}, f32[264,128]{1,0:T(8,128)S(1)}, u32[]{:S(2)}, u32[]{:S(2)}) collective-permute-start(f32[264,128]{1,0:T(8,128)S(1)} %get-tuple-element.186), channel_id=1, source_target_pairs={{0,1},{1,0},{2,3},{3,2},{4,5},{5,4},{6,7},{7,6},{8,9},{9,8},{10,11... | collective-permute-start | bytes 405512 | tf_op jit(solution)/shard_map/ppermute | solution.py:334
  79.9 15.7 %collective-permute-start.23 = (f32[8,128,128]{2,1,0:T(8,128)S(1)}, f32[8,128,128]{2,1,0:T(8,128)S(1)}, u32[]{:S(2)}, u32[]{:S(2)}) collective-permute-start(f32[8,128,128]{2,1,0:T(8,128)S(1)} %get-tuple-element.198.refs_17_), channel_id=1, source_target_pairs={{0,4},{1,5},{2,0},{3,1},{4,6},{5,7},{6,2},{7,3},{8,12},{9,13},{10,... | collective-permute-start | bytes 1572872 | tf_op jit(solution)/shard_map/ppermute | solution.py:354
  100.2 14.2 %collective-permute-start.24 = (f32[8,128,128]{2,1,0:T(8,128)S(1)}, f32[8,128,128]{2,1,0:T(8,128)S(1)}, u32[]{:S(2)}, u32[]{:S(2)}) collective-permute-start(f32[8,128,128]{2,1,0:T(8,128)S(1)} %get-tuple-element.200.refs_18_.refs_19_), channel_id=1, source_target_pairs={{0,16},{16,0},{1,17},{17,1},{2,18},{18,2},{3,19},{19,3},{4,20},{20... | collective-permute-start | bytes 1572872 | tf_op jit(solution)/shard_map/ppermute | solution.py:362
  107.3 17.2 %collective-permute-start.33 = (f32[8,128,128]{2,1,0:T(8,128)S(1)}, f32[8,128,128]{2,1,0:T(8,128)S(1)}, u32[]{:S(2)}, u32[]{:S(2)}) collective-permute-start(f32[8,128,128]{2,1,0:T(8,128)S(1)} %get-tuple-element.219.refs_37_.refs_3_), channel_id=1, source_target_pairs={{0,4},{1,5},{2,0},{3,1},{4,6},{5,7},{6,2},{7,3},{8,12},{9,13},{10,... | collective-permute-start | bytes 1572872 | tf_op jit(solution)/shard_map/ppermute | solution.py:354
  109.9 11.9 %collective-permute-start.29 = (f32[4,128,128]{2,1,0:T(8,128)S(1)}, f32[4,128,128]{2,1,0:T(8,128)S(1)}, u32[]{:S(2)}, u32[]{:S(2)}) collective-permute-start(f32[4,128,128]{2,1,0:T(8,128)S(1)} %collective-permute-done.28.refs_17_.refs_3_), channel_id=1, source_target_pairs={{0,16},{16,0},{1,17},{17,1},{2,18},{18,2},{3,19},{19,3},{4,20},{20... | collective-permute-start | bytes 786440 | tf_op jit(solution)/shard_map/ppermute | solution.py:362
  116.9 15.7 %collective-permute-start.26 = (f32[512,128]{1,0:T(8,128)S(1)}, f32[512,128]{1,0:T(8,128)S(1)}, u32[]{:S(2)}, u32[]{:S(2)}) collective-permute-start(f32[512,128]{1,0:T(8,128)S(1)} %get-tuple-element.207), channel_id=1, source_target_pairs={{0,1},{1,0},{2,3},{3,2},{4,5},{5,4},{6,7},{7,6},{8,9},{9,8},{10,11... | collective-permute-start | bytes 786440 | tf_op jit(solution)/shard_map/ppermute | solution.py:334
  119.1 13.9 %collective-permute-start.27 = (f32[512,128]{1,0:T(8,128)S(1)}, f32[512,128]{1,0:T(8,128)S(1)}, u32[]{:S(2)}, u32[]{:S(2)}) collective-permute-start(f32[512,128]{1,0:T(8,128)S(1)} %get-tuple-element.208), channel_id=1, source_target_pairs={{0,9},{1,8},{2,11},{3,10},{4,13},{5,12},{6,15},{7,14},{8,1},{9,0},... | collective-permute-start | bytes 786440 | tf_op jit(solution)/shard_map/ppermute | solution.py:334
  120.8 19.3 %collective-permute-start.40 = (f32[8,128,128]{2,1,0:T(8,128)S(1)}, f32[8,128,128]{2,1,0:T(8,128)S(1)}, u32[]{:S(2)}, u32[]{:S(2)}) collective-permute-start(f32[8,128,128]{2,1,0:T(8,128)S(1)} %get-tuple-element.231.refs_5_), channel_id=1, source_target_pairs={{0,4},{1,5},{2,0},{3,1},{4,6},{5,7},{6,2},{7,3},{8,12},{9,13},{10,... | collective-permute-start | bytes 1572872 | tf_op jit(solution)/shard_map/ppermute | solution.py:354
  126.3 15.2 %collective-permute-start.34 = (f32[8,128,128]{2,1,0:T(8,128)S(1)}, f32[8,128,128]{2,1,0:T(8,128)S(1)}, u32[]{:S(2)}, u32[]{:S(2)}) collective-permute-start(f32[8,128,128]{2,1,0:T(8,128)S(1)} %get-tuple-element.221.refs_38_.refs_42_), channel_id=1, source_target_pairs={{0,16},{16,0},{1,17},{17,1},{2,18},{18,2},{3,19},{19,3},{4,20},{20... | collective-permute-start | bytes 1572872 | tf_op jit(solution)/shard_map/ppermute | solution.py:362
  128.5 11.6 %collective-permute-start.35 = (f32[4,128,128]{2,1,0:T(8,128)S(1)}, f32[4,128,128]{2,1,0:T(8,128)S(1)}, u32[]{:S(2)}, u32[]{:S(2)}) collective-permute-start(f32[4,128,128]{2,1,0:T(8,128)S(1)} %get-tuple-element.222), channel_id=1, source_target_pairs={{0,4},{1,5},{2,0},{3,1},{4,6},{5,7},{6,2},{7,3},{8,12},{9,13},{10,... | collective-permute-start | bytes 786440 | tf_op jit(solution)/shard_map/ppermute | solution.py:354
  132.6 11.9 %collective-permute-start.31 = (f32[512,128]{1,0:T(8,128)S(1)}, f32[512,128]{1,0:T(8,128)S(1)}, u32[]{:S(2)}, u32[]{:S(2)}) collective-permute-start(f32[512,128]{1,0:T(8,128)S(1)} %get-tuple-element.213), channel_id=1, source_target_pairs={{0,1},{1,0},{2,3},{3,2},{4,5},{5,4},{6,7},{7,6},{8,9},{9,8},{10,11... | collective-permute-start | bytes 786440 | tf_op jit(solution)/shard_map/ppermute | solution.py:334
  133.1 15.0 %collective-permute-start.53 = (f32[8,128,128]{2,1,0:T(8,128)S(1)}, f32[8,128,128]{2,1,0:T(8,128)S(1)}, u32[]{:S(2)}, u32[]{:S(2)}) collective-permute-start(f32[8,128,128]{2,1,0:T(8,128)S(1)} %get-tuple-element.251), channel_id=1, source_target_pairs={{0,8},{1,9},{2,10},{3,11},{4,12},{5,13},{6,14},{7,15},{8,0},{9,1},... | collective-permute-start | bytes 1572872 | tf_op jit(solution)/shard_map/ppermute | solution.py:334
  153.9 29.8 %collective-permute-start.55 = (f32[16,128,128]{2,1,0:T(8,128)S(1)}, f32[16,128,128]{2,1,0:T(8,128)S(1)}, u32[]{:S(2)}, u32[]{:S(2)}) collective-permute-start(f32[16,128,128]{2,1,0:T(8,128)S(1)} %get-tuple-element.253.refs_25_.refs_5_), channel_id=1, source_target_pairs={{0,4},{1,5},{2,0},{3,1},{4,6},{5,7},{6,2},{7,3},{8,12},{9,13},{10,... | collective-permute-start | bytes 3145736 | tf_op jit(solution)/shard_map/ppermute | solution.py:354
  162.1 12.7 %collective-permute-start.39 = (f32[520,128]{1,0:T(8,128)S(1)}, f32[520,128]{1,0:T(8,128)S(1)}, u32[]{:S(2)}, u32[]{:S(2)}) collective-permute-start(f32[520,128]{1,0:T(8,128)S(1)} %get-tuple-element.230), channel_id=1, source_target_pairs={{0,9},{1,8},{2,11},{3,10},{4,13},{5,12},{6,15},{7,14},{8,1},{9,0},... | collective-permute-start | bytes 798728 | tf_op jit(solution)/shard_map/ppermute | solution.py:334
  162.7 14.7 %collective-permute-start.41 = (f32[8,128,128]{2,1,0:T(8,128)S(1)}, f32[8,128,128]{2,1,0:T(8,128)S(1)}, u32[]{:S(2)}, u32[]{:S(2)}) collective-permute-start(f32[8,128,128]{2,1,0:T(8,128)S(1)} %get-tuple-element.232.refs_6_.refs_7_), channel_id=1, source_target_pairs={{0,16},{16,0},{1,17},{17,1},{2,18},{18,2},{3,19},{19,3},{4,20},{20... | collective-permute-start | bytes 1572872 | tf_op jit(solution)/shard_map/ppermute | solution.py:362
  163.8 18.8 %collective-permute-start.49 = (f32[4,128,128]{2,1,0:T(8,128)S(1)}, f32[4,128,128]{2,1,0:T(8,128)S(1)}, u32[]{:S(2)}, u32[]{:S(2)}) collective-permute-start(f32[4,128,128]{2,1,0:T(8,128)S(1)} %collective-permute-done.48.refs_5_), channel_id=1, source_target_pairs={{0,16},{16,0},{1,17},{17,1},{2,18},{18,2},{3,19},{19,3},{4,20},{20... | collective-permute-start | bytes 786440 | tf_op jit(solution)/shard_map/ppermute | solution.py:362
  170.2 15.4 %collective-permute-start.45 = (f32[512,128]{1,0:T(8,128)S(1)}, f32[512,128]{1,0:T(8,128)S(1)}, u32[]{:S(2)}, u32[]{:S(2)}) collective-permute-start(f32[512,128]{1,0:T(8,128)S(1)} %get-tuple-element.238), channel_id=1, source_target_pairs={{0,8},{1,9},{2,10},{3,11},{4,12},{5,13},{6,14},{7,15},{8,0},{9,1},... | collective-permute-start | bytes 786440 | tf_op jit(solution)/shard_map/ppermute | solution.py:334
  174.8 12.4 %collective-permute-start.46 = (f32[512,128]{1,0:T(8,128)S(1)}, f32[512,128]{1,0:T(8,128)S(1)}, u32[]{:S(2)}, u32[]{:S(2)}) collective-permute-start(f32[512,128]{1,0:T(8,128)S(1)} %get-tuple-element.239), channel_id=1, source_target_pairs={{0,1},{1,0},{2,3},{3,2},{4,5},{5,4},{6,7},{7,6},{8,9},{9,8},{10,11... | collective-permute-start | bytes 786440 | tf_op jit(solution)/shard_map/ppermute | solution.py:334
  177.4 11.6 %collective-permute-start.47 = (f32[512,128]{1,0:T(8,128)S(1)}, f32[512,128]{1,0:T(8,128)S(1)}, u32[]{:S(2)}, u32[]{:S(2)}) collective-permute-start(f32[512,128]{1,0:T(8,128)S(1)} %get-tuple-element.240), channel_id=1, source_target_pairs={{0,9},{1,8},{2,11},{3,10},{4,13},{5,12},{6,15},{7,14},{8,1},{9,0},... | collective-permute-start | bytes 786440 | tf_op jit(solution)/shard_map/ppermute | solution.py:334
  182.6 12.6 %collective-permute-start.43 = (f32[512,128]{1,0:T(8,128)S(1)}, f32[512,128]{1,0:T(8,128)S(1)}, u32[]{:S(2)}, u32[]{:S(2)}) collective-permute-start(f32[512,128]{1,0:T(8,128)S(1)} %get-tuple-element.235), channel_id=1, source_target_pairs={{0,1},{1,0},{2,3},{3,2},{4,5},{5,4},{6,7},{7,6},{8,9},{9,8},{10,11... | collective-permute-start | bytes 786440 | tf_op jit(solution)/shard_map/ppermute | solution.py:334
  183.7 16.5 %collective-permute-start.44 = (f32[512,128]{1,0:T(8,128)S(1)}, f32[512,128]{1,0:T(8,128)S(1)}, u32[]{:S(2)}, u32[]{:S(2)}) collective-permute-start(f32[512,128]{1,0:T(8,128)S(1)} %get-tuple-element.236), channel_id=1, source_target_pairs={{0,9},{1,8},{2,11},{3,10},{4,13},{5,12},{6,15},{7,14},{8,1},{9,0},... | collective-permute-start | bytes 786440 | tf_op jit(solution)/shard_map/ppermute | solution.py:334
  185.6 16.1 %collective-permute-start.57 = (f32[4,128,128]{2,1,0:T(8,128)S(1)}, f32[4,128,128]{2,1,0:T(8,128)S(1)}, u32[]{:S(2)}, u32[]{:S(2)}) collective-permute-start(f32[4,128,128]{2,1,0:T(8,128)S(1)} %get-tuple-element.256), channel_id=1, source_target_pairs={{0,4},{1,5},{2,0},{3,1},{4,6},{5,7},{6,2},{7,3},{8,12},{9,13},{10,... | collective-permute-start | bytes 786440 | tf_op jit(solution)/shard_map/ppermute | solution.py:354
  187.2 24.3 %collective-permute-start.56 = (f32[8,128,128]{2,1,0:T(8,128)S(1)}, f32[8,128,128]{2,1,0:T(8,128)S(1)}, u32[]{:S(2)}, u32[]{:S(2)}) collective-permute-start(f32[8,128,128]{2,1,0:T(8,128)S(1)} %get-tuple-element.255.refs_26_.refs_30_), channel_id=1, source_target_pairs={{0,16},{16,0},{1,17},{17,1},{2,18},{18,2},{3,19},{19,3},{4,20},{20... | collective-permute-start | bytes 1572872 | tf_op jit(solution)/shard_map/ppermute | solution.py:362
  191.7 14.8 %collective-permute-start.51 = (f32[512,128]{1,0:T(8,128)S(1)}, f32[512,128]{1,0:T(8,128)S(1)}, u32[]{:S(2)}, u32[]{:S(2)}) collective-permute-start(f32[512,128]{1,0:T(8,128)S(1)} %get-tuple-element.245), channel_id=1, source_target_pairs={{0,1},{1,0},{2,3},{3,2},{4,5},{5,4},{6,7},{7,6},{8,9},{9,8},{10,11... | collective-permute-start | bytes 786440 | tf_op jit(solution)/shard_map/ppermute | solution.py:334
  195.2 16.3 %collective-permute-start.52 = (f32[512,128]{1,0:T(8,128)S(1)}, f32[512,128]{1,0:T(8,128)S(1)}, u32[]{:S(2)}, u32[]{:S(2)}) collective-permute-start(f32[512,128]{1,0:T(8,128)S(1)} %get-tuple-element.246), channel_id=1, source_target_pairs={{0,9},{1,8},{2,11},{3,10},{4,13},{5,12},{6,15},{7,14},{8,1},{9,0},... | collective-permute-start | bytes 786440 | tf_op jit(solution)/shard_map/ppermute | solution.py:334
  200.2 11.2 %collective-permute-start.69 = (f32[4,128,128]{2,1,0:T(8,128)S(1)}, f32[4,128,128]{2,1,0:T(8,128)S(1)}, u32[]{:S(2)}, u32[]{:S(2)}) collective-permute-start(f32[4,128,128]{2,1,0:T(8,128)S(1)} %get-tuple-element.274), channel_id=1, source_target_pairs={{0,4},{1,5},{2,0},{3,1},{4,6},{5,7},{6,2},{7,3},{8,12},{9,13},{10,... | collective-permute-start | bytes 786440 | tf_op jit(solution)/shard_map/ppermute | solution.py:354
  201.7 9.8 %collective-permute-start.58 = (f32[4,128,128]{2,1,0:T(8,128)S(1)}, f32[4,128,128]{2,1,0:T(8,128)S(1)}, u32[]{:S(2)}, u32[]{:S(2)}) collective-permute-start(f32[4,128,128]{2,1,0:T(8,128)S(1)} %collective-permute-done.57.refs_28_), channel_id=1, source_target_pairs={{0,16},{16,0},{1,17},{17,1},{2,18},{18,2},{3,19},{19,3},{4,20},{20... | collective-permute-start | bytes 786440 | tf_op jit(solution)/shard_map/ppermute | solution.py:362
  212.7 34.6 %collective-permute-start.74 = (f32[16,128,128]{2,1,0:T(8,128)S(1)}, f32[16,128,128]{2,1,0:T(8,128)S(1)}, u32[]{:S(2)}, u32[]{:S(2)}) collective-permute-start(f32[16,128,128]{2,1,0:T(8,128)S(1)} %get-tuple-element.284.refs_25_.refs_9_), channel_id=1, source_target_pairs={{0,4},{1,5},{2,0},{3,1},{4,6},{5,7},{6,2},{7,3},{8,12},{9,13},{10,... | collective-permute-start | bytes 3145736 | tf_op jit(solution)/shard_map/ppermute | solution.py:354
  214.8 13.8 %collective-permute-start.62 = (f32[8,128,128]{2,1,0:T(8,128)S(1)}, f32[8,128,128]{2,1,0:T(8,128)S(1)}, u32[]{:S(2)}, u32[]{:S(2)}) collective-permute-start(f32[8,128,128]{2,1,0:T(8,128)S(1)} %get-tuple-element.265.refs_6_.refs_7_), channel_id=1, source_target_pairs={{0,16},{16,0},{1,17},{17,1},{2,18},{18,2},{3,19},{19,3},{4,20},{20... | collective-permute-start | bytes 1572872 | tf_op jit(solution)/shard_map/ppermute | solution.py:362
  219.4 10.3 %collective-permute-start.59 = (f32[520,128]{1,0:T(8,128)S(1)}, f32[520,128]{1,0:T(8,128)S(1)}, u32[]{:S(2)}, u32[]{:S(2)}) collective-permute-start(f32[520,128]{1,0:T(8,128)S(1)} %get-tuple-element.262), channel_id=1, source_target_pairs={{0,8},{1,9},{2,10},{3,11},{4,12},{5,13},{6,14},{7,15},{8,0},{9,1},... | collective-permute-start | bytes 798728 | tf_op jit(solution)/shard_map/ppermute | solution.py:334
  219.6 10.2 %collective-permute-start.60 = (f32[520,128]{1,0:T(8,128)S(1)}, f32[520,128]{1,0:T(8,128)S(1)}, u32[]{:S(2)}, u32[]{:S(2)}) collective-permute-start(f32[520,128]{1,0:T(8,128)S(1)} %get-tuple-element.263), channel_id=1, source_target_pairs={{0,1},{1,0},{2,3},{3,2},{4,5},{5,4},{6,7},{7,6},{8,9},{9,8},{10,11... | collective-permute-start | bytes 798728 | tf_op jit(solution)/shard_map/ppermute | solution.py:334
  220.8 12.6 %collective-permute-start.61 = (f32[520,128]{1,0:T(8,128)S(1)}, f32[520,128]{1,0:T(8,128)S(1)}, u32[]{:S(2)}, u32[]{:S(2)}) collective-permute-start(f32[520,128]{1,0:T(8,128)S(1)} %get-tuple-element.264), channel_id=1, source_target_pairs={{0,9},{1,8},{2,11},{3,10},{4,13},{5,12},{6,15},{7,14},{8,1},{9,0},... | collective-permute-start | bytes 798728 | tf_op jit(solution)/shard_map/ppermute | solution.py:334
  228.6 9.3 %collective-permute-start.70 = (f32[4,128,128]{2,1,0:T(8,128)S(1)}, f32[4,128,128]{2,1,0:T(8,128)S(1)}, u32[]{:S(2)}, u32[]{:S(2)}) collective-permute-start(f32[4,128,128]{2,1,0:T(8,128)S(1)} %collective-permute-done.69.refs_5_), channel_id=1, source_target_pairs={{0,16},{16,0},{1,17},{17,1},{2,18},{18,2},{3,19},{19,3},{4,20},{20... | collective-permute-start | bytes 786440 | tf_op jit(solution)/shard_map/ppermute | solution.py:362
  229.8 10.4 %collective-permute-start.67 = (f32[512,128]{1,0:T(8,128)S(1)}, f32[512,128]{1,0:T(8,128)S(1)}, u32[]{:S(2)}, u32[]{:S(2)}) collective-permute-start(f32[512,128]{1,0:T(8,128)S(1)} %get-tuple-element.272), channel_id=1, source_target_pairs={{0,1},{1,0},{2,3},{3,2},{4,5},{5,4},{6,7},{7,6},{8,9},{9,8},{10,11... | collective-permute-start | bytes 786440 | tf_op jit(solution)/shard_map/ppermute | solution.py:334
  233.5 11.2 %collective-permute-start.68 = (f32[512,128]{1,0:T(8,128)S(1)}, f32[512,128]{1,0:T(8,128)S(1)}, u32[]{:S(2)}, u32[]{:S(2)}) collective-permute-start(f32[512,128]{1,0:T(8,128)S(1)} %get-tuple-element.273), channel_id=1, source_target_pairs={{0,9},{1,8},{2,11},{3,10},{4,13},{5,12},{6,15},{7,14},{8,1},{9,0},... | collective-permute-start | bytes 786440 | tf_op jit(solution)/shard_map/ppermute | solution.py:334
  249.6 14.7 %collective-permute-start.76 = (f32[8,128,128]{2,1,0:T(8,128)S(1)}, f32[8,128,128]{2,1,0:T(8,128)S(1)}, u32[]{:S(2)}, u32[]{:S(2)}) collective-permute-start(f32[8,128,128]{2,1,0:T(8,128)S(1)} %get-tuple-element.286), channel_id=1, source_target_pairs={{0,4},{1,5},{2,0},{3,1},{4,6},{5,7},{6,2},{7,3},{8,12},{9,13},{10,... | collective-permute-start | bytes 1572872 | tf_op jit(solution)/shard_map/ppermute | solution.py:354
  252.6 27.4 %collective-permute-start.75 = (f32[16,128,128]{2,1,0:T(8,128)S(1)}, f32[16,128,128]{2,1,0:T(8,128)S(1)}, u32[]{:S(2)}, u32[]{:S(2)}) collective-permute-start(f32[16,128,128]{2,1,0:T(8,128)S(1)} %collective-permute-done.74.refs_1_.refs_26_.refs_30_.refs_10_.refs_14_), channel_id=1, source_target_pairs={{0,16},{16,0},{1,17},{17,1},{2,18},{18,2},{3,19},{19,3},{4,20},{20... | collective-permute-start | bytes 3145736 | tf_op jit(solution)/shard_map/ppermute | solution.py:362
  252.7 13.6 %collective-permute-start.63 = (f32[512,128]{1,0:T(8,128)S(1)}, f32[512,128]{1,0:T(8,128)S(1)}, u32[]{:S(2)}, u32[]{:S(2)}) collective-permute-start(f32[512,128]{1,0:T(8,128)S(1)} %get-tuple-element.267), channel_id=1, source_target_pairs={{0,8},{1,9},{2,10},{3,11},{4,12},{5,13},{6,14},{7,15},{8,0},{9,1},... | collective-permute-start | bytes 786440 | tf_op jit(solution)/shard_map/ppermute | solution.py:334
  252.7 13.5 %collective-permute-start.64 = (f32[512,128]{1,0:T(8,128)S(1)}, f32[512,128]{1,0:T(8,128)S(1)}, u32[]{:S(2)}, u32[]{:S(2)}) collective-permute-start(f32[512,128]{1,0:T(8,128)S(1)} %get-tuple-element.268), channel_id=1, source_target_pairs={{0,1},{1,0},{2,3},{3,2},{4,5},{5,4},{6,7},{7,6},{8,9},{9,8},{10,11... | collective-permute-start | bytes 786440 | tf_op jit(solution)/shard_map/ppermute | solution.py:334
  253.8 13.7 %collective-permute-start.65 = (f32[512,128]{1,0:T(8,128)S(1)}, f32[512,128]{1,0:T(8,128)S(1)}, u32[]{:S(2)}, u32[]{:S(2)}) collective-permute-start(f32[512,128]{1,0:T(8,128)S(1)} %get-tuple-element.269), channel_id=1, source_target_pairs={{0,9},{1,8},{2,11},{3,10},{4,13},{5,12},{6,15},{7,14},{8,1},{9,0},... | collective-permute-start | bytes 786440 | tf_op jit(solution)/shard_map/ppermute | solution.py:334
  264.4 24.7 %collective-permute-start.77 = (f32[8,128,128]{2,1,0:T(8,128)S(1)}, f32[8,128,128]{2,1,0:T(8,128)S(1)}, u32[]{:S(2)}, u32[]{:S(2)}) collective-permute-start(f32[8,128,128]{2,1,0:T(8,128)S(1)} %collective-permute-done.76.refs_28_.refs_12_), channel_id=1, source_target_pairs={{0,16},{16,0},{1,17},{17,1},{2,18},{18,2},{3,19},{19,3},{4,20},{20... | collective-permute-start | bytes 1572872 | tf_op jit(solution)/shard_map/ppermute | solution.py:362
  267.5 12.6 %collective-permute-start.73 = (f32[512,128]{1,0:T(8,128)S(1)}, f32[512,128]{1,0:T(8,128)S(1)}, u32[]{:S(2)}, u32[]{:S(2)}) collective-permute-start(f32[512,128]{1,0:T(8,128)S(1)} %get-tuple-element.279), channel_id=1, source_target_pairs={{0,9},{1,8},{2,11},{3,10},{4,13},{5,12},{6,15},{7,14},{8,1},{9,0},... | collective-permute-start | bytes 786440 | tf_op jit(solution)/shard_map/ppermute | solution.py:334
  292.3 24.9 %collective-permute-start.78 = (f32[520,128]{1,0:T(8,128)S(1)}, f32[520,128]{1,0:T(8,128)S(1)}, u32[]{:S(2)}, u32[]{:S(2)}) collective-permute-start(f32[520,128]{1,0:T(8,128)S(1)} %get-tuple-element.289), channel_id=1, source_target_pairs={{0,8},{1,9},{2,10},{3,11},{4,12},{5,13},{6,14},{7,15},{8,0},{9,1},... | collective-permute-start | bytes 798728 | tf_op jit(solution)/shard_map/ppermute | solution.py:334
  292.8 24.4 %collective-permute-start.79 = (f32[520,128]{1,0:T(8,128)S(1)}, f32[520,128]{1,0:T(8,128)S(1)}, u32[]{:S(2)}, u32[]{:S(2)}) collective-permute-start(f32[520,128]{1,0:T(8,128)S(1)} %get-tuple-element.290), channel_id=1, source_target_pairs={{0,1},{1,0},{2,3},{3,2},{4,5},{5,4},{6,7},{7,6},{8,9},{9,8},{10,11... | collective-permute-start | bytes 798728 | tf_op jit(solution)/shard_map/ppermute | solution.py:334
  293.9 23.3 %collective-permute-start.80 = (f32[520,128]{1,0:T(8,128)S(1)}, f32[520,128]{1,0:T(8,128)S(1)}, u32[]{:S(2)}, u32[]{:S(2)}) collective-permute-start(f32[520,128]{1,0:T(8,128)S(1)} %get-tuple-element.291), channel_id=1, source_target_pairs={{0,9},{1,8},{2,11},{3,10},{4,13},{5,12},{6,15},{7,14},{8,1},{9,0},... | collective-permute-start | bytes 798728 | tf_op jit(solution)/shard_map/ppermute | solution.py:334
  294.3 19.1 %collective-permute-start.82 = (f32[512,128]{1,0:T(8,128)S(1)}, f32[512,128]{1,0:T(8,128)S(1)}, u32[]{:S(2)}, u32[]{:S(2)}) collective-permute-start(f32[512,128]{1,0:T(8,128)S(1)} %get-tuple-element.294), channel_id=1, source_target_pairs={{0,1},{1,0},{2,3},{3,2},{4,5},{5,4},{6,7},{7,6},{8,9},{9,8},{10,11... | collective-permute-start | bytes 786440 | tf_op jit(solution)/shard_map/ppermute | solution.py:334
  295.4 21.9 %collective-permute-start.83 = (f32[512,128]{1,0:T(8,128)S(1)}, f32[512,128]{1,0:T(8,128)S(1)}, u32[]{:S(2)}, u32[]{:S(2)}) collective-permute-start(f32[512,128]{1,0:T(8,128)S(1)} %get-tuple-element.295), channel_id=1, source_target_pairs={{0,9},{1,8},{2,11},{3,10},{4,13},{5,12},{6,15},{7,14},{8,1},{9,0},... | collective-permute-start | bytes 786440 | tf_op jit(solution)/shard_map/ppermute | solution.py:334
  323.2 10.0 %collective-permute-start.92 = (f32[256,128]{1,0:T(8,128)S(1)}, f32[256,128]{1,0:T(8,128)S(1)}, u32[]{:S(2)}, u32[]{:S(2)}) collective-permute-start(f32[256,128]{1,0:T(8,128)S(1)} %get-tuple-element.310), channel_id=1, source_target_pairs={{0,1},{1,0},{2,3},{3,2},{4,5},{5,4},{6,7},{7,6},{8,9},{9,8},{10,11... | collective-permute-start | bytes 393224 | tf_op jit(solution)/shard_map/ppermute | solution.py:334
  324.3 10.2 %collective-permute-start.93 = (f32[256,128]{1,0:T(8,128)S(1)}, f32[256,128]{1,0:T(8,128)S(1)}, u32[]{:S(2)}, u32[]{:S(2)}) collective-permute-start(f32[256,128]{1,0:T(8,128)S(1)} %get-tuple-element.311), channel_id=1, source_target_pairs={{0,9},{1,8},{2,11},{3,10},{4,13},{5,12},{6,15},{7,14},{8,1},{9,0},... | collective-permute-start | bytes 393224 | tf_op jit(solution)/shard_map/ppermute | solution.py:334
  327.4 9.4 %collective-permute-start.87 = (f32[256,128]{1,0:T(8,128)S(1)}, f32[256,128]{1,0:T(8,128)S(1)}, u32[]{:S(2)}, u32[]{:S(2)}) collective-permute-start(f32[256,128]{1,0:T(8,128)S(1)} %get-tuple-element.303), channel_id=1, source_target_pairs={{0,8},{1,9},{2,10},{3,11},{4,12},{5,13},{6,14},{7,15},{8,0},{9,1},... | collective-permute-start | bytes 393224 | tf_op jit(solution)/shard_map/ppermute | solution.py:334
  328.8 9.8 %collective-permute-start.88 = (f32[256,128]{1,0:T(8,128)S(1)}, f32[256,128]{1,0:T(8,128)S(1)}, u32[]{:S(2)}, u32[]{:S(2)}) collective-permute-start(f32[256,128]{1,0:T(8,128)S(1)} %get-tuple-element.304), channel_id=1, source_target_pairs={{0,1},{1,0},{2,3},{3,2},{4,5},{5,4},{6,7},{7,6},{8,9},{9,8},{10,11... | collective-permute-start | bytes 393224 | tf_op jit(solution)/shard_map/ppermute | solution.py:334
  329.7 9.9 %collective-permute-start.89 = (f32[256,128]{1,0:T(8,128)S(1)}, f32[256,128]{1,0:T(8,128)S(1)}, u32[]{:S(2)}, u32[]{:S(2)}) collective-permute-start(f32[256,128]{1,0:T(8,128)S(1)} %get-tuple-element.305), channel_id=1, source_target_pairs={{0,9},{1,8},{2,11},{3,10},{4,13},{5,12},{6,15},{7,14},{8,1},{9,0},... | collective-permute-start | bytes 393224 | tf_op jit(solution)/shard_map/ppermute | solution.py:334
  333.2 23.9 %collective-permute-start.98 = (f32[128,1024]{1,0:T(8,128)}, f32[128,1024]{1,0:T(8,128)}, u32[]{:S(2)}, u32[]{:S(2)}) collective-permute-start(f32[128,1024]{1,0:T(8,128)} %get-tuple-element.318), channel_id=1, source_target_pairs={{0,4},{1,5},{2,0},{3,1},{4,6},{5,7},{6,2},{7,3},{8,12},{9,13},{10,... | collective-permute-start | bytes 1572872 | tf_op jit(solution)/shard_map/ppermute | solution.py:334
  336.2 23.1 %collective-permute-start.94 = (f32[128,1024]{1,0:T(8,128)}, f32[128,1024]{1,0:T(8,128)}, u32[]{:S(2)}, u32[]{:S(2)}) collective-permute-start(f32[128,1024]{1,0:T(8,128)} %get-tuple-element.312), channel_id=1, source_target_pairs={{0,6},{1,7},{2,4},{3,5},{4,2},{5,3},{6,0},{7,1},{8,14},{9,15},{10,... | collective-permute-start | bytes 1572872 | tf_op jit(solution)/shard_map/ppermute | solution.py:334
  341.5 39.0 %collective-permute-start.90 = (f32[128,1024]{1,0:T(8,128)}, f32[128,1024]{1,0:T(8,128)}, u32[]{:S(2)}, u32[]{:S(2)}) collective-permute-start(f32[128,1024]{1,0:T(8,128)} %get-tuple-element.306), channel_id=1, source_target_pairs={{0,2},{1,3},{2,6},{3,7},{4,0},{5,1},{6,4},{7,5},{8,10},{9,11},{10,... | collective-permute-start | bytes 1572872 | tf_op jit(solution)/shard_map/ppermute | solution.py:334
  (42 other events, 271.4 us)

commit v7 on v6

--- a/solution.py
+++ b/solution.py
@@ -484,8 +484,8 @@
             (left_parts[1],) = four_pieces(left, far, near)
             pairs = [swapped(factors, 1, marks) for factors in (right_factors, left_factors)]
         if layer == 2:
-            far, _ = near_half(near, marks)
-            right_parts[3], left_parts[3] = four_pieces(part, far, near)
+            moved = near_halves(near, marks)
+            right_parts[3], left_parts[3] = [apart(part, n, *moved[n]) for n in range(2)]
         if layer + 2 < layers:
             waits = [far, *right_last, *mixed[0][2:], *mixed[1][2:]]
             part = own(pairs, layer % 2, waits)

time: 388 us -> 374 us (0.964)
  waiting for transfers between devices: 222 us -> 201 us
  starting transfers between devices: 87.6 us -> 96.3 us
    ppermute x73, waiting for transfers between devices: 157 us -> 142 us  [routed(): return lax.ppermute(value, ('segment', 'block'), route)]
    ppermute x13 -> x14, waiting for transfers between devices: 29.1 us -> 21.4 us  [group_ring(): return lax.ppermute(value, ('groups', 'segment', 'block'), route)]
    ppermute x73, starting transfers between devices: 45.4 us -> 50.8 us  [routed(): return lax.ppermute(value, ('segment', 'block'), route)]
    ppermute x14 -> x16, starting transfers between devices: 19.3 us -> 21.9 us  [group_swap(): return lax.ppermute(value, 'groups', [(0, 1), (1, 0)])]
    ppermute x14 -> x16, waiting for transfers between devices: 35.7 us -> 37.8 us  [group_swap(): return lax.ppermute(value, 'groups', [(0, 1), (1, 0)])]
    ppermute x13 -> x14, starting transfers between devices: 22.9 us -> 23.6 us  [group_ring(): return lax.ppermute(value, ('groups', 'segment', 'block'), route)]
  transfers between devices with their start and end apart: 100 -> 103, of which waited for: 50 -> 50; matrix products, arithmetic and copies ran while one was open for 0% -> 0% of each run, Pallas kernels for 15% -> 17%
where the time goes in v7:
time: 374 us
  waiting for transfers between devices  201 us (54%)
  starting transfers between devices  96.3 us (26%)
  Pallas kernels  70 us (19%)
    ppermute x73, waiting for transfers between devices, routed(): return lax.ppermute(value, ('segment', 'block'), route)  142 us
    pallas_call x35, Pallas kernels, call(): pl.pallas_call(functools.partial(marked, kernel, len(operands), len(waits...  70 us
    ppermute x73, starting transfers between devices, routed(): return lax.ppermute(value, ('segment', 'block'), route)  50.8 us
    ppermute x16, waiting for transfers between devices, group_swap(): return lax.ppermute(value, 'groups', [(0, 1), (1, 0)])  37.8 us
    ppermute x14, starting transfers between devices, group_ring(): return lax.ppermute(value, ('groups', 'segment', 'block'), route)  23.6 us
    ppermute x16, starting transfers between devices, group_swap(): return lax.ppermute(value, 'groups', [(0, 1), (1, 0)])  21.9 us
    ppermute x14, waiting for transfers between devices, group_ring(): return lax.ppermute(value, ('groups', 'segment', 'block'), route)  21.4 us
  transfers between devices with their start and end apart: 103, of which 50 were waited for; matrix products, arithmetic and copies ran while one was open for 0% of the time, Pallas kernels for 17%

profile of v7, /device:TPU:0, one launch (start us, length us, event | category | flops | bytes accessed | tf_op | source)
XLA Modules:
  0.0 374.1 jit_solution(16443474848223612368)
XLA Ops:
  0.0 2.5 constant_dynamic-slice_fusion.4
  4.2 1.9 collective-permute-done.2.refs_2_
  7.3 3.9 %collective-permute-start.4 = (f32[8,128,128]{2,1,0:T(8,128)S(1)}, f32[8,128,128]{2,1,0:T(8,128)S(1)}, u32[]{:S(2)}, u32[]{:S(2)}) collective-permute-start(f32[8,128,128]{2,1,0:T(8,128)S(1)} %get-tuple-element.167.refs_2_), channel_id=1, source_target_pairs={{0,4},{1,5},{2,0},{3,1},{4,6},{5,7},{6,2},{7,3},{8,12},{9,13},{10,... | collective-permute-start | bytes 1572872 | tf_op jit(solution)/shard_map/ppermute | solution.py:354
  16.3 7.1 %collective-permute-done.4.refs_2_.refs_1_ = f32[8,128,128]{2,1,0:T(8,128)S(1)} collective-permute-done((f32[8,128,128]{2,1,0:T(8,128)S(1)}, f32[8,128,128]{2,1,0:T(8,128)S(1)}, u32[]{:S(2)}, u32[]{:S(2)}) %collective-permute-start.4) | collective-permute-done | bytes 524320 | tf_op jit(solution)/shard_map/ppermute | solution.py:354
  23.4 2.5 collective-permute-start.5
  29.6 7.1 %collective-permute-done.5.refs_3_ = f32[8,128,128]{2,1,0:T(8,128)S(1)} collective-permute-done((f32[8,128,128]{2,1,0:T(8,128)S(1)}, f32[8,128,128]{2,1,0:T(8,128)S(1)}, u32[]{:S(2)}, u32[]{:S(2)}) %collective-permute-start.5) | collective-permute-done | bytes 524320 | tf_op jit(solution)/shard_map/ppermute | solution.py:362
  38.2 2.4 shard_map.50
  40.6 8.5 %collective-permute-done.6.refs_3_.refs_1_ = f32[136,1024]{1,0:T(8,128)S(1)} collective-permute-done((f32[136,1024]{1,0:T(8,128)S(1)}, f32[136,1024]{1,0:T(8,128)S(1)}, u32[]{:S(2)}, u32[]{:S(2)}) %collective-permute-start.6) | collective-permute-done | bytes 557088 | tf_op jit(solution)/shard_map/ppermute | solution.py:334
  50.6 21.7 %collective-permute-done.7.refs_4_.refs_1_ = f32[136,1024]{1,0:T(8,128)S(1)} collective-permute-done((f32[136,1024]{1,0:T(8,128)S(1)}, f32[136,1024]{1,0:T(8,128)S(1)}, u32[]{:S(2)}, u32[]{:S(2)}) %collective-permute-start.7) | collective-permute-done | bytes 557088 | tf_op jit(solution)/shard_map/ppermute | solution.py:334
  73.5 2.0 shard_map.51
  75.6 2.4 shard_map.52
  78.0 1.8 shard_map.55
  79.8 3.1 collective-permute-start.23
  86.9 5.4 %collective-permute-done.9.refs_3_ = f32[4,128,128]{2,1,0:T(8,128)S(1)} collective-permute-done((f32[4,128,128]{2,1,0:T(8,128)S(1)}, f32[4,128,128]{2,1,0:T(8,128)S(1)}, u32[]{:S(2)}, u32[]{:S(2)}) %collective-permute-start.9) | collective-permute-done | bytes 262176 | tf_op jit(solution)/shard_map/ppermute | solution.py:362
  92.3 2.4 shard_map.53
  97.2 2.4 collective-permute-start.28
  101.3 4.7 %collective-permute-done.17.refs_11_.refs_4_.refs_19_ = f32[264,128]{1,0:T(8,128)S(1)} collective-permute-done((f32[264,128]{1,0:T(8,128)S(1)}, f32[264,128]{1,0:T(8,128)S(1)}, u32[]{:S(2)}, u32[]{:S(2)}) %collective-permute-start.17) | collective-permute-done | bytes 135200 | tf_op jit(solution)/shard_map/ppermute | solution.py:334
  107.2 2.2 collective-permute-start.33
  109.9 2.1 collective-permute-start.29
  114.3 2.5 shard_map.57
  116.8 2.1 collective-permute-start.26
  121.8 2.6 shard_map.58
  126.2 2.2 collective-permute-start.34
  132.9 7.2 %collective-permute-done.35.refs_40_.refs_2_ = f32[4,128,128]{2,1,0:T(8,128)S(1)} collective-permute-done((f32[4,128,128]{2,1,0:T(8,128)S(1)}, f32[4,128,128]{2,1,0:T(8,128)S(1)}, u32[]{:S(2)}, u32[]{:S(2)}) %collective-permute-start.35) | collective-permute-done | bytes 262176 | tf_op jit(solution)/shard_map/ppermute | solution.py:354
  145.0 3.0 collective-permute-done.32.refs_32_.refs_10_
  148.0 2.0 collective-permute-done.36.refs_41_.refs_6_
  150.0 2.5 collective-permute-done.48.refs_5_
  157.3 3.4 shard_map.61
  164.4 6.9 %collective-permute-done.38.refs_3_.refs_11_ = f32[520,128]{1,0:T(8,128)S(1)} collective-permute-done((f32[520,128]{1,0:T(8,128)S(1)}, f32[520,128]{1,0:T(8,128)S(1)}, u32[]{:S(2)}, u32[]{:S(2)}) %collective-permute-start.38) | collective-permute-done | bytes 266272 | tf_op jit(solution)/shard_map/ppermute | solution.py:334
  171.2 4.0 %collective-permute-done.39.refs_4_.refs_12_ = f32[520,128]{1,0:T(8,128)S(1)} collective-permute-done((f32[520,128]{1,0:T(8,128)S(1)}, f32[520,128]{1,0:T(8,128)S(1)}, u32[]{:S(2)}, u32[]{:S(2)}) %collective-permute-start.39) | collective-permute-done | bytes 266272 | tf_op jit(solution)/shard_map/ppermute | solution.py:334
  177.5 2.5 shard_map.64
  181.8 1.9 shard_map.69
  186.5 3.5 collective-permute-done.47.refs_4_
  190.0 2.6 shard_map.65
  193.7 1.9 collective-permute-done.43.refs_15_.refs_8_
  196.4 4.9 %collective-permute-done.44.refs_16_.refs_9_ = f32[512,128]{1,0:T(8,128)S(1)} collective-permute-done((f32[512,128]{1,0:T(8,128)S(1)}, f32[512,128]{1,0:T(8,128)S(1)}, u32[]{:S(2)}, u32[]{:S(2)}) %collective-permute-start.44) | collective-permute-done | bytes 262176 | tf_op jit(solution)/shard_map/ppermute | solution.py:334
  201.2 1.8 collective-permute-start.69
  203.5 3.3 collective-permute-done.51.refs_19_.refs_10_
  207.0 5.5 %collective-permute-done.52.refs_20_.refs_11_ = f32[512,128]{1,0:T(8,128)S(1)} collective-permute-done((f32[512,128]{1,0:T(8,128)S(1)}, f32[512,128]{1,0:T(8,128)S(1)}, u32[]{:S(2)}, u32[]{:S(2)}) %collective-permute-start.52) | collective-permute-done | bytes 262176 | tf_op jit(solution)/shard_map/ppermute | solution.py:334
  213.8 1.8 collective-permute-start.74
  216.2 3.4 shard_map.70
  221.5 8.1 %collective-permute-done.62.refs_7_.refs_8_ = f32[8,128,128]{2,1,0:T(8,128)S(1)} collective-permute-done((f32[8,128,128]{2,1,0:T(8,128)S(1)}, f32[8,128,128]{2,1,0:T(8,128)S(1)}, u32[]{:S(2)}, u32[]{:S(2)}) %collective-permute-start.62) | collective-permute-done | bytes 524320 | tf_op jit(solution)/shard_map/ppermute | solution.py:362
  231.3 2.4 collective-permute-done.61.refs_4_.refs_12_
  235.4 2.5 shard_map.71
  240.2 4.7 %collective-permute-done.68.refs_4_ = f32[512,128]{1,0:T(8,128)S(1)} collective-permute-done((f32[512,128]{1,0:T(8,128)S(1)}, f32[512,128]{1,0:T(8,128)S(1)}, u32[]{:S(2)}, u32[]{:S(2)}) %collective-permute-start.68) | collective-permute-done | bytes 262176 | tf_op jit(solution)/shard_map/ppermute | solution.py:334
  244.9 2.6 shard_map.72
  248.4 1.8 shard_map.74
  254.3 1.9 collective-permute-done.65.refs_16_
  265.8 1.9 collective-permute-start.86
  267.8 2.9 collective-permute-done.77.refs_29_
  270.7 3.3 shard_map.75
  275.7 6.2 %collective-permute-done.84.refs_11_.refs_15_ = f32[8,128,128]{2,1,0:T(8,128)S(1)} collective-permute-done((f32[8,128,128]{2,1,0:T(8,128)S(1)}, f32[8,128,128]{2,1,0:T(8,128)S(1)}, u32[]{:S(2)}, u32[]{:S(2)}) %collective-permute-start.84) | collective-permute-done | bytes 524320 | tf_op jit(solution)/shard_map/ppermute | solution.py:362
  281.9 4.7 %collective-permute-done.86.refs_13_ = f32[4,128,128]{2,1,0:T(8,128)S(1)} collective-permute-done((f32[4,128,128]{2,1,0:T(8,128)S(1)}, f32[4,128,128]{2,1,0:T(8,128)S(1)}, u32[]{:S(2)}, u32[]{:S(2)}) %collective-permute-start.86) | collective-permute-done | bytes 262176 | tf_op jit(solution)/shard_map/ppermute | solution.py:362
  287.7 8.1 %collective-permute-done.82.refs_7_ = f32[512,128]{1,0:T(8,128)S(1)} collective-permute-done((f32[512,128]{1,0:T(8,128)S(1)}, f32[512,128]{1,0:T(8,128)S(1)}, u32[]{:S(2)}, u32[]{:S(2)}) %collective-permute-start.82) | collective-permute-done | bytes 262176 | tf_op jit(solution)/shard_map/ppermute | solution.py:334
  295.8 5.7 %collective-permute-done.83.refs_8_ = f32[512,128]{1,0:T(8,128)S(1)} collective-permute-done((f32[512,128]{1,0:T(8,128)S(1)}, f32[512,128]{1,0:T(8,128)S(1)}, u32[]{:S(2)}, u32[]{:S(2)}) %collective-permute-start.83) | collective-permute-done | bytes 262176 | tf_op jit(solution)/shard_map/ppermute | solution.py:334
  301.5 3.0 shard_map.76
  308.3 2.6 collective-permute-done.99.refs_9_
  311.0 1.9 collective-permute-done.100.refs_10_
  320.3 3.6 collective-permute-start.97
  325.9 2.9 collective-permute-start.93
  331.0 4.6 %collective-permute-done.88.refs_9_ = f32[256,128]{1,0:T(8,128)S(1)} collective-permute-done((f32[256,128]{1,0:T(8,128)S(1)}, f32[256,128]{1,0:T(8,128)S(1)}, u32[]{:S(2)}, u32[]{:S(2)}) %collective-permute-start.88) | collective-permute-done | bytes 131104 | tf_op jit(solution)/shard_map/ppermute | solution.py:334
  338.1 8.3 %collective-permute-done.97 = f32[128,1024]{1,0:T(8,128)} collective-permute-done((f32[128,1024]{1,0:T(8,128)}, f32[128,1024]{1,0:T(8,128)}, u32[]{:S(2)}, u32[]{:S(2)}) %collective-permute-start.97) | collective-permute-done | bytes 524320 | tf_op jit(solution)/shard_map/ppermute | solution.py:334
  346.4 21.5 %collective-permute-done.93 = f32[128,1024]{1,0:T(8,128)} collective-permute-done((f32[128,1024]{1,0:T(8,128)}, f32[128,1024]{1,0:T(8,128)}, u32[]{:S(2)}, u32[]{:S(2)}) %collective-permute-start.93) | collective-permute-done | bytes 524320 | tf_op jit(solution)/shard_map/ppermute | solution.py:334
  370.1 2.5 collective-permute-done.102
  (193 shorter events, 108.4 us)
Async XLA Ops:
  2.5 9.9 %collective-permute-start = (f32[256,1024]{1,0:T(8,128)}, f32[256,1024]{1,0:T(8,128)S(1)}, u32[]{:S(2)}, u32[]{:S(2)}) collective-permute-start(f32[256,1024]{1,0:T(8,128)} %constant_dynamic-slice_fusion.4), channel_id=1, source_target_pairs={{0,8},{1,9},{2,10},{3,11},{4,12},{5,13},{6,14},{7,15},{8,0},{9,1},... | collective-permute-start | bytes 3145736 | tf_op jit(solution)/shard_map/ppermute | solution.py:334
  7.3 16.2 %collective-permute-start.4 = (f32[8,128,128]{2,1,0:T(8,128)S(1)}, f32[8,128,128]{2,1,0:T(8,128)S(1)}, u32[]{:S(2)}, u32[]{:S(2)}) collective-permute-start(f32[8,128,128]{2,1,0:T(8,128)S(1)} %get-tuple-element.167.refs_2_), channel_id=1, source_target_pairs={{0,4},{1,5},{2,0},{3,1},{4,6},{5,7},{6,2},{7,3},{8,12},{9,13},{10,... | collective-permute-start | bytes 1572872 | tf_op jit(solution)/shard_map/ppermute | solution.py:354
  13.8 24.3 %collective-permute-start.3 = (f32[136,1024]{1,0:T(8,128)S(1)}, f32[136,1024]{1,0:T(8,128)S(1)}, u32[]{:S(2)}, u32[]{:S(2)}) collective-permute-start(f32[136,1024]{1,0:T(8,128)S(1)} %get-tuple-element.169), channel_id=1, source_target_pairs={{0,4},{1,5},{2,0},{3,1},{4,6},{5,7},{6,2},{7,3},{8,12},{9,13},{10,... | collective-permute-start | bytes 1671176 | tf_op jit(solution)/shard_map/ppermute | solution.py:334
  15.4 33.7 %collective-permute-start.6 = (f32[136,1024]{1,0:T(8,128)S(1)}, f32[136,1024]{1,0:T(8,128)S(1)}, u32[]{:S(2)}, u32[]{:S(2)}) collective-permute-start(f32[136,1024]{1,0:T(8,128)S(1)} %get-tuple-element.172), channel_id=1, source_target_pairs={{0,6},{1,7},{2,4},{3,5},{4,2},{5,3},{6,0},{7,1},{8,14},{9,15},{10,... | collective-permute-start | bytes 1671176 | tf_op jit(solution)/shard_map/ppermute | solution.py:334
  15.4 56.9 %collective-permute-start.7 = (f32[136,1024]{1,0:T(8,128)S(1)}, f32[136,1024]{1,0:T(8,128)S(1)}, u32[]{:S(2)}, u32[]{:S(2)}) collective-permute-start(f32[136,1024]{1,0:T(8,128)S(1)} %get-tuple-element.173), channel_id=1, source_target_pairs={{0,2},{1,3},{2,6},{3,7},{4,0},{5,1},{6,4},{7,5},{8,10},{9,11},{10,... | collective-permute-start | bytes 1671176 | tf_op jit(solution)/shard_map/ppermute | solution.py:334
  23.4 13.2 %collective-permute-start.5 = (f32[8,128,128]{2,1,0:T(8,128)S(1)}, f32[8,128,128]{2,1,0:T(8,128)S(1)}, u32[]{:S(2)}, u32[]{:S(2)}) collective-permute-start(f32[8,128,128]{2,1,0:T(8,128)S(1)} %collective-permute-done.4.refs_2_.refs_1_), channel_id=1, source_target_pairs={{0,16},{16,0},{1,17},{17,1},{2,18},{18,2},{3,19},{19,3},{4,20},{20... | collective-permute-start | bytes 1572872 | tf_op jit(solution)/shard_map/ppermute | solution.py:362
  27.7 50.3 %collective-permute-start.22 = (f32[8,128,128]{2,1,0:T(8,128)S(1)}, f32[8,128,128]{2,1,0:T(8,128)S(1)}, u32[]{:S(2)}, u32[]{:S(2)}) collective-permute-start(f32[8,128,128]{2,1,0:T(8,128)S(1)} %get-tuple-element.200), channel_id=1, source_target_pairs={{0,8},{1,9},{2,10},{3,11},{4,12},{5,13},{6,14},{7,15},{8,0},{9,1},... | collective-permute-start | bytes 1572872 | tf_op jit(solution)/shard_map/ppermute | solution.py:334
  36.6 38.8 %collective-permute-start.11 = (f32[264,128]{1,0:T(8,128)S(1)}, f32[264,128]{1,0:T(8,128)S(1)}, u32[]{:S(2)}, u32[]{:S(2)}) collective-permute-start(f32[264,128]{1,0:T(8,128)S(1)} %get-tuple-element.185), channel_id=1, source_target_pairs={{0,1},{1,0},{2,3},{3,2},{4,5},{5,4},{6,7},{7,6},{8,9},{9,8},{10,11... | collective-permute-start | bytes 405512 | tf_op jit(solution)/shard_map/ppermute | solution.py:334
  38.2 39.8 %collective-permute-start.12 = (f32[264,128]{1,0:T(8,128)S(1)}, f32[264,128]{1,0:T(8,128)S(1)}, u32[]{:S(2)}, u32[]{:S(2)}) collective-permute-start(f32[264,128]{1,0:T(8,128)S(1)} %get-tuple-element.186), channel_id=1, source_target_pairs={{0,9},{1,8},{2,11},{3,10},{4,13},{5,12},{6,15},{7,14},{8,1},{9,0},... | collective-permute-start | bytes 405512 | tf_op jit(solution)/shard_map/ppermute | solution.py:334
  49.1 28.9 %collective-permute-start.14 = (f32[264,128]{1,0:T(8,128)S(1)}, f32[264,128]{1,0:T(8,128)S(1)}, u32[]{:S(2)}, u32[]{:S(2)}) collective-permute-start(f32[264,128]{1,0:T(8,128)S(1)} %get-tuple-element.189), channel_id=1, source_target_pairs={{0,1},{1,0},{2,3},{3,2},{4,5},{5,4},{6,7},{7,6},{8,9},{9,8},{10,11... | collective-permute-start | bytes 405512 | tf_op jit(solution)/shard_map/ppermute | solution.py:334
  79.8 15.7 %collective-permute-start.23 = (f32[8,128,128]{2,1,0:T(8,128)S(1)}, f32[8,128,128]{2,1,0:T(8,128)S(1)}, u32[]{:S(2)}, u32[]{:S(2)}) collective-permute-start(f32[8,128,128]{2,1,0:T(8,128)S(1)} %get-tuple-element.201.refs_17_), channel_id=1, source_target_pairs={{0,4},{1,5},{2,0},{3,1},{4,6},{5,7},{6,2},{7,3},{8,12},{9,13},{10,... | collective-permute-start | bytes 1572872 | tf_op jit(solution)/shard_map/ppermute | solution.py:354
  100.1 14.2 %collective-permute-start.24 = (f32[8,128,128]{2,1,0:T(8,128)S(1)}, f32[8,128,128]{2,1,0:T(8,128)S(1)}, u32[]{:S(2)}, u32[]{:S(2)}) collective-permute-start(f32[8,128,128]{2,1,0:T(8,128)S(1)} %get-tuple-element.203.refs_18_.refs_19_), channel_id=1, source_target_pairs={{0,16},{16,0},{1,17},{17,1},{2,18},{18,2},{3,19},{19,3},{4,20},{20... | collective-permute-start | bytes 1572872 | tf_op jit(solution)/shard_map/ppermute | solution.py:362
  107.2 17.3 %collective-permute-start.33 = (f32[8,128,128]{2,1,0:T(8,128)S(1)}, f32[8,128,128]{2,1,0:T(8,128)S(1)}, u32[]{:S(2)}, u32[]{:S(2)}) collective-permute-start(f32[8,128,128]{2,1,0:T(8,128)S(1)} %get-tuple-element.222.refs_37_.refs_3_), channel_id=1, source_target_pairs={{0,4},{1,5},{2,0},{3,1},{4,6},{5,7},{6,2},{7,3},{8,12},{9,13},{10,... | collective-permute-start | bytes 1572872 | tf_op jit(solution)/shard_map/ppermute | solution.py:354
  109.9 12.0 %collective-permute-start.29 = (f32[4,128,128]{2,1,0:T(8,128)S(1)}, f32[4,128,128]{2,1,0:T(8,128)S(1)}, u32[]{:S(2)}, u32[]{:S(2)}) collective-permute-start(f32[4,128,128]{2,1,0:T(8,128)S(1)} %collective-permute-done.28.refs_17_.refs_3_), channel_id=1, source_target_pairs={{0,16},{16,0},{1,17},{17,1},{2,18},{18,2},{3,19},{19,3},{4,20},{20... | collective-permute-start | bytes 786440 | tf_op jit(solution)/shard_map/ppermute | solution.py:362
  116.8 15.6 %collective-permute-start.26 = (f32[512,128]{1,0:T(8,128)S(1)}, f32[512,128]{1,0:T(8,128)S(1)}, u32[]{:S(2)}, u32[]{:S(2)}) collective-permute-start(f32[512,128]{1,0:T(8,128)S(1)} %get-tuple-element.210), channel_id=1, source_target_pairs={{0,1},{1,0},{2,3},{3,2},{4,5},{5,4},{6,7},{7,6},{8,9},{9,8},{10,11... | collective-permute-start | bytes 786440 | tf_op jit(solution)/shard_map/ppermute | solution.py:334
  118.9 14.0 %collective-permute-start.27 = (f32[512,128]{1,0:T(8,128)S(1)}, f32[512,128]{1,0:T(8,128)S(1)}, u32[]{:S(2)}, u32[]{:S(2)}) collective-permute-start(f32[512,128]{1,0:T(8,128)S(1)} %get-tuple-element.211), channel_id=1, source_target_pairs={{0,9},{1,8},{2,11},{3,10},{4,13},{5,12},{6,15},{7,14},{8,1},{9,0},... | collective-permute-start | bytes 786440 | tf_op jit(solution)/shard_map/ppermute | solution.py:334
  120.7 19.3 %collective-permute-start.40 = (f32[8,128,128]{2,1,0:T(8,128)S(1)}, f32[8,128,128]{2,1,0:T(8,128)S(1)}, u32[]{:S(2)}, u32[]{:S(2)}) collective-permute-start(f32[8,128,128]{2,1,0:T(8,128)S(1)} %get-tuple-element.234.refs_5_), channel_id=1, source_target_pairs={{0,4},{1,5},{2,0},{3,1},{4,6},{5,7},{6,2},{7,3},{8,12},{9,13},{10,... | collective-permute-start | bytes 1572872 | tf_op jit(solution)/shard_map/ppermute | solution.py:354
  126.2 15.3 %collective-permute-start.34 = (f32[8,128,128]{2,1,0:T(8,128)S(1)}, f32[8,128,128]{2,1,0:T(8,128)S(1)}, u32[]{:S(2)}, u32[]{:S(2)}) collective-permute-start(f32[8,128,128]{2,1,0:T(8,128)S(1)} %get-tuple-element.224.refs_38_.refs_42_), channel_id=1, source_target_pairs={{0,16},{16,0},{1,17},{17,1},{2,18},{18,2},{3,19},{19,3},{4,20},{20... | collective-permute-start | bytes 1572872 | tf_op jit(solution)/shard_map/ppermute | solution.py:362
  128.4 11.7 %collective-permute-start.35 = (f32[4,128,128]{2,1,0:T(8,128)S(1)}, f32[4,128,128]{2,1,0:T(8,128)S(1)}, u32[]{:S(2)}, u32[]{:S(2)}) collective-permute-start(f32[4,128,128]{2,1,0:T(8,128)S(1)} %get-tuple-element.225), channel_id=1, source_target_pairs={{0,4},{1,5},{2,0},{3,1},{4,6},{5,7},{6,2},{7,3},{8,12},{9,13},{10,... | collective-permute-start | bytes 786440 | tf_op jit(solution)/shard_map/ppermute | solution.py:354
  132.4 12.0 %collective-permute-start.31 = (f32[512,128]{1,0:T(8,128)S(1)}, f32[512,128]{1,0:T(8,128)S(1)}, u32[]{:S(2)}, u32[]{:S(2)}) collective-permute-start(f32[512,128]{1,0:T(8,128)S(1)} %get-tuple-element.216), channel_id=1, source_target_pairs={{0,1},{1,0},{2,3},{3,2},{4,5},{5,4},{6,7},{7,6},{8,9},{9,8},{10,11... | collective-permute-start | bytes 786440 | tf_op jit(solution)/shard_map/ppermute | solution.py:334
  132.9 15.1 %collective-permute-start.53 = (f32[8,128,128]{2,1,0:T(8,128)S(1)}, f32[8,128,128]{2,1,0:T(8,128)S(1)}, u32[]{:S(2)}, u32[]{:S(2)}) collective-permute-start(f32[8,128,128]{2,1,0:T(8,128)S(1)} %get-tuple-element.254), channel_id=1, source_target_pairs={{0,8},{1,9},{2,10},{3,11},{4,12},{5,13},{6,14},{7,15},{8,0},{9,1},... | collective-permute-start | bytes 1572872 | tf_op jit(solution)/shard_map/ppermute | solution.py:334
  153.8 28.0 %collective-permute-start.55 = (f32[16,128,128]{2,1,0:T(8,128)S(1)}, f32[16,128,128]{2,1,0:T(8,128)S(1)}, u32[]{:S(2)}, u32[]{:S(2)}) collective-permute-start(f32[16,128,128]{2,1,0:T(8,128)S(1)} %get-tuple-element.256.refs_25_.refs_5_), channel_id=1, source_target_pairs={{0,4},{1,5},{2,0},{3,1},{4,6},{5,7},{6,2},{7,3},{8,12},{9,13},{10,... | collective-permute-start | bytes 3145736 | tf_op jit(solution)/shard_map/ppermute | solution.py:354
  160.9 15.3 %collective-permute-start.41 = (f32[8,128,128]{2,1,0:T(8,128)S(1)}, f32[8,128,128]{2,1,0:T(8,128)S(1)}, u32[]{:S(2)}, u32[]{:S(2)}) collective-permute-start(f32[8,128,128]{2,1,0:T(8,128)S(1)} %get-tuple-element.235.refs_6_.refs_7_), channel_id=1, source_target_pairs={{0,16},{16,0},{1,17},{17,1},{2,18},{18,2},{3,19},{19,3},{4,20},{20... | collective-permute-start | bytes 1572872 | tf_op jit(solution)/shard_map/ppermute | solution.py:362
  163.0 12.2 %collective-permute-start.39 = (f32[520,128]{1,0:T(8,128)S(1)}, f32[520,128]{1,0:T(8,128)S(1)}, u32[]{:S(2)}, u32[]{:S(2)}) collective-permute-start(f32[520,128]{1,0:T(8,128)S(1)} %get-tuple-element.233), channel_id=1, source_target_pairs={{0,9},{1,8},{2,11},{3,10},{4,13},{5,12},{6,15},{7,14},{8,1},{9,0},... | collective-permute-start | bytes 798728 | tf_op jit(solution)/shard_map/ppermute | solution.py:334
  163.4 17.3 %collective-permute-start.49 = (f32[4,128,128]{2,1,0:T(8,128)S(1)}, f32[4,128,128]{2,1,0:T(8,128)S(1)}, u32[]{:S(2)}, u32[]{:S(2)}) collective-permute-start(f32[4,128,128]{2,1,0:T(8,128)S(1)} %collective-permute-done.48.refs_5_), channel_id=1, source_target_pairs={{0,16},{16,0},{1,17},{17,1},{2,18},{18,2},{3,19},{19,3},{4,20},{20... | collective-permute-start | bytes 786440 | tf_op jit(solution)/shard_map/ppermute | solution.py:362
  171.2 12.5 %collective-permute-start.45 = (f32[512,128]{1,0:T(8,128)S(1)}, f32[512,128]{1,0:T(8,128)S(1)}, u32[]{:S(2)}, u32[]{:S(2)}) collective-permute-start(f32[512,128]{1,0:T(8,128)S(1)} %get-tuple-element.241), channel_id=1, source_target_pairs={{0,8},{1,9},{2,10},{3,11},{4,12},{5,13},{6,14},{7,15},{8,0},{9,1},... | collective-permute-start | bytes 786440 | tf_op jit(solution)/shard_map/ppermute | solution.py:334
  175.2 10.1 %collective-permute-start.46 = (f32[512,128]{1,0:T(8,128)S(1)}, f32[512,128]{1,0:T(8,128)S(1)}, u32[]{:S(2)}, u32[]{:S(2)}) collective-permute-start(f32[512,128]{1,0:T(8,128)S(1)} %get-tuple-element.242), channel_id=1, source_target_pairs={{0,1},{1,0},{2,3},{3,2},{4,5},{5,4},{6,7},{7,6},{8,9},{9,8},{10,11... | collective-permute-start | bytes 786440 | tf_op jit(solution)/shard_map/ppermute | solution.py:334
  176.2 13.8 %collective-permute-start.47 = (f32[512,128]{1,0:T(8,128)S(1)}, f32[512,128]{1,0:T(8,128)S(1)}, u32[]{:S(2)}, u32[]{:S(2)}) collective-permute-start(f32[512,128]{1,0:T(8,128)S(1)} %get-tuple-element.243), channel_id=1, source_target_pairs={{0,9},{1,8},{2,11},{3,10},{4,13},{5,12},{6,15},{7,14},{8,1},{9,0},... | collective-permute-start | bytes 786440 | tf_op jit(solution)/shard_map/ppermute | solution.py:334
  180.7 14.9 %collective-permute-start.43 = (f32[512,128]{1,0:T(8,128)S(1)}, f32[512,128]{1,0:T(8,128)S(1)}, u32[]{:S(2)}, u32[]{:S(2)}) collective-permute-start(f32[512,128]{1,0:T(8,128)S(1)} %get-tuple-element.238), channel_id=1, source_target_pairs={{0,1},{1,0},{2,3},{3,2},{4,5},{5,4},{6,7},{7,6},{8,9},{9,8},{10,11... | collective-permute-start | bytes 786440 | tf_op jit(solution)/shard_map/ppermute | solution.py:334
  181.8 19.4 %collective-permute-start.44 = (f32[512,128]{1,0:T(8,128)S(1)}, f32[512,128]{1,0:T(8,128)S(1)}, u32[]{:S(2)}, u32[]{:S(2)}) collective-permute-start(f32[512,128]{1,0:T(8,128)S(1)} %get-tuple-element.239), channel_id=1, source_target_pairs={{0,9},{1,8},{2,11},{3,10},{4,13},{5,12},{6,15},{7,14},{8,1},{9,0},... | collective-permute-start | bytes 786440 | tf_op jit(solution)/shard_map/ppermute | solution.py:334
  183.7 19.3 %collective-permute-start.57 = (f32[4,128,128]{2,1,0:T(8,128)S(1)}, f32[4,128,128]{2,1,0:T(8,128)S(1)}, u32[]{:S(2)}, u32[]{:S(2)}) collective-permute-start(f32[4,128,128]{2,1,0:T(8,128)S(1)} %get-tuple-element.259), channel_id=1, source_target_pairs={{0,4},{1,5},{2,0},{3,1},{4,6},{5,7},{6,2},{7,3},{8,12},{9,13},{10,... | collective-permute-start | bytes 786440 | tf_op jit(solution)/shard_map/ppermute | solution.py:354
  185.3 27.3 %collective-permute-start.56 = (f32[8,128,128]{2,1,0:T(8,128)S(1)}, f32[8,128,128]{2,1,0:T(8,128)S(1)}, u32[]{:S(2)}, u32[]{:S(2)}) collective-permute-start(f32[8,128,128]{2,1,0:T(8,128)S(1)} %get-tuple-element.258.refs_26_.refs_30_), channel_id=1, source_target_pairs={{0,16},{16,0},{1,17},{17,1},{2,18},{18,2},{3,19},{19,3},{4,20},{20... | collective-permute-start | bytes 1572872 | tf_op jit(solution)/shard_map/ppermute | solution.py:362
  192.6 14.2 %collective-permute-start.51 = (f32[512,128]{1,0:T(8,128)S(1)}, f32[512,128]{1,0:T(8,128)S(1)}, u32[]{:S(2)}, u32[]{:S(2)}) collective-permute-start(f32[512,128]{1,0:T(8,128)S(1)} %get-tuple-element.248), channel_id=1, source_target_pairs={{0,1},{1,0},{2,3},{3,2},{4,5},{5,4},{6,7},{7,6},{8,9},{9,8},{10,11... | collective-permute-start | bytes 786440 | tf_op jit(solution)/shard_map/ppermute | solution.py:334
  195.6 16.9 %collective-permute-start.52 = (f32[512,128]{1,0:T(8,128)S(1)}, f32[512,128]{1,0:T(8,128)S(1)}, u32[]{:S(2)}, u32[]{:S(2)}) collective-permute-start(f32[512,128]{1,0:T(8,128)S(1)} %get-tuple-element.249), channel_id=1, source_target_pairs={{0,9},{1,8},{2,11},{3,10},{4,13},{5,12},{6,15},{7,14},{8,1},{9,0},... | collective-permute-start | bytes 786440 | tf_op jit(solution)/shard_map/ppermute | solution.py:334
  201.2 11.3 %collective-permute-start.69 = (f32[4,128,128]{2,1,0:T(8,128)S(1)}, f32[4,128,128]{2,1,0:T(8,128)S(1)}, u32[]{:S(2)}, u32[]{:S(2)}) collective-permute-start(f32[4,128,128]{2,1,0:T(8,128)S(1)} %get-tuple-element.277), channel_id=1, source_target_pairs={{0,4},{1,5},{2,0},{3,1},{4,6},{5,7},{6,2},{7,3},{8,12},{9,13},{10,... | collective-permute-start | bytes 786440 | tf_op jit(solution)/shard_map/ppermute | solution.py:354
  213.8 34.6 %collective-permute-start.74 = (f32[16,128,128]{2,1,0:T(8,128)S(1)}, f32[16,128,128]{2,1,0:T(8,128)S(1)}, u32[]{:S(2)}, u32[]{:S(2)}) collective-permute-start(f32[16,128,128]{2,1,0:T(8,128)S(1)} %get-tuple-element.287.refs_25_.refs_9_), channel_id=1, source_target_pairs={{0,4},{1,5},{2,0},{3,1},{4,6},{5,7},{6,2},{7,3},{8,12},{9,13},{10,... | collective-permute-start | bytes 3145736 | tf_op jit(solution)/shard_map/ppermute | solution.py:354
  215.7 14.0 %collective-permute-start.62 = (f32[8,128,128]{2,1,0:T(8,128)S(1)}, f32[8,128,128]{2,1,0:T(8,128)S(1)}, u32[]{:S(2)}, u32[]{:S(2)}) collective-permute-start(f32[8,128,128]{2,1,0:T(8,128)S(1)} %get-tuple-element.268.refs_6_.refs_7_), channel_id=1, source_target_pairs={{0,16},{16,0},{1,17},{17,1},{2,18},{18,2},{3,19},{19,3},{4,20},{20... | collective-permute-start | bytes 1572872 | tf_op jit(solution)/shard_map/ppermute | solution.py:362
  219.6 10.6 %collective-permute-start.59 = (f32[520,128]{1,0:T(8,128)S(1)}, f32[520,128]{1,0:T(8,128)S(1)}, u32[]{:S(2)}, u32[]{:S(2)}) collective-permute-start(f32[520,128]{1,0:T(8,128)S(1)} %get-tuple-element.265), channel_id=1, source_target_pairs={{0,8},{1,9},{2,10},{3,11},{4,12},{5,13},{6,14},{7,15},{8,0},{9,1},... | collective-permute-start | bytes 798728 | tf_op jit(solution)/shard_map/ppermute | solution.py:334
  219.6 10.5 %collective-permute-start.60 = (f32[520,128]{1,0:T(8,128)S(1)}, f32[520,128]{1,0:T(8,128)S(1)}, u32[]{:S(2)}, u32[]{:S(2)}) collective-permute-start(f32[520,128]{1,0:T(8,128)S(1)} %get-tuple-element.266), channel_id=1, source_target_pairs={{0,1},{1,0},{2,3},{3,2},{4,5},{5,4},{6,7},{7,6},{8,9},{9,8},{10,11... | collective-permute-start | bytes 798728 | tf_op jit(solution)/shard_map/ppermute | solution.py:334
  220.8 12.9 %collective-permute-start.61 = (f32[520,128]{1,0:T(8,128)S(1)}, f32[520,128]{1,0:T(8,128)S(1)}, u32[]{:S(2)}, u32[]{:S(2)}) collective-permute-start(f32[520,128]{1,0:T(8,128)S(1)} %get-tuple-element.267), channel_id=1, source_target_pairs={{0,9},{1,8},{2,11},{3,10},{4,13},{5,12},{6,15},{7,14},{8,1},{9,0},... | collective-permute-start | bytes 798728 | tf_op jit(solution)/shard_map/ppermute | solution.py:334
  230.1 10.1 %collective-permute-start.67 = (f32[512,128]{1,0:T(8,128)S(1)}, f32[512,128]{1,0:T(8,128)S(1)}, u32[]{:S(2)}, u32[]{:S(2)}) collective-permute-start(f32[512,128]{1,0:T(8,128)S(1)} %get-tuple-element.275), channel_id=1, source_target_pairs={{0,1},{1,0},{2,3},{3,2},{4,5},{5,4},{6,7},{7,6},{8,9},{9,8},{10,11... | collective-permute-start | bytes 786440 | tf_op jit(solution)/shard_map/ppermute | solution.py:334
  233.7 11.2 %collective-permute-start.68 = (f32[512,128]{1,0:T(8,128)S(1)}, f32[512,128]{1,0:T(8,128)S(1)}, u32[]{:S(2)}, u32[]{:S(2)}) collective-permute-start(f32[512,128]{1,0:T(8,128)S(1)} %get-tuple-element.276), channel_id=1, source_target_pairs={{0,9},{1,8},{2,11},{3,10},{4,13},{5,12},{6,15},{7,14},{8,1},{9,0},... | collective-permute-start | bytes 786440 | tf_op jit(solution)/shard_map/ppermute | solution.py:334
  237.9 13.9 %collective-permute-start.63 = (f32[512,128]{1,0:T(8,128)S(1)}, f32[512,128]{1,0:T(8,128)S(1)}, u32[]{:S(2)}, u32[]{:S(2)}) collective-permute-start(f32[512,128]{1,0:T(8,128)S(1)} %get-tuple-element.270), channel_id=1, source_target_pairs={{0,8},{1,9},{2,10},{3,11},{4,12},{5,13},{6,14},{7,15},{8,0},{9,1},... | collective-permute-start | bytes 786440 | tf_op jit(solution)/shard_map/ppermute | solution.py:334
  238.0 15.2 %collective-permute-start.64 = (f32[512,128]{1,0:T(8,128)S(1)}, f32[512,128]{1,0:T(8,128)S(1)}, u32[]{:S(2)}, u32[]{:S(2)}) collective-permute-start(f32[512,128]{1,0:T(8,128)S(1)} %get-tuple-element.271), channel_id=1, source_target_pairs={{0,1},{1,0},{2,3},{3,2},{4,5},{5,4},{6,7},{7,6},{8,9},{9,8},{10,11... | collective-permute-start | bytes 786440 | tf_op jit(solution)/shard_map/ppermute | solution.py:334
  240.2 15.9 %collective-permute-start.65 = (f32[512,128]{1,0:T(8,128)S(1)}, f32[512,128]{1,0:T(8,128)S(1)}, u32[]{:S(2)}, u32[]{:S(2)}) collective-permute-start(f32[512,128]{1,0:T(8,128)S(1)} %get-tuple-element.272), channel_id=1, source_target_pairs={{0,9},{1,8},{2,11},{3,10},{4,13},{5,12},{6,15},{7,14},{8,1},{9,0},... | collective-permute-start | bytes 786440 | tf_op jit(solution)/shard_map/ppermute | solution.py:334
  247.6 10.2 %collective-permute-start.71 = (f32[512,128]{1,0:T(8,128)S(1)}, f32[512,128]{1,0:T(8,128)S(1)}, u32[]{:S(2)}, u32[]{:S(2)}) collective-permute-start(f32[512,128]{1,0:T(8,128)S(1)} %get-tuple-element.280), channel_id=1, source_target_pairs={{0,8},{1,9},{2,10},{3,11},{4,12},{5,13},{6,14},{7,15},{8,0},{9,1},... | collective-permute-start | bytes 786440 | tf_op jit(solution)/shard_map/ppermute | solution.py:334
  250.2 17.5 %collective-permute-start.75 = (f32[8,128,128]{2,1,0:T(8,128)S(1)}, f32[8,128,128]{2,1,0:T(8,128)S(1)}, u32[]{:S(2)}, u32[]{:S(2)}) collective-permute-start(f32[8,128,128]{2,1,0:T(8,128)S(1)} %get-tuple-element.289.refs_26_.refs_30_), channel_id=1, source_target_pairs={{0,16},{16,0},{1,17},{17,1},{2,18},{18,2},{3,19},{19,3},{4,20},{20... | collective-permute-start | bytes 1572872 | tf_op jit(solution)/shard_map/ppermute | solution.py:362
  257.8 10.0 %collective-permute-start.73 = (f32[512,128]{1,0:T(8,128)S(1)}, f32[512,128]{1,0:T(8,128)S(1)}, u32[]{:S(2)}, u32[]{:S(2)}) collective-permute-start(f32[512,128]{1,0:T(8,128)S(1)} %get-tuple-element.282), channel_id=1, source_target_pairs={{0,9},{1,8},{2,11},{3,10},{4,13},{5,12},{6,15},{7,14},{8,1},{9,0},... | collective-permute-start | bytes 786440 | tf_op jit(solution)/shard_map/ppermute | solution.py:334
  259.8 10.9 %collective-permute-start.77 = (f32[4,128,128]{2,1,0:T(8,128)S(1)}, f32[4,128,128]{2,1,0:T(8,128)S(1)}, u32[]{:S(2)}, u32[]{:S(2)}) collective-permute-start(f32[4,128,128]{2,1,0:T(8,128)S(1)} %collective-permute-done.76.refs_28_), channel_id=1, source_target_pairs={{0,16},{16,0},{1,17},{17,1},{2,18},{18,2},{3,19},{19,3},{4,20},{20... | collective-permute-start | bytes 786440 | tf_op jit(solution)/shard_map/ppermute | solution.py:362
  262.7 19.2 %collective-permute-start.84 = (f32[8,128,128]{2,1,0:T(8,128)S(1)}, f32[8,128,128]{2,1,0:T(8,128)S(1)}, u32[]{:S(2)}, u32[]{:S(2)}) collective-permute-start(f32[8,128,128]{2,1,0:T(8,128)S(1)} %get-tuple-element.300.refs_10_.refs_14_), channel_id=1, source_target_pairs={{0,16},{16,0},{1,17},{17,1},{2,18},{18,2},{3,19},{19,3},{4,20},{20... | collective-permute-start | bytes 1572872 | tf_op jit(solution)/shard_map/ppermute | solution.py:362
  265.8 20.7 %collective-permute-start.86 = (f32[4,128,128]{2,1,0:T(8,128)S(1)}, f32[4,128,128]{2,1,0:T(8,128)S(1)}, u32[]{:S(2)}, u32[]{:S(2)}) collective-permute-start(f32[4,128,128]{2,1,0:T(8,128)S(1)} %collective-permute-done.85.refs_12_), channel_id=1, source_target_pairs={{0,16},{16,0},{1,17},{17,1},{2,18},{18,2},{3,19},{19,3},{4,20},{20... | collective-permute-start | bytes 786440 | tf_op jit(solution)/shard_map/ppermute | solution.py:362
  274.0 13.7 %collective-permute-start.81 = (f32[512,128]{1,0:T(8,128)S(1)}, f32[512,128]{1,0:T(8,128)S(1)}, u32[]{:S(2)}, u32[]{:S(2)}) collective-permute-start(f32[512,128]{1,0:T(8,128)S(1)} %get-tuple-element.297), channel_id=1, source_target_pairs={{0,8},{1,9},{2,10},{3,11},{4,12},{5,13},{6,14},{7,15},{8,0},{9,1},... | collective-permute-start | bytes 786440 | tf_op jit(solution)/shard_map/ppermute | solution.py:334
  274.1 27.4 %collective-permute-start.78 = (f32[520,128]{1,0:T(8,128)S(1)}, f32[520,128]{1,0:T(8,128)S(1)}, u32[]{:S(2)}, u32[]{:S(2)}) collective-permute-start(f32[520,128]{1,0:T(8,128)S(1)} %get-tuple-element.293), channel_id=1, source_target_pairs={{0,8},{1,9},{2,10},{3,11},{4,12},{5,13},{6,14},{7,15},{8,0},{9,1},... | collective-permute-start | bytes 798728 | tf_op jit(solution)/shard_map/ppermute | solution.py:334
  274.6 26.9 %collective-permute-start.79 = (f32[520,128]{1,0:T(8,128)S(1)}, f32[520,128]{1,0:T(8,128)S(1)}, u32[]{:S(2)}, u32[]{:S(2)}) collective-permute-start(f32[520,128]{1,0:T(8,128)S(1)} %get-tuple-element.294), channel_id=1, source_target_pairs={{0,1},{1,0},{2,3},{3,2},{4,5},{5,4},{6,7},{7,6},{8,9},{9,8},{10,11... | collective-permute-start | bytes 798728 | tf_op jit(solution)/shard_map/ppermute | solution.py:334
  281.9 19.6 %collective-permute-start.80 = (f32[520,128]{1,0:T(8,128)S(1)}, f32[520,128]{1,0:T(8,128)S(1)}, u32[]{:S(2)}, u32[]{:S(2)}) collective-permute-start(f32[520,128]{1,0:T(8,128)S(1)} %get-tuple-element.295), channel_id=1, source_target_pairs={{0,9},{1,8},{2,11},{3,10},{4,13},{5,12},{6,15},{7,14},{8,1},{9,0},... | collective-permute-start | bytes 798728 | tf_op jit(solution)/shard_map/ppermute | solution.py:334
  287.7 13.8 %collective-permute-start.83 = (f32[512,128]{1,0:T(8,128)S(1)}, f32[512,128]{1,0:T(8,128)S(1)}, u32[]{:S(2)}, u32[]{:S(2)}) collective-permute-start(f32[512,128]{1,0:T(8,128)S(1)} %get-tuple-element.299), channel_id=1, source_target_pairs={{0,9},{1,8},{2,11},{3,10},{4,13},{5,12},{6,15},{7,14},{8,1},{9,0},... | collective-permute-start | bytes 786440 | tf_op jit(solution)/shard_map/ppermute | solution.py:334
  306.8 9.9 %collective-permute-start.95 = (f32[256,128]{1,0:T(8,128)S(1)}, f32[256,128]{1,0:T(8,128)S(1)}, u32[]{:S(2)}, u32[]{:S(2)}) collective-permute-start(f32[256,128]{1,0:T(8,128)S(1)} %get-tuple-element.316), channel_id=1, source_target_pairs={{0,1},{1,0},{2,3},{3,2},{4,5},{5,4},{6,7},{7,6},{8,9},{9,8},{10,11... | collective-permute-start | bytes 393224 | tf_op jit(solution)/shard_map/ppermute | solution.py:334
  307.7 10.8 %collective-permute-start.96 = (f32[256,128]{1,0:T(8,128)S(1)}, f32[256,128]{1,0:T(8,128)S(1)}, u32[]{:S(2)}, u32[]{:S(2)}) collective-permute-start(f32[256,128]{1,0:T(8,128)S(1)} %get-tuple-element.317), channel_id=1, source_target_pairs={{0,9},{1,8},{2,11},{3,10},{4,13},{5,12},{6,15},{7,14},{8,1},{9,0},... | collective-permute-start | bytes 393224 | tf_op jit(solution)/shard_map/ppermute | solution.py:334
  311.0 12.9 %collective-permute-start.90 = (f32[256,128]{1,0:T(8,128)S(1)}, f32[256,128]{1,0:T(8,128)S(1)}, u32[]{:S(2)}, u32[]{:S(2)}) collective-permute-start(f32[256,128]{1,0:T(8,128)S(1)} %get-tuple-element.309), channel_id=1, source_target_pairs={{0,8},{1,9},{2,10},{3,11},{4,12},{5,13},{6,14},{7,15},{8,0},{9,1},... | collective-permute-start | bytes 393224 | tf_op jit(solution)/shard_map/ppermute | solution.py:334
  312.9 11.0 %collective-permute-start.91 = (f32[256,128]{1,0:T(8,128)S(1)}, f32[256,128]{1,0:T(8,128)S(1)}, u32[]{:S(2)}, u32[]{:S(2)}) collective-permute-start(f32[256,128]{1,0:T(8,128)S(1)} %get-tuple-element.310), channel_id=1, source_target_pairs={{0,1},{1,0},{2,3},{3,2},{4,5},{5,4},{6,7},{7,6},{8,9},{9,8},{10,11... | collective-permute-start | bytes 393224 | tf_op jit(solution)/shard_map/ppermute | solution.py:334
  313.7 10.4 %collective-permute-start.92 = (f32[256,128]{1,0:T(8,128)S(1)}, f32[256,128]{1,0:T(8,128)S(1)}, u32[]{:S(2)}, u32[]{:S(2)}) collective-permute-start(f32[256,128]{1,0:T(8,128)S(1)} %get-tuple-element.311), channel_id=1, source_target_pairs={{0,9},{1,8},{2,11},{3,10},{4,13},{5,12},{6,15},{7,14},{8,1},{9,0},... | collective-permute-start | bytes 393224 | tf_op jit(solution)/shard_map/ppermute | solution.py:334
  316.8 21.3 %collective-permute-start.101 = (f32[128,1024]{1,0:T(8,128)}, f32[128,1024]{1,0:T(8,128)}, u32[]{:S(2)}, u32[]{:S(2)}) collective-permute-start(f32[128,1024]{1,0:T(8,128)} %get-tuple-element.324), channel_id=1, source_target_pairs={{0,4},{1,5},{2,0},{3,1},{4,6},{5,7},{6,2},{7,3},{8,12},{9,13},{10,... | collective-permute-start | bytes 1572872 | tf_op jit(solution)/shard_map/ppermute | solution.py:334
  320.3 26.1 %collective-permute-start.97 = (f32[128,1024]{1,0:T(8,128)}, f32[128,1024]{1,0:T(8,128)}, u32[]{:S(2)}, u32[]{:S(2)}) collective-permute-start(f32[128,1024]{1,0:T(8,128)} %get-tuple-element.318), channel_id=1, source_target_pairs={{0,6},{1,7},{2,4},{3,5},{4,2},{5,3},{6,0},{7,1},{8,14},{9,15},{10,... | collective-permute-start | bytes 1572872 | tf_op jit(solution)/shard_map/ppermute | solution.py:334
  325.9 42.0 %collective-permute-start.93 = (f32[128,1024]{1,0:T(8,128)}, f32[128,1024]{1,0:T(8,128)}, u32[]{:S(2)}, u32[]{:S(2)}) collective-permute-start(f32[128,1024]{1,0:T(8,128)} %get-tuple-element.312), channel_id=1, source_target_pairs={{0,2},{1,3},{2,6},{3,7},{4,0},{5,1},{6,4},{7,5},{8,10},{9,11},{10,... | collective-permute-start | bytes 1572872 | tf_op jit(solution)/shard_map/ppermute | solution.py:334
  (43 other events, 275.2 us)
